TPU v7x, 128 devices: a whole 4x4x4 slice. The times are simulated.
128 devices in a mesh: head: 4 (over z_lo, core), band: 32 (over y, x, z_hi).
Axes of the slice: x: 4, y: 4, z: 4 (z_hi: 2, z_lo: 2; z = z_hi * 2 + z_lo), core: 2. Of those that a mesh axis runs over, the one named last changes fastest.
Arguments:
- queries: bfloat16 [2048, 5120], P('band', 'head'), may hold values from -20 to 20, as said below
- keys: bfloat16 [2048, 5120], P('band', 'head'), may hold values from -20 to 20, as said below
- values: bfloat16 [2048, 5120], P('band', 'head'), may hold values from -6 to 6
- w_first: bfloat16 [40, 128], replicated, may hold values from -1 to 1
- b_first: float32 [128], replicated, may hold values from -4 to 4
- w_second: bfloat16 [128, 64], replicated, may hold values from -0.5 to 0.5
- b_second: float32 [64], replicated, may hold values from -3 to 3
- rel_table: bfloat16 [65, 64], replicated, may hold values from -4 to 4
- chain_lengths: int32 [4], replicated, may hold values from 1 to 1024, 2048 in all
Outputs:
- context: bfloat16 [2048, 5120], P('band', 'head')
- pair: bfloat16 [64, 2048, 2048], P(None, 'band', 'head')
Inputs may be any that keep to these rules, and one draw needn't show every extreme that they name: Entries of the queries stay within this range. Entries of the keys stay within this range. `chain_lengths`: the chain lengths sum to 2048; the longest chain has exactly 1024 residues.
All inputs are finite; a program needn't handle non-finite values.
Results may differ from a plain program's by a relative error of at most 0.012.
Values may be sent and summed in bfloat16 or wider, within the bound.
No kernel may reach another device: no remote copies, remote signals or barrier semaphores. Data moves between devices by JAX's collectives and lax.ppermute only.
A program may use at most 128 MiB of HBM per device.

v0:
```python
import math

import jax
import jax.numpy as jnp
from jax import lax
from jax.sharding import PartitionSpec as P

HEAD_DIM = 128
CLIP = 32
GAP = 512
BINS = 65


def local(queries, keys, values, w_first, b_first, w_second, b_second, rel_table, chain_lengths):
    tok_rows = queries.shape[0]
    row_width = queries.shape[1]
    head_count = row_width // HEAD_DIM
    band_index = lax.axis_index("band")
    head_index = lax.axis_index("head")
    seq_len = tok_rows * lax.axis_size("band")
    col_count = seq_len // lax.axis_size("head")
    score_scale = 1.0 / math.sqrt(HEAD_DIM)
    local_queries = queries.reshape(tok_rows, head_count, HEAD_DIM)
    piece = lax.all_gather(keys, "band", axis=0, tiled=True)
    keyed = piece.reshape(piece.shape[0], head_count, HEAD_DIM)
    scores = (
        jnp.einsum("qhd,khd->hqk", local_queries, keyed, preferred_element_type=jnp.float32)
        * score_scale
    )
    row_max = jnp.max(scores, axis=2)
    lifted = jnp.exp(scores - row_max[:, :, None])
    row_sum = jnp.sum(lifted, axis=2)
    maps = (lifted / row_sum[:, :, None]).astype(jnp.bfloat16)
    piece = lax.all_gather(values, "band", axis=0, tiled=True)
    valued = piece.reshape(piece.shape[0], head_count, HEAD_DIM)
    summed = jnp.einsum("hqk,khd->qhd", maps, valued, preferred_element_type=jnp.float32)
    context = summed.reshape(tok_rows, row_width).astype(jnp.bfloat16)
    turned_maps = jnp.swapaxes(maps, 1, 2)
    mirrored = lax.all_to_all(turned_maps, "band", split_axis=1, concat_axis=2, tiled=True)
    symmetric = (
        (maps.astype(jnp.float32) + mirrored.astype(jnp.float32)) * (0.5 * seq_len)
    ).astype(jnp.bfloat16)
    hidden = (
        jnp.einsum(
            "hnc,hk->knc",
            lax.all_to_all(symmetric, "head", split_axis=2, concat_axis=0, tiled=True),
            w_first,
            preferred_element_type=jnp.float32,
        )
        + b_first[:, None, None]
    )
    hidden = jnp.maximum(hidden, 0.0).astype(jnp.bfloat16)
    projected = jnp.einsum("knc,ko->onc", hidden, w_second, preferred_element_type=jnp.float32)
    chain_ends = jnp.cumsum(chain_lengths)[:-1]

    def residue_index(positions):
        crossed = jnp.sum((positions[:, None] >= chain_ends[None, :]).astype(jnp.int32), axis=1)
        return positions + GAP * crossed

    row_pos = band_index * tok_rows + jnp.arange(tok_rows, dtype=jnp.int32)
    col_pos = head_index * col_count + jnp.arange(col_count, dtype=jnp.int32)
    bins = (
        jnp.clip(residue_index(col_pos)[None, :] - residue_index(row_pos)[:, None], -CLIP, CLIP)
        + CLIP
    )
    levels = jnp.arange(BINS, dtype=jnp.int32)
    indicator = (bins[None, :, :] == levels[:, None, None]).astype(jnp.bfloat16)
    relative = jnp.einsum("bo,bnc->onc", rel_table, indicator, preferred_element_type=jnp.float32)
    pair = (projected + b_second[:, None, None] + relative).astype(jnp.bfloat16)
    return (context, pair)


def solution(mesh):
    return jax.shard_map(
        local,
        mesh=mesh,
        in_specs=(
            P("band", "head"),
            P("band", "head"),
            P("band", "head"),
            P(),
            P(),
            P(),
            P(),
            P(),
            P(),
        ),
        out_specs=(P("band", "head"), P(None, "band", "head")),
        check_vma=False,
    )
```

profile of v0, /device:TPU:1, one launch (start us, length us, event | category | flops | bytes accessed | tf_op | source)
XLA Modules:
  0.0 312.9 jit_solution(12720565142611550289)
XLA Ops:
  7.2 0.0 copy-start
  7.2 0.0 all-gather.3.cloned.1.call-start
  7.2 0.7 all-gather.3.cloned.1.call-update
  7.9 0.0 all-gather.5.cloned.1.call-start
  8.0 0.7 all-gather.5.cloned.1.call-update
  8.7 92.0 %all-gather.3.cloned.1.call-done = bf16[2048,1280]{1,0:T(8,128)(2,1)} async-done(((bf16[64,1280]{1,0:T(8,128)(2,1)}), bf16[2048,1280]{1,0:T(8,128)(2,1)}) %all-gather.3.cloned.1.call-update) | async-done | bytes 5242896 | tf_op jit(solution)/shard_map/all_gather | solution.py:24
  100.6 8.0 %copy.49 = bf16[2048,1280]{0,1:T(8,128)(2,1)} copy(bf16[2048,1280]{1,0:T(8,128)(2,1)} %all-gather.3.cloned.1.call-done) | data formatting | bytes 10485760 | tf_op jit(solution)/shard_map/all_gather | solution.py:24
  108.6 0.0 copy-done
  108.6 3.3 %fusion.15 = f32[10,64,2048]{2,1,0:T(8,128)S(1)} fusion(bf16[2048,10,128]{0,2,1:T(8,128)(2,1)} %bitcast.55, bf16[64,1280]{1,0:T(8,128)(2,1)S(1)} %copy-done), kind=kOutput, calls=%fused_computation.20 | convolution fusion | flops 335544320 | bytes 10649600 | tf_op jit(solution)/shard_map/qhd,khd->hqk/dot_general | solution.py:27
  111.9 2.6 fusion.24
  114.5 2.3 copy-done.2
  116.8 0.8 fusion.28
  117.7 8.6 %copy.55 = bf16[10,2048,64]{2,0,1:T(8,128)(2,1)} copy(bf16[10,2048,64]{1,2,0:T(8,128)(2,1)S(1)} %fusion.28) | data formatting | bytes 5242880 | tf_op jit(solution)/shard_map/div | solution.py:33
  126.3 11.8 %reshape.90 = bf16[32,2,20480]{2,1,0:T(2,128)(2,1)} reshape(bf16[2048,10,64]{2,1,0:T(8,128)(2,1)} %bitcast.56) | data formatting | bytes 5242880
  138.2 5.6 %all-to-all-start = ((bf16[32,2,20480]{2,1,0:T(2,128)(2,1)}), bf16[32,2,20480]{2,1,0:T(2,128)(2,1)S(1)}, u32[]{:S(2)}, u32[]{:S(2)}) async-start(bf16[32,2,20480]{2,1,0:T(2,128)(2,1)} %reshape.90), calls=%async_computation | async-start | bytes 5242880 | tf_op jit(solution)/shard_map/all_to_all | solution.py:39
  143.8 0.0 copy-done.6
  143.8 0.2 reduce-window.4
  144.0 0.1 convert_reduce_fusion.1
  144.1 39.9 %all-to-all-done = bf16[32,2,20480]{2,1,0:T(2,128)(2,1)S(1)} async-done(((bf16[32,2,20480]{2,1,0:T(2,128)(2,1)}), bf16[32,2,20480]{2,1,0:T(2,128)(2,1)S(1)}, u32[]{:S(2)}, u32[]{:S(2)}) %all-to-all-start) | async-done | bytes 2621472 | tf_op jit(solution)/shard_map/all_to_all | solution.py:39
  183.9 6.7 %reshape.91 = bf16[2048,10,64]{2,1,0:T(8,128)(2,1)} reshape(bf16[32,2,20480]{2,1,0:T(2,128)(2,1)S(1)} %all-to-all-done) | data formatting | bytes 5242880
  190.6 10.5 %copy.78 = f32[10,32,64,64]{3,1,2,0:T(8,128)} copy(bf16[10,32,64,64]{3,0,2,1:T(8,128)(2,1)} %bitcast.57) | data formatting | bytes 7864320 | tf_op jit(solution)/shard_map/convert_element_type | solution.py:41
  201.1 9.9 %reshape.85 = f32[10,64,2048]{2,1,0:T(8,128)} reshape(f32[10,64,32,64]{3,2,1,0:T(8,128)} %bitcast.54) | data formatting | bytes 10485760 | tf_op jit(solution)/shard_map/convert_element_type | solution.py:41
  211.0 5.5 %multiply_convert_fusion = bf16[10,64,2048]{2,1,0:T(8,128)(2,1)S(1)} fusion(f32[10,64,2048]{2,1,0:T(8,128)} %reshape.85, f32[10,64,2048]{2,1,0:T(8,128)} %copy-done.2, f32[10,64]{1,0:T(8,128)S(1)} %get-tuple-element.12), kind=kLoop, calls=%fused_computation.8 | loop fusion | flops 7864320 | bytes 13109760 | tf_op jit(solution)/shard_map/convert_element_type | solution.py:42
  216.5 8.6 %copy.57 = bf16[10,64,2048]{1,0,2:T(8,128)(2,1)} copy(bf16[10,64,2048]{2,1,0:T(8,128)(2,1)S(1)} %multiply_convert_fusion) | data formatting | bytes 5242880 | tf_op jit(solution)/shard_map/convert_element_type | solution.py:42
  225.2 7.5 %reshape.92 = bf16[4,2,163840]{2,1,0:T(2,128)(2,1)} reshape(bf16[2048,10,64]{2,1,0:T(8,128)(2,1)} %bitcast.58) | data formatting | bytes 5242880
  232.7 6.5 %all-to-all-start.1 = ((bf16[4,2,163840]{2,1,0:T(2,128)(2,1)}), bf16[4,2,163840]{2,1,0:T(2,128)(2,1)S(1)}, u32[]{:S(2)}, u32[]{:S(2)}) async-start(bf16[4,2,163840]{2,1,0:T(2,128)(2,1)} %reshape.92), calls=%async_computation.1 | async-start | bytes 5242880 | tf_op jit(solution)/shard_map/all_to_all | solution.py:46
  239.1 0.1 convert_reduce_fusion
  239.2 0.1 clamp_add_fusion
  239.3 0.0 copy-done.3
  239.3 5.0 %fusion.1 = f32[64,512,64]{1,2,0:T(8,128)} fusion(s32[64,512]{1,0:T(8,128)S(1)} %clamp_add_fusion, bf16[65,64]{0,1:T(8,128)(2,1)S(1)} %copy-done.3), kind=kOutput, calls=%fused_computation.4 | convolution fusion | flops 274759680 | bytes 8528000 | tf_op jit(solution)/shard_map/bo,bnc->onc/dot_general | solution.py:68
  244.3 7.9 %copy.52 = bf16[2048,1280]{0,1:T(8,128)(2,1)} copy(bf16[2048,1280]{1,0:T(8,128)(2,1)} %all-gather.5.cloned.1.call-done) | data formatting | bytes 10485760 | tf_op jit(solution)/shard_map/all_gather | solution.py:34
  252.3 6.0 %fusion.14 = bf16[10,8,8,128]{3,2,1,0:T(8,128)(2,1)S(1)} fusion(bf16[2048,10,128]{0,2,1:T(8,128)(2,1)} %bitcast.61, f32[10,64,2048]{2,1,0:T(8,128)} %copy-done.2, f32[10,64]{1,0:T(8,128)S(1)} %get-tuple-element.12), kind=kOutput, calls=%fused_computation.18 | convolution fusion | flops 338247680 | bytes 10652160 | tf_op jit(solution)/shard_map/hqk,khd->qhd/dot_general | solution.py:36
  258.3 0.7 copy.79
  259.0 10.6 %all-to-all-done.1 = bf16[4,2,163840]{2,1,0:T(2,128)(2,1)S(1)} async-done(((bf16[4,2,163840]{2,1,0:T(2,128)(2,1)}), bf16[4,2,163840]{2,1,0:T(2,128)(2,1)S(1)}, u32[]{:S(2)}, u32[]{:S(2)}) %all-to-all-start.1) | async-done | bytes 2621472 | tf_op jit(solution)/shard_map/all_to_all | solution.py:46
  269.6 5.8 %reshape.93 = bf16[2048,10,64]{2,1,0:T(8,128)(2,1)} reshape(bf16[4,2,163840]{2,1,0:T(2,128)(2,1)S(1)} %all-to-all-done.1) | data formatting | bytes 5242880
  275.4 9.7 %copy.66 = bf16[10,64,4,512]{3,2,1,0:T(4,128)(2,1)S(1)} copy(bf16[10,64,4,512]{1,0,3,2:T(8,128)(2,1)} %bitcast.59) | data formatting | bytes 5242880 | tf_op jit(solution)/shard_map/all_to_all | solution.py:46
  285.1 0.0 copy-start.4
  285.1 0.0 copy-start.5
  285.1 0.0 copy-start.7
  285.1 0.0 copy-start.8
  285.1 2.1 copy.59
  287.2 0.0 copy-done.4
  287.2 0.0 copy-done.5
  287.2 0.0 copy-done.7
  287.2 0.0 copy-done.8
  287.3 0.0 copy-start.1
  287.3 12.2 %fusion.8 = bf16[64,64,512]{2,0,1:T(8,128)(2,1)} fusion(f32[64,512,64]{1,2,0:T(8,128)} %fusion.1, f32[64]{0:T(128)S(1)} %copy-done.7, f32[128]{0:T(128)S(1)} %copy-done.8, bf16[40,64,512]{2,1,0:T(8,128)(2,1)} %bitcast.62, bf16[128,64]{0,1:T(8,128)(2,1)S(1)} %copy-done.4, bf16[40,128]{1,0:T(8,128)(2,1)S(1)} %copy-done.5), kind=kOutput, calls=%fused_computation.14 | convolution fusion | flops 891289600 | bytes 15231744 | tf_op jit(solution)/shard_map/knc,ko->onc/dot_general | solution.py:53
  299.5 6.5 %copy.62 = bf16[64,64,512]{2,1,0:T(8,128)(2,1)} copy(bf16[64,64,512]{2,0,1:T(8,128)(2,1)} %fusion.8) | data formatting | bytes 8388608
  (10 shorter events, 0.0 us)
Async XLA Ops:
  7.2 101.4 %copy-start = (bf16[64,1280]{1,0:T(8,128)(2,1)S(1)}, bf16[64,1280]{1,0:T(8,128)(2,1)}, u32[]{:S(2)}) copy-start(bf16[64,1280]{1,0:T(8,128)(2,1)} %param.9) | copy-start | bytes 491524
  7.2 93.4 %all-gather.3.cloned.1.call-start = ((), (), s32[]{:S(2)}) async-start(), calls=%async_computation.2 | async-start | bytes 5406720 | tf_op jit(solution)/shard_map/all_gather | solution.py:24
  7.9 236.4 %all-gather.5.cloned.1.call-start = ((), (), s32[]{:S(2)}) async-start(), calls=%async_computation.3 | async-start | bytes 5406720 | tf_op jit(solution)/shard_map/all_gather | solution.py:34
  114.5 2.3 copy-start.2
  138.2 5.6 %copy-start.6 = (s32[4]{0:T(128)S(1)}, s32[4]{0:T(128)}, u32[]{:S(2)}) copy-start(s32[4]{0:T(128)} %param.17) | copy-start | bytes 52
  138.2 45.8 %all-to-all-start = ((bf16[32,2,20480]{2,1,0:T(2,128)(2,1)}), bf16[32,2,20480]{2,1,0:T(2,128)(2,1)S(1)}, u32[]{:S(2)}, u32[]{:S(2)}) async-start(bf16[32,2,20480]{2,1,0:T(2,128)(2,1)} %reshape.90), calls=%async_computation | async-start | bytes 5242880 | tf_op jit(solution)/shard_map/all_to_all | solution.py:39
  232.7 6.7 %copy-start.3 = (bf16[65,64]{0,1:T(8,128)(2,1)S(1)}, bf16[65,64]{0,1:T(8,128)(2,1)}, u32[]{:S(2)}) copy-start(bf16[65,64]{0,1:T(8,128)(2,1)} %param.16) | copy-start | bytes 24964
  232.7 36.9 %all-to-all-start.1 = ((bf16[4,2,163840]{2,1,0:T(2,128)(2,1)}), bf16[4,2,163840]{2,1,0:T(2,128)(2,1)S(1)}, u32[]{:S(2)}, u32[]{:S(2)}) async-start(bf16[4,2,163840]{2,1,0:T(2,128)(2,1)} %reshape.92), calls=%async_computation.1 | async-start | bytes 5242880 | tf_op jit(solution)/shard_map/all_to_all | solution.py:46
  285.1 2.1 copy-start.4
  285.1 2.1 copy-start.5
  285.1 2.1 copy-start.7
  285.1 2.1 copy-start.8
  287.3 18.8 %copy-start.1 = (bf16[64,1280]{1,0:T(8,128)(2,1)S(1)}, bf16[64,1280]{1,0:T(8,128)(2,1)}, u32[]{:S(2)}) copy-start(bf16[64,1280]{1,0:T(8,128)(2,1)} %param.9) | copy-start | bytes 491524
Sparse Core Ops, SparseCore 0:
  11.0 89.5 all-gather.2
  103.6 101.0 all-gather.4
where the time goes:
time: 314 us; the launch traced here: 313 us
  waiting for transfers between devices  144 us (46%)
  local copies, waits for them, and re-layouts  107 us (34%)
  matrix products  26.6 us (8%)
  between operations  14.2 us (5%)
  starting transfers between devices  12.1 us (4%)
  other arithmetic  9.43 us (3%)
    all_gather x1, waiting for transfers between devices, local(): piece = lax.all_gather(keys, 'band', axis=0, tiled=True)  92 us
    unnamed x23, local copies, waits for them, and re-layouts  40.7 us
    all_to_all x1, waiting for transfers between devices, local(): lax.all_to_all(turned_maps, 'band', split_axis=1, concat_axis=2, tiled=True)  39.9 us
    convert_element_type x2, local copies, waits for them, and re-layouts, local(): mirrored.astype(jnp.float32)  20.4 us
    dot_general x1, matrix products, local(): jnp.einsum('knc,ko->onc', hidden, w_second, preferred_element_type=jnp.fl...  12.2 us
    all_to_all x2, local copies, waits for them, and re-layouts, local(): lax.all_to_all(symmetric, 'head', split_axis=2, concat_axis=0, tiled=True)  11.8 us
    all_to_all x1, waiting for transfers between devices, local(): lax.all_to_all(symmetric, 'head', split_axis=2, concat_axis=0, tiled=True)  10.6 us
    convert_element_type x1, local copies, waits for them, and re-layouts, local(): symmetric = ((maps.astype(jnp.float32) + mirrored.astype(jnp.float32)) *...  8.65 us
  transfers between devices with their start and end apart: 4, of which 3 were waited for; matrix products, arithmetic and copies ran while one was open for 33% of the time, Pallas kernels for 0%

commit v1 on v0

v1 whole, which is shorter than its diff:
```python
import functools
import itertools
import math

import jax
import jax.numpy as jnp
from jax import lax
from jax.experimental import pallas as pl
from jax.experimental.pallas import tpu as pltpu
from jax.sharding import PartitionSpec as P

HEAD_DIM = 128
CLIP = 32
GAP = 512
BINS = 65
GROUP = 5
WIDE = GROUP * HEAD_DIM
BLOCK = 128
HALF = 64
TILE = 512
ROWS = 16
SCALE = math.log2(math.e) / math.sqrt(HEAD_DIM)
AXES = ("head", "band")
MIB = 1 << 20


def place(y, x, z, c):
    return c * 32 + y * 8 + x * 2 + z


def moves(to):
    return [
        (place(y, x, z, c), place(*to(y, x, z, c)))
        for c, y, x, z in itertools.product(range(4), range(4), range(4), range(2))
    ]


def send(value, to):
    return lax.ppermute(value, AXES, moves(to))


def nt(a, b):
    return lax.dot_general(a, b, (((1,), (1,)), ((), ())), preferred_element_type=jnp.float32)


def fetch(where, row_blocks, column_blocks, rows_ref, columns_ref, sems):
    y, x, z, c = (where[i] for i in range(4))
    copies = []
    for d in range(4):
        away = lax.rem(lax.bitwise_xor(c, d) - y + 4, 4)
        for part in range(2):
            start = pl.multiple_of(away * BLOCK + lax.bitwise_xor(z, part) * HALF, HALF)
            copies.append(
                pltpu.make_async_copy(
                    row_blocks[d].at[pl.ds(part * HALF, HALF), pl.ds(0, 2 * WIDE)],
                    rows_ref.at[pl.ds(start, HALF)],
                    sems.at[2 * d + part],
                )
            )
        start = pl.multiple_of(lax.rem(x - d + 4, 4) * BLOCK, BLOCK)
        copies.append(
            pltpu.make_async_copy(
                column_blocks[d], columns_ref.at[pl.ds(start, BLOCK)], sems.at[8 + d]
            )
        )
    for copy in copies:
        copy.start()
    for copy in copies:
        copy.wait()


def head(ref, part, h, rows=slice(None)):
    return ref[rows, part * WIDE + h * HEAD_DIM : part * WIDE + (h + 1) * HEAD_DIM]


def stats_kernel(where, *refs):
    row_blocks, column_blocks = refs[0:4], refs[4:8]
    by_row, by_column, rows_ref, columns_ref, sems = refs[8:]
    fetch(where, row_blocks, column_blocks, rows_ref, columns_ref, sems)
    by_row[...] = jnp.zeros_like(by_row)
    by_column[...] = jnp.zeros_like(by_column)
    for h in range(GROUP):
        for out, left, right in (
            (by_row, head(columns_ref, 1, h), head(rows_ref, 0, h)),
            (by_column, head(rows_ref, 1, h), head(columns_ref, 0, h)),
        ):
            scores = nt(left, right) * SCALE
            top = jnp.max(scores, axis=0, keepdims=True)
            out[h : h + 1, :] = top
            out[8 + h : 9 + h, :] = jnp.sum(jnp.exp2(scores - top), axis=0, keepdims=True)


def merged(refs):
    top = functools.reduce(jnp.maximum, [ref[0:8, :] for ref in refs])
    total = sum(ref[8:16, :] * jnp.exp2(ref[0:8, :] - top) for ref in refs)
    return top, total


def turned(value):
    return jnp.transpose(jnp.concatenate([value] * 16, axis=0))


def symmetric_kernel(where, *refs):
    row_blocks, column_blocks, row_stats, column_stats = refs[0:4], refs[4:8], refs[8:12], refs[12:16]
    outs = refs[16:24]
    rows_ref, columns_ref, sems = refs[24:]
    fetch(where, row_blocks, column_blocks, rows_ref, columns_ref, sems)
    row_top, row_total = merged(row_stats)
    column_top, column_total = merged(column_stats)
    row_top, row_gain = turned(row_top), turned(1024.0 / row_total)
    column_gain = 1024.0 / column_total
    for h in range(GROUP):
        straight = nt(head(rows_ref, 0, h), head(columns_ref, 1, h)) * SCALE
        mirrored = nt(head(rows_ref, 1, h), head(columns_ref, 0, h)) * SCALE
        summed = (
            jnp.exp2(straight - row_top[:, h : h + 1]) * row_gain[:, h : h + 1]
            + jnp.exp2(mirrored - column_top[h : h + 1, :]) * column_gain[h : h + 1, :]
        ).astype(jnp.bfloat16)
        for p in range(8):
            outs[p][h] = summed[p * HALF : (p + 1) * HALF]


def context_kernel(where, *refs):
    row_blocks, column_blocks, row_stats = refs[0:4], refs[4:8], refs[8:12]
    outs = refs[12:16]
    rows_ref, columns_ref, held, sems = refs[16:]
    fetch(where, row_blocks, column_blocks, rows_ref, columns_ref, sems)
    row_top, row_total = merged(row_stats)
    row_top, row_gain = turned(row_top), turned(1.0 / row_total)
    for h in range(GROUP):
        straight = nt(head(rows_ref, 0, h), head(columns_ref, 1, h)) * SCALE
        maps = jnp.exp2(straight - row_top[:, h : h + 1]) * row_gain[:, h : h + 1]
        part = jnp.dot(
            maps.astype(jnp.bfloat16), head(columns_ref, 2, h), preferred_element_type=jnp.float32
        )
        held[:, h * HEAD_DIM : (h + 1) * HEAD_DIM] = part.astype(jnp.bfloat16)
    y, c = where[0], where[3]
    for d in range(4):
        away = lax.rem(lax.bitwise_xor(c, d) - y + 4, 4)
        outs[d][...] = held[pl.ds(pl.multiple_of(away * BLOCK, BLOCK), BLOCK), :]


def relative_kernel(row_residue, column_residue, table, out):
    bins = (
        jnp.clip(column_residue[...] - row_residue[...], -CLIP, CLIP) + CLIP
    )
    for half in range(2):
        own = bins[half * 8 : half * 8 + 8]
        levels = lax.broadcasted_iota(jnp.int32, (72, 8, TILE), 0)
        spread = (own[None] == levels).astype(jnp.float32).reshape(72 * 8, TILE)
        part = jnp.dot(
            table[...], spread.astype(jnp.bfloat16), preferred_element_type=jnp.float32
        )
        part = part.reshape(-1, 8, TILE)
        if half == 0:
            first = part
    out[...] = jnp.concatenate([first, part], axis=1).astype(jnp.bfloat16)


def pair_kernel(*refs):
    tiles = refs[0:8]
    first, first_bias, second, second_bias, relative, out = refs[8:]
    loaded = [ref[...].astype(jnp.float32) for ref in tiles]
    halves = []
    for half in range(2):
        stacked = jnp.concatenate(
            [t[:, half * 8 : half * 8 + 8, :].reshape(GROUP * 8, TILE) for t in loaded], axis=0
        ).astype(jnp.bfloat16)
        hidden = jnp.dot(first[...], stacked, preferred_element_type=jnp.float32)
        hidden = jnp.maximum(hidden + jnp.concatenate([first_bias[...]] * 4, axis=1), 0.0)
        projected = jnp.dot(
            second[...], hidden.astype(jnp.bfloat16), preferred_element_type=jnp.float32
        )
        projected = projected + jnp.concatenate([second_bias[...]] * 4, axis=1)
        halves.append(projected.reshape(-1, 8, TILE))
    out[...] = (
        jnp.concatenate(halves, axis=1) + relative[...].astype(jnp.float32)
    ).astype(jnp.bfloat16)


SMEM = pl.BlockSpec(memory_space=pltpu.SMEM)
ANY = pl.BlockSpec(memory_space=pl.ANY)
VMEM = pl.BlockSpec(memory_space=pltpu.VMEM)


def params(mib):
    return pltpu.CompilerParams(vmem_limit_bytes=mib * MIB)


def blocks_scratch():
    return [
        pltpu.VMEM((TILE, 2 * WIDE), jnp.bfloat16),
        pltpu.VMEM((TILE, 3 * WIDE), jnp.bfloat16),
    ]


def shape(dims, kind=jnp.bfloat16):
    return jax.ShapeDtypeStruct(dims, kind)


def local(queries, keys, values, w_first, b_first, w_second, b_second, rel_table, chain_lengths):
    band, c = lax.axis_index("band"), lax.axis_index("head")
    y, x, z = band // 8, (band // 2) % 4, band % 2
    where = jnp.stack([y, x, z, c]).astype(jnp.int32)
    hid, outs = w_first.shape[1], w_second.shape[1]

    chain_ends = jnp.cumsum(chain_lengths)[:-1]

    def residue_index(positions):
        crossed = jnp.sum((positions[:, None] >= chain_ends[None, :]).astype(jnp.int32), axis=1)
        return positions + GAP * crossed

    row_residue = residue_index(band * HALF + jnp.arange(HALF, dtype=jnp.int32))[:, None]
    column_residue = residue_index(c * TILE + jnp.arange(TILE, dtype=jnp.int32))[None, :]
    eye = jnp.eye(8, dtype=jnp.bfloat16)

    def spread(matrix):
        wide = matrix[:, None, :, None] * eye[None, :, None, :]
        return wide.reshape(matrix.shape[0] * 8, matrix.shape[1] * 8)

    table = spread(jnp.pad(rel_table, ((0, 72 - BINS), (0, 0))).T)
    relative = pl.pallas_call(
        relative_kernel,
        grid=(HALF // ROWS,),
        in_specs=[
            pl.BlockSpec((ROWS, 1), lambda i: (i, 0)),
            pl.BlockSpec((1, TILE), lambda i: (0, 0)),
            pl.BlockSpec((outs * 8, 72 * 8), lambda i: (0, 0)),
        ],
        out_specs=pl.BlockSpec((outs, ROWS, TILE), lambda i: (0, i, 0)),
        out_shape=shape((outs, HALF, TILE)),
        compiler_params=params(40),
        name="relative",
    )(row_residue, column_residue, table)

    near = jnp.concatenate([queries[:, :WIDE], keys[:, :WIDE], values[:, :WIDE]], axis=1)
    far = jnp.concatenate([queries[:, WIDE:], keys[:, WIDE:], values[:, WIDE:]], axis=1)
    same = send(jnp.where(z == 0, near, far), lambda y, x, z, c: (c, x, z, y))
    other = send(jnp.where(z == 0, far, near), lambda y, x, z, c: (c, x, 1 - z, y))
    block = jnp.where(
        z == 0,
        jnp.concatenate([same, other], axis=0),
        jnp.concatenate([other, same], axis=0),
    )

    column_blocks = [block] + [
        send(block, lambda y, x, z, c, d=d: (y, (x + d) % 4, z, c)) for d in (1, 2, 3)
    ]
    narrow = block[:, : 2 * WIDE]
    row_blocks = [narrow] + [send(narrow, lambda y, x, z, c, d=d: (y, x, z, c ^ d)) for d in (1, 2, 3)]
    blocks = row_blocks + column_blocks

    by_row, by_column = pl.pallas_call(
        stats_kernel,
        in_specs=[SMEM] + [ANY] * 8,
        out_specs=[VMEM, VMEM],
        out_shape=[shape((16, TILE), jnp.float32)] * 2,
        scratch_shapes=blocks_scratch() + [pltpu.SemaphoreType.DMA((12,))],
        compiler_params=params(40),
        name="stats",
    )(where, *blocks)
    row_stats = [by_row] + [send(by_row, lambda y, x, z, c, d=d: (y, x, z, c ^ d)) for d in (1, 2, 3)]
    column_stats = [by_column] + [
        send(by_column, lambda y, x, z, c, d=d: (y, (x + d) % 4, z, c)) for d in (1, 2, 3)
    ]

    tiles = pl.pallas_call(
        symmetric_kernel,
        in_specs=[SMEM] + [ANY] * 8 + [VMEM] * 8,
        out_specs=[VMEM] * 8,
        out_shape=[shape((GROUP, HALF, TILE))] * 8,
        scratch_shapes=blocks_scratch() + [pltpu.SemaphoreType.DMA((12,))],
        compiler_params=params(40),
        name="symmetric",
    )(where, *blocks, *row_stats, *column_stats)
    received = [
        tiles[p]
        if p == 0
        else send(tiles[p], lambda y, x, z, c, p=p: ((y + p // 2) % 4, x, z ^ (p % 2), c))
        for p in range(8)
    ]

    partials = pl.pallas_call(
        context_kernel,
        in_specs=[SMEM] + [ANY] * 8 + [VMEM] * 4,
        out_specs=[VMEM] * 4,
        out_shape=[shape((BLOCK, WIDE))] * 4,
        scratch_shapes=blocks_scratch()
        + [pltpu.VMEM((TILE, WIDE), jnp.bfloat16), pltpu.SemaphoreType.DMA((12,))],
        compiler_params=params(40),
        name="context",
    )(where, *blocks, *row_stats)
    summed = partials[0].astype(jnp.float32)
    for d in (1, 2, 3):
        summed = summed + send(partials[d], lambda y, x, z, c, d=d: (y, x, z, c ^ d)).astype(jnp.float32)
    summed = summed.astype(jnp.bfloat16)
    same = send(summed[:HALF], lambda y, x, z, c: (c, x, z, y))
    other = send(summed[HALF:], lambda y, x, z, c: (c, x, 1 - z, y))
    context = jnp.where(
        z == 0,
        jnp.concatenate([same, other], axis=1),
        jnp.concatenate([other, same], axis=1),
    )

    order = jnp.stack([2 * ((y - p // 2) % 4) + z * (1 - p % 2) + (1 - z) * (p % 2) for p in range(8)])
    first = spread(jnp.take(w_first.reshape(8, GROUP, hid), order, axis=0).reshape(8 * GROUP, hid).T)
    second = spread(w_second.T)
    first_bias = jnp.broadcast_to(b_first[:, None, None], (hid, 8, 128)).reshape(hid * 8, 128)
    second_bias = jnp.broadcast_to(b_second[:, None, None], (outs, 8, 128)).reshape(outs * 8, 128)
    pair = pl.pallas_call(
        pair_kernel,
        grid=(HALF // ROWS,),
        in_specs=[pl.BlockSpec((GROUP, ROWS, TILE), lambda i: (0, i, 0))] * 8
        + [
            pl.BlockSpec((hid * 8, 8 * GROUP * 8), lambda i: (0, 0)),
            pl.BlockSpec((hid * 8, 128), lambda i: (0, 0)),
            pl.BlockSpec((outs * 8, hid * 8), lambda i: (0, 0)),
            pl.BlockSpec((outs * 8, 128), lambda i: (0, 0)),
            pl.BlockSpec((outs, ROWS, TILE), lambda i: (0, i, 0)),
        ],
        out_specs=pl.BlockSpec((outs, ROWS, TILE), lambda i: (0, i, 0)),
        out_shape=shape((outs, HALF, TILE)),
        compiler_params=params(40),
        name="pair",
    )(*received, first, first_bias, second, second_bias, relative)
    return (context, pair)


def solution(mesh):
    return jax.shard_map(
        local,
        mesh=mesh,
        in_specs=(
            P("band", "head"),
            P("band", "head"),
            P("band", "head"),
            P(),
            P(),
            P(),
            P(),
            P(),
            P(),
        ),
        out_specs=(P("band", "head"), P(None, "band", "head")),
        check_vma=False,
    )
```

time: 314 us -> 193 us (0.61)
  waiting for transfers between devices: 144 us -> 19.9 us
  local copies, waits for them, and re-layouts: 107 us -> 63 us
  starting transfers between devices: 12.1 us -> 52.9 us
  Pallas kernels: 0 us -> 36.3 us
  matrix products: 26.6 us -> 0 us
  between operations: 14.2 us -> 1.08 us
  other arithmetic: 9.43 us -> 17.5 us
    all_gather x2 -> x0, waiting for transfers between devices: 92 us -> none  [the longest x1 92 us: local(): piece = lax.all_gather(keys, 'band', axis=0, tiled=True)]
    mul x0 -> x6, local copies, waits for them, and re-layouts: none -> 57 us  [the longest x5 56.9 us: spread(): wide = matrix[:, None, :, None] * eye[None, :, None, :]]
    ppermute x0 -> x26, starting transfers between devices: none -> 52.9 us  [send(): return lax.ppermute(value, AXES, moves(to))]
    all_to_all x2 -> x0, waiting for transfers between devices: 50.4 us -> none  [the longest x1 39.9 us: local(): lax.all_to_all(turned_maps, 'band', split_axis=1, concat_axis=2, tiled=True)]
    unnamed x23 -> x16, local copies, waits for them, and re-layouts: 40.7 us -> 0.75 us
    pallas_call x0 -> x5, Pallas kernels: none -> 36.3 us  [the longest x1 11.8 us: local(): pl.pallas_call(pair_kernel, grid=(HALF // ROWS,), in_specs=[pl.BlockSpec(...]
    convert_element_type x4 -> x1, local copies, waits for them, and re-layouts: 29.7 us -> 0.08 us  [local(): eye = jnp.eye(8, dtype=jnp.bfloat16)]
    dot_general x4 -> x0, matrix products: 26.6 us -> none  [the longest x1 12.2 us: local(): jnp.einsum('knc,ko->onc', hidden, w_second, preferred_element_type=jnp.fl...]
  transfers between devices with their start and end apart: 4 -> 26, of which waited for: 3 -> 8; matrix products, arithmetic and copies ran while one was open for 33% -> 41% of each run, Pallas kernels for 0% -> 9%
where the time goes in v1:
time: 193 us; the launch traced here: 191 us
  local copies, waits for them, and re-layouts  63 us (33%)
  starting transfers between devices  52.9 us (27%)
  Pallas kernels  36.3 us (19%)
  waiting for transfers between devices  19.9 us (10%)
  other arithmetic  17.5 us (9%)
    mul x5, local copies, waits for them, and re-layouts, spread(): wide = matrix[:, None, :, None] * eye[None, :, None, :]  56.9 us
    ppermute x26, starting transfers between devices, send(): return lax.ppermute(value, AXES, moves(to))  52.9 us
    ppermute x26, waiting for transfers between devices, send(): return lax.ppermute(value, AXES, moves(to))  19.9 us
    mul x3, other arithmetic, spread(): wide = matrix[:, None, :, None] * eye[None, :, None, :]  15 us
    pallas_call x1, Pallas kernels, local(): pl.pallas_call(pair_kernel, grid=(HALF // ROWS,), in_specs=[pl.BlockSpec(...  11.8 us
    pallas_call x1, Pallas kernels, local(): pl.pallas_call(symmetric_kernel, in_specs=[SMEM] + [ANY] * 8 + [VMEM] * 8...  7.45 us
    pallas_call x1, Pallas kernels, local(): pl.pallas_call(stats_kernel, in_specs=[SMEM] + [ANY] * 8, out_specs=[VMEM...  6.78 us
    pallas_call x1, Pallas kernels, local(): pl.pallas_call(context_kernel, in_specs=[SMEM] + [ANY] * 8 + [VMEM] * 4,...  5.81 us
  transfers between devices with their start and end apart: 26, of which 8 were waited for; matrix products, arithmetic and copies ran while one was open for 41% of the time, Pallas kernels for 9%

profile of v1, /device:TPU:1, one launch (start us, length us, event | category | flops | bytes accessed | tf_op | source)
XLA Modules:
  0.0 190.7 jit_solution(16997094816604871014)
XLA Ops:
  0.7 0.9 fusion.5
  1.6 1.0 fusion.3
  2.7 6.1 %collective-permute-start.1 = (bf16[64,1920]{1,0:T(8,128)(2,1)S(1)}, bf16[64,1920]{1,0:T(8,128)(2,1)S(1)}, u32[]{:S(2)}, u32[]{:S(2)}) collective-permute-start(bf16[64,1920]{1,0:T(8,128)(2,1)S(1)} %get-tuple-element.31), channel_id=1, source_target_pairs={{0,1},{1,0},{2,3},{3,2},{4,5},{5,4},{6,7},{7,6},{8,33},{9,32},{10,... | collective-permute-start | bytes 737288 | tf_op jit(solution)/shard_map/ppermute | solution.py:39
  8.8 1.9 %collective-permute-start = (bf16[64,1920]{1,0:T(8,128)(2,1)S(1)}, bf16[64,1920]{1,0:T(8,128)(2,1)S(1)}, u32[]{:S(2)}, u32[]{:S(2)}) collective-permute-start(bf16[64,1920]{1,0:T(8,128)(2,1)S(1)} %get-tuple-element.30), channel_id=1, source_target_pairs={{0,0},{1,1},{2,2},{3,3},{4,4},{5,5},{6,6},{7,7},{8,32},{9,33},{10,... | collective-permute-start | bytes 737288 | tf_op jit(solution)/shard_map/ppermute | solution.py:39
  10.8 0.7 reshape.439
  11.7 0.6 gather_fusion
  12.6 0.7 pad_bitcast_fusion
  13.5 4.3 %broadcast_multiply_fusion.2 = bf16[64,8,72,8]{1,0,3,2:T(8,128)(2,1)} fusion(bf16[8,8]{0,1:T(8,128)(2,1)S(1)} %fusion, bf16[64,72]{0,1:T(8,128)(2,1)S(1)} %copy.26), kind=kLoop, calls=%fused_computation.3 | loop fusion | flops 294912 | bytes 599168 | tf_op jit(solution)/shard_map/mul | solution.py:218
  17.8 6.0 %broadcast_multiply_fusion = bf16[64,8,128,8]{3,2,1,0:T(8,128)(2,1)} fusion(bf16[8,8]{1,0:T(8,128)(2,1)S(1)} %copy.23, bf16[64,128]{1,0:T(8,128)(2,1)S(1)} %bitcast.43), kind=kLoop, calls=%fused_computation.1 | loop fusion | flops 524288 | bytes 1065088 | tf_op jit(solution)/shard_map/mul | solution.py:218
  23.8 4.8 %broadcast_multiply_fusion.1 = bf16[128,8,40,8]{1,0,3,2:T(8,128)(2,1)} fusion(bf16[8,8]{0,1:T(8,128)(2,1)S(1)} %fusion, bf16[128,40]{0,1:T(8,128)(2,1)S(1)} %select_bitcast_fusion), kind=kLoop, calls=%fused_computation.2 | loop fusion | flops 327680 | bytes 665728 | tf_op jit(solution)/shard_map/mul | solution.py:218
  29.0 1.3 collective-permute-start.5
  30.2 2.5 %collective-permute-start.6 = (bf16[128,1920]{1,0:T(8,128)(2,1)S(1)}, bf16[128,1920]{1,0:T(8,128)(2,1)S(1)}, u32[]{:S(2)}, u32[]{:S(2)}) collective-permute-start(bf16[128,1920]{1,0:T(8,128)(2,1)S(1)} %maximum_select_fusion.refs_4_), channel_id=1, source_target_pairs={{0,4},{1,5},{2,6},{3,7},{4,0},{5,1},{6,2},{7,3},{8,12},{9,13},{10,... | collective-permute-start | bytes 1474568 | tf_op jit(solution)/shard_map/ppermute | solution.py:39
  32.7 1.2 collective-permute-start.7
  33.9 3.6 %collective-permute-start.3 = (bf16[128,1280]{1,0:T(8,128)(2,1)S(1)}, bf16[128,1280]{1,0:T(8,128)(2,1)S(1)}, u32[]{:S(2)}, u32[]{:S(2)}) collective-permute-start(bf16[128,1280]{1,0:T(8,128)(2,1)S(1)} %slice.43.refs_0_), channel_id=1, source_target_pairs={{0,64},{1,65},{2,66},{3,67},{4,68},{5,69},{6,70},{7,71},{8,72},{9,... | collective-permute-start | bytes 983048 | tf_op jit(solution)/shard_map/ppermute | solution.py:39
  37.6 0.9 collective-permute-start.4
  38.6 6.1 %collective-permute-done.3.refs_2_ = bf16[128,1280]{1,0:T(8,128)(2,1)S(1)} collective-permute-done((bf16[128,1280]{1,0:T(8,128)(2,1)S(1)}, bf16[128,1280]{1,0:T(8,128)(2,1)S(1)}, u32[]{:S(2)}, u32[]{:S(2)}) %collective-permute-start.3) | collective-permute-done | bytes 327712 | tf_op jit(solution)/shard_map/ppermute | solution.py:39
  44.7 8.1 %collective-permute-done.4.refs_3_ = bf16[128,1280]{1,0:T(8,128)(2,1)S(1)} collective-permute-done((bf16[128,1280]{1,0:T(8,128)(2,1)S(1)}, bf16[128,1280]{1,0:T(8,128)(2,1)S(1)}, u32[]{:S(2)}, u32[]{:S(2)}) %collective-permute-start.4) | collective-permute-done | bytes 327712 | tf_op jit(solution)/shard_map/ppermute | solution.py:39
  52.9 1.3 collective-permute-done.6.refs_6_
  54.1 6.8 %stats.1 = (f32[16,512]{1,0:T(8,128)S(1)}, f32[16,512]{1,0:T(8,128)S(1)}) custom-call(s32[4]{0:T(128)S(1)} %pad_add_fusion.where, bf16[128,1280]{1,0:T(8,128)(2,1)S(1)} %slice.43.refs_0_, bf16[128,1280]{1,0:T(8,128)(2,1)S(1)} %collective-permute-done.2.refs_1_, bf16[128,1280]{1,0:T(8,128)(2,1)S(1)} %collective-permute-done.3.refs_2_, ...), custom_call_target="tpu_custom_call" | custom-call | tf_op jit(solution)/shard_map/stats/pallas_call | solution.py:253
  60.9 1.3 collective-permute-start.8
  62.3 3.6 %collective-permute-start.9 = (f32[16,512]{1,0:T(8,128)S(1)}, f32[16,512]{1,0:T(8,128)S(1)}, u32[]{:S(2)}, u32[]{:S(2)}) collective-permute-start(f32[16,512]{1,0:T(8,128)S(1)} %get-tuple-element.16.refs_8_), channel_id=1, source_target_pairs={{0,64},{1,65},{2,66},{3,67},{4,68},{5,69},{6,70},{7,71},{8,72},{9,... | collective-permute-start | bytes 98312 | tf_op jit(solution)/shard_map/ppermute | solution.py:39
  66.0 1.1 collective-permute-start.16
  67.1 0.5 collective-permute-done.9.refs_10_
  67.6 1.7 collective-permute-done.10.refs_11_
  69.3 5.8 %context.1 = (bf16[128,640]{1,0:T(8,128)(2,1)S(1)}, bf16[128,640]{1,0:T(8,128)(2,1)S(1)}, bf16[128,640]{1,0:T(8,128)(2,1)S(1)}, bf16[128,640]{1,0:T(8,128)(2,1)S(1)}) custom-call(s32[4]{0:T(128)S(1)} %pad_add_fusion.where, bf16[128,1280]{1,0:T(8,128)(2,1)S(1)} %slice.43.refs_0_, bf16[128,1280]{1,0:T(8,128)(2,1)S(1)} %collective-permute-done.2.refs_1_, ...), custom_call_target="tpu_custom_call" | custom-call | tf_op jit(solution)/shard_map/context/pallas_call | solution.py:283
  75.1 0.8 collective-permute-start.13
  75.8 1.0 collective-permute-start.12
  76.9 0.4 collective-permute-start.11
  77.3 2.4 %collective-permute-start.17 = (f32[16,512]{1,0:T(8,128)S(1)}, f32[16,512]{1,0:T(8,128)S(1)}, u32[]{:S(2)}, u32[]{:S(2)}) collective-permute-start(f32[16,512]{1,0:T(8,128)S(1)} %get-tuple-element.21.refs_12_), channel_id=1, source_target_pairs={{0,4},{1,5},{2,6},{3,7},{4,0},{5,1},{6,2},{7,3},{8,12},{9,13},{10,... | collective-permute-start | bytes 98312 | tf_op jit(solution)/shard_map/ppermute | solution.py:39
  79.7 1.1 collective-permute-start.18
  80.8 0.7 collective-permute-done.17.refs_14_
  81.6 1.2 collective-permute-done.18.refs_15_
  82.8 7.5 %symmetric.1 = (bf16[5,64,512]{2,1,0:T(8,128)(2,1)S(1)}, bf16[5,64,512]{2,1,0:T(8,128)(2,1)S(1)}, bf16[5,64,512]{2,1,0:T(8,128)(2,1)S(1)}, bf16[5,64,512]{2,1,0:...) custom-call(s32[4]{0:T(128)S(1)} %pad_add_fusion.where, ...), custom_call_target="tpu_custom_call" | custom-call | tf_op jit(solution)/shard_map/symmetric/pallas_call | solution.py:267
  90.2 0.7 copy-done
  91.2 5.4 %collective-permute-start.15 = (bf16[64,640]{1,0:T(8,128)(2,1)S(1)}, bf16[64,640]{1,0:T(8,128)(2,1)S(1)}, u32[]{:S(2)}, u32[]{:S(2)}) collective-permute-start(bf16[64,640]{1,0:T(8,128)(2,1)S(1)} %get-tuple-element.33), channel_id=1, source_target_pairs={{0,1},{1,0},{2,3},{3,2},{4,5},{5,4},{6,7},{7,6},{8,33},{9,32},{10,... | collective-permute-start | bytes 245768 | tf_op jit(solution)/shard_map/ppermute | solution.py:39
  96.6 1.9 %collective-permute-start.14 = (bf16[64,640]{1,0:T(8,128)(2,1)S(1)}, bf16[64,640]{1,0:T(8,128)(2,1)S(1)}, u32[]{:S(2)}, u32[]{:S(2)}) collective-permute-start(bf16[64,640]{1,0:T(8,128)(2,1)S(1)} %get-tuple-element.32), channel_id=1, source_target_pairs={{0,0},{1,1},{2,2},{3,3},{4,4},{5,5},{6,6},{7,7},{8,32},{9,33},{10,... | collective-permute-start | bytes 245768 | tf_op jit(solution)/shard_map/ppermute | solution.py:39
  98.6 0.3 collective-permute-done.15
  98.9 10.4 %collective-permute-start.22 = (bf16[5,64,512]{2,1,0:T(8,128)(2,1)}, bf16[5,64,512]{2,1,0:T(8,128)(2,1)}, u32[]{:S(2)}, u32[]{:S(2)}) collective-permute-start(bf16[5,64,512]{2,1,0:T(8,128)(2,1)} %get-tuple-element.26), channel_id=1, source_target_pairs={{0,16},{1,17},{2,18},{3,19},{4,20},{5,21},{6,22},{7,23},{8,24},{9,... | collective-permute-start | bytes 983048 | tf_op jit(solution)/shard_map/ppermute | solution.py:39
  109.4 2.3 %collective-permute-start.23 = (bf16[5,64,512]{2,1,0:T(8,128)(2,1)}, bf16[5,64,512]{2,1,0:T(8,128)(2,1)}, u32[]{:S(2)}, u32[]{:S(2)}) collective-permute-start(bf16[5,64,512]{2,1,0:T(8,128)(2,1)} %get-tuple-element.27), channel_id=1, source_target_pairs={{0,17},{1,16},{2,19},{3,18},{4,21},{5,20},{6,23},{7,22},{8,25},{9,... | collective-permute-start | bytes 983048 | tf_op jit(solution)/shard_map/ppermute | solution.py:39
  111.7 3.3 %collective-permute-start.25 = (bf16[5,64,512]{2,1,0:T(8,128)(2,1)}, bf16[5,64,512]{2,1,0:T(8,128)(2,1)}, u32[]{:S(2)}, u32[]{:S(2)}) collective-permute-start(bf16[5,64,512]{2,1,0:T(8,128)(2,1)} %get-tuple-element.29), channel_id=1, source_target_pairs={{0,25},{1,24},{2,27},{3,26},{4,29},{5,28},{6,31},{7,30},{8,1},{9,0... | collective-permute-start | bytes 983048 | tf_op jit(solution)/shard_map/ppermute | solution.py:39
  115.0 15.7 %mul.112 = bf16[1024,320]{0,1:T(8,128)(2,1)S(1)} reshape(bf16[128,8,40,8]{1,0,3,2:T(8,128)(2,1)} %broadcast_multiply_fusion.1) | data formatting | bytes 1310720 | tf_op jit(solution)/shard_map/mul | solution.py:218
  130.8 0.4 copy.28.refs_8_
  131.3 24.5 %mul.116.refs_10_ = bf16[512,1024]{1,0:T(8,128)(2,1)S(1)} reshape(bf16[64,8,128,8]{3,2,1,0:T(8,128)(2,1)} %broadcast_multiply_fusion) | data formatting | bytes 2097152 | tf_op jit(solution)/shard_map/mul | solution.py:218
  156.0 15.0 %mul.128 = bf16[512,576]{0,1:T(8,128)(2,1)} reshape(bf16[64,8,72,8]{1,0,3,2:T(8,128)(2,1)} %broadcast_multiply_fusion.2) | data formatting | bytes 1179648 | tf_op jit(solution)/shard_map/mul | solution.py:218
  171.0 1.4 copy.27.table
  172.3 4.5 %relative.1.refs_12_ = bf16[64,64,512]{2,1,0:T(8,128)(2,1)S(1)} custom-call(s32[64,1]{1,0:T(8,128)S(1)} %add_add_fusion.row_residue, s32[1,512]{1,0:T(1,128)S(1)} %add_add_fusion.1.column_residue, bf16[512,576]{1,0:T(8,128)(2,1)S(1)} %copy.27.table), custom_call_target="tpu_custom_call" | custom-call | tf_op jit(solution)/shard_map/relative/pallas_call | solution.py:222
  176.9 1.7 maximum_select_fusion.1
  178.9 11.8 %pair.1 = bf16[64,64,512]{2,1,0:T(8,128)(2,1)} custom-call(bf16[5,64,512]{2,1,0:T(8,128)(2,1)S(1)} %copy-done.1, bf16[5,64,512]{2,1,0:T(8,128)(2,1)S(1)} %collective-permute-done.19.refs_1_, bf16[5,64,512]{2,1,0:T(8,128)(2,1)S(1)} %collective-permute-done.20.refs_2_, bf16[5,64,512]{2,1,0:T(8,128)(2,1)} %collective-permute-done.21.refs_3_, ...), custom_call_target="tpu_custom_call" | custom-call | tf_op jit(solution)/shard_map/pair/pallas_call | solution.py:310
  (74 shorter events, 2.6 us)
Async XLA Ops:
  0.6 17.2 %copy-start.4 = (bf16[128,64]{0,1:T(8,128)(2,1)S(1)}, bf16[128,64]{0,1:T(8,128)(2,1)}, u32[]{:S(2)}) copy-start(bf16[128,64]{0,1:T(8,128)(2,1)} %param.14) | copy-start | bytes 49156
  2.7 26.0 %collective-permute-start.1 = (bf16[64,1920]{1,0:T(8,128)(2,1)S(1)}, bf16[64,1920]{1,0:T(8,128)(2,1)S(1)}, u32[]{:S(2)}, u32[]{:S(2)}) collective-permute-start(bf16[64,1920]{1,0:T(8,128)(2,1)S(1)} %get-tuple-element.31), channel_id=1, source_target_pairs={{0,1},{1,0},{2,3},{3,2},{4,5},{5,4},{6,7},{7,6},{8,33},{9,32},{10,... | collective-permute-start | bytes 737288 | tf_op jit(solution)/shard_map/ppermute | solution.py:39
  8.8 19.9 %collective-permute-start = (bf16[64,1920]{1,0:T(8,128)(2,1)S(1)}, bf16[64,1920]{1,0:T(8,128)(2,1)S(1)}, u32[]{:S(2)}, u32[]{:S(2)}) collective-permute-start(bf16[64,1920]{1,0:T(8,128)(2,1)S(1)} %get-tuple-element.30), channel_id=1, source_target_pairs={{0,0},{1,1},{2,2},{3,3},{4,4},{5,5},{6,6},{7,7},{8,32},{9,33},{10,... | collective-permute-start | bytes 737288 | tf_op jit(solution)/shard_map/ppermute | solution.py:39
  17.8 10.8 %copy-start.7 = (s32[4]{0:T(128)S(1)}, s32[4]{0:T(128)}, u32[]{:S(2)}) copy-start(s32[4]{0:T(128)} %param.17) | copy-start | bytes 52
  28.9 8.7 %collective-permute-start.2 = (bf16[128,1280]{1,0:T(8,128)(2,1)S(1)}, bf16[128,1280]{1,0:T(8,128)(2,1)S(1)}, u32[]{:S(2)}, u32[]{:S(2)}) collective-permute-start(bf16[128,1280]{1,0:T(8,128)(2,1)S(1)} %slice.43.refs_0_), channel_id=1, source_target_pairs={{0,32},{1,33},{2,34},{3,35},{4,36},{5,37},{6,38},{7,39},{8,40},{9,... | collective-permute-start | bytes 983048 | tf_op jit(solution)/shard_map/ppermute | solution.py:39
  29.0 23.9 %collective-permute-start.5 = (bf16[128,1920]{1,0:T(8,128)(2,1)S(1)}, bf16[128,1920]{1,0:T(8,128)(2,1)S(1)}, u32[]{:S(2)}, u32[]{:S(2)}) collective-permute-start(bf16[128,1920]{1,0:T(8,128)(2,1)S(1)} %maximum_select_fusion.refs_4_), channel_id=1, source_target_pairs={{0,2},{1,3},{2,4},{3,5},{4,6},{5,7},{6,0},{7,1},{8,10},{9,11},{10,... | collective-permute-start | bytes 1474568 | tf_op jit(solution)/shard_map/ppermute | solution.py:39
  30.2 23.9 %collective-permute-start.6 = (bf16[128,1920]{1,0:T(8,128)(2,1)S(1)}, bf16[128,1920]{1,0:T(8,128)(2,1)S(1)}, u32[]{:S(2)}, u32[]{:S(2)}) collective-permute-start(bf16[128,1920]{1,0:T(8,128)(2,1)S(1)} %maximum_select_fusion.refs_4_), channel_id=1, source_target_pairs={{0,4},{1,5},{2,6},{3,7},{4,0},{5,1},{6,2},{7,3},{8,12},{9,13},{10,... | collective-permute-start | bytes 1474568 | tf_op jit(solution)/shard_map/ppermute | solution.py:39
  32.7 21.4 %collective-permute-start.7 = (bf16[128,1920]{1,0:T(8,128)(2,1)S(1)}, bf16[128,1920]{1,0:T(8,128)(2,1)S(1)}, u32[]{:S(2)}, u32[]{:S(2)}) collective-permute-start(bf16[128,1920]{1,0:T(8,128)(2,1)S(1)} %maximum_select_fusion.refs_4_), channel_id=1, source_target_pairs={{0,6},{1,7},{2,0},{3,1},{4,2},{5,3},{6,4},{7,5},{8,14},{9,15},{10,... | collective-permute-start | bytes 1474568 | tf_op jit(solution)/shard_map/ppermute | solution.py:39
  33.9 10.8 %collective-permute-start.3 = (bf16[128,1280]{1,0:T(8,128)(2,1)S(1)}, bf16[128,1280]{1,0:T(8,128)(2,1)S(1)}, u32[]{:S(2)}, u32[]{:S(2)}) collective-permute-start(bf16[128,1280]{1,0:T(8,128)(2,1)S(1)} %slice.43.refs_0_), channel_id=1, source_target_pairs={{0,64},{1,65},{2,66},{3,67},{4,68},{5,69},{6,70},{7,71},{8,72},{9,... | collective-permute-start | bytes 983048 | tf_op jit(solution)/shard_map/ppermute | solution.py:39
  37.6 15.3 %collective-permute-start.4 = (bf16[128,1280]{1,0:T(8,128)(2,1)S(1)}, bf16[128,1280]{1,0:T(8,128)(2,1)S(1)}, u32[]{:S(2)}, u32[]{:S(2)}) collective-permute-start(bf16[128,1280]{1,0:T(8,128)(2,1)S(1)} %slice.43.refs_0_), channel_id=1, source_target_pairs={{0,96},{1,97},{2,98},{3,99},{4,100},{5,101},{6,102},{7,103},{8,104... | collective-permute-start | bytes 983048 | tf_op jit(solution)/shard_map/ppermute | solution.py:39
  60.9 70.2 %copy-start.5 = (f32[128]{0:T(128)S(1)}, f32[128]{0:T(128)}, u32[]{:S(2)}) copy-start(f32[128]{0:T(128)} %param.13) | copy-start | bytes 1540
  60.9 6.2 %collective-permute-start.8 = (f32[16,512]{1,0:T(8,128)S(1)}, f32[16,512]{1,0:T(8,128)S(1)}, u32[]{:S(2)}, u32[]{:S(2)}) collective-permute-start(f32[16,512]{1,0:T(8,128)S(1)} %get-tuple-element.16.refs_8_), channel_id=1, source_target_pairs={{0,32},{1,33},{2,34},{3,35},{4,36},{5,37},{6,38},{7,39},{8,40},{9,... | collective-permute-start | bytes 98312 | tf_op jit(solution)/shard_map/ppermute | solution.py:39
  62.3 5.3 %collective-permute-start.9 = (f32[16,512]{1,0:T(8,128)S(1)}, f32[16,512]{1,0:T(8,128)S(1)}, u32[]{:S(2)}, u32[]{:S(2)}) collective-permute-start(f32[16,512]{1,0:T(8,128)S(1)} %get-tuple-element.16.refs_8_), channel_id=1, source_target_pairs={{0,64},{1,65},{2,66},{3,67},{4,68},{5,69},{6,70},{7,71},{8,72},{9,... | collective-permute-start | bytes 98312 | tf_op jit(solution)/shard_map/ppermute | solution.py:39
  65.9 3.4 %collective-permute-start.10 = (f32[16,512]{1,0:T(8,128)S(1)}, f32[16,512]{1,0:T(8,128)S(1)}, u32[]{:S(2)}, u32[]{:S(2)}) collective-permute-start(f32[16,512]{1,0:T(8,128)S(1)} %get-tuple-element.16.refs_8_), channel_id=1, source_target_pairs={{0,96},{1,97},{2,98},{3,99},{4,100},{5,101},{6,102},{7,103},{8,104... | collective-permute-start | bytes 98312 | tf_op jit(solution)/shard_map/ppermute | solution.py:39
  66.0 13.7 %collective-permute-start.16 = (f32[16,512]{1,0:T(8,128)S(1)}, f32[16,512]{1,0:T(8,128)S(1)}, u32[]{:S(2)}, u32[]{:S(2)}) collective-permute-start(f32[16,512]{1,0:T(8,128)S(1)} %get-tuple-element.21.refs_12_), channel_id=1, source_target_pairs={{0,2},{1,3},{2,4},{3,5},{4,6},{5,7},{6,0},{7,1},{8,10},{9,11},{10,... | collective-permute-start | bytes 98312 | tf_op jit(solution)/shard_map/ppermute | solution.py:39
  75.1 16.0 %collective-permute-start.13 = (bf16[128,640]{1,0:T(8,128)(2,1)S(1)}, bf16[128,640]{1,0:T(8,128)(2,1)S(1)}, u32[]{:S(2)}, u32[]{:S(2)}) collective-permute-start(bf16[128,640]{1,0:T(8,128)(2,1)S(1)} %get-tuple-element.20), channel_id=1, source_target_pairs={{0,96},{1,97},{2,98},{3,99},{4,100},{5,101},{6,102},{7,103},{8,104... | collective-permute-start | bytes 491528 | tf_op jit(solution)/shard_map/ppermute | solution.py:39
  75.8 15.3 %collective-permute-start.12 = (bf16[128,640]{1,0:T(8,128)(2,1)S(1)}, bf16[128,640]{1,0:T(8,128)(2,1)S(1)}, u32[]{:S(2)}, u32[]{:S(2)}) collective-permute-start(bf16[128,640]{1,0:T(8,128)(2,1)S(1)} %get-tuple-element.19), channel_id=1, source_target_pairs={{0,64},{1,65},{2,66},{3,67},{4,68},{5,69},{6,70},{7,71},{8,72},{9,... | collective-permute-start | bytes 491528 | tf_op jit(solution)/shard_map/ppermute | solution.py:39
  76.9 14.2 %collective-permute-start.11 = (bf16[128,640]{1,0:T(8,128)(2,1)S(1)}, bf16[128,640]{1,0:T(8,128)(2,1)S(1)}, u32[]{:S(2)}, u32[]{:S(2)}) collective-permute-start(bf16[128,640]{1,0:T(8,128)(2,1)S(1)} %get-tuple-element.18), channel_id=1, source_target_pairs={{0,32},{1,33},{2,34},{3,35},{4,36},{5,37},{6,38},{7,39},{8,40},{9,... | collective-permute-start | bytes 491528 | tf_op jit(solution)/shard_map/ppermute | solution.py:39
  77.3 4.3 %collective-permute-start.17 = (f32[16,512]{1,0:T(8,128)S(1)}, f32[16,512]{1,0:T(8,128)S(1)}, u32[]{:S(2)}, u32[]{:S(2)}) collective-permute-start(f32[16,512]{1,0:T(8,128)S(1)} %get-tuple-element.21.refs_12_), channel_id=1, source_target_pairs={{0,4},{1,5},{2,6},{3,7},{4,0},{5,1},{6,2},{7,3},{8,12},{9,13},{10,... | collective-permute-start | bytes 98312 | tf_op jit(solution)/shard_map/ppermute | solution.py:39
  79.7 3.1 %collective-permute-start.18 = (f32[16,512]{1,0:T(8,128)S(1)}, f32[16,512]{1,0:T(8,128)S(1)}, u32[]{:S(2)}, u32[]{:S(2)}) collective-permute-start(f32[16,512]{1,0:T(8,128)S(1)} %get-tuple-element.21.refs_12_), channel_id=1, source_target_pairs={{0,6},{1,7},{2,0},{3,1},{4,2},{5,3},{6,4},{7,5},{8,14},{9,15},{10,... | collective-permute-start | bytes 98312 | tf_op jit(solution)/shard_map/ppermute | solution.py:39
  90.2 0.7 copy-start
  90.9 20.7 %collective-permute-start.19 = (bf16[5,64,512]{2,1,0:T(8,128)(2,1)S(1)}, bf16[5,64,512]{2,1,0:T(8,128)(2,1)S(1)}, u32[]{:S(2)}, u32[]{:S(2)}) collective-permute-start(bf16[5,64,512]{2,1,0:T(8,128)(2,1)S(1)} %get-tuple-element.23), channel_id=1, source_target_pairs={{0,1},{1,0},{2,3},{3,2},{4,5},{5,4},{6,7},{7,6},{8,9},{9,8},{10,11... | collective-permute-start | bytes 983048 | tf_op jit(solution)/shard_map/ppermute | solution.py:39
  90.9 20.7 %collective-permute-start.20 = (bf16[5,64,512]{2,1,0:T(8,128)(2,1)S(1)}, bf16[5,64,512]{2,1,0:T(8,128)(2,1)S(1)}, u32[]{:S(2)}, u32[]{:S(2)}) collective-permute-start(bf16[5,64,512]{2,1,0:T(8,128)(2,1)S(1)} %get-tuple-element.24), channel_id=1, source_target_pairs={{0,8},{1,9},{2,10},{3,11},{4,12},{5,13},{6,14},{7,15},{8,16},{9,17... | collective-permute-start | bytes 983048 | tf_op jit(solution)/shard_map/ppermute | solution.py:39
  91.2 7.7 %collective-permute-start.15 = (bf16[64,640]{1,0:T(8,128)(2,1)S(1)}, bf16[64,640]{1,0:T(8,128)(2,1)S(1)}, u32[]{:S(2)}, u32[]{:S(2)}) collective-permute-start(bf16[64,640]{1,0:T(8,128)(2,1)S(1)} %get-tuple-element.33), channel_id=1, source_target_pairs={{0,1},{1,0},{2,3},{3,2},{4,5},{5,4},{6,7},{7,6},{8,33},{9,32},{10,... | collective-permute-start | bytes 245768 | tf_op jit(solution)/shard_map/ppermute | solution.py:39
  96.6 12.8 %collective-permute-start.14 = (bf16[64,640]{1,0:T(8,128)(2,1)S(1)}, bf16[64,640]{1,0:T(8,128)(2,1)S(1)}, u32[]{:S(2)}, u32[]{:S(2)}) collective-permute-start(bf16[64,640]{1,0:T(8,128)(2,1)S(1)} %get-tuple-element.32), channel_id=1, source_target_pairs={{0,0},{1,1},{2,2},{3,3},{4,4},{5,5},{6,6},{7,7},{8,32},{9,33},{10,... | collective-permute-start | bytes 245768 | tf_op jit(solution)/shard_map/ppermute | solution.py:39
  98.5 80.0 %collective-permute-start.21 = (bf16[5,64,512]{2,1,0:T(8,128)(2,1)}, bf16[5,64,512]{2,1,0:T(8,128)(2,1)}, u32[]{:S(2)}, u32[]{:S(2)}) collective-permute-start(bf16[5,64,512]{2,1,0:T(8,128)(2,1)} %get-tuple-element.25), channel_id=1, source_target_pairs={{0,9},{1,8},{2,11},{3,10},{4,13},{5,12},{6,15},{7,14},{8,17},{9,16... | collective-permute-start | bytes 983048 | tf_op jit(solution)/shard_map/ppermute | solution.py:39
  98.9 16.1 %copy-start.2 = (bf16[64,640]{1,0:T(8,128)(2,1)}, bf16[64,640]{1,0:T(8,128)(2,1)S(1)}, u32[]{:S(2)}) copy-start(bf16[64,640]{1,0:T(8,128)(2,1)S(1)} %collective-permute-done.15) | copy-start | bytes 245764
  98.9 79.7 %collective-permute-start.22 = (bf16[5,64,512]{2,1,0:T(8,128)(2,1)}, bf16[5,64,512]{2,1,0:T(8,128)(2,1)}, u32[]{:S(2)}, u32[]{:S(2)}) collective-permute-start(bf16[5,64,512]{2,1,0:T(8,128)(2,1)} %get-tuple-element.26), channel_id=1, source_target_pairs={{0,16},{1,17},{2,18},{3,19},{4,20},{5,21},{6,22},{7,23},{8,24},{9,... | collective-permute-start | bytes 983048 | tf_op jit(solution)/shard_map/ppermute | solution.py:39
  109.4 5.7 %copy-start.3 = (bf16[64,640]{1,0:T(8,128)(2,1)}, bf16[64,640]{1,0:T(8,128)(2,1)S(1)}, u32[]{:S(2)}) copy-start(bf16[64,640]{1,0:T(8,128)(2,1)S(1)} %collective-permute-done.14) | copy-start | bytes 245764
  109.4 69.2 %collective-permute-start.23 = (bf16[5,64,512]{2,1,0:T(8,128)(2,1)}, bf16[5,64,512]{2,1,0:T(8,128)(2,1)}, u32[]{:S(2)}, u32[]{:S(2)}) collective-permute-start(bf16[5,64,512]{2,1,0:T(8,128)(2,1)} %get-tuple-element.27), channel_id=1, source_target_pairs={{0,17},{1,16},{2,19},{3,18},{4,21},{5,20},{6,23},{7,22},{8,25},{9,... | collective-permute-start | bytes 983048 | tf_op jit(solution)/shard_map/ppermute | solution.py:39
  111.7 66.9 %collective-permute-start.24 = (bf16[5,64,512]{2,1,0:T(8,128)(2,1)}, bf16[5,64,512]{2,1,0:T(8,128)(2,1)}, u32[]{:S(2)}, u32[]{:S(2)}) collective-permute-start(bf16[5,64,512]{2,1,0:T(8,128)(2,1)} %get-tuple-element.28), channel_id=1, source_target_pairs={{0,24},{1,25},{2,26},{3,27},{4,28},{5,29},{6,30},{7,31},{8,0},{9,1... | collective-permute-start | bytes 983048 | tf_op jit(solution)/shard_map/ppermute | solution.py:39
  111.7 66.9 %collective-permute-start.25 = (bf16[5,64,512]{2,1,0:T(8,128)(2,1)}, bf16[5,64,512]{2,1,0:T(8,128)(2,1)}, u32[]{:S(2)}, u32[]{:S(2)}) collective-permute-start(bf16[5,64,512]{2,1,0:T(8,128)(2,1)} %get-tuple-element.29), channel_id=1, source_target_pairs={{0,25},{1,24},{2,27},{3,26},{4,29},{5,28},{6,31},{7,30},{8,1},{9,0... | collective-permute-start | bytes 983048 | tf_op jit(solution)/shard_map/ppermute | solution.py:39
  130.8 25.0 %copy-start.6 = (f32[64]{0:T(128)S(1)}, f32[64]{0:T(128)}, u32[]{:S(2)}) copy-start(f32[64]{0:T(128)} %param.15) | copy-start | bytes 772
  155.8 23.1 %copy-start.1 = (bf16[5,64,512]{2,1,0:T(8,128)(2,1)S(1)}, bf16[5,64,512]{2,1,0:T(8,128)(2,1)}, u32[]{:S(2)}) copy-start(bf16[5,64,512]{2,1,0:T(8,128)(2,1)} %copy-done) | copy-start | bytes 983044

commit v2 on v0

v2 whole, which is shorter than its diff:
```python
import functools
import itertools
import math

import jax
import jax.numpy as jnp
from jax import lax
from jax.experimental import pallas as pl
from jax.experimental.pallas import tpu as pltpu
from jax.sharding import PartitionSpec as P

HEAD_DIM = 128
CLIP = 32
GAP = 512
BINS = 65
GROUP = 5
WIDE = GROUP * HEAD_DIM
BLOCK = 128
HALF = 64
TILE = 512
ROWS = 16
SCALE = math.log2(math.e) / math.sqrt(HEAD_DIM)
AXES = ("head", "band")
MIB = 1 << 20


def place(y, x, z, c):
    return c * 32 + y * 8 + x * 2 + z


def moves(to):
    return [
        (place(y, x, z, c), place(*to(y, x, z, c)))
        for c, y, x, z in itertools.product(range(4), range(4), range(4), range(2))
    ]


def send(value, to):
    return lax.ppermute(value, AXES, moves(to))


def over_columns_of(values):
    return [send(values[d], lambda y, x, z, c, d=d: (y, (x + d) % 4, z, c)) for d in (1, 2, 3)]


def over_columns(value):
    return over_columns_of([value] * 4)


def over_rows(value):
    return [send(value, lambda y, x, z, c, d=d: (y, x, z, c ^ d)) for d in (1, 2, 3)]


def nt(a, b):
    return lax.dot_general(a, b, (((1,), (1,)), ((), ())), preferred_element_type=jnp.float32)


def fetch(where, row_blocks, column_blocks, rows_ref, columns_ref, sems):
    y, x, z, c = (where[i] for i in range(4))
    copies = []
    for d in range(4):
        away = lax.rem(lax.bitwise_xor(c, d) - y + 4, 4)
        for part in range(2):
            start = pl.multiple_of(away * BLOCK + lax.bitwise_xor(z, part) * HALF, HALF)
            copies.append(
                pltpu.make_async_copy(
                    row_blocks[d].at[pl.ds(part * HALF, HALF)],
                    rows_ref.at[pl.ds(start, HALF)],
                    sems.at[2 * d + part],
                )
            )
        start = pl.multiple_of(lax.rem(x - d + 4, 4) * BLOCK, BLOCK)
        copies.append(
            pltpu.make_async_copy(
                column_blocks[d], columns_ref.at[pl.ds(start, BLOCK)], sems.at[8 + d]
            )
        )
    for copy in copies:
        copy.start()
    for copy in copies:
        copy.wait()


def head(ref, part, h):
    return ref[:, part * WIDE + h * HEAD_DIM : part * WIDE + (h + 1) * HEAD_DIM]


def stats_kernel(where, *refs):
    by_row, by_column, row_lifted, column_lifted = refs[8:12]
    partials, (rows_ref, columns_ref, held, sems) = refs[12:16], refs[16:]
    fetch(where, refs[0:4], refs[4:8], rows_ref, columns_ref, sems)
    by_column[...] = jnp.zeros_like(by_column)
    lane = lax.broadcasted_iota(jnp.int32, (TILE, 128), 1)
    kept = jnp.zeros((TILE, 128), jnp.float32)
    for h in range(GROUP):
        scores = nt(head(rows_ref, 0, h), head(columns_ref, 1, h)) * SCALE
        top = jnp.max(scores, axis=1, keepdims=True)
        lifted = jnp.exp2(scores - top)
        row_lifted[h] = lifted.astype(jnp.bfloat16)
        kept = jnp.where(lane == h, top, kept)
        kept = jnp.where(lane == 8 + h, jnp.sum(lifted, axis=1, keepdims=True), kept)
        scores = nt(head(rows_ref, 1, h), head(columns_ref, 0, h)) * SCALE
        top = jnp.max(scores, axis=0, keepdims=True)
        lifted = jnp.exp2(scores - top)
        by_column[h : h + 1, :] = top
        by_column[8 + h : 9 + h, :] = jnp.sum(lifted, axis=0, keepdims=True)
        lifted = lifted.astype(jnp.bfloat16)
        column_lifted[h] = lifted
        part = lax.dot_general(
            head(rows_ref, 2, h),
            lifted,
            (((0,), (0,)), ((), ())),
            preferred_element_type=jnp.float32,
        )
        held[h * HEAD_DIM : (h + 1) * HEAD_DIM, :] = part.astype(jnp.bfloat16)
    by_row[...] = jnp.transpose(kept)[0:16]
    for d in range(4):
        owner = lax.rem(where[1] + d, 4)
        partials[d][...] = held[:, pl.ds(pl.multiple_of(owner * BLOCK, BLOCK), BLOCK)]


def factors(refs):
    top = functools.reduce(jnp.maximum, [ref[0:8, :] for ref in refs])
    total = sum(ref[8:16, :] * jnp.exp2(ref[0:8, :] - top) for ref in refs)
    return jnp.exp2(refs[0][0:8, :] - top) / total


def turned(value):
    return jnp.transpose(jnp.concatenate([value] * 16, axis=0))


def symmetric_kernel(where, *refs):
    row_stats, column_stats = refs[0:4], refs[4:8]
    row_lifted, column_lifted, out = refs[8:]
    by_row = turned(factors(row_stats) * 1024.0)
    by_column = factors(column_stats) * 1024.0
    y, z = where[0], where[2]
    for p in range(8):
        owner = lax.rem(y + p // 2, 4) * 2 + lax.bitwise_xor(z, p % 2)
        here = slice(p * HALF, (p + 1) * HALF)
        for h in range(GROUP):
            out[owner, h] = (
                row_lifted[h, here].astype(jnp.float32) * by_row[here, h : h + 1]
                + column_lifted[h, here].astype(jnp.float32) * by_column[h : h + 1, :]
            ).astype(jnp.bfloat16)


def context_kernel(where, *refs):
    column_stats, partials = refs[0:4], refs[4:8]
    same, other, held = refs[8:]
    here = pl.ds(pl.multiple_of(where[1] * BLOCK, BLOCK), BLOCK)
    tops = [ref[0:8, here] for ref in column_stats]
    top = functools.reduce(jnp.maximum, tops)
    scales = [jnp.exp2(own - top) for own in tops]
    total = sum(ref[8:16, here] * scale for ref, scale in zip(column_stats, scales))
    scales = [scale / total for scale in scales]
    for h in range(GROUP):
        at = slice(h * HEAD_DIM, (h + 1) * HEAD_DIM)
        summed = sum(
            ref[at, :].astype(jnp.float32) * scale[h : h + 1, :]
            for ref, scale in zip(partials, scales)
        )
        held[:, at] = jnp.transpose(summed).astype(jnp.bfloat16)
    z = where[2]
    same[...] = held[pl.ds(pl.multiple_of(z * HALF, HALF), HALF), :]
    other[...] = held[pl.ds(pl.multiple_of((1 - z) * HALF, HALF), HALF), :]


def one_hot(indices, axis):
    return (indices == lax.broadcasted_iota(jnp.int32, indices.shape, axis)).astype(jnp.float32)


def expanded(matrix, row_of, row_lane, column_of, column_lane, left, right):
    k, m = matrix.shape
    one = one_hot(row_of(lax.broadcasted_iota(jnp.int32, (left, m), 0)), 1)
    tall = nt(one.astype(jnp.bfloat16), matrix).astype(jnp.bfloat16)
    one = one_hot(column_of(lax.broadcasted_iota(jnp.int32, (k, right), 1)), 0)
    wide = jnp.dot(tall, one.astype(jnp.bfloat16), preferred_element_type=jnp.float32)
    at_row = row_lane(lax.broadcasted_iota(jnp.int32, (left, right), 0))
    at_column = column_lane(lax.broadcasted_iota(jnp.int32, (left, right), 1))
    return jnp.where(at_row == at_column, wide, 0.0).astype(jnp.bfloat16)


def repeated(bias, row_of, left):
    one = one_hot(row_of(lax.broadcasted_iota(jnp.int32, (left, bias.shape[0]), 0)), 1)
    wide = jnp.broadcast_to(bias[...], (bias.shape[0], 128))
    return jnp.dot(one, wide, precision=lax.Precision.HIGHEST, preferred_element_type=jnp.float32)


def spread_kernel(
    first, first_bias, second, second_bias, table, first_out, first_bias_out, second_out,
    second_bias_out, table_out,
):
    by_eight, eight = lambda r: r // 8, lambda r: r % 8
    by_four, four = lambda r: r // 4, lambda r: r % 4
    hid, outs = first.shape[1], second.shape[1]
    channel = lambda r: r % (hid * 4) // 4
    first_out[...] = expanded(
        first[...],
        channel,
        lambda r: r // (hid * 4) * 4 + r % 4,
        by_eight,
        eight,
        hid * 8,
        first_out.shape[1],
    )
    first_bias_out[...] = repeated(first_bias, channel, hid * 8)
    second_out[: outs * 4] = expanded(second[...], by_four, four, by_four, four, outs * 4, hid * 4)
    second_out[outs * 4 :] = expanded(
        second[...], lambda r: r // 4 + 1 - r // 4 % 2 * 2, four, by_four, four, outs * 4, hid * 4
    )
    second_bias_out[...] = repeated(second_bias, by_eight, outs * 8)
    table_out[...] = expanded(
        table[...], by_eight, eight, by_eight, eight, outs * 8, table_out.shape[1]
    )


def relative_kernel(where, lengths, table, out):
    ends = [lengths[0], lengths[0] + lengths[1], lengths[0] + lengths[1] + lengths[2]]

    def residue(positions):
        return positions + GAP * sum((positions >= end).astype(jnp.int32) for end in ends)

    band = where[0] * 8 + where[1] * 2 + where[2]
    first_row = band * HALF + pl.program_id(0) * ROWS
    levels = lax.broadcasted_iota(jnp.int32, (72, 8, TILE), 0)
    columns = residue(where[3] * TILE + lax.broadcasted_iota(jnp.int32, (8, TILE), 1))
    halves = []
    for half in range(ROWS // 8):
        rows = residue(first_row + half * 8 + lax.broadcasted_iota(jnp.int32, (8, TILE), 0))
        bins = jnp.clip(columns - rows, -CLIP, CLIP) + CLIP
        spread = (bins[None] == levels).astype(jnp.float32).reshape(72 * 8, TILE)
        part = jnp.dot(
            table[...], spread.astype(jnp.bfloat16), preferred_element_type=jnp.float32
        )
        halves.append(part.reshape(-1, 8, TILE))
    out[...] = jnp.concatenate(halves, axis=1).astype(jnp.bfloat16)


def pair_kernel(
    where, tiles, first, first_bias, second, second_bias, relative, same, other, out, context
):
    z = where[2]

    @pl.when(pl.program_id(0) == 0)
    def _():
        context[:, pl.ds(pl.multiple_of(z * WIDE, WIDE), WIDE)] = same[...]
        context[:, pl.ds(pl.multiple_of((1 - z) * WIDE, WIDE), WIDE)] = other[...]

    loaded = tiles[...].astype(jnp.float32)
    outs, hid = second.shape[0] // 8, first.shape[0] // 8
    upper = lax.broadcasted_iota(jnp.int32, (outs // 2, 8, TILE), 1) < 4
    halves = []
    for half in range(ROWS // 8):
        stacked = loaded[:, half * 8 : half * 8 + 8, :].reshape(-1, TILE).astype(jnp.bfloat16)
        hidden = jnp.dot(first[...], stacked, preferred_element_type=jnp.float32)
        hidden = jnp.maximum(hidden + jnp.concatenate([first_bias[...]] * 4, axis=1), 0.0)
        hidden = hidden.astype(jnp.bfloat16)
        low, high = (
            jnp.dot(
                second[part * outs * 4 : (part + 1) * outs * 4],
                hidden[part * hid * 4 : (part + 1) * hid * 4],
                preferred_element_type=jnp.float32,
            ).reshape(outs // 2, 8, TILE)
            for part in range(2)
        )
        even = jnp.where(upper, low, high)
        odd = pltpu.roll(jnp.where(upper, high, low), 4, 1)
        projected = jnp.stack([even, odd], axis=1).reshape(outs, 8, TILE)
        halves.append(
            projected + jnp.concatenate([second_bias[...]] * 4, axis=1).reshape(outs, 8, TILE)
        )
    out[...] = (
        jnp.concatenate(halves, axis=1) + relative[...].astype(jnp.float32)
    ).astype(jnp.bfloat16)


SMEM = pl.BlockSpec(memory_space=pltpu.SMEM)
ANY = pl.BlockSpec(memory_space=pl.ANY)
VMEM = pl.BlockSpec(memory_space=pltpu.VMEM)


def params(mib):
    return pltpu.CompilerParams(vmem_limit_bytes=mib * MIB)


def in_hbm(value):
    return pltpu.with_memory_space_constraint(value, pltpu.HBM)


def vmem(rows, columns):
    return pltpu.VMEM((rows, columns), jnp.bfloat16)


def shape(dims, kind=jnp.bfloat16):
    return jax.ShapeDtypeStruct(dims, kind)


def local(queries, keys, values, w_first, b_first, w_second, b_second, rel_table, chain_lengths):
    band, c = lax.axis_index("band"), lax.axis_index("head")
    y, x, z = band // 8, (band // 2) % 4, band % 2
    where = jnp.stack([y, x, z, c]).astype(jnp.int32)
    hid, outs = w_first.shape[1], w_second.shape[1]

    first, first_bias, second, second_bias, table = pl.pallas_call(
        spread_kernel,
        in_specs=[VMEM] * 5,
        out_specs=[VMEM] * 5,
        out_shape=[
            pltpu.HBM((hid * 8, 8 * GROUP * 8), jnp.bfloat16),
            pltpu.HBM((hid * 8, 128), jnp.float32),
            pltpu.HBM((outs * 8, hid * 4), jnp.bfloat16),
            pltpu.HBM((outs * 8, 128), jnp.float32),
            shape((outs * 8, 72 * 8)),
        ],
        compiler_params=params(6),
        name="spread",
    )(w_first, b_first[:, None], w_second, b_second[:, None], jnp.pad(rel_table, ((0, 72 - BINS), (0, 0))))

    near = jnp.concatenate([queries[:, :WIDE], keys[:, :WIDE], values[:, :WIDE]], axis=1)
    far = jnp.concatenate([queries[:, WIDE:], keys[:, WIDE:], values[:, WIDE:]], axis=1)
    same = send(jnp.where(z == 0, near, far), lambda y, x, z, c: (c, x, z, y))
    other = send(jnp.where(z == 0, far, near), lambda y, x, z, c: (c, x, 1 - z, y))
    block = jnp.where(
        z == 0,
        jnp.concatenate([same, other], axis=0),
        jnp.concatenate([other, same], axis=0),
    )

    block, first, first_bias, second, second_bias, table = lax.optimization_barrier(
        (block, first, first_bias, second, second_bias, table)
    )
    narrow = block[:, : 2 * WIDE]

    column_blocks = [narrow] + over_columns(narrow)
    row_blocks = [block] + over_rows(block)

    relative = pl.pallas_call(
        relative_kernel,
        grid=(HALF // ROWS,),
        in_specs=[SMEM, SMEM, pl.BlockSpec((outs * 8, 72 * 8), lambda i: (0, 0))],
        out_specs=pl.BlockSpec((outs, ROWS, TILE), lambda i: (0, i, 0)),
        out_shape=pltpu.HBM((outs, HALF, TILE), jnp.bfloat16),
        compiler_params=params(8),
        name="relative",
    )(where, chain_lengths, table)
    where, relative = lax.optimization_barrier((where, relative))

    by_row, by_column, row_lifted, column_lifted, *partials = pl.pallas_call(
        stats_kernel,
        in_specs=[SMEM] + [ANY] * 8,
        out_specs=[VMEM] * 8,
        out_shape=[shape((16, TILE), jnp.float32)] * 2
        + [shape((GROUP, TILE, TILE))] * 2
        + [pltpu.HBM((WIDE, BLOCK), jnp.bfloat16)]
        + [shape((WIDE, BLOCK))] * 3,
        scratch_shapes=[
            vmem(TILE, 3 * WIDE),
            vmem(TILE, 2 * WIDE),
            vmem(WIDE, TILE),
            pltpu.SemaphoreType.DMA((12,)),
        ],
        compiler_params=params(12),
        name="stats",
    )(where, *row_blocks, *column_blocks)
    row_stats = [by_row] + over_rows(by_row)
    column_stats = [by_column] + over_columns(by_column)

    tiles = pl.pallas_call(
        symmetric_kernel,
        in_specs=[SMEM] + [VMEM] * 10,
        out_specs=VMEM,
        out_shape=shape((8, GROUP, HALF, TILE)),
        compiler_params=params(8),
        name="symmetric",
    )(where, *row_stats, *column_stats, row_lifted, column_lifted)
    where, tiles = lax.optimization_barrier((where, tiles))
    groups = [[y * 8 + x * 2 + z for y in range(4) for z in range(2)] for x in range(4)]
    received = lax.all_to_all(
        tiles, "band", split_axis=0, concat_axis=0, axis_index_groups=groups, tiled=True
    ).reshape(8 * GROUP, HALF, TILE)

    same, other = pl.pallas_call(
        context_kernel,
        in_specs=[SMEM] + [VMEM] * 8,
        out_specs=[VMEM] * 2,
        out_shape=[shape((HALF, WIDE))] * 2,
        scratch_shapes=[vmem(BLOCK, WIDE)],
        compiler_params=params(4),
        name="context",
    )(where, *column_stats, in_hbm(partials[0]), *over_columns_of(partials))
    same = send(same, lambda y, x, z, c: (c, x, z, y))
    other = send(other, lambda y, x, z, c: (c, x, 1 - z, y))

    pair, context = pl.pallas_call(
        pair_kernel,
        grid=(HALF // ROWS,),
        in_specs=[
            SMEM,
            pl.BlockSpec((8 * GROUP, ROWS, TILE), lambda i: (0, i, 0)),
            pl.BlockSpec((hid * 8, 8 * GROUP * 8), lambda i: (0, 0)),
            pl.BlockSpec((hid * 8, 128), lambda i: (0, 0)),
            pl.BlockSpec((outs * 8, hid * 4), lambda i: (0, 0)),
            pl.BlockSpec((outs * 8, 128), lambda i: (0, 0)),
            pl.BlockSpec((outs, ROWS, TILE), lambda i: (0, i, 0)),
            pl.BlockSpec((HALF, WIDE), lambda i: (0, 0)),
            pl.BlockSpec((HALF, WIDE), lambda i: (0, 0)),
        ],
        out_specs=[
            pl.BlockSpec((outs, ROWS, TILE), lambda i: (0, i, 0)),
            pl.BlockSpec((HALF, 2 * WIDE), lambda i: (0, 0)),
        ],
        out_shape=[shape((outs, HALF, TILE)), shape((HALF, 2 * WIDE))],
        compiler_params=params(13),
        name="pair",
    )(
        where,
        received,
        *(in_hbm(a) for a in (first, first_bias, second, second_bias, relative, same, other)),
    )
    return (context, pair)


def solution(mesh):
    return jax.shard_map(
        local,
        mesh=mesh,
        in_specs=(
            P("band", "head"),
            P("band", "head"),
            P("band", "head"),
            P(),
            P(),
            P(),
            P(),
            P(),
            P(),
        ),
        out_specs=(P("band", "head"), P(None, "band", "head")),
        check_vma=False,
    )
```

time: 314 us -> 126 us (0.40)
  waiting for transfers between devices: 144 us -> 43.2 us
  local copies, waits for them, and re-layouts: 107 us -> 7.83 us
  Pallas kernels: 0 us -> 32.4 us
  starting transfers between devices: 12.1 us -> 40.8 us
  matrix products: 26.6 us -> 0 us
  between operations: 14.2 us -> 0.78 us
  other arithmetic: 9.43 us -> 0.25 us
    all_gather x2 -> x0, waiting for transfers between devices: 92 us -> none  [the longest x1 92 us: local(): piece = lax.all_gather(keys, 'band', axis=0, tiled=True)]
    all_to_all x2 -> x1, waiting for transfers between devices: 50.4 us -> 0.01 us  [local(): lax.all_to_all(tiles, 'band', split_axis=0, concat_axis=0, axis_index_gro...]
    ppermute x0 -> x19, waiting for transfers between devices: none -> 43.2 us  [send(): return lax.ppermute(value, AXES, moves(to))]
    unnamed x23 -> x18, local copies, waits for them, and re-layouts: 40.7 us -> 4.29 us
    ppermute x0 -> x19, starting transfers between devices: none -> 34.7 us  [send(): return lax.ppermute(value, AXES, moves(to))]
    pallas_call x0 -> x6, Pallas kernels: none -> 32.4 us  [the longest x1 10.9 us: local(): pl.pallas_call(pair_kernel, grid=(HALF // ROWS,), in_specs=[SMEM, pl.Bloc...]
    convert_element_type x4 -> x0, local copies, waits for them, and re-layouts: 29.7 us -> none  [the longest x2 20.4 us: local(): mirrored.astype(jnp.float32)]
    dot_general x4 -> x0, matrix products: 26.6 us -> none  [the longest x1 12.2 us: local(): jnp.einsum('knc,ko->onc', hidden, w_second, preferred_element_type=jnp.fl...]
  transfers between devices with their start and end apart: 4 -> 20, of which waited for: 3 -> 12; matrix products, arithmetic and copies ran while one was open for 33% -> 3% of each run, Pallas kernels for 0% -> 8%
where the time goes in v2:
time: 126 us; the launch traced here: 125 us
  waiting for transfers between devices  43.2 us (34%)
  starting transfers between devices  40.8 us (32%)
  Pallas kernels  32.4 us (26%)
  local copies, waits for them, and re-layouts  7.83 us (6%)
    ppermute x19, waiting for transfers between devices, send(): return lax.ppermute(value, AXES, moves(to))  43.2 us
    ppermute x19, starting transfers between devices, send(): return lax.ppermute(value, AXES, moves(to))  34.7 us
    pallas_call x1, Pallas kernels, local(): pl.pallas_call(pair_kernel, grid=(HALF // ROWS,), in_specs=[SMEM, pl.Bloc...  10.9 us
    pallas_call x1, Pallas kernels, local(): pl.pallas_call(stats_kernel, in_specs=[SMEM] + [ANY] * 8, out_specs=[VMEM...  8.67 us
    all_to_all x1, starting transfers between devices, local(): lax.all_to_all(tiles, 'band', split_axis=0, concat_axis=0, axis_index_gro...  6.02 us
    pallas_call x1, Pallas kernels, local(): pl.pallas_call(relative_kernel, grid=(HALF // ROWS,), in_specs=[SMEM, SME...  5.7 us
    unnamed x18, local copies, waits for them, and re-layouts  4.29 us
    pallas_call x1, Pallas kernels, local(): pl.pallas_call(symmetric_kernel, in_specs=[SMEM] + [VMEM] * 10, out_specs...  3.22 us
  transfers between devices with their start and end apart: 20, of which 12 were waited for; matrix products, arithmetic and copies ran while one was open for 3% of the time, Pallas kernels for 8%

profile of v2, /device:TPU:1, one launch (start us, length us, event | category | flops | bytes accessed | tf_op | source)
XLA Modules:
  0.0 125.2 jit_solution(2007884718590149574)
XLA Ops:
  0.7 0.9 fusion.2
  1.6 1.0 fusion
  2.6 0.1 broadcast_select_fusion.1
  2.7 4.6 %collective-permute-start = (bf16[64,1920]{1,0:T(8,128)(2,1)S(1)}, bf16[64,1920]{1,0:T(8,128)(2,1)S(1)}, u32[]{:S(2)}, u32[]{:S(2)}) collective-permute-start(bf16[64,1920]{1,0:T(8,128)(2,1)S(1)} %get-tuple-element.56), channel_id=1, source_target_pairs={{0,0},{1,1},{2,2},{3,3},{4,4},{5,5},{6,6},{7,7},{8,32},{9,33},{10,... | collective-permute-start | bytes 737288 | tf_op jit(solution)/shard_map/ppermute | solution.py:39
  7.3 3.4 %collective-permute-start.1 = (bf16[64,1920]{1,0:T(8,128)(2,1)S(1)}, bf16[64,1920]{1,0:T(8,128)(2,1)S(1)}, u32[]{:S(2)}, u32[]{:S(2)}) collective-permute-start(bf16[64,1920]{1,0:T(8,128)(2,1)S(1)} %get-tuple-element.57), channel_id=1, source_target_pairs={{0,1},{1,0},{2,3},{3,2},{4,5},{5,4},{6,7},{7,6},{8,33},{9,32},{10,... | collective-permute-start | bytes 737288 | tf_op jit(solution)/shard_map/ppermute | solution.py:39
  10.7 0.8 copy.11
  11.6 0.8 copy.13.second
  12.4 0.8 copy.14.second_bias
  13.2 0.8 copy.12.first_bias
  13.9 0.7 copy-done
  14.6 2.8 %spread.1 = (bf16[1024,320]{1,0:T(8,128)(2,1)}, f32[1024,128]{1,0:T(8,128)}, bf16[512,512]{1,0:T(8,128)(2,1)}, f32[512,128]{1,0:T(8,128)}, bf16[512,576]{1,0:T(8,128)(2,1)S(1)}) custom-call(bf16[40,128]{1,0:T(8,128)(2,1)S(1)} %copy-done, f32[128,1]{1,0:T(8,128)S(1)} %copy.12.first_bias, bf16[128,64]{1,0:T(8,128)(2,1)S(1)} %copy.13.second, ...), custom_call_target="tpu_custom_call" | custom-call | tf_op jit(solution)/shard_map/spread/pallas_call | solution.py:305
  17.4 2.8 %collective-permute-done.1 = bf16[64,1920]{1,0:T(8,128)(2,1)S(1)} collective-permute-done((bf16[64,1920]{1,0:T(8,128)(2,1)S(1)}, bf16[64,1920]{1,0:T(8,128)(2,1)S(1)}, u32[]{:S(2)}, u32[]{:S(2)}) %collective-permute-start.1) | collective-permute-done | bytes 245792 | tf_op jit(solution)/shard_map/ppermute | solution.py:39
  20.3 0.1 maximum_select_fusion.refs_0_
  20.4 2.5 %collective-permute-start.7 = (bf16[128,1280]{1,0:T(8,128)(2,1)S(1)}, bf16[128,1280]{1,0:T(8,128)(2,1)S(1)}, u32[]{:S(2)}, u32[]{:S(2)}) collective-permute-start(bf16[128,1280]{1,0:T(8,128)(2,1)S(1)} %slice.27.refs_4_), channel_id=1, source_target_pairs={{0,6},{1,7},{2,0},{3,1},{4,2},{5,3},{6,4},{7,5},{8,14},{9,15},{10,... | collective-permute-start | bytes 983048 | tf_op jit(solution)/shard_map/ppermute | solution.py:39
  22.9 1.4 %collective-permute-start.4 = (bf16[128,1920]{1,0:T(8,128)(2,1)S(1)}, bf16[128,1920]{1,0:T(8,128)(2,1)S(1)}, u32[]{:S(2)}, u32[]{:S(2)}) collective-permute-start(bf16[128,1920]{1,0:T(8,128)(2,1)S(1)} %maximum_select_fusion.refs_0_), channel_id=1, source_target_pairs={{0,96},{1,97},{2,98},{3,99},{4,100},{5,101},{6,102},{7,103},{8,104... | collective-permute-start | bytes 1474568 | tf_op jit(solution)/shard_map/ppermute | solution.py:39
  24.3 3.5 %collective-permute-start.3 = (bf16[128,1920]{1,0:T(8,128)(2,1)S(1)}, bf16[128,1920]{1,0:T(8,128)(2,1)S(1)}, u32[]{:S(2)}, u32[]{:S(2)}) collective-permute-start(bf16[128,1920]{1,0:T(8,128)(2,1)S(1)} %maximum_select_fusion.refs_0_), channel_id=1, source_target_pairs={{0,64},{1,65},{2,66},{3,67},{4,68},{5,69},{6,70},{7,71},{8,72},{9,... | collective-permute-start | bytes 1474568 | tf_op jit(solution)/shard_map/ppermute | solution.py:39
  27.8 0.4 collective-permute-start.2
  28.1 0.5 collective-permute-start.6
  28.7 1.0 collective-permute-done.7.refs_7_
  29.7 1.0 collective-permute-start.5
  30.7 0.1 pad_add_fusion.where
  30.8 5.7 %relative.1 = bf16[64,64,512]{2,1,0:T(8,128)(2,1)} custom-call(s32[4]{0:T(128)S(1)} %pad_add_fusion.where, s32[4]{0:T(128)S(1)} %copy-done.1, bf16[512,576]{1,0:T(8,128)(2,1)S(1)} %get-tuple-element.34.table), custom_call_target="tpu_custom_call" | custom-call | tf_op jit(solution)/shard_map/relative/pallas_call | solution.py:338
  36.5 2.4 %collective-permute-done.6.refs_6_ = bf16[128,1280]{1,0:T(8,128)(2,1)} collective-permute-done((bf16[128,1280]{1,0:T(8,128)(2,1)S(1)}, bf16[128,1280]{1,0:T(8,128)(2,1)}, u32[]{:S(2)}, u32[]{:S(2)}) %collective-permute-start.6) | collective-permute-done | bytes 327712 | tf_op jit(solution)/shard_map/ppermute | solution.py:39
  38.9 8.4 %collective-permute-done.5.refs_5_ = bf16[128,1280]{1,0:T(8,128)(2,1)} collective-permute-done((bf16[128,1280]{1,0:T(8,128)(2,1)S(1)}, bf16[128,1280]{1,0:T(8,128)(2,1)}, u32[]{:S(2)}, u32[]{:S(2)}) %collective-permute-start.5) | collective-permute-done | bytes 327712 | tf_op jit(solution)/shard_map/ppermute | solution.py:39
  47.4 8.7 %stats.1 = (f32[16,512]{1,0:T(8,128)S(1)}, f32[16,512]{1,0:T(8,128)S(1)}, bf16[5,512,512]{2,1,0:T(8,128)(2,1)S(1)}, bf16[5,512,512]{2,1,0:T(8,128)(2,1)S(1)}, bf...) custom-call(s32[4]{0:T(128)S(1)} %pad_add_fusion.where, ...), custom_call_target="tpu_custom_call" | custom-call | tf_op jit(solution)/shard_map/stats/pallas_call | solution.py:349
  56.1 0.7 copy-done.2
  56.7 0.7 copy-done.4
  57.4 1.0 collective-permute-start.10
  58.3 2.0 %collective-permute-start.9 = (f32[16,512]{1,0:T(8,128)S(1)}, f32[16,512]{1,0:T(8,128)S(1)}, u32[]{:S(2)}, u32[]{:S(2)}) collective-permute-start(f32[16,512]{1,0:T(8,128)S(1)} %get-tuple-element.37.refs_0_), channel_id=1, source_target_pairs={{0,64},{1,65},{2,66},{3,67},{4,68},{5,69},{6,70},{7,71},{8,72},{9,... | collective-permute-start | bytes 98312 | tf_op jit(solution)/shard_map/ppermute | solution.py:39
  60.4 1.5 %collective-permute-start.13 = (f32[16,512]{1,0:T(8,128)S(1)}, f32[16,512]{1,0:T(8,128)S(1)}, u32[]{:S(2)}, u32[]{:S(2)}) collective-permute-start(f32[16,512]{1,0:T(8,128)S(1)} %get-tuple-element.38.refs_4_.refs_0_), channel_id=1, source_target_pairs={{0,6},{1,7},{2,0},{3,1},{4,2},{5,3},{6,4},{7,5},{8,14},{9,15},{10,... | collective-permute-start | bytes 98312 | tf_op jit(solution)/shard_map/ppermute | solution.py:39
  61.9 0.6 collective-permute-start.11
  62.5 0.7 collective-permute-done.13.refs_7_.refs_3_
  63.1 3.1 %collective-permute-done.12.refs_6_.refs_2_ = f32[16,512]{1,0:T(8,128)S(1)} collective-permute-done((f32[16,512]{1,0:T(8,128)S(1)}, f32[16,512]{1,0:T(8,128)S(1)}, u32[]{:S(2)}, u32[]{:S(2)}) %collective-permute-start.12) | collective-permute-done | bytes 32800 | tf_op jit(solution)/shard_map/ppermute | solution.py:39
  66.2 3.2 %symmetric.1 = bf16[8,5,64,512]{3,2,1,0:T(8,128)(2,1)} custom-call(s32[4]{0:T(128)S(1)} %pad_add_fusion.where, f32[16,512]{1,0:T(8,128)S(1)} %get-tuple-element.37.refs_0_, f32[16,512]{1,0:T(8,128)S(1)} %collective-permute-done.8.refs_1_, f32[16,512]{1,0:T(8,128)S(1)} %collective-permute-done.9.refs_2_, f32[16,512]{1,0:T(8,128)S(1)} %collective-permute-done.10.refs_3_, ...), custom_call_target="tpu_custom_call" | custom-call | tf_op jit(solution)/shard_map/symmetric/pallas_call | solution.py:369
  69.4 6.0 %all-to-all-start = ((bf16[8,5,64,512]{3,2,1,0:T(8,128)(2,1)}), bf16[8,5,64,512]{3,2,1,0:T(8,128)(2,1)S(1)}, u32[]{:S(2)}, u32[]{:S(2)}) async-start(bf16[8,5,64,512]{3,2,1,0:T(8,128)(2,1)} %symmetric.1), calls=%async_computation | async-start | bytes 5242880 | tf_op jit(solution)/shard_map/all_to_all | solution.py:379
  75.5 0.1 collective-permute-start.14
  75.5 2.1 %collective-permute-start.15 = (bf16[640,128]{1,0:T(8,128)(2,1)S(1)}, bf16[640,128]{1,0:T(8,128)(2,1)S(1)}, u32[]{:S(2)}, u32[]{:S(2)}) collective-permute-start(bf16[640,128]{1,0:T(8,128)(2,1)S(1)} %copy-done.3), channel_id=1, source_target_pairs={{0,4},{1,5},{2,6},{3,7},{4,0},{5,1},{6,2},{7,3},{8,12},{9,13},{10,... | collective-permute-start | bytes 491528 | tf_op jit(solution)/shard_map/ppermute | solution.py:39
  77.6 1.4 %collective-permute-start.16 = (bf16[640,128]{1,0:T(8,128)(2,1)S(1)}, bf16[640,128]{1,0:T(8,128)(2,1)S(1)}, u32[]{:S(2)}, u32[]{:S(2)}) collective-permute-start(bf16[640,128]{1,0:T(8,128)(2,1)S(1)} %get-tuple-element.51), channel_id=1, source_target_pairs={{0,6},{1,7},{2,0},{3,1},{4,2},{5,3},{6,4},{7,5},{8,14},{9,15},{10,... | collective-permute-start | bytes 491528 | tf_op jit(solution)/shard_map/ppermute | solution.py:39
  79.0 3.8 %collective-permute-done.14.refs_5_ = bf16[640,128]{1,0:T(8,128)(2,1)S(1)} collective-permute-done((bf16[640,128]{1,0:T(8,128)(2,1)S(1)}, bf16[640,128]{1,0:T(8,128)(2,1)S(1)}, u32[]{:S(2)}, u32[]{:S(2)}) %collective-permute-start.14) | collective-permute-done | bytes 163872 | tf_op jit(solution)/shard_map/ppermute | solution.py:39
  82.8 0.8 collective-permute-done.15.refs_6_
  83.5 0.8 collective-permute-done.16.refs_7_
  84.3 1.2 context.1
  85.4 6.3 %collective-permute-start.17 = (bf16[64,640]{1,0:T(8,128)(2,1)S(1)}, bf16[64,640]{1,0:T(8,128)(2,1)S(1)}, u32[]{:S(2)}, u32[]{:S(2)}) collective-permute-start(bf16[64,640]{1,0:T(8,128)(2,1)S(1)} %get-tuple-element.52), channel_id=1, source_target_pairs={{0,0},{1,1},{2,2},{3,3},{4,4},{5,5},{6,6},{7,7},{8,32},{9,33},{10,... | collective-permute-start | bytes 245768 | tf_op jit(solution)/shard_map/ppermute | solution.py:39
  91.8 2.5 %collective-permute-start.18 = (bf16[64,640]{1,0:T(8,128)(2,1)S(1)}, bf16[64,640]{1,0:T(8,128)(2,1)S(1)}, u32[]{:S(2)}, u32[]{:S(2)}) collective-permute-start(bf16[64,640]{1,0:T(8,128)(2,1)S(1)} %get-tuple-element.53), channel_id=1, source_target_pairs={{0,1},{1,0},{2,3},{3,2},{4,5},{5,4},{6,7},{7,6},{8,33},{9,32},{10,... | collective-permute-start | bytes 245768 | tf_op jit(solution)/shard_map/ppermute | solution.py:39
  94.3 17.4 %collective-permute-done.17.same = bf16[64,640]{1,0:T(8,128)(2,1)S(1)} collective-permute-done((bf16[64,640]{1,0:T(8,128)(2,1)S(1)}, bf16[64,640]{1,0:T(8,128)(2,1)S(1)}, u32[]{:S(2)}, u32[]{:S(2)}) %collective-permute-start.17) | collective-permute-done | bytes 81952 | tf_op jit(solution)/shard_map/ppermute | solution.py:39
  111.7 1.9 %collective-permute-done.18.other = bf16[64,640]{1,0:T(8,128)(2,1)S(1)} collective-permute-done((bf16[64,640]{1,0:T(8,128)(2,1)S(1)}, bf16[64,640]{1,0:T(8,128)(2,1)S(1)}, u32[]{:S(2)}, u32[]{:S(2)}) %collective-permute-start.18) | collective-permute-done | bytes 81952 | tf_op jit(solution)/shard_map/ppermute | solution.py:39
  113.7 0.6 copy-done.7
  114.3 10.9 %pair.1 = (bf16[64,64,512]{2,1,0:T(8,128)(2,1)}, bf16[64,1280]{1,0:T(8,128)(2,1)}) custom-call(s32[4]{0:T(128)S(1)} %pad_add_fusion.where, bf16[40,64,512]{2,1,0:T(8,128)(2,1)S(1)} %bitcast.7, bf16[1024,320]{1,0:T(8,128)(2,1)} %get-tuple-element.43.first, f32[1024,128]{1,0:T(8,128)} %get-tuple-element.44.first_bias, ...), custom_call_target="tpu_custom_call" | custom-call | tf_op jit(solution)/shard_map/pair/pallas_call | solution.py:395
  (25 shorter events, 0.1 us)
Async XLA Ops:
  0.6 30.2 %copy-start.1 = (s32[4]{0:T(128)S(1)}, s32[4]{0:T(128)}, u32[]{:S(2)}) copy-start(s32[4]{0:T(128)} %lengths.1) | copy-start | bytes 52
  2.7 14.7 %collective-permute-start = (bf16[64,1920]{1,0:T(8,128)(2,1)S(1)}, bf16[64,1920]{1,0:T(8,128)(2,1)S(1)}, u32[]{:S(2)}, u32[]{:S(2)}) collective-permute-start(bf16[64,1920]{1,0:T(8,128)(2,1)S(1)} %get-tuple-element.56), channel_id=1, source_target_pairs={{0,0},{1,1},{2,2},{3,3},{4,4},{5,5},{6,6},{7,7},{8,32},{9,33},{10,... | collective-permute-start | bytes 737288 | tf_op jit(solution)/shard_map/ppermute | solution.py:39
  7.3 12.9 %collective-permute-start.1 = (bf16[64,1920]{1,0:T(8,128)(2,1)S(1)}, bf16[64,1920]{1,0:T(8,128)(2,1)S(1)}, u32[]{:S(2)}, u32[]{:S(2)}) collective-permute-start(bf16[64,1920]{1,0:T(8,128)(2,1)S(1)} %get-tuple-element.57), channel_id=1, source_target_pairs={{0,1},{1,0},{2,3},{3,2},{4,5},{5,4},{6,7},{7,6},{8,33},{9,32},{10,... | collective-permute-start | bytes 737288 | tf_op jit(solution)/shard_map/ppermute | solution.py:39
  13.9 0.7 copy-start
  20.4 9.3 %collective-permute-start.7 = (bf16[128,1280]{1,0:T(8,128)(2,1)S(1)}, bf16[128,1280]{1,0:T(8,128)(2,1)S(1)}, u32[]{:S(2)}, u32[]{:S(2)}) collective-permute-start(bf16[128,1280]{1,0:T(8,128)(2,1)S(1)} %slice.27.refs_4_), channel_id=1, source_target_pairs={{0,6},{1,7},{2,0},{3,1},{4,2},{5,3},{6,4},{7,5},{8,14},{9,15},{10,... | collective-permute-start | bytes 983048 | tf_op jit(solution)/shard_map/ppermute | solution.py:39
  22.9 24.4 %collective-permute-start.4 = (bf16[128,1920]{1,0:T(8,128)(2,1)S(1)}, bf16[128,1920]{1,0:T(8,128)(2,1)S(1)}, u32[]{:S(2)}, u32[]{:S(2)}) collective-permute-start(bf16[128,1920]{1,0:T(8,128)(2,1)S(1)} %maximum_select_fusion.refs_0_), channel_id=1, source_target_pairs={{0,96},{1,97},{2,98},{3,99},{4,100},{5,101},{6,102},{7,103},{8,104... | collective-permute-start | bytes 1474568 | tf_op jit(solution)/shard_map/ppermute | solution.py:39
  24.3 23.1 %collective-permute-start.3 = (bf16[128,1920]{1,0:T(8,128)(2,1)S(1)}, bf16[128,1920]{1,0:T(8,128)(2,1)S(1)}, u32[]{:S(2)}, u32[]{:S(2)}) collective-permute-start(bf16[128,1920]{1,0:T(8,128)(2,1)S(1)} %maximum_select_fusion.refs_0_), channel_id=1, source_target_pairs={{0,64},{1,65},{2,66},{3,67},{4,68},{5,69},{6,70},{7,71},{8,72},{9,... | collective-permute-start | bytes 1474568 | tf_op jit(solution)/shard_map/ppermute | solution.py:39
  27.8 19.6 %collective-permute-start.2 = (bf16[128,1920]{1,0:T(8,128)(2,1)S(1)}, bf16[128,1920]{1,0:T(8,128)(2,1)S(1)}, u32[]{:S(2)}, u32[]{:S(2)}) collective-permute-start(bf16[128,1920]{1,0:T(8,128)(2,1)S(1)} %maximum_select_fusion.refs_0_), channel_id=1, source_target_pairs={{0,32},{1,33},{2,34},{3,35},{4,36},{5,37},{6,38},{7,39},{8,40},{9,... | collective-permute-start | bytes 1474568 | tf_op jit(solution)/shard_map/ppermute | solution.py:39
  28.1 10.8 %collective-permute-start.6 = (bf16[128,1280]{1,0:T(8,128)(2,1)S(1)}, bf16[128,1280]{1,0:T(8,128)(2,1)}, u32[]{:S(2)}, u32[]{:S(2)}) collective-permute-start(bf16[128,1280]{1,0:T(8,128)(2,1)S(1)} %slice.27.refs_4_), channel_id=1, source_target_pairs={{0,4},{1,5},{2,6},{3,7},{4,0},{5,1},{6,2},{7,3},{8,12},{9,13},{10,... | collective-permute-start | bytes 983048 | tf_op jit(solution)/shard_map/ppermute | solution.py:39
  29.7 17.6 %collective-permute-start.5 = (bf16[128,1280]{1,0:T(8,128)(2,1)S(1)}, bf16[128,1280]{1,0:T(8,128)(2,1)}, u32[]{:S(2)}, u32[]{:S(2)}) collective-permute-start(bf16[128,1280]{1,0:T(8,128)(2,1)S(1)} %slice.27.refs_4_), channel_id=1, source_target_pairs={{0,2},{1,3},{2,4},{3,5},{4,6},{5,7},{6,0},{7,1},{8,10},{9,11},{10,... | collective-permute-start | bytes 983048 | tf_op jit(solution)/shard_map/ppermute | solution.py:39
  56.1 0.7 copy-start.2
  56.7 0.7 copy-start.4
  57.4 4.5 %collective-permute-start.10 = (f32[16,512]{1,0:T(8,128)S(1)}, f32[16,512]{1,0:T(8,128)S(1)}, u32[]{:S(2)}, u32[]{:S(2)}) collective-permute-start(f32[16,512]{1,0:T(8,128)S(1)} %get-tuple-element.37.refs_0_), channel_id=1, source_target_pairs={{0,96},{1,97},{2,98},{3,99},{4,100},{5,101},{6,102},{7,103},{8,104... | collective-permute-start | bytes 98312 | tf_op jit(solution)/shard_map/ppermute | solution.py:39
  58.3 4.1 %collective-permute-start.9 = (f32[16,512]{1,0:T(8,128)S(1)}, f32[16,512]{1,0:T(8,128)S(1)}, u32[]{:S(2)}, u32[]{:S(2)}) collective-permute-start(f32[16,512]{1,0:T(8,128)S(1)} %get-tuple-element.37.refs_0_), channel_id=1, source_target_pairs={{0,64},{1,65},{2,66},{3,67},{4,68},{5,69},{6,70},{7,71},{8,72},{9,... | collective-permute-start | bytes 98312 | tf_op jit(solution)/shard_map/ppermute | solution.py:39
  60.4 2.1 %collective-permute-start.8 = (f32[16,512]{1,0:T(8,128)S(1)}, f32[16,512]{1,0:T(8,128)S(1)}, u32[]{:S(2)}, u32[]{:S(2)}) collective-permute-start(f32[16,512]{1,0:T(8,128)S(1)} %get-tuple-element.37.refs_0_), channel_id=1, source_target_pairs={{0,32},{1,33},{2,34},{3,35},{4,36},{5,37},{6,38},{7,39},{8,40},{9,... | collective-permute-start | bytes 98312 | tf_op jit(solution)/shard_map/ppermute | solution.py:39
  60.4 2.8 %collective-permute-start.13 = (f32[16,512]{1,0:T(8,128)S(1)}, f32[16,512]{1,0:T(8,128)S(1)}, u32[]{:S(2)}, u32[]{:S(2)}) collective-permute-start(f32[16,512]{1,0:T(8,128)S(1)} %get-tuple-element.38.refs_4_.refs_0_), channel_id=1, source_target_pairs={{0,6},{1,7},{2,0},{3,1},{4,2},{5,3},{6,4},{7,5},{8,14},{9,15},{10,... | collective-permute-start | bytes 98312 | tf_op jit(solution)/shard_map/ppermute | solution.py:39
  61.9 4.3 %collective-permute-start.12 = (f32[16,512]{1,0:T(8,128)S(1)}, f32[16,512]{1,0:T(8,128)S(1)}, u32[]{:S(2)}, u32[]{:S(2)}) collective-permute-start(f32[16,512]{1,0:T(8,128)S(1)} %get-tuple-element.38.refs_4_.refs_0_), channel_id=1, source_target_pairs={{0,4},{1,5},{2,6},{3,7},{4,0},{5,1},{6,2},{7,3},{8,12},{9,13},{10,... | collective-permute-start | bytes 98312 | tf_op jit(solution)/shard_map/ppermute | solution.py:39
  61.9 4.3 %collective-permute-start.11 = (f32[16,512]{1,0:T(8,128)S(1)}, f32[16,512]{1,0:T(8,128)S(1)}, u32[]{:S(2)}, u32[]{:S(2)}) collective-permute-start(f32[16,512]{1,0:T(8,128)S(1)} %get-tuple-element.38.refs_4_.refs_0_), channel_id=1, source_target_pairs={{0,2},{1,3},{2,4},{3,5},{4,6},{5,7},{6,0},{7,1},{8,10},{9,11},{10,... | collective-permute-start | bytes 98312 | tf_op jit(solution)/shard_map/ppermute | solution.py:39
  69.4 6.0 %copy-start.5 = (bf16[640,128]{1,0:T(8,128)(2,1)S(1)}, bf16[640,128]{1,0:T(8,128)(2,1)}, u32[]{:S(2)}) copy-start(bf16[640,128]{1,0:T(8,128)(2,1)} %copy-done.4) | copy-start | bytes 491524
  69.4 6.1 %copy-start.3 = (bf16[640,128]{1,0:T(8,128)(2,1)S(1)}, bf16[640,128]{1,0:T(8,128)(2,1)}, u32[]{:S(2)}) copy-start(bf16[640,128]{1,0:T(8,128)(2,1)} %copy-done.2) | copy-start | bytes 491524
  69.4 44.3 %all-to-all-start = ((bf16[8,5,64,512]{3,2,1,0:T(8,128)(2,1)}), bf16[8,5,64,512]{3,2,1,0:T(8,128)(2,1)S(1)}, u32[]{:S(2)}, u32[]{:S(2)}) async-start(bf16[8,5,64,512]{3,2,1,0:T(8,128)(2,1)} %symmetric.1), calls=%async_computation | async-start | bytes 5242880 | tf_op jit(solution)/shard_map/all_to_all | solution.py:379
  75.5 7.3 %collective-permute-start.14 = (bf16[640,128]{1,0:T(8,128)(2,1)S(1)}, bf16[640,128]{1,0:T(8,128)(2,1)S(1)}, u32[]{:S(2)}, u32[]{:S(2)}) collective-permute-start(bf16[640,128]{1,0:T(8,128)(2,1)S(1)} %copy-done.5), channel_id=1, source_target_pairs={{0,2},{1,3},{2,4},{3,5},{4,6},{5,7},{6,0},{7,1},{8,10},{9,11},{10,... | collective-permute-start | bytes 491528 | tf_op jit(solution)/shard_map/ppermute | solution.py:39
  75.5 8.0 %collective-permute-start.15 = (bf16[640,128]{1,0:T(8,128)(2,1)S(1)}, bf16[640,128]{1,0:T(8,128)(2,1)S(1)}, u32[]{:S(2)}, u32[]{:S(2)}) collective-permute-start(bf16[640,128]{1,0:T(8,128)(2,1)S(1)} %copy-done.3), channel_id=1, source_target_pairs={{0,4},{1,5},{2,6},{3,7},{4,0},{5,1},{6,2},{7,3},{8,12},{9,13},{10,... | collective-permute-start | bytes 491528 | tf_op jit(solution)/shard_map/ppermute | solution.py:39
  77.6 6.6 %collective-permute-start.16 = (bf16[640,128]{1,0:T(8,128)(2,1)S(1)}, bf16[640,128]{1,0:T(8,128)(2,1)S(1)}, u32[]{:S(2)}, u32[]{:S(2)}) collective-permute-start(bf16[640,128]{1,0:T(8,128)(2,1)S(1)} %get-tuple-element.51), channel_id=1, source_target_pairs={{0,6},{1,7},{2,0},{3,1},{4,2},{5,3},{6,4},{7,5},{8,14},{9,15},{10,... | collective-permute-start | bytes 491528 | tf_op jit(solution)/shard_map/ppermute | solution.py:39
  85.4 26.3 %collective-permute-start.17 = (bf16[64,640]{1,0:T(8,128)(2,1)S(1)}, bf16[64,640]{1,0:T(8,128)(2,1)S(1)}, u32[]{:S(2)}, u32[]{:S(2)}) collective-permute-start(bf16[64,640]{1,0:T(8,128)(2,1)S(1)} %get-tuple-element.52), channel_id=1, source_target_pairs={{0,0},{1,1},{2,2},{3,3},{4,4},{5,5},{6,6},{7,7},{8,32},{9,33},{10,... | collective-permute-start | bytes 245768 | tf_op jit(solution)/shard_map/ppermute | solution.py:39
  91.8 21.9 %collective-permute-start.18 = (bf16[64,640]{1,0:T(8,128)(2,1)S(1)}, bf16[64,640]{1,0:T(8,128)(2,1)S(1)}, u32[]{:S(2)}, u32[]{:S(2)}) collective-permute-start(bf16[64,640]{1,0:T(8,128)(2,1)S(1)} %get-tuple-element.53), channel_id=1, source_target_pairs={{0,1},{1,0},{2,3},{3,2},{4,5},{5,4},{6,7},{7,6},{8,33},{9,32},{10,... | collective-permute-start | bytes 245768 | tf_op jit(solution)/shard_map/ppermute | solution.py:39
  111.7 2.0 %copy-start.6 = (bf16[64,640]{1,0:T(8,128)(2,1)}, bf16[64,640]{1,0:T(8,128)(2,1)S(1)}, u32[]{:S(2)}) copy-start(bf16[64,640]{1,0:T(8,128)(2,1)S(1)} %collective-permute-done.17.same) | copy-start | bytes 245764
  113.7 0.6 copy-start.7

commit v3 on v2

--- a/solution.py
+++ b/solution.py
@@ -19,6 +19,7 @@
 HALF = 64
 TILE = 512
 ROWS = 16
+ONES = 16
 SCALE = math.log2(math.e) / math.sqrt(HEAD_DIM)
 AXES = ("head", "band")
 MIB = 1 << 20
@@ -55,24 +56,30 @@
     return lax.dot_general(a, b, (((1,), (1,)), ((), ())), preferred_element_type=jnp.float32)
 
 
-def fetch(where, row_blocks, column_blocks, rows_ref, columns_ref, sems):
+def fetch(where, row_blocks, row_parts, column_blocks, column_part, sems):
     y, x, z, c = (where[i] for i in range(4))
     copies = []
     for d in range(4):
         away = lax.rem(lax.bitwise_xor(c, d) - y + 4, 4)
         for part in range(2):
             start = pl.multiple_of(away * BLOCK + lax.bitwise_xor(z, part) * HALF, HALF)
-            copies.append(
-                pltpu.make_async_copy(
-                    row_blocks[d].at[pl.ds(part * HALF, HALF)],
-                    rows_ref.at[pl.ds(start, HALF)],
-                    sems.at[2 * d + part],
+            for ref, at in row_parts:
+                copies.append(
+                    pltpu.make_async_copy(
+                        row_blocks[d].at[pl.ds(part * HALF, HALF), pl.ds(at * WIDE, WIDE)],
+                        ref.at[pl.ds(start, HALF)],
+                        sems.at[len(copies)],
+                    )
                 )
-            )
-        start = pl.multiple_of(lax.rem(x - d + 4, 4) * BLOCK, BLOCK)
+    ref, at = column_part
+    for block, d, skip in zip(column_blocks, (0, 1, 3, 2, 2), (0, 0, 0, 0, HALF)):
+        rows = block.shape[0]
+        start = pl.multiple_of(lax.rem(x - d + 4, 4) * BLOCK + skip, HALF)
         copies.append(
             pltpu.make_async_copy(
-                column_blocks[d], columns_ref.at[pl.ds(start, BLOCK)], sems.at[8 + d]
+                block.at[:, pl.ds(at * WIDE, WIDE)],
+                ref.at[pl.ds(start, rows)],
+                sems.at[len(copies)],
             )
         )
     for copy in copies:
@@ -81,39 +88,42 @@
         copy.wait()
 
 
-def head(ref, part, h):
-    return ref[:, part * WIDE + h * HEAD_DIM : part * WIDE + (h + 1) * HEAD_DIM]
-
-
-def stats_kernel(where, *refs):
-    by_row, by_column, row_lifted, column_lifted = refs[8:12]
-    partials, (rows_ref, columns_ref, held, sems) = refs[12:16], refs[16:]
-    fetch(where, refs[0:4], refs[4:8], rows_ref, columns_ref, sems)
-    by_column[...] = jnp.zeros_like(by_column)
+def head(ref, h):
+    return ref[:, h * HEAD_DIM : (h + 1) * HEAD_DIM]
+
+
+def row_kernel(where, *refs):
+    by_row, lifted_out, queries, keys, sems = refs[9:]
+    fetch(where, refs[0:4], [(queries, 0)], refs[4:9], (keys, 1), sems)
     lane = lax.broadcasted_iota(jnp.int32, (TILE, 128), 1)
     kept = jnp.zeros((TILE, 128), jnp.float32)
     for h in range(GROUP):
-        scores = nt(head(rows_ref, 0, h), head(columns_ref, 1, h)) * SCALE
+        scores = nt(head(queries, h), head(keys, h)) * SCALE
         top = jnp.max(scores, axis=1, keepdims=True)
         lifted = jnp.exp2(scores - top)
-        row_lifted[h] = lifted.astype(jnp.bfloat16)
+        lifted_out[h] = lifted.astype(jnp.bfloat16)
         kept = jnp.where(lane == h, top, kept)
         kept = jnp.where(lane == 8 + h, jnp.sum(lifted, axis=1, keepdims=True), kept)
-        scores = nt(head(rows_ref, 1, h), head(columns_ref, 0, h)) * SCALE
+    by_row[...] = jnp.transpose(kept)[0:16]
+
+
+def column_kernel(where, *refs):
+    by_column, lifted_out = refs[9:11]
+    partials, (keys, values, queries, held, sems) = refs[11:15], refs[15:]
+    fetch(where, refs[0:4], [(keys, 1), (values, 2)], refs[4:9], (queries, 0), sems)
+    by_column[...] = jnp.zeros_like(by_column)
+    for h in range(GROUP):
+        scores = nt(head(keys, h), head(queries, h)) * SCALE
         top = jnp.max(scores, axis=0, keepdims=True)
         lifted = jnp.exp2(scores - top)
         by_column[h : h + 1, :] = top
         by_column[8 + h : 9 + h, :] = jnp.sum(lifted, axis=0, keepdims=True)
         lifted = lifted.astype(jnp.bfloat16)
-        column_lifted[h] = lifted
+        lifted_out[h] = lifted
         part = lax.dot_general(
-            head(rows_ref, 2, h),
-            lifted,
-            (((0,), (0,)), ((), ())),
-            preferred_element_type=jnp.float32,
+            head(values, h), lifted, (((0,), (0,)), ((), ())), preferred_element_type=jnp.float32
         )
         held[h * HEAD_DIM : (h + 1) * HEAD_DIM, :] = part.astype(jnp.bfloat16)
-    by_row[...] = jnp.transpose(kept)[0:16]
     for d in range(4):
         owner = lax.rem(where[1] + d, 4)
         partials[d][...] = held[:, pl.ds(pl.multiple_of(owner * BLOCK, BLOCK), BLOCK)]
@@ -131,18 +141,23 @@
 
 def symmetric_kernel(where, *refs):
     row_stats, column_stats = refs[0:4], refs[4:8]
-    row_lifted, column_lifted, out = refs[8:]
+    row_lifted, column_lifted, out, held, sems = refs[8:]
     by_row = turned(factors(row_stats) * 1024.0)
     by_column = factors(column_stats) * 1024.0
     y, z = where[0], where[2]
+    copies = []
     for p in range(8):
         owner = lax.rem(y + p // 2, 4) * 2 + lax.bitwise_xor(z, p % 2)
         here = slice(p * HALF, (p + 1) * HALF)
         for h in range(GROUP):
-            out[owner, h] = (
+            held[p, h] = (
                 row_lifted[h, here].astype(jnp.float32) * by_row[here, h : h + 1]
                 + column_lifted[h, here].astype(jnp.float32) * by_column[h : h + 1, :]
             ).astype(jnp.bfloat16)
+        copies.append(pltpu.make_async_copy(held.at[p], out.at[owner], sems.at[p]))
+        copies[p].start()
+    for copy in copies:
+        copy.wait()
 
 
 def context_kernel(where, *refs):
@@ -188,23 +203,30 @@
 
 
 def spread_kernel(
-    first, first_bias, second, second_bias, table, first_out, first_bias_out, second_out,
-    second_bias_out, table_out,
+    first, first_bias, second, second_bias, table, first_out, second_out, second_bias_out, table_out
 ):
     by_eight, eight = lambda r: r // 8, lambda r: r % 8
     by_four, four = lambda r: r // 4, lambda r: r % 4
     hid, outs = first.shape[1], second.shape[1]
     channel = lambda r: r % (hid * 4) // 4
-    first_out[...] = expanded(
+    width = first.shape[0] * 8
+    first_out[:, :width] = expanded(
         first[...],
         channel,
         lambda r: r // (hid * 4) * 4 + r % 4,
         by_eight,
         eight,
         hid * 8,
-        first_out.shape[1],
-    )
-    first_bias_out[...] = repeated(first_bias, channel, hid * 8)
+        width,
+    )
+    rest, parts = repeated(first_bias, channel, hid * 8)[:, :ONES], []
+    for _ in range(3):
+        parts.append(rest.astype(jnp.bfloat16).astype(jnp.float32))
+        rest = rest - parts[-1]
+    lane = lax.broadcasted_iota(jnp.int32, (hid * 8, ONES), 1)
+    first_out[:, width:] = sum(
+        jnp.where(lane == i, part, 0.0) for i, part in enumerate(parts)
+    ).astype(jnp.bfloat16)
     second_out[: outs * 4] = expanded(second[...], by_four, four, by_four, four, outs * 4, hid * 4)
     second_out[outs * 4 :] = expanded(
         second[...], lambda r: r // 4 + 1 - r // 4 % 2 * 2, four, by_four, four, outs * 4, hid * 4
@@ -237,9 +259,7 @@
     out[...] = jnp.concatenate(halves, axis=1).astype(jnp.bfloat16)
 
 
-def pair_kernel(
-    where, tiles, first, first_bias, second, second_bias, relative, same, other, out, context
-):
+def pair_kernel(where, tiles, first, second, second_bias, relative, same, other, out, context):
     z = where[2]
 
     @pl.when(pl.program_id(0) == 0)
@@ -250,12 +270,13 @@
     loaded = tiles[...].astype(jnp.float32)
     outs, hid = second.shape[0] // 8, first.shape[0] // 8
     upper = lax.broadcasted_iota(jnp.int32, (outs // 2, 8, TILE), 1) < 4
+    ones = jnp.ones((ONES, TILE), jnp.bfloat16)
     halves = []
     for half in range(ROWS // 8):
         stacked = loaded[:, half * 8 : half * 8 + 8, :].reshape(-1, TILE).astype(jnp.bfloat16)
+        stacked = jnp.concatenate([stacked, ones], axis=0)
         hidden = jnp.dot(first[...], stacked, preferred_element_type=jnp.float32)
-        hidden = jnp.maximum(hidden + jnp.concatenate([first_bias[...]] * 4, axis=1), 0.0)
-        hidden = hidden.astype(jnp.bfloat16)
+        hidden = jnp.maximum(hidden, 0.0).astype(jnp.bfloat16)
         low, high = (
             jnp.dot(
                 second[part * outs * 4 : (part + 1) * outs * 4],
@@ -277,11 +298,18 @@
 
 SMEM = pl.BlockSpec(memory_space=pltpu.SMEM)
 ANY = pl.BlockSpec(memory_space=pl.ANY)
+HBM = pl.BlockSpec(memory_space=pltpu.HBM)
 VMEM = pl.BlockSpec(memory_space=pltpu.VMEM)
 
 
 def params(mib):
     return pltpu.CompilerParams(vmem_limit_bytes=mib * MIB)
+
+
+def cost(flops, bytes_accessed, exponentials=0):
+    return pl.CostEstimate(
+        flops=int(flops), bytes_accessed=int(bytes_accessed), transcendentals=int(exponentials)
+    )
 
 
 def in_hbm(value):
@@ -302,20 +330,26 @@
     where = jnp.stack([y, x, z, c]).astype(jnp.int32)
     hid, outs = w_first.shape[1], w_second.shape[1]
 
-    first, first_bias, second, second_bias, table = pl.pallas_call(
+    first, second, second_bias, table = pl.pallas_call(
         spread_kernel,
         in_specs=[VMEM] * 5,
-        out_specs=[VMEM] * 5,
+        out_specs=[VMEM] * 4,
         out_shape=[
-            pltpu.HBM((hid * 8, 8 * GROUP * 8), jnp.bfloat16),
-            pltpu.HBM((hid * 8, 128), jnp.float32),
+            pltpu.HBM((hid * 8, 8 * GROUP * 8 + ONES), jnp.bfloat16),
             pltpu.HBM((outs * 8, hid * 4), jnp.bfloat16),
             pltpu.HBM((outs * 8, 128), jnp.float32),
             shape((outs * 8, 72 * 8)),
         ],
         compiler_params=params(6),
+        cost_estimate=cost(4e8, 6e6),
         name="spread",
-    )(w_first, b_first[:, None], w_second, b_second[:, None], jnp.pad(rel_table, ((0, 72 - BINS), (0, 0))))
+    )(
+        w_first,
+        b_first[:, None],
+        w_second,
+        b_second[:, None],
+        jnp.pad(rel_table, ((0, 72 - BINS), (0, 0))),
+    )
 
     near = jnp.concatenate([queries[:, :WIDE], keys[:, :WIDE], values[:, :WIDE]], axis=1)
     far = jnp.concatenate([queries[:, WIDE:], keys[:, WIDE:], values[:, WIDE:]], axis=1)
@@ -327,14 +361,14 @@
         jnp.concatenate([other, same], axis=0),
     )
 
-    block, first, first_bias, second, second_bias, table = lax.optimization_barrier(
-        (block, first, first_bias, second, second_bias, table)
+    block, first, second, second_bias, table = lax.optimization_barrier(
+        (block, first, second, second_bias, table)
     )
     narrow = block[:, : 2 * WIDE]
 
-    column_blocks = [narrow] + over_columns(narrow)
-    row_blocks = [block] + over_rows(block)
-
+    across = send(block, lambda y, x, z, c: (y, x, z, c ^ 2))
+    right = send(narrow, lambda y, x, z, c: (y, (x + 1) % 4, z, c))
+    left = send(narrow, lambda y, x, z, c: (y, (x + 3) % 4, z, c))
     relative = pl.pallas_call(
         relative_kernel,
         grid=(HALF // ROWS,),
@@ -342,26 +376,42 @@
         out_specs=pl.BlockSpec((outs, ROWS, TILE), lambda i: (0, i, 0)),
         out_shape=pltpu.HBM((outs, HALF, TILE), jnp.bfloat16),
         compiler_params=params(8),
+        cost_estimate=cost(2.4e9, 6e6),
         name="relative",
     )(where, chain_lengths, table)
-    where, relative = lax.optimization_barrier((where, relative))
-
-    by_row, by_column, row_lifted, column_lifted, *partials = pl.pallas_call(
-        stats_kernel,
-        in_specs=[SMEM] + [ANY] * 8,
-        out_specs=[VMEM] * 8,
-        out_shape=[shape((16, TILE), jnp.float32)] * 2
-        + [shape((GROUP, TILE, TILE))] * 2
-        + [pltpu.HBM((WIDE, BLOCK), jnp.bfloat16)]
-        + [shape((WIDE, BLOCK))] * 3,
-        scratch_shapes=[
-            vmem(TILE, 3 * WIDE),
-            vmem(TILE, 2 * WIDE),
-            vmem(WIDE, TILE),
-            pltpu.SemaphoreType.DMA((12,)),
-        ],
+    where, relative, left, right = lax.optimization_barrier((where, relative, left, right))
+    column_blocks = [
+        narrow,
+        right,
+        left,
+        send(right[:HALF], lambda y, x, z, c: (y, (x + 1) % 4, z, c)),
+        send(left[HALF:], lambda y, x, z, c: (y, (x + 3) % 4, z, c)),
+    ]
+    relative, across, block = lax.optimization_barrier((relative, across, block))
+    beside = send(block, lambda y, x, z, c: (y, x, z, c ^ 1))
+    row_blocks = [block, beside, across, send(across, lambda y, x, z, c: (y, x, z, c ^ 1))]
+
+    by_row, row_lifted = pl.pallas_call(
+        row_kernel,
+        in_specs=[SMEM] + [ANY] * 9,
+        out_specs=[VMEM] * 2,
+        out_shape=[shape((16, TILE), jnp.float32), shape((GROUP, TILE, TILE))],
+        scratch_shapes=[vmem(TILE, WIDE)] * 2 + [pltpu.SemaphoreType.DMA((13,))],
         compiler_params=params(12),
-        name="stats",
+        cost_estimate=cost(4e8, 8e6, 1.4e6),
+        name="rows",
+    )(where, *row_blocks, *column_blocks)
+    by_column, column_lifted, *partials = pl.pallas_call(
+        column_kernel,
+        in_specs=[SMEM] + [ANY] * 9,
+        out_specs=[VMEM] * 6,
+        out_shape=[shape((16, TILE), jnp.float32), shape((GROUP, TILE, TILE))]
+        + [shape((WIDE, BLOCK))] * 4,
+        scratch_shapes=[vmem(TILE, WIDE)] * 3
+        + [vmem(WIDE, TILE), pltpu.SemaphoreType.DMA((21,))],
+        compiler_params=params(12),
+        cost_estimate=cost(7e8, 9e6, 1.4e6),
+        name="columns",
     )(where, *row_blocks, *column_blocks)
     row_stats = [by_row] + over_rows(by_row)
     column_stats = [by_column] + over_columns(by_column)
@@ -369,9 +419,14 @@
     tiles = pl.pallas_call(
         symmetric_kernel,
         in_specs=[SMEM] + [VMEM] * 10,
-        out_specs=VMEM,
+        out_specs=HBM,
         out_shape=shape((8, GROUP, HALF, TILE)),
+        scratch_shapes=[
+            pltpu.VMEM((8, GROUP, HALF, TILE), jnp.bfloat16),
+            pltpu.SemaphoreType.DMA((8,)),
+        ],
         compiler_params=params(8),
+        cost_estimate=cost(1e7, 9e6),
         name="symmetric",
     )(where, *row_stats, *column_stats, row_lifted, column_lifted)
     where, tiles = lax.optimization_barrier((where, tiles))
@@ -387,8 +442,9 @@
         out_shape=[shape((HALF, WIDE))] * 2,
         scratch_shapes=[vmem(BLOCK, WIDE)],
         compiler_params=params(4),
+        cost_estimate=cost(1e6, 2e6),
         name="context",
-    )(where, *column_stats, in_hbm(partials[0]), *over_columns_of(partials))
+    )(where, *column_stats, partials[0], *over_columns_of(partials))
     same = send(same, lambda y, x, z, c: (c, x, z, y))
     other = send(other, lambda y, x, z, c: (c, x, 1 - z, y))
 
@@ -398,8 +454,7 @@
         in_specs=[
             SMEM,
             pl.BlockSpec((8 * GROUP, ROWS, TILE), lambda i: (0, i, 0)),
-            pl.BlockSpec((hid * 8, 8 * GROUP * 8), lambda i: (0, 0)),
-            pl.BlockSpec((hid * 8, 128), lambda i: (0, 0)),
+            pl.BlockSpec((hid * 8, 8 * GROUP * 8 + ONES), lambda i: (0, 0)),
             pl.BlockSpec((outs * 8, hid * 4), lambda i: (0, 0)),
             pl.BlockSpec((outs * 8, 128), lambda i: (0, 0)),
             pl.BlockSpec((outs, ROWS, TILE), lambda i: (0, i, 0)),
@@ -411,12 +466,13 @@
             pl.BlockSpec((HALF, 2 * WIDE), lambda i: (0, 0)),
         ],
         out_shape=[shape((outs, HALF, TILE)), shape((HALF, 2 * WIDE))],
-        compiler_params=params(13),
+        compiler_params=params(14),
+        cost_estimate=cost(5e9, 14e6),
         name="pair",
     )(
         where,
         received,
-        *(in_hbm(a) for a in (first, first_bias, second, second_bias, relative, same, other)),
+        *(in_hbm(a) for a in (first, second, second_bias, relative, same, other)),
     )
     return (context, pair)
 

time: 126 us -> 119 us (0.944)
  waiting for transfers between devices: 43.2 us -> 39.8 us
  Pallas kernels: 32.4 us -> 29.3 us
  local copies, waits for them, and re-layouts: 7.83 us -> 6.54 us
    ppermute x19 -> x20, waiting for transfers between devices: 43.2 us -> 39.8 us  [send(): return lax.ppermute(value, AXES, moves(to))]
    pallas_call x2 -> x3, Pallas kernels: 11.4 us -> 9.16 us  [the longest x1 4.01 us: local(): pl.pallas_call(column_kernel, in_specs=[SMEM] + [ANY] * 9, out_specs=[VME...]
    ppermute x19 -> x20, starting transfers between devices: 34.7 us -> 36.4 us  [send(): return lax.ppermute(value, AXES, moves(to))]
    unnamed x18 -> x10, local copies, waits for them, and re-layouts: 4.29 us -> 2.99 us
  transfers between devices with their start and end apart: 20 -> 21, of which waited for: 12 -> 10; matrix products, arithmetic and copies ran while one was open for 3% -> 3% of each run, Pallas kernels for 8% -> 10%
where the time goes in v3:
time: 119 us; the launch traced here: 118 us
  starting transfers between devices  41.4 us (35%)
  waiting for transfers between devices  39.8 us (33%)
  Pallas kernels  29.3 us (25%)
  local copies, waits for them, and re-layouts  6.54 us (5%)
    ppermute x20, waiting for transfers between devices, send(): return lax.ppermute(value, AXES, moves(to))  39.8 us
    ppermute x20, starting transfers between devices, send(): return lax.ppermute(value, AXES, moves(to))  36.4 us
    pallas_call x1, Pallas kernels, local(): pl.pallas_call(pair_kernel, grid=(HALF // ROWS,), in_specs=[SMEM, pl.Bloc...  10.7 us
    pallas_call x1, Pallas kernels, local(): pl.pallas_call(relative_kernel, grid=(HALF // ROWS,), in_specs=[SMEM, SME...  5.73 us
    all_to_all x1, starting transfers between devices, local(): lax.all_to_all(tiles, 'band', split_axis=0, concat_axis=0, axis_index_gro...  5.04 us
    pallas_call x1, Pallas kernels, local(): pl.pallas_call(column_kernel, in_specs=[SMEM] + [ANY] * 9, out_specs=[VME...  4.01 us
    unnamed x10, local copies, waits for them, and re-layouts  2.99 us
    pallas_call x1, Pallas kernels, local(): pl.pallas_call(symmetric_kernel, in_specs=[SMEM] + [VMEM] * 10, out_specs...  2.87 us
  transfers between devices with their start and end apart: 21, of which 10 were waited for; matrix products, arithmetic and copies ran while one was open for 3% of the time, Pallas kernels for 10%

profile of v3, /device:TPU:1, one launch (start us, length us, event | category | flops | bytes accessed | tf_op | source)
XLA Modules:
  0.0 118.0 jit_solution(6749100698147638686)
XLA Ops:
  0.6 0.9 fusion.2
  1.6 1.0 fusion
  2.6 0.1 broadcast_select_fusion.1
  2.7 4.6 %collective-permute-start = (bf16[64,1920]{1,0:T(8,128)(2,1)S(1)}, bf16[64,1920]{1,0:T(8,128)(2,1)S(1)}, u32[]{:S(2)}, u32[]{:S(2)}) collective-permute-start(bf16[64,1920]{1,0:T(8,128)(2,1)S(1)} %get-tuple-element.62), channel_id=1, source_target_pairs={{0,0},{1,1},{2,2},{3,3},{4,4},{5,5},{6,6},{7,7},{8,32},{9,33},{10,... | collective-permute-start | bytes 737288 | tf_op jit(solution)/shard_map/ppermute | solution.py:40
  7.3 3.4 %collective-permute-start.1 = (bf16[64,1920]{1,0:T(8,128)(2,1)S(1)}, bf16[64,1920]{1,0:T(8,128)(2,1)S(1)}, u32[]{:S(2)}, u32[]{:S(2)}) collective-permute-start(bf16[64,1920]{1,0:T(8,128)(2,1)S(1)} %get-tuple-element.63), channel_id=1, source_target_pairs={{0,1},{1,0},{2,3},{3,2},{4,5},{5,4},{6,7},{7,6},{8,33},{9,32},{10,... | collective-permute-start | bytes 737288 | tf_op jit(solution)/shard_map/ppermute | solution.py:40
  10.7 0.8 copy.11
  11.6 0.8 copy.13.second
  12.4 0.8 copy.14.second_bias
  13.2 0.8 copy.12.first_bias
  13.9 0.0 copy-start
  13.9 0.7 copy-done
  14.6 2.7 %spread.1 = (bf16[1024,336]{1,0:T(8,128)(2,1)}, bf16[512,512]{1,0:T(8,128)(2,1)}, f32[512,128]{1,0:T(8,128)}, bf16[512,576]{1,0:T(8,128)(2,1)S(1)}) custom-call(bf16[40,128]{1,0:T(8,128)(2,1)S(1)} %copy-done, f32[128,1]{1,0:T(8,128)S(1)} %copy.12.first_bias, bf16[128,64]{1,0:T(8,128)(2,1)S(1)} %copy.13.second, f32[64,1]{1,0:T(8,128)S(1)} %copy.14.second_bias, ...), custom_call_target="tpu_custom_call" | custom-call | flops 400000000 | bytes 6000000 | tf_op jit(solution)/shard_map/spread/pallas_call | solution.py:333
  17.3 2.9 %collective-permute-done.1 = bf16[64,1920]{1,0:T(8,128)(2,1)S(1)} collective-permute-done((bf16[64,1920]{1,0:T(8,128)(2,1)S(1)}, bf16[64,1920]{1,0:T(8,128)(2,1)S(1)}, u32[]{:S(2)}, u32[]{:S(2)}) %collective-permute-start.1) | collective-permute-done | bytes 245792 | tf_op jit(solution)/shard_map/ppermute | solution.py:40
  20.3 0.1 maximum_select_fusion.refs_0_
  20.3 4.9 %collective-permute-start.4 = (bf16[128,1920]{1,0:T(8,128)(2,1)S(1)}, bf16[128,1920]{1,0:T(8,128)(2,1)S(1)}, u32[]{:S(2)}, u32[]{:S(2)}) collective-permute-start(bf16[128,1920]{1,0:T(8,128)(2,1)S(1)} %maximum_select_fusion.refs_0_), channel_id=1, source_target_pairs={{0,64},{1,65},{2,66},{3,67},{4,68},{5,69},{6,70},{7,71},{8,72},{9,... | collective-permute-start | bytes 1474568 | tf_op jit(solution)/shard_map/ppermute | solution.py:40
  25.3 1.3 %collective-permute-start.3 = (bf16[128,1280]{1,0:T(8,128)(2,1)S(1)}, bf16[128,1280]{1,0:T(8,128)(2,1)S(1)}, u32[]{:S(2)}, u32[]{:S(2)}) collective-permute-start(bf16[128,1280]{1,0:T(8,128)(2,1)S(1)} %slice.33.refs_4_), channel_id=1, source_target_pairs={{0,2},{1,3},{2,4},{3,5},{4,6},{5,7},{6,0},{7,1},{8,10},{9,11},{10,... | collective-permute-start | bytes 983048 | tf_op jit(solution)/shard_map/ppermute | solution.py:40
  26.5 1.5 %collective-permute-start.2 = (bf16[128,1280]{1,0:T(8,128)(2,1)S(1)}, bf16[128,1280]{1,0:T(8,128)(2,1)S(1)}, u32[]{:S(2)}, u32[]{:S(2)}) collective-permute-start(bf16[128,1280]{1,0:T(8,128)(2,1)S(1)} %slice.33.refs_4_), channel_id=1, source_target_pairs={{0,6},{1,7},{2,0},{3,1},{4,2},{5,3},{6,4},{7,5},{8,14},{9,15},{10,... | collective-permute-start | bytes 983048 | tf_op jit(solution)/shard_map/ppermute | solution.py:40
  28.0 0.1 pad_add_fusion.where
  28.1 5.7 %relative.1 = bf16[64,64,512]{2,1,0:T(8,128)(2,1)} custom-call(s32[4]{0:T(128)S(1)} %pad_add_fusion.where, s32[4]{0:T(128)S(1)} %copy-done.1, bf16[512,576]{1,0:T(8,128)(2,1)S(1)} %get-tuple-element.36.table), custom_call_target="tpu_custom_call" | custom-call | flops 2400000000 | bytes 6000000 | tf_op jit(solution)/shard_map/relative/pallas_call | solution.py:372
  33.8 0.2 collective-permute-done.4.refs_2_
  34.1 0.5 collective-permute-start.6
  34.6 2.5 %collective-permute-start.8 = (bf16[64,1280]{1,0:T(8,128)(2,1)S(1)}, bf16[64,1280]{1,0:T(8,128)(2,1)S(1)}, u32[]{:S(2)}, u32[]{:S(2)}) collective-permute-start(bf16[64,1280]{1,0:T(8,128)(2,1)S(1)} %slice.35), channel_id=1, source_target_pairs={{0,6},{1,7},{2,0},{3,1},{4,2},{5,3},{6,4},{7,5},{8,14},{9,15},{10,... | collective-permute-start | bytes 491528 | tf_op jit(solution)/shard_map/ppermute | solution.py:40
  37.2 3.6 %collective-permute-done.8.refs_8_ = bf16[64,1280]{1,0:T(8,128)(2,1)S(1)} collective-permute-done((bf16[64,1280]{1,0:T(8,128)(2,1)S(1)}, bf16[64,1280]{1,0:T(8,128)(2,1)S(1)}, u32[]{:S(2)}, u32[]{:S(2)}) %collective-permute-start.8) | collective-permute-done | bytes 163872 | tf_op jit(solution)/shard_map/ppermute | solution.py:40
  40.8 3.1 %collective-permute-done.7.refs_7_ = bf16[64,1280]{1,0:T(8,128)(2,1)S(1)} collective-permute-done((bf16[64,1280]{1,0:T(8,128)(2,1)S(1)}, bf16[64,1280]{1,0:T(8,128)(2,1)S(1)}, u32[]{:S(2)}, u32[]{:S(2)}) %collective-permute-start.7) | collective-permute-done | bytes 163872 | tf_op jit(solution)/shard_map/ppermute | solution.py:40
  43.9 4.0 %columns.1 = (f32[16,512]{1,0:T(8,128)S(1)}, bf16[5,512,512]{2,1,0:T(8,128)(2,1)S(1)}, bf16[640,128]{1,0:T(8,128)(2,1)S(1)}, bf16[640,128]{1,0:T(8,128)(2,1)S(1)...) custom-call(s32[4]{0:T(128)S(1)} %pad_add_fusion.where, bf16[128,1920]{1,0:T(8,128)(2,1)S(1)} %maximum_select_fusion.refs_0_, ...), custom_call_target="tpu_custom_call" | custom-call | flops 700000000 | bytes 9000000 | tf_op jit(solution)/shard_map/columns/pallas_call | solution.py:404
  47.9 0.4 collective-permute-start.14
  48.3 0.6 collective-permute-start.13
  48.9 0.6 collective-permute-start.12
  49.5 2.5 %rows.1 = (f32[16,512]{1,0:T(8,128)S(1)}, bf16[5,512,512]{2,1,0:T(8,128)(2,1)S(1)}) custom-call(s32[4]{0:T(128)S(1)} %pad_add_fusion.where, bf16[128,1920]{1,0:T(8,128)(2,1)S(1)} %maximum_select_fusion.refs_0_, bf16[128,1920]{1,0:T(8,128)(2,1)S(1)} %collective-permute-done.5.refs_1_, bf16[128,1920]{1,0:T(8,128)(2,1)S(1)} %collective-permute-done.4.refs_2_, ...), custom_call_target="tpu_custom_call" | custom-call | flops 400000000 | bytes 8000000 | tf_op jit(solution)/shard_map/rows/pallas_call | solution.py:394
  51.9 2.6 %collective-permute-start.11 = (f32[16,512]{1,0:T(8,128)S(1)}, f32[16,512]{1,0:T(8,128)S(1)}, u32[]{:S(2)}, u32[]{:S(2)}) collective-permute-start(f32[16,512]{1,0:T(8,128)S(1)} %get-tuple-element.44.refs_0_), channel_id=1, source_target_pairs={{0,96},{1,97},{2,98},{3,99},{4,100},{5,101},{6,102},{7,103},{8,104... | collective-permute-start | bytes 98312 | tf_op jit(solution)/shard_map/ppermute | solution.py:40
  54.5 0.5 collective-permute-start.10
  55.0 0.2 collective-permute-start.9
  55.2 1.3 %collective-permute-done.11.refs_3_ = f32[16,512]{1,0:T(8,128)S(1)} collective-permute-done((f32[16,512]{1,0:T(8,128)S(1)}, f32[16,512]{1,0:T(8,128)S(1)}, u32[]{:S(2)}, u32[]{:S(2)}) %collective-permute-start.11) | collective-permute-done | bytes 32800 | tf_op jit(solution)/shard_map/ppermute | solution.py:40
  56.5 1.2 collective-permute-done.10.refs_2_
  57.7 2.9 %symmetric.1 = bf16[8,5,64,512]{3,2,1,0:T(8,128)(2,1)} custom-call(s32[4]{0:T(128)S(1)} %pad_add_fusion.where, f32[16,512]{1,0:T(8,128)S(1)} %get-tuple-element.44.refs_0_, f32[16,512]{1,0:T(8,128)S(1)} %collective-permute-done.9.refs_1_, f32[16,512]{1,0:T(8,128)S(1)} %collective-permute-done.10.refs_2_, f32[16,512]{1,0:T(8,128)S(1)} %collective-permute-done.11.refs_3_, ...), custom_call_target="tpu_custom_call" | custom-call | flops 10000000 | bytes 9000000 | tf_op jit(solution)/shard_map/symmetric/pallas_call | solution.py:419
  60.6 5.0 %all-to-all-start = ((bf16[8,5,64,512]{3,2,1,0:T(8,128)(2,1)}), bf16[8,5,64,512]{3,2,1,0:T(8,128)(2,1)S(1)}, u32[]{:S(2)}, u32[]{:S(2)}) async-start(bf16[8,5,64,512]{3,2,1,0:T(8,128)(2,1)} %symmetric.1), calls=%async_computation | async-start | bytes 5242880 | tf_op jit(solution)/shard_map/all_to_all | solution.py:434
  65.6 1.5 %collective-permute-start.15 = (bf16[640,128]{1,0:T(8,128)(2,1)S(1)}, bf16[640,128]{1,0:T(8,128)(2,1)S(1)}, u32[]{:S(2)}, u32[]{:S(2)}) collective-permute-start(bf16[640,128]{1,0:T(8,128)(2,1)S(1)} %get-tuple-element.55), channel_id=1, source_target_pairs={{0,2},{1,3},{2,4},{3,5},{4,6},{5,7},{6,0},{7,1},{8,10},{9,11},{10,... | collective-permute-start | bytes 491528 | tf_op jit(solution)/shard_map/ppermute | solution.py:40
  67.1 2.5 %collective-permute-start.16 = (bf16[640,128]{1,0:T(8,128)(2,1)S(1)}, bf16[640,128]{1,0:T(8,128)(2,1)S(1)}, u32[]{:S(2)}, u32[]{:S(2)}) collective-permute-start(bf16[640,128]{1,0:T(8,128)(2,1)S(1)} %get-tuple-element.56), channel_id=1, source_target_pairs={{0,4},{1,5},{2,6},{3,7},{4,0},{5,1},{6,2},{7,3},{8,12},{9,13},{10,... | collective-permute-start | bytes 491528 | tf_op jit(solution)/shard_map/ppermute | solution.py:40
  69.6 2.0 %collective-permute-start.17 = (bf16[640,128]{1,0:T(8,128)(2,1)S(1)}, bf16[640,128]{1,0:T(8,128)(2,1)S(1)}, u32[]{:S(2)}, u32[]{:S(2)}) collective-permute-start(bf16[640,128]{1,0:T(8,128)(2,1)S(1)} %get-tuple-element.57), channel_id=1, source_target_pairs={{0,6},{1,7},{2,0},{3,1},{4,2},{5,3},{6,4},{7,5},{8,14},{9,15},{10,... | collective-permute-start | bytes 491528 | tf_op jit(solution)/shard_map/ppermute | solution.py:40
  71.6 0.4 collective-permute-done.15.refs_5_
  71.9 5.0 %collective-permute-done.16.refs_6_ = bf16[640,128]{1,0:T(8,128)(2,1)S(1)} collective-permute-done((bf16[640,128]{1,0:T(8,128)(2,1)S(1)}, bf16[640,128]{1,0:T(8,128)(2,1)S(1)}, u32[]{:S(2)}, u32[]{:S(2)}) %collective-permute-start.16) | collective-permute-done | bytes 163872 | tf_op jit(solution)/shard_map/ppermute | solution.py:40
  77.0 0.8 context.1
  77.7 4.5 %collective-permute-start.18 = (bf16[64,640]{1,0:T(8,128)(2,1)S(1)}, bf16[64,640]{1,0:T(8,128)(2,1)S(1)}, u32[]{:S(2)}, u32[]{:S(2)}) collective-permute-start(bf16[64,640]{1,0:T(8,128)(2,1)S(1)} %get-tuple-element.58), channel_id=1, source_target_pairs={{0,0},{1,1},{2,2},{3,3},{4,4},{5,5},{6,6},{7,7},{8,32},{9,33},{10,... | collective-permute-start | bytes 245768 | tf_op jit(solution)/shard_map/ppermute | solution.py:40
  82.2 2.5 %collective-permute-start.19 = (bf16[64,640]{1,0:T(8,128)(2,1)S(1)}, bf16[64,640]{1,0:T(8,128)(2,1)S(1)}, u32[]{:S(2)}, u32[]{:S(2)}) collective-permute-start(bf16[64,640]{1,0:T(8,128)(2,1)S(1)} %get-tuple-element.59), channel_id=1, source_target_pairs={{0,1},{1,0},{2,3},{3,2},{4,5},{5,4},{6,7},{7,6},{8,33},{9,32},{10,... | collective-permute-start | bytes 245768 | tf_op jit(solution)/shard_map/ppermute | solution.py:40
  84.7 18.7 %collective-permute-done.18.same = bf16[64,640]{1,0:T(8,128)(2,1)S(1)} collective-permute-done((bf16[64,640]{1,0:T(8,128)(2,1)S(1)}, bf16[64,640]{1,0:T(8,128)(2,1)S(1)}, u32[]{:S(2)}, u32[]{:S(2)}) %collective-permute-start.18) | collective-permute-done | bytes 81952 | tf_op jit(solution)/shard_map/ppermute | solution.py:40
  103.4 3.3 %collective-permute-done.19.other = bf16[64,640]{1,0:T(8,128)(2,1)S(1)} collective-permute-done((bf16[64,640]{1,0:T(8,128)(2,1)S(1)}, bf16[64,640]{1,0:T(8,128)(2,1)S(1)}, u32[]{:S(2)}, u32[]{:S(2)}) %collective-permute-start.19) | collective-permute-done | bytes 81952 | tf_op jit(solution)/shard_map/ppermute | solution.py:40
  106.7 0.6 copy-done.3
  107.3 10.7 %pair.1 = (bf16[64,64,512]{2,1,0:T(8,128)(2,1)}, bf16[64,1280]{1,0:T(8,128)(2,1)}) custom-call(s32[4]{0:T(128)S(1)} %pad_add_fusion.where, bf16[40,64,512]{2,1,0:T(8,128)(2,1)S(1)} %bitcast.7, bf16[1024,336]{1,0:T(8,128)(2,1)} %get-tuple-element.50.first, bf16[512,512]{1,0:T(8,128)(2,1)} %get-tuple-element.51.second, ...), custom_call_target="tpu_custom_call" | custom-call | flops 5000000000 | bytes 14000000 | tf_op jit(solution)/shard_map/pair/pallas_call | solution.py:451
  (22 shorter events, 0.1 us)
Async XLA Ops:
  1.6 26.5 %copy-start.1 = (s32[4]{0:T(128)S(1)}, s32[4]{0:T(128)}, u32[]{:S(2)}) copy-start(s32[4]{0:T(128)} %lengths.1) | copy-start | bytes 52
  2.7 14.6 %collective-permute-start = (bf16[64,1920]{1,0:T(8,128)(2,1)S(1)}, bf16[64,1920]{1,0:T(8,128)(2,1)S(1)}, u32[]{:S(2)}, u32[]{:S(2)}) collective-permute-start(bf16[64,1920]{1,0:T(8,128)(2,1)S(1)} %get-tuple-element.62), channel_id=1, source_target_pairs={{0,0},{1,1},{2,2},{3,3},{4,4},{5,5},{6,6},{7,7},{8,32},{9,33},{10,... | collective-permute-start | bytes 737288 | tf_op jit(solution)/shard_map/ppermute | solution.py:40
  7.3 12.9 %collective-permute-start.1 = (bf16[64,1920]{1,0:T(8,128)(2,1)S(1)}, bf16[64,1920]{1,0:T(8,128)(2,1)S(1)}, u32[]{:S(2)}, u32[]{:S(2)}) collective-permute-start(bf16[64,1920]{1,0:T(8,128)(2,1)S(1)} %get-tuple-element.63), channel_id=1, source_target_pairs={{0,1},{1,0},{2,3},{3,2},{4,5},{5,4},{6,7},{7,6},{8,33},{9,32},{10,... | collective-permute-start | bytes 737288 | tf_op jit(solution)/shard_map/ppermute | solution.py:40
  13.9 0.7 copy-start
  20.3 13.7 %collective-permute-start.4 = (bf16[128,1920]{1,0:T(8,128)(2,1)S(1)}, bf16[128,1920]{1,0:T(8,128)(2,1)S(1)}, u32[]{:S(2)}, u32[]{:S(2)}) collective-permute-start(bf16[128,1920]{1,0:T(8,128)(2,1)S(1)} %maximum_select_fusion.refs_0_), channel_id=1, source_target_pairs={{0,64},{1,65},{2,66},{3,67},{4,68},{5,69},{6,70},{7,71},{8,72},{9,... | collective-permute-start | bytes 1474568 | tf_op jit(solution)/shard_map/ppermute | solution.py:40
  25.3 8.6 %collective-permute-start.3 = (bf16[128,1280]{1,0:T(8,128)(2,1)S(1)}, bf16[128,1280]{1,0:T(8,128)(2,1)S(1)}, u32[]{:S(2)}, u32[]{:S(2)}) collective-permute-start(bf16[128,1280]{1,0:T(8,128)(2,1)S(1)} %slice.33.refs_4_), channel_id=1, source_target_pairs={{0,2},{1,3},{2,4},{3,5},{4,6},{5,7},{6,0},{7,1},{8,10},{9,11},{10,... | collective-permute-start | bytes 983048 | tf_op jit(solution)/shard_map/ppermute | solution.py:40
  26.5 7.3 %collective-permute-start.2 = (bf16[128,1280]{1,0:T(8,128)(2,1)S(1)}, bf16[128,1280]{1,0:T(8,128)(2,1)S(1)}, u32[]{:S(2)}, u32[]{:S(2)}) collective-permute-start(bf16[128,1280]{1,0:T(8,128)(2,1)S(1)} %slice.33.refs_4_), channel_id=1, source_target_pairs={{0,6},{1,7},{2,0},{3,1},{4,2},{5,3},{6,4},{7,5},{8,14},{9,15},{10,... | collective-permute-start | bytes 983048 | tf_op jit(solution)/shard_map/ppermute | solution.py:40
  34.1 9.8 %collective-permute-start.5 = (bf16[128,1920]{1,0:T(8,128)(2,1)S(1)}, bf16[128,1920]{1,0:T(8,128)(2,1)S(1)}, u32[]{:S(2)}, u32[]{:S(2)}) collective-permute-start(bf16[128,1920]{1,0:T(8,128)(2,1)S(1)} %maximum_select_fusion.refs_0_), channel_id=1, source_target_pairs={{0,32},{1,33},{2,34},{3,35},{4,36},{5,37},{6,38},{7,39},{8,40},{9,... | collective-permute-start | bytes 1474568 | tf_op jit(solution)/shard_map/ppermute | solution.py:40
  34.1 9.8 %collective-permute-start.6 = (bf16[128,1920]{1,0:T(8,128)(2,1)S(1)}, bf16[128,1920]{1,0:T(8,128)(2,1)S(1)}, u32[]{:S(2)}, u32[]{:S(2)}) collective-permute-start(bf16[128,1920]{1,0:T(8,128)(2,1)S(1)} %collective-permute-done.4.refs_2_), channel_id=1, source_target_pairs={{0,32},{1,33},{2,34},{3,35},{4,36},{5,37},{6,38},{7,39},{8,40},{9,... | collective-permute-start | bytes 1474568 | tf_op jit(solution)/shard_map/ppermute | solution.py:40
  34.6 6.2 %collective-permute-start.8 = (bf16[64,1280]{1,0:T(8,128)(2,1)S(1)}, bf16[64,1280]{1,0:T(8,128)(2,1)S(1)}, u32[]{:S(2)}, u32[]{:S(2)}) collective-permute-start(bf16[64,1280]{1,0:T(8,128)(2,1)S(1)} %slice.35), channel_id=1, source_target_pairs={{0,6},{1,7},{2,0},{3,1},{4,2},{5,3},{6,4},{7,5},{8,14},{9,15},{10,... | collective-permute-start | bytes 491528 | tf_op jit(solution)/shard_map/ppermute | solution.py:40
  37.2 6.7 %collective-permute-start.7 = (bf16[64,1280]{1,0:T(8,128)(2,1)S(1)}, bf16[64,1280]{1,0:T(8,128)(2,1)S(1)}, u32[]{:S(2)}, u32[]{:S(2)}) collective-permute-start(bf16[64,1280]{1,0:T(8,128)(2,1)S(1)} %slice.34), channel_id=1, source_target_pairs={{0,2},{1,3},{2,4},{3,5},{4,6},{5,7},{6,0},{7,1},{8,10},{9,11},{10,... | collective-permute-start | bytes 491528 | tf_op jit(solution)/shard_map/ppermute | solution.py:40
  47.9 7.1 %collective-permute-start.14 = (f32[16,512]{1,0:T(8,128)S(1)}, f32[16,512]{1,0:T(8,128)S(1)}, u32[]{:S(2)}, u32[]{:S(2)}) collective-permute-start(f32[16,512]{1,0:T(8,128)S(1)} %get-tuple-element.45.refs_4_.refs_0_), channel_id=1, source_target_pairs={{0,6},{1,7},{2,0},{3,1},{4,2},{5,3},{6,4},{7,5},{8,14},{9,15},{10,... | collective-permute-start | bytes 98312 | tf_op jit(solution)/shard_map/ppermute | solution.py:40
  48.3 6.9 %collective-permute-start.13 = (f32[16,512]{1,0:T(8,128)S(1)}, f32[16,512]{1,0:T(8,128)S(1)}, u32[]{:S(2)}, u32[]{:S(2)}) collective-permute-start(f32[16,512]{1,0:T(8,128)S(1)} %get-tuple-element.45.refs_4_.refs_0_), channel_id=1, source_target_pairs={{0,4},{1,5},{2,6},{3,7},{4,0},{5,1},{6,2},{7,3},{8,12},{9,13},{10,... | collective-permute-start | bytes 98312 | tf_op jit(solution)/shard_map/ppermute | solution.py:40
  48.9 6.3 %collective-permute-start.12 = (f32[16,512]{1,0:T(8,128)S(1)}, f32[16,512]{1,0:T(8,128)S(1)}, u32[]{:S(2)}, u32[]{:S(2)}) collective-permute-start(f32[16,512]{1,0:T(8,128)S(1)} %get-tuple-element.45.refs_4_.refs_0_), channel_id=1, source_target_pairs={{0,2},{1,3},{2,4},{3,5},{4,6},{5,7},{6,0},{7,1},{8,10},{9,11},{10,... | collective-permute-start | bytes 98312 | tf_op jit(solution)/shard_map/ppermute | solution.py:40
  51.9 4.6 %collective-permute-start.11 = (f32[16,512]{1,0:T(8,128)S(1)}, f32[16,512]{1,0:T(8,128)S(1)}, u32[]{:S(2)}, u32[]{:S(2)}) collective-permute-start(f32[16,512]{1,0:T(8,128)S(1)} %get-tuple-element.44.refs_0_), channel_id=1, source_target_pairs={{0,96},{1,97},{2,98},{3,99},{4,100},{5,101},{6,102},{7,103},{8,104... | collective-permute-start | bytes 98312 | tf_op jit(solution)/shard_map/ppermute | solution.py:40
  54.5 3.2 %collective-permute-start.10 = (f32[16,512]{1,0:T(8,128)S(1)}, f32[16,512]{1,0:T(8,128)S(1)}, u32[]{:S(2)}, u32[]{:S(2)}) collective-permute-start(f32[16,512]{1,0:T(8,128)S(1)} %get-tuple-element.44.refs_0_), channel_id=1, source_target_pairs={{0,64},{1,65},{2,66},{3,67},{4,68},{5,69},{6,70},{7,71},{8,72},{9,... | collective-permute-start | bytes 98312 | tf_op jit(solution)/shard_map/ppermute | solution.py:40
  55.0 2.7 %collective-permute-start.9 = (f32[16,512]{1,0:T(8,128)S(1)}, f32[16,512]{1,0:T(8,128)S(1)}, u32[]{:S(2)}, u32[]{:S(2)}) collective-permute-start(f32[16,512]{1,0:T(8,128)S(1)} %get-tuple-element.44.refs_0_), channel_id=1, source_target_pairs={{0,32},{1,33},{2,34},{3,35},{4,36},{5,37},{6,38},{7,39},{8,40},{9,... | collective-permute-start | bytes 98312 | tf_op jit(solution)/shard_map/ppermute | solution.py:40
  60.6 46.1 %all-to-all-start = ((bf16[8,5,64,512]{3,2,1,0:T(8,128)(2,1)}), bf16[8,5,64,512]{3,2,1,0:T(8,128)(2,1)S(1)}, u32[]{:S(2)}, u32[]{:S(2)}) async-start(bf16[8,5,64,512]{3,2,1,0:T(8,128)(2,1)} %symmetric.1), calls=%async_computation | async-start | bytes 5242880 | tf_op jit(solution)/shard_map/all_to_all | solution.py:434
  65.6 6.3 %collective-permute-start.15 = (bf16[640,128]{1,0:T(8,128)(2,1)S(1)}, bf16[640,128]{1,0:T(8,128)(2,1)S(1)}, u32[]{:S(2)}, u32[]{:S(2)}) collective-permute-start(bf16[640,128]{1,0:T(8,128)(2,1)S(1)} %get-tuple-element.55), channel_id=1, source_target_pairs={{0,2},{1,3},{2,4},{3,5},{4,6},{5,7},{6,0},{7,1},{8,10},{9,11},{10,... | collective-permute-start | bytes 491528 | tf_op jit(solution)/shard_map/ppermute | solution.py:40
  67.1 9.8 %collective-permute-start.16 = (bf16[640,128]{1,0:T(8,128)(2,1)S(1)}, bf16[640,128]{1,0:T(8,128)(2,1)S(1)}, u32[]{:S(2)}, u32[]{:S(2)}) collective-permute-start(bf16[640,128]{1,0:T(8,128)(2,1)S(1)} %get-tuple-element.56), channel_id=1, source_target_pairs={{0,4},{1,5},{2,6},{3,7},{4,0},{5,1},{6,2},{7,3},{8,12},{9,13},{10,... | collective-permute-start | bytes 491528 | tf_op jit(solution)/shard_map/ppermute | solution.py:40
  69.6 7.4 %collective-permute-start.17 = (bf16[640,128]{1,0:T(8,128)(2,1)S(1)}, bf16[640,128]{1,0:T(8,128)(2,1)S(1)}, u32[]{:S(2)}, u32[]{:S(2)}) collective-permute-start(bf16[640,128]{1,0:T(8,128)(2,1)S(1)} %get-tuple-element.57), channel_id=1, source_target_pairs={{0,6},{1,7},{2,0},{3,1},{4,2},{5,3},{6,4},{7,5},{8,14},{9,15},{10,... | collective-permute-start | bytes 491528 | tf_op jit(solution)/shard_map/ppermute | solution.py:40
  77.7 25.6 %collective-permute-start.18 = (bf16[64,640]{1,0:T(8,128)(2,1)S(1)}, bf16[64,640]{1,0:T(8,128)(2,1)S(1)}, u32[]{:S(2)}, u32[]{:S(2)}) collective-permute-start(bf16[64,640]{1,0:T(8,128)(2,1)S(1)} %get-tuple-element.58), channel_id=1, source_target_pairs={{0,0},{1,1},{2,2},{3,3},{4,4},{5,5},{6,6},{7,7},{8,32},{9,33},{10,... | collective-permute-start | bytes 245768 | tf_op jit(solution)/shard_map/ppermute | solution.py:40
  82.2 24.5 %collective-permute-start.19 = (bf16[64,640]{1,0:T(8,128)(2,1)S(1)}, bf16[64,640]{1,0:T(8,128)(2,1)S(1)}, u32[]{:S(2)}, u32[]{:S(2)}) collective-permute-start(bf16[64,640]{1,0:T(8,128)(2,1)S(1)} %get-tuple-element.59), channel_id=1, source_target_pairs={{0,1},{1,0},{2,3},{3,2},{4,5},{5,4},{6,7},{7,6},{8,33},{9,32},{10,... | collective-permute-start | bytes 245768 | tf_op jit(solution)/shard_map/ppermute | solution.py:40
  103.4 3.3 %copy-start.2 = (bf16[64,640]{1,0:T(8,128)(2,1)}, bf16[64,640]{1,0:T(8,128)(2,1)S(1)}, u32[]{:S(2)}) copy-start(bf16[64,640]{1,0:T(8,128)(2,1)S(1)} %collective-permute-done.18.same) | copy-start | bytes 245764
  106.7 0.6 copy-start.3

commit v4 on v3

--- a/solution.py
+++ b/solution.py
@@ -18,6 +18,7 @@
 BLOCK = 128
 HALF = 64
 TILE = 512
+NEAR, FAR = (0, 1, 3), 2
 ROWS = 16
 ONES = 16
 SCALE = math.log2(math.e) / math.sqrt(HEAD_DIM)
@@ -25,13 +26,13 @@
 MIB = 1 << 20
 
 
-def place(y, x, z, c):
+def device(y, x, z, c):
     return c * 32 + y * 8 + x * 2 + z
 
 
 def moves(to):
     return [
-        (place(y, x, z, c), place(*to(y, x, z, c)))
+        (device(y, x, z, c), device(*to(y, x, z, c)))
         for c, y, x, z in itertools.product(range(4), range(4), range(4), range(2))
     ]
 
@@ -57,7 +58,7 @@
 
 
 def fetch(where, row_blocks, row_parts, column_blocks, column_part, sems):
-    y, x, z, c = (where[i] for i in range(4))
+    y, z, c = where[0], where[2], where[3]
     copies = []
     for d in range(4):
         away = lax.rem(lax.bitwise_xor(c, d) - y + 4, 4)
@@ -72,16 +73,16 @@
                     )
                 )
     ref, at = column_part
-    for block, d, skip in zip(column_blocks, (0, 1, 3, 2, 2), (0, 0, 0, 0, HALF)):
-        rows = block.shape[0]
-        start = pl.multiple_of(lax.rem(x - d + 4, 4) * BLOCK + skip, HALF)
+    start = 0
+    for block in column_blocks:
         copies.append(
             pltpu.make_async_copy(
                 block.at[:, pl.ds(at * WIDE, WIDE)],
-                ref.at[pl.ds(start, rows)],
+                ref.at[pl.ds(start, block.shape[0])],
                 sems.at[len(copies)],
             )
         )
+        start += block.shape[0]
     for copy in copies:
         copy.start()
     for copy in copies:
@@ -107,11 +108,11 @@
     by_row[...] = jnp.transpose(kept)[0:16]
 
 
-def column_kernel(where, *refs):
-    by_column, lifted_out = refs[9:11]
-    partials, (keys, values, queries, held, sems) = refs[11:15], refs[15:]
-    fetch(where, refs[0:4], [(keys, 1), (values, 2)], refs[4:9], (queries, 0), sems)
-    by_column[...] = jnp.zeros_like(by_column)
+def place(x, d):
+    return pl.ds(pl.multiple_of(lax.rem(x - d + 4, 4) * BLOCK, BLOCK), BLOCK)
+
+
+def columns_of(keys, values, queries, by_column, lifted_out, partials):
     for h in range(GROUP):
         scores = nt(head(keys, h), head(queries, h)) * SCALE
         top = jnp.max(scores, axis=0, keepdims=True)
@@ -122,11 +123,29 @@
         lifted_out[h] = lifted
         part = lax.dot_general(
             head(values, h), lifted, (((0,), (0,)), ((), ())), preferred_element_type=jnp.float32
-        )
-        held[h * HEAD_DIM : (h + 1) * HEAD_DIM, :] = part.astype(jnp.bfloat16)
-    for d in range(4):
-        owner = lax.rem(where[1] + d, 4)
-        partials[d][...] = held[:, pl.ds(pl.multiple_of(owner * BLOCK, BLOCK), BLOCK)]
+        ).astype(jnp.bfloat16)
+        for i, out in enumerate(partials):
+            out[h * HEAD_DIM : (h + 1) * HEAD_DIM, :] = part[:, i * BLOCK : (i + 1) * BLOCK]
+
+
+def column_kernel(where, *refs):
+    by_column, lifted_out, partials = refs[7], refs[8], refs[9:12]
+    keys, values, queries, sems = refs[12:]
+    fetch(where, refs[0:4], [(keys, 1), (values, 2)], refs[4:7], (queries, 0), sems)
+    by_column[...] = jnp.zeros_like(by_column)
+    columns_of(keys, values, queries, by_column, lifted_out, partials)
+
+
+def last_column_kernel(where, *refs):
+    others, by_column, lifted_out, partial = refs[6:10]
+    keys, values, queries, own, sems = refs[10:]
+    fetch(where, refs[0:4], [(keys, 1), (values, 2)], refs[4:6], (queries, 0), sems)
+    own[...] = jnp.zeros_like(own)
+    columns_of(keys, values, queries, own, lifted_out, [partial])
+    x = where[1]
+    for i, d in enumerate(NEAR):
+        by_column[:, place(x, d)] = others[:, i * BLOCK : (i + 1) * BLOCK]
+    by_column[:, place(x, FAR)] = own[...]
 
 
 def factors(refs):
@@ -141,19 +160,24 @@
 
 def symmetric_kernel(where, *refs):
     row_stats, column_stats = refs[0:4], refs[4:8]
-    row_lifted, column_lifted, out, held, sems = refs[8:]
+    row_lifted, near_lifted, far_lifted, out, by_column, held, sems = refs[8:]
     by_row = turned(factors(row_stats) * 1024.0)
-    by_column = factors(column_stats) * 1024.0
-    y, z = where[0], where[2]
+    by_column[...] = factors(column_stats) * 1024.0
+    y, x, z = (where[i] for i in range(3))
+    places = [place(x, d) for d in (*NEAR, FAR)]
+    gains = [by_column[:, at] for at in places]
     copies = []
     for p in range(8):
         owner = lax.rem(y + p // 2, 4) * 2 + lax.bitwise_xor(z, p % 2)
         here = slice(p * HALF, (p + 1) * HALF)
         for h in range(GROUP):
-            held[p, h] = (
-                row_lifted[h, here].astype(jnp.float32) * by_row[here, h : h + 1]
-                + column_lifted[h, here].astype(jnp.float32) * by_column[h : h + 1, :]
-            ).astype(jnp.bfloat16)
+            for i, at in enumerate(places):
+                columns = slice(i * BLOCK, (i + 1) * BLOCK)
+                mirrored = near_lifted[h, here, columns] if i < len(NEAR) else far_lifted[h, here]
+                held[p, h, :, at] = (
+                    row_lifted[h, here, columns].astype(jnp.float32) * by_row[here, h : h + 1]
+                    + mirrored.astype(jnp.float32) * gains[i][h : h + 1, :]
+                ).astype(jnp.bfloat16)
         copies.append(pltpu.make_async_copy(held.at[p], out.at[owner], sems.at[p]))
         copies[p].start()
     for copy in copies:
@@ -391,6 +415,41 @@
     beside = send(block, lambda y, x, z, c: (y, x, z, c ^ 1))
     row_blocks = [block, beside, across, send(across, lambda y, x, z, c: (y, x, z, c ^ 1))]
 
+    near_stats, near_lifted, own_partial, right_partial, left_partial = pl.pallas_call(
+        column_kernel,
+        in_specs=[SMEM] + [ANY] * 7,
+        out_specs=[VMEM] * 5,
+        out_shape=[
+            shape((16, len(NEAR) * BLOCK), jnp.float32),
+            shape((GROUP, TILE, len(NEAR) * BLOCK)),
+        ]
+        + [shape((WIDE, BLOCK))] * 3,
+        scratch_shapes=[vmem(TILE, WIDE)] * 2
+        + [vmem(len(NEAR) * BLOCK, WIDE), pltpu.SemaphoreType.DMA((19,))],
+        compiler_params=params(12),
+        cost_estimate=cost(5e8, 7e6, 1e6),
+        name="columns",
+    )(where, *row_blocks, *column_blocks[:3])
+    near_stats, *column_blocks[3:] = lax.optimization_barrier((near_stats, *column_blocks[3:]))
+    by_column, far_lifted, far_partial = pl.pallas_call(
+        last_column_kernel,
+        in_specs=[SMEM] + [ANY] * 6 + [VMEM],
+        out_specs=[VMEM] * 3,
+        out_shape=[
+            shape((16, TILE), jnp.float32),
+            shape((GROUP, TILE, BLOCK)),
+            shape((WIDE, BLOCK)),
+        ],
+        scratch_shapes=[vmem(TILE, WIDE)] * 2
+        + [
+            vmem(BLOCK, WIDE),
+            pltpu.VMEM((16, BLOCK), jnp.float32),
+            pltpu.SemaphoreType.DMA((18,)),
+        ],
+        compiler_params=params(12),
+        cost_estimate=cost(2e8, 3e6, 3e5),
+        name="last_columns",
+    )(where, *row_blocks, *column_blocks[3:], near_stats)
     by_row, row_lifted = pl.pallas_call(
         row_kernel,
         in_specs=[SMEM] + [ANY] * 9,
@@ -401,34 +460,24 @@
         cost_estimate=cost(4e8, 8e6, 1.4e6),
         name="rows",
     )(where, *row_blocks, *column_blocks)
-    by_column, column_lifted, *partials = pl.pallas_call(
-        column_kernel,
-        in_specs=[SMEM] + [ANY] * 9,
-        out_specs=[VMEM] * 6,
-        out_shape=[shape((16, TILE), jnp.float32), shape((GROUP, TILE, TILE))]
-        + [shape((WIDE, BLOCK))] * 4,
-        scratch_shapes=[vmem(TILE, WIDE)] * 3
-        + [vmem(WIDE, TILE), pltpu.SemaphoreType.DMA((21,))],
-        compiler_params=params(12),
-        cost_estimate=cost(7e8, 9e6, 1.4e6),
-        name="columns",
-    )(where, *row_blocks, *column_blocks)
+    partials = [own_partial, left_partial, far_partial, right_partial]
     row_stats = [by_row] + over_rows(by_row)
     column_stats = [by_column] + over_columns(by_column)
 
     tiles = pl.pallas_call(
         symmetric_kernel,
-        in_specs=[SMEM] + [VMEM] * 10,
+        in_specs=[SMEM] + [VMEM] * 11,
         out_specs=HBM,
         out_shape=shape((8, GROUP, HALF, TILE)),
         scratch_shapes=[
+            pltpu.VMEM((8, TILE), jnp.float32),
             pltpu.VMEM((8, GROUP, HALF, TILE), jnp.bfloat16),
             pltpu.SemaphoreType.DMA((8,)),
         ],
         compiler_params=params(8),
         cost_estimate=cost(1e7, 9e6),
         name="symmetric",
-    )(where, *row_stats, *column_stats, row_lifted, column_lifted)
+    )(where, *row_stats, *column_stats, row_lifted, near_lifted, far_lifted)
     where, tiles = lax.optimization_barrier((where, tiles))
     groups = [[y * 8 + x * 2 + z for y in range(4) for z in range(2)] for x in range(4)]
     received = lax.all_to_all(

time: 119 us -> 114 us (0.958)
  waiting for transfers between devices: 39.8 us -> 32.1 us
  starting transfers between devices: 41.4 us -> 43.5 us
    ppermute x20, waiting for transfers between devices: 39.8 us -> 32.1 us  [send(): return lax.ppermute(value, AXES, moves(to))]
    ppermute x20, starting transfers between devices: 36.4 us -> 39.1 us  [send(): return lax.ppermute(value, AXES, moves(to))]
    pallas_call x2 -> x3, Pallas kernels: 6.88 us -> 7.81 us  [the longest x1 3.21 us: local(): pl.pallas_call(column_kernel, in_specs=[SMEM] + [ANY] * 7, out_specs=[VME...]
  transfers between devices with their start and end apart: 21 -> 21, of which waited for: 10 -> 10; matrix products, arithmetic and copies ran while one was open for 3% -> 3% of each run, Pallas kernels for 10% -> 13%
where the time goes in v4:
time: 114 us; the launch traced here: 113 us
  starting transfers between devices  43.5 us (38%)
  waiting for transfers between devices  32.1 us (28%)
  Pallas kernels  30.1 us (26%)
  local copies, waits for them, and re-layouts  6.53 us (6%)
    ppermute x20, starting transfers between devices, send(): return lax.ppermute(value, AXES, moves(to))  39.1 us
    ppermute x20, waiting for transfers between devices, send(): return lax.ppermute(value, AXES, moves(to))  32.1 us
    pallas_call x1, Pallas kernels, local(): pl.pallas_call(pair_kernel, grid=(HALF // ROWS,), in_specs=[SMEM, pl.Bloc...  10.8 us
    pallas_call x1, Pallas kernels, local(): pl.pallas_call(relative_kernel, grid=(HALF // ROWS,), in_specs=[SMEM, SME...  5.66 us
    all_to_all x1, starting transfers between devices, local(): lax.all_to_all(tiles, 'band', split_axis=0, concat_axis=0, axis_index_gro...  4.37 us
    pallas_call x1, Pallas kernels, local(): pl.pallas_call(column_kernel, in_specs=[SMEM] + [ANY] * 7, out_specs=[VME...  3.21 us
    unnamed x10, local copies, waits for them, and re-layouts  2.96 us
    pallas_call x1, Pallas kernels, local(): pl.pallas_call(spread_kernel, in_specs=[VMEM] * 5, out_specs=[VMEM] * 4,...  2.67 us
  transfers between devices with their start and end apart: 21, of which 10 were waited for; matrix products, arithmetic and copies ran while one was open for 3% of the time, Pallas kernels for 13%

profile of v4, /device:TPU:1, one launch (start us, length us, event | category | flops | bytes accessed | tf_op | source)
XLA Modules:
  0.0 113.3 jit_solution(16078252552477167996)
XLA Ops:
  0.6 0.9 fusion.2
  1.6 0.0 copy-start.1
  1.6 1.0 fusion
  2.6 0.1 broadcast_select_fusion.1
  2.7 6.1 %collective-permute-start.1 = (bf16[64,1920]{1,0:T(8,128)(2,1)S(1)}, bf16[64,1920]{1,0:T(8,128)(2,1)S(1)}, u32[]{:S(2)}, u32[]{:S(2)}) collective-permute-start(bf16[64,1920]{1,0:T(8,128)(2,1)S(1)} %get-tuple-element.73), channel_id=1, source_target_pairs={{0,1},{1,0},{2,3},{3,2},{4,5},{5,4},{6,7},{7,6},{8,33},{9,32},{10,... | collective-permute-start | bytes 737288 | tf_op jit(solution)/shard_map/ppermute | solution.py:41
  8.8 1.9 %collective-permute-start = (bf16[64,1920]{1,0:T(8,128)(2,1)S(1)}, bf16[64,1920]{1,0:T(8,128)(2,1)S(1)}, u32[]{:S(2)}, u32[]{:S(2)}) collective-permute-start(bf16[64,1920]{1,0:T(8,128)(2,1)S(1)} %get-tuple-element.72), channel_id=1, source_target_pairs={{0,0},{1,1},{2,2},{3,3},{4,4},{5,5},{6,6},{7,7},{8,32},{9,33},{10,... | collective-permute-start | bytes 737288 | tf_op jit(solution)/shard_map/ppermute | solution.py:41
  10.7 0.8 copy.12.first_bias
  11.5 0.8 copy.13.second
  12.3 0.8 copy.14.second_bias
  13.1 0.8 copy.11
  13.9 0.7 copy-done
  14.6 2.7 %spread.1 = (bf16[1024,336]{1,0:T(8,128)(2,1)}, bf16[512,512]{1,0:T(8,128)(2,1)}, f32[512,128]{1,0:T(8,128)}, bf16[512,576]{1,0:T(8,128)(2,1)S(1)}) custom-call(bf16[40,128]{1,0:T(8,128)(2,1)S(1)} %copy-done, f32[128,1]{1,0:T(8,128)S(1)} %copy.12.first_bias, bf16[128,64]{1,0:T(8,128)(2,1)S(1)} %copy.13.second, f32[64,1]{1,0:T(8,128)S(1)} %copy.14.second_bias, ...), custom_call_target="tpu_custom_call" | custom-call | flops 400000000 | bytes 6000000 | tf_op jit(solution)/shard_map/spread/pallas_call | solution.py:357
  17.3 0.1 maximum_select_fusion.refs_0_
  17.4 5.8 %collective-permute-start.4 = (bf16[128,1920]{1,0:T(8,128)(2,1)S(1)}, bf16[128,1920]{1,0:T(8,128)(2,1)S(1)}, u32[]{:S(2)}, u32[]{:S(2)}) collective-permute-start(bf16[128,1920]{1,0:T(8,128)(2,1)S(1)} %maximum_select_fusion.refs_0_), channel_id=1, source_target_pairs={{0,64},{1,65},{2,66},{3,67},{4,68},{5,69},{6,70},{7,71},{8,72},{9,... | collective-permute-start | bytes 1474568 | tf_op jit(solution)/shard_map/ppermute | solution.py:41
  23.2 2.5 %collective-permute-start.2 = (bf16[128,1280]{1,0:T(8,128)(2,1)S(1)}, bf16[128,1280]{1,0:T(8,128)(2,1)S(1)}, u32[]{:S(2)}, u32[]{:S(2)}) collective-permute-start(bf16[128,1280]{1,0:T(8,128)(2,1)S(1)} %slice.33.refs_4_), channel_id=1, source_target_pairs={{0,6},{1,7},{2,0},{3,1},{4,2},{5,3},{6,4},{7,5},{8,14},{9,15},{10,... | collective-permute-start | bytes 983048 | tf_op jit(solution)/shard_map/ppermute | solution.py:41
  25.8 0.1 pad_add_fusion.where
  25.9 5.7 %relative.1 = bf16[64,64,512]{2,1,0:T(8,128)(2,1)} custom-call(s32[4]{0:T(128)S(1)} %pad_add_fusion.where, s32[4]{0:T(128)S(1)} %copy-done.1, bf16[512,576]{1,0:T(8,128)(2,1)S(1)} %get-tuple-element.41.table), custom_call_target="tpu_custom_call" | custom-call | flops 2400000000 | bytes 6000000 | tf_op jit(solution)/shard_map/relative/pallas_call | solution.py:396
  31.5 0.6 collective-permute-done.2.refs_6_
  32.1 3.4 %collective-permute-done.3.refs_5_ = bf16[128,1280]{1,0:T(8,128)(2,1)S(1)} collective-permute-done((bf16[128,1280]{1,0:T(8,128)(2,1)S(1)}, bf16[128,1280]{1,0:T(8,128)(2,1)S(1)}, u32[]{:S(2)}, u32[]{:S(2)}) %collective-permute-start.3) | collective-permute-done | bytes 327712 | tf_op jit(solution)/shard_map/ppermute | solution.py:41
  35.5 0.5 collective-permute-start.6
  36.0 0.1 collective-permute-start.7
  36.1 2.7 %collective-permute-start.8 = (bf16[64,1280]{1,0:T(8,128)(2,1)S(1)}, bf16[64,1280]{1,0:T(8,128)(2,1)S(1)}, u32[]{:S(2)}, u32[]{:S(2)}) collective-permute-start(bf16[64,1280]{1,0:T(8,128)(2,1)S(1)} %slice.35), channel_id=1, source_target_pairs={{0,6},{1,7},{2,0},{3,1},{4,2},{5,3},{6,4},{7,5},{8,14},{9,15},{10,... | collective-permute-start | bytes 491528 | tf_op jit(solution)/shard_map/ppermute | solution.py:41
  38.9 3.2 %columns.1 = (f32[16,384]{1,0:T(8,128)S(1)}, bf16[5,512,384]{2,1,0:T(8,128)(2,1)S(1)}, bf16[640,128]{1,0:T(8,128)(2,1)S(1)}, bf16[640,128]{1,0:T(8,128)(2,1)S(1)}, bf16[640,128]{1,0:T(8,128)(2,1)S(1)}) custom-call(s32[4]{0:T(128)S(1)} %pad_add_fusion.where, bf16[128,1920]{1,0:T(8,128)(2,1)S(1)} %maximum_select_fusion.refs_0_, ...), custom_call_target="tpu_custom_call" | custom-call | flops 500000000 | bytes 7000000 | tf_op jit(solution)/shard_map/columns/pallas_call | solution.py:418
  42.1 1.1 collective-permute-done.7.refs_7_.refs_4_
  43.1 2.4 %rows.1 = (f32[16,512]{1,0:T(8,128)S(1)}, bf16[5,512,512]{2,1,0:T(8,128)(2,1)S(1)}) custom-call(s32[4]{0:T(128)S(1)} %pad_add_fusion.where, bf16[128,1920]{1,0:T(8,128)(2,1)S(1)} %maximum_select_fusion.refs_0_, bf16[128,1920]{1,0:T(8,128)(2,1)S(1)} %collective-permute-done.5.refs_1_, bf16[128,1920]{1,0:T(8,128)(2,1)S(1)} %collective-permute-done.4.refs_2_, ...), custom_call_target="tpu_custom_call" | custom-call | flops 400000000 | bytes 8000000 | tf_op jit(solution)/shard_map/rows/pallas_call | solution.py:453
  45.6 0.9 collective-permute-start.9
  46.5 1.7 %collective-permute-start.11 = (f32[16,512]{1,0:T(8,128)S(1)}, f32[16,512]{1,0:T(8,128)S(1)}, u32[]{:S(2)}, u32[]{:S(2)}) collective-permute-start(f32[16,512]{1,0:T(8,128)S(1)} %get-tuple-element.52.refs_0_), channel_id=1, source_target_pairs={{0,96},{1,97},{2,98},{3,99},{4,100},{5,101},{6,102},{7,103},{8,104... | collective-permute-start | bytes 98312 | tf_op jit(solution)/shard_map/ppermute | solution.py:41
  48.2 2.0 %last_columns.1 = (f32[16,512]{1,0:T(8,128)S(1)}, bf16[5,512,128]{2,1,0:T(8,128)(2,1)S(1)}, bf16[640,128]{1,0:T(8,128)(2,1)S(1)}) custom-call(s32[4]{0:T(128)S(1)} %pad_add_fusion.where, bf16[128,1920]{1,0:T(8,128)(2,1)S(1)} %maximum_select_fusion.refs_0_, bf16[128,1920]{1,0:T(8,128)(2,1)S(1)} %collective-permute-done.5.refs_1_, ...), custom_call_target="tpu_custom_call" | custom-call | flops 200000000 | bytes 3000000 | tf_op jit(solution)/shard_map/last_columns/pallas_call | solution.py:434
  50.2 0.3 collective-permute-start.12
  50.4 3.9 %collective-permute-start.13 = (f32[16,512]{1,0:T(8,128)S(1)}, f32[16,512]{1,0:T(8,128)S(1)}, u32[]{:S(2)}, u32[]{:S(2)}) collective-permute-start(f32[16,512]{1,0:T(8,128)S(1)} %get-tuple-element.54.refs_4_.refs_0_), channel_id=1, source_target_pairs={{0,4},{1,5},{2,6},{3,7},{4,0},{5,1},{6,2},{7,3},{8,12},{9,13},{10,... | collective-permute-start | bytes 98312 | tf_op jit(solution)/shard_map/ppermute | solution.py:41
  54.4 0.1 collective-permute-done.12.refs_5_.refs_1_
  54.5 1.7 %collective-permute-done.13.refs_6_.refs_2_ = f32[16,512]{1,0:T(8,128)S(1)} collective-permute-done((f32[16,512]{1,0:T(8,128)S(1)}, f32[16,512]{1,0:T(8,128)S(1)}, u32[]{:S(2)}, u32[]{:S(2)}) %collective-permute-start.13) | collective-permute-done | bytes 32800 | tf_op jit(solution)/shard_map/ppermute | solution.py:41
  56.1 1.0 collective-permute-done.14.refs_7_.refs_3_
  57.1 2.6 %symmetric.1 = bf16[8,5,64,512]{3,2,1,0:T(8,128)(2,1)} custom-call(s32[4]{0:T(128)S(1)} %pad_add_fusion.where, f32[16,512]{1,0:T(8,128)S(1)} %get-tuple-element.52.refs_0_, f32[16,512]{1,0:T(8,128)S(1)} %collective-permute-done.9.refs_1_, f32[16,512]{1,0:T(8,128)S(1)} %collective-permute-done.10.refs_2_, f32[16,512]{1,0:T(8,128)S(1)} %collective-permute-done.11.refs_3_, ...), custom_call_target="tpu_custom_call" | custom-call | flops 10000000 | bytes 9000000 | tf_op jit(solution)/shard_map/symmetric/pallas_call | solution.py:467
  59.8 4.4 %all-to-all-start = ((bf16[8,5,64,512]{3,2,1,0:T(8,128)(2,1)}), bf16[8,5,64,512]{3,2,1,0:T(8,128)(2,1)S(1)}, u32[]{:S(2)}, u32[]{:S(2)}) async-start(bf16[8,5,64,512]{3,2,1,0:T(8,128)(2,1)} %symmetric.1), calls=%async_computation | async-start | bytes 5242880 | tf_op jit(solution)/shard_map/all_to_all | solution.py:483
  64.1 0.0 collective-permute-start.15
  64.2 2.6 %collective-permute-start.16 = (bf16[640,128]{1,0:T(8,128)(2,1)S(1)}, bf16[640,128]{1,0:T(8,128)(2,1)S(1)}, u32[]{:S(2)}, u32[]{:S(2)}) collective-permute-start(bf16[640,128]{1,0:T(8,128)(2,1)S(1)} %get-tuple-element.66), channel_id=1, source_target_pairs={{0,4},{1,5},{2,6},{3,7},{4,0},{5,1},{6,2},{7,3},{8,12},{9,13},{10,... | collective-permute-start | bytes 491528 | tf_op jit(solution)/shard_map/ppermute | solution.py:41
  66.8 0.9 collective-permute-start.17
  67.7 1.8 %collective-permute-done.15.refs_5_ = bf16[640,128]{1,0:T(8,128)(2,1)S(1)} collective-permute-done((bf16[640,128]{1,0:T(8,128)(2,1)S(1)}, bf16[640,128]{1,0:T(8,128)(2,1)S(1)}, u32[]{:S(2)}, u32[]{:S(2)}) %collective-permute-start.15) | collective-permute-done | bytes 163872 | tf_op jit(solution)/shard_map/ppermute | solution.py:41
  69.5 3.1 %collective-permute-done.16.refs_6_ = bf16[640,128]{1,0:T(8,128)(2,1)S(1)} collective-permute-done((bf16[640,128]{1,0:T(8,128)(2,1)S(1)}, bf16[640,128]{1,0:T(8,128)(2,1)S(1)}, u32[]{:S(2)}, u32[]{:S(2)}) %collective-permute-start.16) | collective-permute-done | bytes 163872 | tf_op jit(solution)/shard_map/ppermute | solution.py:41
  72.7 0.0 collective-permute-done.17.refs_7_
  72.7 0.8 context.1
  73.5 6.6 %collective-permute-start.18 = (bf16[64,640]{1,0:T(8,128)(2,1)S(1)}, bf16[64,640]{1,0:T(8,128)(2,1)S(1)}, u32[]{:S(2)}, u32[]{:S(2)}) collective-permute-start(bf16[64,640]{1,0:T(8,128)(2,1)S(1)} %get-tuple-element.68), channel_id=1, source_target_pairs={{0,0},{1,1},{2,2},{3,3},{4,4},{5,5},{6,6},{7,7},{8,32},{9,33},{10,... | collective-permute-start | bytes 245768 | tf_op jit(solution)/shard_map/ppermute | solution.py:41
  80.1 2.5 %collective-permute-start.19 = (bf16[64,640]{1,0:T(8,128)(2,1)S(1)}, bf16[64,640]{1,0:T(8,128)(2,1)S(1)}, u32[]{:S(2)}, u32[]{:S(2)}) collective-permute-start(bf16[64,640]{1,0:T(8,128)(2,1)S(1)} %get-tuple-element.69), channel_id=1, source_target_pairs={{0,1},{1,0},{2,3},{3,2},{4,5},{5,4},{6,7},{7,6},{8,33},{9,32},{10,... | collective-permute-start | bytes 245768 | tf_op jit(solution)/shard_map/ppermute | solution.py:41
  82.6 17.6 %collective-permute-done.18.same = bf16[64,640]{1,0:T(8,128)(2,1)S(1)} collective-permute-done((bf16[64,640]{1,0:T(8,128)(2,1)S(1)}, bf16[64,640]{1,0:T(8,128)(2,1)S(1)}, u32[]{:S(2)}, u32[]{:S(2)}) %collective-permute-start.18) | collective-permute-done | bytes 81952 | tf_op jit(solution)/shard_map/ppermute | solution.py:41
  100.2 1.7 %collective-permute-done.19.other = bf16[64,640]{1,0:T(8,128)(2,1)S(1)} collective-permute-done((bf16[64,640]{1,0:T(8,128)(2,1)S(1)}, bf16[64,640]{1,0:T(8,128)(2,1)S(1)}, u32[]{:S(2)}, u32[]{:S(2)}) %collective-permute-start.19) | collective-permute-done | bytes 81952 | tf_op jit(solution)/shard_map/ppermute | solution.py:41
  101.9 0.6 copy-done.3
  102.5 10.8 %pair.1 = (bf16[64,64,512]{2,1,0:T(8,128)(2,1)}, bf16[64,1280]{1,0:T(8,128)(2,1)}) custom-call(s32[4]{0:T(128)S(1)} %pad_add_fusion.where, bf16[40,64,512]{2,1,0:T(8,128)(2,1)S(1)} %bitcast.7, bf16[1024,336]{1,0:T(8,128)(2,1)} %get-tuple-element.60.first, bf16[512,512]{1,0:T(8,128)(2,1)} %get-tuple-element.61.second, ...), custom_call_target="tpu_custom_call" | custom-call | flops 5000000000 | bytes 14000000 | tf_op jit(solution)/shard_map/pair/pallas_call | solution.py:500
  (23 shorter events, 0.1 us)
Async XLA Ops:
  1.6 24.3 %copy-start.1 = (s32[4]{0:T(128)S(1)}, s32[4]{0:T(128)}, u32[]{:S(2)}) copy-start(s32[4]{0:T(128)} %lengths.1) | copy-start | bytes 52
  2.7 14.6 %collective-permute-start.1 = (bf16[64,1920]{1,0:T(8,128)(2,1)S(1)}, bf16[64,1920]{1,0:T(8,128)(2,1)S(1)}, u32[]{:S(2)}, u32[]{:S(2)}) collective-permute-start(bf16[64,1920]{1,0:T(8,128)(2,1)S(1)} %get-tuple-element.73), channel_id=1, source_target_pairs={{0,1},{1,0},{2,3},{3,2},{4,5},{5,4},{6,7},{7,6},{8,33},{9,32},{10,... | collective-permute-start | bytes 737288 | tf_op jit(solution)/shard_map/ppermute | solution.py:41
  8.8 8.5 %collective-permute-start = (bf16[64,1920]{1,0:T(8,128)(2,1)S(1)}, bf16[64,1920]{1,0:T(8,128)(2,1)S(1)}, u32[]{:S(2)}, u32[]{:S(2)}) collective-permute-start(bf16[64,1920]{1,0:T(8,128)(2,1)S(1)} %get-tuple-element.72), channel_id=1, source_target_pairs={{0,0},{1,1},{2,2},{3,3},{4,4},{5,5},{6,6},{7,7},{8,32},{9,33},{10,... | collective-permute-start | bytes 737288 | tf_op jit(solution)/shard_map/ppermute | solution.py:41
  13.9 0.7 copy-start
  17.4 18.1 %collective-permute-start.4 = (bf16[128,1920]{1,0:T(8,128)(2,1)S(1)}, bf16[128,1920]{1,0:T(8,128)(2,1)S(1)}, u32[]{:S(2)}, u32[]{:S(2)}) collective-permute-start(bf16[128,1920]{1,0:T(8,128)(2,1)S(1)} %maximum_select_fusion.refs_0_), channel_id=1, source_target_pairs={{0,64},{1,65},{2,66},{3,67},{4,68},{5,69},{6,70},{7,71},{8,72},{9,... | collective-permute-start | bytes 1474568 | tf_op jit(solution)/shard_map/ppermute | solution.py:41
  23.2 8.9 %collective-permute-start.2 = (bf16[128,1280]{1,0:T(8,128)(2,1)S(1)}, bf16[128,1280]{1,0:T(8,128)(2,1)S(1)}, u32[]{:S(2)}, u32[]{:S(2)}) collective-permute-start(bf16[128,1280]{1,0:T(8,128)(2,1)S(1)} %slice.33.refs_4_), channel_id=1, source_target_pairs={{0,6},{1,7},{2,0},{3,1},{4,2},{5,3},{6,4},{7,5},{8,14},{9,15},{10,... | collective-permute-start | bytes 983048 | tf_op jit(solution)/shard_map/ppermute | solution.py:41
  25.8 9.7 %collective-permute-start.3 = (bf16[128,1280]{1,0:T(8,128)(2,1)S(1)}, bf16[128,1280]{1,0:T(8,128)(2,1)S(1)}, u32[]{:S(2)}, u32[]{:S(2)}) collective-permute-start(bf16[128,1280]{1,0:T(8,128)(2,1)S(1)} %slice.33.refs_4_), channel_id=1, source_target_pairs={{0,2},{1,3},{2,4},{3,5},{4,6},{5,7},{6,0},{7,1},{8,10},{9,11},{10,... | collective-permute-start | bytes 983048 | tf_op jit(solution)/shard_map/ppermute | solution.py:41
  35.5 3.4 %collective-permute-start.5 = (bf16[128,1920]{1,0:T(8,128)(2,1)S(1)}, bf16[128,1920]{1,0:T(8,128)(2,1)S(1)}, u32[]{:S(2)}, u32[]{:S(2)}) collective-permute-start(bf16[128,1920]{1,0:T(8,128)(2,1)S(1)} %maximum_select_fusion.refs_0_), channel_id=1, source_target_pairs={{0,32},{1,33},{2,34},{3,35},{4,36},{5,37},{6,38},{7,39},{8,40},{9,... | collective-permute-start | bytes 1474568 | tf_op jit(solution)/shard_map/ppermute | solution.py:41
  35.5 3.4 %collective-permute-start.6 = (bf16[128,1920]{1,0:T(8,128)(2,1)S(1)}, bf16[128,1920]{1,0:T(8,128)(2,1)S(1)}, u32[]{:S(2)}, u32[]{:S(2)}) collective-permute-start(bf16[128,1920]{1,0:T(8,128)(2,1)S(1)} %collective-permute-done.4.refs_2_), channel_id=1, source_target_pairs={{0,32},{1,33},{2,34},{3,35},{4,36},{5,37},{6,38},{7,39},{8,40},{9,... | collective-permute-start | bytes 1474568 | tf_op jit(solution)/shard_map/ppermute | solution.py:41
  36.0 7.1 %collective-permute-start.7 = (bf16[64,1280]{1,0:T(8,128)(2,1)S(1)}, bf16[64,1280]{1,0:T(8,128)(2,1)S(1)}, u32[]{:S(2)}, u32[]{:S(2)}) collective-permute-start(bf16[64,1280]{1,0:T(8,128)(2,1)S(1)} %slice.34), channel_id=1, source_target_pairs={{0,2},{1,3},{2,4},{3,5},{4,6},{5,7},{6,0},{7,1},{8,10},{9,11},{10,... | collective-permute-start | bytes 491528 | tf_op jit(solution)/shard_map/ppermute | solution.py:41
  36.1 7.0 %collective-permute-start.8 = (bf16[64,1280]{1,0:T(8,128)(2,1)S(1)}, bf16[64,1280]{1,0:T(8,128)(2,1)S(1)}, u32[]{:S(2)}, u32[]{:S(2)}) collective-permute-start(bf16[64,1280]{1,0:T(8,128)(2,1)S(1)} %slice.35), channel_id=1, source_target_pairs={{0,6},{1,7},{2,0},{3,1},{4,2},{5,3},{6,4},{7,5},{8,14},{9,15},{10,... | collective-permute-start | bytes 491528 | tf_op jit(solution)/shard_map/ppermute | solution.py:41
  45.6 8.7 %collective-permute-start.9 = (f32[16,512]{1,0:T(8,128)S(1)}, f32[16,512]{1,0:T(8,128)S(1)}, u32[]{:S(2)}, u32[]{:S(2)}) collective-permute-start(f32[16,512]{1,0:T(8,128)S(1)} %get-tuple-element.52.refs_0_), channel_id=1, source_target_pairs={{0,32},{1,33},{2,34},{3,35},{4,36},{5,37},{6,38},{7,39},{8,40},{9,... | collective-permute-start | bytes 98312 | tf_op jit(solution)/shard_map/ppermute | solution.py:41
  46.5 7.9 %collective-permute-start.10 = (f32[16,512]{1,0:T(8,128)S(1)}, f32[16,512]{1,0:T(8,128)S(1)}, u32[]{:S(2)}, u32[]{:S(2)}) collective-permute-start(f32[16,512]{1,0:T(8,128)S(1)} %get-tuple-element.52.refs_0_), channel_id=1, source_target_pairs={{0,64},{1,65},{2,66},{3,67},{4,68},{5,69},{6,70},{7,71},{8,72},{9,... | collective-permute-start | bytes 98312 | tf_op jit(solution)/shard_map/ppermute | solution.py:41
  46.5 7.9 %collective-permute-start.11 = (f32[16,512]{1,0:T(8,128)S(1)}, f32[16,512]{1,0:T(8,128)S(1)}, u32[]{:S(2)}, u32[]{:S(2)}) collective-permute-start(f32[16,512]{1,0:T(8,128)S(1)} %get-tuple-element.52.refs_0_), channel_id=1, source_target_pairs={{0,96},{1,97},{2,98},{3,99},{4,100},{5,101},{6,102},{7,103},{8,104... | collective-permute-start | bytes 98312 | tf_op jit(solution)/shard_map/ppermute | solution.py:41
  50.2 4.3 %collective-permute-start.12 = (f32[16,512]{1,0:T(8,128)S(1)}, f32[16,512]{1,0:T(8,128)S(1)}, u32[]{:S(2)}, u32[]{:S(2)}) collective-permute-start(f32[16,512]{1,0:T(8,128)S(1)} %get-tuple-element.54.refs_4_.refs_0_), channel_id=1, source_target_pairs={{0,2},{1,3},{2,4},{3,5},{4,6},{5,7},{6,0},{7,1},{8,10},{9,11},{10,... | collective-permute-start | bytes 98312 | tf_op jit(solution)/shard_map/ppermute | solution.py:41
  50.4 5.7 %collective-permute-start.13 = (f32[16,512]{1,0:T(8,128)S(1)}, f32[16,512]{1,0:T(8,128)S(1)}, u32[]{:S(2)}, u32[]{:S(2)}) collective-permute-start(f32[16,512]{1,0:T(8,128)S(1)} %get-tuple-element.54.refs_4_.refs_0_), channel_id=1, source_target_pairs={{0,4},{1,5},{2,6},{3,7},{4,0},{5,1},{6,2},{7,3},{8,12},{9,13},{10,... | collective-permute-start | bytes 98312 | tf_op jit(solution)/shard_map/ppermute | solution.py:41
  54.4 2.8 %collective-permute-start.14 = (f32[16,512]{1,0:T(8,128)S(1)}, f32[16,512]{1,0:T(8,128)S(1)}, u32[]{:S(2)}, u32[]{:S(2)}) collective-permute-start(f32[16,512]{1,0:T(8,128)S(1)} %get-tuple-element.54.refs_4_.refs_0_), channel_id=1, source_target_pairs={{0,6},{1,7},{2,0},{3,1},{4,2},{5,3},{6,4},{7,5},{8,14},{9,15},{10,... | collective-permute-start | bytes 98312 | tf_op jit(solution)/shard_map/ppermute | solution.py:41
  59.8 42.2 %all-to-all-start = ((bf16[8,5,64,512]{3,2,1,0:T(8,128)(2,1)}), bf16[8,5,64,512]{3,2,1,0:T(8,128)(2,1)S(1)}, u32[]{:S(2)}, u32[]{:S(2)}) async-start(bf16[8,5,64,512]{3,2,1,0:T(8,128)(2,1)} %symmetric.1), calls=%async_computation | async-start | bytes 5242880 | tf_op jit(solution)/shard_map/all_to_all | solution.py:483
  64.1 5.4 %collective-permute-start.15 = (bf16[640,128]{1,0:T(8,128)(2,1)S(1)}, bf16[640,128]{1,0:T(8,128)(2,1)S(1)}, u32[]{:S(2)}, u32[]{:S(2)}) collective-permute-start(bf16[640,128]{1,0:T(8,128)(2,1)S(1)} %get-tuple-element.65), channel_id=1, source_target_pairs={{0,2},{1,3},{2,4},{3,5},{4,6},{5,7},{6,0},{7,1},{8,10},{9,11},{10,... | collective-permute-start | bytes 491528 | tf_op jit(solution)/shard_map/ppermute | solution.py:41
  64.2 8.5 %collective-permute-start.16 = (bf16[640,128]{1,0:T(8,128)(2,1)S(1)}, bf16[640,128]{1,0:T(8,128)(2,1)S(1)}, u32[]{:S(2)}, u32[]{:S(2)}) collective-permute-start(bf16[640,128]{1,0:T(8,128)(2,1)S(1)} %get-tuple-element.66), channel_id=1, source_target_pairs={{0,4},{1,5},{2,6},{3,7},{4,0},{5,1},{6,2},{7,3},{8,12},{9,13},{10,... | collective-permute-start | bytes 491528 | tf_op jit(solution)/shard_map/ppermute | solution.py:41
  66.8 5.9 %collective-permute-start.17 = (bf16[640,128]{1,0:T(8,128)(2,1)S(1)}, bf16[640,128]{1,0:T(8,128)(2,1)S(1)}, u32[]{:S(2)}, u32[]{:S(2)}) collective-permute-start(bf16[640,128]{1,0:T(8,128)(2,1)S(1)} %get-tuple-element.67), channel_id=1, source_target_pairs={{0,6},{1,7},{2,0},{3,1},{4,2},{5,3},{6,4},{7,5},{8,14},{9,15},{10,... | collective-permute-start | bytes 491528 | tf_op jit(solution)/shard_map/ppermute | solution.py:41
  73.5 26.7 %collective-permute-start.18 = (bf16[64,640]{1,0:T(8,128)(2,1)S(1)}, bf16[64,640]{1,0:T(8,128)(2,1)S(1)}, u32[]{:S(2)}, u32[]{:S(2)}) collective-permute-start(bf16[64,640]{1,0:T(8,128)(2,1)S(1)} %get-tuple-element.68), channel_id=1, source_target_pairs={{0,0},{1,1},{2,2},{3,3},{4,4},{5,5},{6,6},{7,7},{8,32},{9,33},{10,... | collective-permute-start | bytes 245768 | tf_op jit(solution)/shard_map/ppermute | solution.py:41
  80.1 21.8 %collective-permute-start.19 = (bf16[64,640]{1,0:T(8,128)(2,1)S(1)}, bf16[64,640]{1,0:T(8,128)(2,1)S(1)}, u32[]{:S(2)}, u32[]{:S(2)}) collective-permute-start(bf16[64,640]{1,0:T(8,128)(2,1)S(1)} %get-tuple-element.69), channel_id=1, source_target_pairs={{0,1},{1,0},{2,3},{3,2},{4,5},{5,4},{6,7},{7,6},{8,33},{9,32},{10,... | collective-permute-start | bytes 245768 | tf_op jit(solution)/shard_map/ppermute | solution.py:41
  100.2 1.7 %copy-start.2 = (bf16[64,640]{1,0:T(8,128)(2,1)}, bf16[64,640]{1,0:T(8,128)(2,1)S(1)}, u32[]{:S(2)}) copy-start(bf16[64,640]{1,0:T(8,128)(2,1)S(1)} %collective-permute-done.18.same) | copy-start | bytes 245764
  101.9 0.6 copy-start.3

commit v5 on v3

--- a/solution.py
+++ b/solution.py
@@ -18,6 +18,7 @@
 BLOCK = 128
 HALF = 64
 TILE = 512
+NEAR, FAR = (0, 1, 3), 2
 ROWS = 16
 ONES = 16
 SCALE = math.log2(math.e) / math.sqrt(HEAD_DIM)
@@ -25,13 +26,13 @@
 MIB = 1 << 20
 
 
-def place(y, x, z, c):
+def device(y, x, z, c):
     return c * 32 + y * 8 + x * 2 + z
 
 
 def moves(to):
     return [
-        (place(y, x, z, c), place(*to(y, x, z, c)))
+        (device(y, x, z, c), device(*to(y, x, z, c)))
         for c, y, x, z in itertools.product(range(4), range(4), range(4), range(2))
     ]
 
@@ -56,64 +57,36 @@
     return lax.dot_general(a, b, (((1,), (1,)), ((), ())), preferred_element_type=jnp.float32)
 
 
-def fetch(where, row_blocks, row_parts, column_blocks, column_part, sems):
-    y, x, z, c = (where[i] for i in range(4))
-    copies = []
-    for d in range(4):
-        away = lax.rem(lax.bitwise_xor(c, d) - y + 4, 4)
-        for part in range(2):
-            start = pl.multiple_of(away * BLOCK + lax.bitwise_xor(z, part) * HALF, HALF)
-            for ref, at in row_parts:
-                copies.append(
-                    pltpu.make_async_copy(
-                        row_blocks[d].at[pl.ds(part * HALF, HALF), pl.ds(at * WIDE, WIDE)],
-                        ref.at[pl.ds(start, HALF)],
-                        sems.at[len(copies)],
-                    )
-                )
-    ref, at = column_part
-    for block, d, skip in zip(column_blocks, (0, 1, 3, 2, 2), (0, 0, 0, 0, HALF)):
-        rows = block.shape[0]
-        start = pl.multiple_of(lax.rem(x - d + 4, 4) * BLOCK + skip, HALF)
-        copies.append(
-            pltpu.make_async_copy(
-                block.at[:, pl.ds(at * WIDE, WIDE)],
-                ref.at[pl.ds(start, rows)],
-                sems.at[len(copies)],
-            )
-        )
-    for copy in copies:
-        copy.start()
-    for copy in copies:
-        copy.wait()
-
-
-def head(ref, h):
-    return ref[:, h * HEAD_DIM : (h + 1) * HEAD_DIM]
-
-
-def row_kernel(where, *refs):
-    by_row, lifted_out, queries, keys, sems = refs[9:]
-    fetch(where, refs[0:4], [(queries, 0)], refs[4:9], (keys, 1), sems)
+def head(blocks, part, h):
+    at = slice(part * WIDE + h * HEAD_DIM, part * WIDE + (h + 1) * HEAD_DIM)
+    return jnp.concatenate([block[:, at] for block in blocks], axis=0)
+
+
+def rows_of(rows, columns, lifted_out):
     lane = lax.broadcasted_iota(jnp.int32, (TILE, 128), 1)
     kept = jnp.zeros((TILE, 128), jnp.float32)
     for h in range(GROUP):
-        scores = nt(head(queries, h), head(keys, h)) * SCALE
+        scores = nt(head(rows, 0, h), head(columns, 1, h)) * SCALE
         top = jnp.max(scores, axis=1, keepdims=True)
         lifted = jnp.exp2(scores - top)
         lifted_out[h] = lifted.astype(jnp.bfloat16)
         kept = jnp.where(lane == h, top, kept)
         kept = jnp.where(lane == 8 + h, jnp.sum(lifted, axis=1, keepdims=True), kept)
-    by_row[...] = jnp.transpose(kept)[0:16]
-
-
-def column_kernel(where, *refs):
-    by_column, lifted_out = refs[9:11]
-    partials, (keys, values, queries, held, sems) = refs[11:15], refs[15:]
-    fetch(where, refs[0:4], [(keys, 1), (values, 2)], refs[4:9], (queries, 0), sems)
+    return jnp.transpose(kept)[0:16]
+
+
+def place(x, d):
+    return pl.ds(pl.multiple_of(lax.rem(x - d + 4, 4) * BLOCK, BLOCK), BLOCK)
+
+
+def row_place(c, d):
+    return pl.ds(pl.multiple_of(lax.bitwise_xor(c, d) * BLOCK, BLOCK), BLOCK)
+
+
+def columns_of(rows, columns, by_column, lifted_out, partials):
     by_column[...] = jnp.zeros_like(by_column)
     for h in range(GROUP):
-        scores = nt(head(keys, h), head(queries, h)) * SCALE
+        scores = nt(head(rows, 1, h), head(columns, 0, h)) * SCALE
         top = jnp.max(scores, axis=0, keepdims=True)
         lifted = jnp.exp2(scores - top)
         by_column[h : h + 1, :] = top
@@ -121,18 +94,45 @@
         lifted = lifted.astype(jnp.bfloat16)
         lifted_out[h] = lifted
         part = lax.dot_general(
-            head(values, h), lifted, (((0,), (0,)), ((), ())), preferred_element_type=jnp.float32
-        )
-        held[h * HEAD_DIM : (h + 1) * HEAD_DIM, :] = part.astype(jnp.bfloat16)
+            head(rows, 2, h),
+            lifted,
+            (((0,), (0,)), ((), ())),
+            preferred_element_type=jnp.float32,
+        ).astype(jnp.bfloat16)
+        for i, out in enumerate(partials):
+            out[h * HEAD_DIM : (h + 1) * HEAD_DIM, :] = part[:, i * BLOCK : (i + 1) * BLOCK]
+
+
+def near_kernel(*refs):
+    rows, columns = refs[0:4], refs[4:7]
+    by_row, by_column, row_lifted, column_lifted = refs[7:11]
+    columns_of(rows, columns, by_column, column_lifted, refs[11:14])
+    by_row[...] = rows_of(rows, columns, row_lifted)
+
+
+def far_kernel(where, *refs):
+    rows, columns, near_by_row, near_by_column = refs[0:4], refs[4:6], refs[6], refs[7]
+    by_row, top, by_column, row_lifted, column_lifted, partial, own = refs[8:]
+    x, c = where[1], where[3]
+    columns_of(rows, columns, own, column_lifted, [partial])
+    for i, d in enumerate(NEAR):
+        by_column[:, place(x, d)] = near_by_column[:, i * BLOCK : (i + 1) * BLOCK]
+    by_column[:, place(x, FAR)] = own[...]
+    far_by_row = rows_of(rows, columns, row_lifted)
+    tops = near_by_row[0:8], far_by_row[0:8]
+    both = jnp.maximum(*tops)
+    total = near_by_row[8:16] * jnp.exp2(tops[0] - both) + far_by_row[8:16] * jnp.exp2(
+        tops[1] - both
+    )
+    top[...] = tops[1]
     for d in range(4):
-        owner = lax.rem(where[1] + d, 4)
-        partials[d][...] = held[:, pl.ds(pl.multiple_of(owner * BLOCK, BLOCK), BLOCK)]
-
-
-def factors(refs):
+        by_row[0:8, row_place(c, d)] = both[:, d * BLOCK : (d + 1) * BLOCK]
+        by_row[8:16, row_place(c, d)] = total[:, d * BLOCK : (d + 1) * BLOCK]
+
+
+def merged(refs):
     top = functools.reduce(jnp.maximum, [ref[0:8, :] for ref in refs])
-    total = sum(ref[8:16, :] * jnp.exp2(ref[0:8, :] - top) for ref in refs)
-    return jnp.exp2(refs[0][0:8, :] - top) / total
+    return top, sum(ref[8:16, :] * jnp.exp2(ref[0:8, :] - top) for ref in refs)
 
 
 def turned(value):
@@ -141,19 +141,33 @@
 
 def symmetric_kernel(where, *refs):
     row_stats, column_stats = refs[0:4], refs[4:8]
-    row_lifted, column_lifted, out, held, sems = refs[8:]
-    by_row = turned(factors(row_stats) * 1024.0)
-    by_column = factors(column_stats) * 1024.0
-    y, z = where[0], where[2]
+    row_tops, row_lifted, column_lifted = refs[8:10], refs[10:12], refs[12:14]
+    out, totals, held, sems = refs[14:]
+    x, z, c = (where[i] for i in range(1, 4))
+    totals[0:8, :], totals[8:16, :] = merged(row_stats)
+    top, total = (
+        jnp.concatenate([totals[at : at + 8, row_place(c, d)] for d in range(4)], axis=1)
+        for at in (0, 8)
+    )
+    by_row = [turned(jnp.exp2(ref[0:8, :] - top) * (1024.0 / total)) for ref in row_tops]
+    top, total = merged(column_stats)
+    totals[0:8, :] = jnp.exp2(column_stats[0][0:8, :] - top) * (1024.0 / total)
+    places = [place(x, d) for d in (*NEAR, FAR)]
+    gains = [totals[0:8, at] for at in places]
     copies = []
     for p in range(8):
-        owner = lax.rem(y + p // 2, 4) * 2 + lax.bitwise_xor(z, p % 2)
+        owner = lax.bitwise_xor(c, p // 2) * 2 + p % 2
         here = slice(p * HALF, (p + 1) * HALF)
         for h in range(GROUP):
-            held[p, h] = (
-                row_lifted[h, here].astype(jnp.float32) * by_row[here, h : h + 1]
-                + column_lifted[h, here].astype(jnp.float32) * by_column[h : h + 1, :]
-            ).astype(jnp.bfloat16)
+            for i, at in enumerate(places):
+                part, block = divmod(i, len(NEAR))
+                columns = slice(block * BLOCK, (block + 1) * BLOCK)
+                held[p, h, :, at] = (
+                    row_lifted[part][h, here, columns].astype(jnp.float32)
+                    * by_row[part][here, h : h + 1]
+                    + column_lifted[part][h, here, columns].astype(jnp.float32)
+                    * gains[i][h : h + 1, :]
+                ).astype(jnp.bfloat16)
         copies.append(pltpu.make_async_copy(held.at[p], out.at[owner], sems.at[p]))
         copies[p].start()
     for copy in copies:
@@ -351,10 +365,17 @@
         jnp.pad(rel_table, ((0, 72 - BINS), (0, 0))),
     )
 
-    near = jnp.concatenate([queries[:, :WIDE], keys[:, :WIDE], values[:, :WIDE]], axis=1)
-    far = jnp.concatenate([queries[:, WIDE:], keys[:, WIDE:], values[:, WIDE:]], axis=1)
-    same = send(jnp.where(z == 0, near, far), lambda y, x, z, c: (c, x, z, y))
-    other = send(jnp.where(z == 0, far, near), lambda y, x, z, c: (c, x, 1 - z, y))
+    def half(at):
+        near, far = (
+            jnp.concatenate([a[:, lo : lo + WIDE] for a in (queries, keys, values)], axis=1)
+            for lo in (0, WIDE)
+        )
+        return jnp.where(at == 0, near, far)
+
+    crossing = half(1 - z)
+    crossing, z = lax.optimization_barrier((crossing, z))
+    other = send(crossing, lambda y, x, z, c: (c, x, 1 - z, y))
+    same = send(half(z), lambda y, x, z, c: (c, x, z, y))
     block = jnp.where(
         z == 0,
         jnp.concatenate([same, other], axis=0),
@@ -391,44 +412,67 @@
     beside = send(block, lambda y, x, z, c: (y, x, z, c ^ 1))
     row_blocks = [block, beside, across, send(across, lambda y, x, z, c: (y, x, z, c ^ 1))]
 
-    by_row, row_lifted = pl.pallas_call(
-        row_kernel,
-        in_specs=[SMEM] + [ANY] * 9,
-        out_specs=[VMEM] * 2,
-        out_shape=[shape((16, TILE), jnp.float32), shape((GROUP, TILE, TILE))],
-        scratch_shapes=[vmem(TILE, WIDE)] * 2 + [pltpu.SemaphoreType.DMA((13,))],
+    near = len(NEAR) * BLOCK
+    near_outs = [
+        shape((16, TILE), jnp.float32),
+        shape((16, near), jnp.float32),
+        *[shape((GROUP, TILE, near))] * 2,
+        *[shape((WIDE, BLOCK))] * 3,
+    ]
+    near_by_row, near_by_column, *near_lifted, own_partial, right_partial, left_partial = (
+        pl.pallas_call(
+            near_kernel,
+            in_specs=[VMEM] * 7,
+            out_specs=[VMEM] * len(near_outs),
+            out_shape=near_outs,
+            compiler_params=params(16),
+            cost_estimate=cost(8e8, 12e6, 2e6),
+            name="near",
+        )(*row_blocks, *column_blocks[:3])
+    )
+    near_by_row, *column_blocks[3:] = lax.optimization_barrier((near_by_row, *column_blocks[3:]))
+    far_outs = [
+        shape((16, TILE), jnp.float32),
+        shape((8, TILE), jnp.float32),
+        shape((16, TILE), jnp.float32),
+        *[shape((GROUP, TILE, BLOCK))] * 2,
+        shape((WIDE, BLOCK)),
+    ]
+    by_row, far_top, by_column, *far_lifted, far_partial = pl.pallas_call(
+        far_kernel,
+        in_specs=[SMEM] + [VMEM] * 8,
+        out_specs=[VMEM] * len(far_outs),
+        out_shape=far_outs,
+        scratch_shapes=[pltpu.VMEM((16, BLOCK), jnp.float32)],
         compiler_params=params(12),
-        cost_estimate=cost(4e8, 8e6, 1.4e6),
-        name="rows",
-    )(where, *row_blocks, *column_blocks)
-    by_column, column_lifted, *partials = pl.pallas_call(
-        column_kernel,
-        in_specs=[SMEM] + [ANY] * 9,
-        out_specs=[VMEM] * 6,
-        out_shape=[shape((16, TILE), jnp.float32), shape((GROUP, TILE, TILE))]
-        + [shape((WIDE, BLOCK))] * 4,
-        scratch_shapes=[vmem(TILE, WIDE)] * 3
-        + [vmem(WIDE, TILE), pltpu.SemaphoreType.DMA((21,))],
-        compiler_params=params(12),
-        cost_estimate=cost(7e8, 9e6, 1.4e6),
-        name="columns",
-    )(where, *row_blocks, *column_blocks)
+        cost_estimate=cost(3e8, 5e6, 7e5),
+        name="far",
+    )(where, *row_blocks, *column_blocks[3:], near_by_row, near_by_column)
+    partials = [own_partial, left_partial, far_partial, right_partial]
     row_stats = [by_row] + over_rows(by_row)
     column_stats = [by_column] + over_columns(by_column)
 
     tiles = pl.pallas_call(
         symmetric_kernel,
-        in_specs=[SMEM] + [VMEM] * 10,
+        in_specs=[SMEM] + [VMEM] * 14,
         out_specs=HBM,
         out_shape=shape((8, GROUP, HALF, TILE)),
         scratch_shapes=[
+            pltpu.VMEM((16, TILE), jnp.float32),
             pltpu.VMEM((8, GROUP, HALF, TILE), jnp.bfloat16),
             pltpu.SemaphoreType.DMA((8,)),
         ],
         compiler_params=params(8),
         cost_estimate=cost(1e7, 9e6),
         name="symmetric",
-    )(where, *row_stats, *column_stats, row_lifted, column_lifted)
+    )(
+        where,
+        *row_stats,
+        *column_stats,
+        near_by_row,
+        far_top,
+        *(part for parts in zip(near_lifted, far_lifted) for part in parts),
+    )
     where, tiles = lax.optimization_barrier((where, tiles))
     groups = [[y * 8 + x * 2 + z for y in range(4) for z in range(2)] for x in range(4)]
     received = lax.all_to_all(

time: 119 us -> 111 us (0.933)
  waiting for transfers between devices: 39.8 us -> 36.3 us
  starting transfers between devices: 41.4 us -> 39.5 us
  local copies, waits for them, and re-layouts: 6.54 us -> 5.21 us
    ppermute x20, waiting for transfers between devices: 39.8 us -> 36.3 us  [send(): return lax.ppermute(value, AXES, moves(to))]
    unnamed x10 -> x12, local copies, waits for them, and re-layouts: 2.99 us -> 2.3 us
  transfers between devices with their start and end apart: 21 -> 21, of which waited for: 10 -> 13; matrix products, arithmetic and copies ran while one was open for 3% -> 2% of each run, Pallas kernels for 10% -> 12%
where the time goes in v5:
time: 111 us
  starting transfers between devices  39.5 us (36%)
  waiting for transfers between devices  36.3 us (33%)
  Pallas kernels  28.7 us (26%)
  local copies, waits for them, and re-layouts  5.21 us (5%)
    ppermute x20, waiting for transfers between devices, send(): return lax.ppermute(value, AXES, moves(to))  36.3 us
    ppermute x20, starting transfers between devices, send(): return lax.ppermute(value, AXES, moves(to))  35.2 us
    pallas_call x1, Pallas kernels, local(): pl.pallas_call(pair_kernel, grid=(HALF // ROWS,), in_specs=[SMEM, pl.Bloc...  10.8 us
    pallas_call x1, Pallas kernels, local(): pl.pallas_call(relative_kernel, grid=(HALF // ROWS,), in_specs=[SMEM, SME...  5.74 us
    all_to_all x1, starting transfers between devices, local(): lax.all_to_all(tiles, 'band', split_axis=0, concat_axis=0, axis_index_gro...  4.31 us
    pallas_call x1, Pallas kernels, local(): pl.pallas_call(near_kernel, in_specs=[VMEM] * 7, out_specs=[VMEM] * len(n...  3.59 us
    pallas_call x1, Pallas kernels, local(): pl.pallas_call(symmetric_kernel, in_specs=[SMEM] + [VMEM] * 14, out_specs...  3.01 us
    pallas_call x1, Pallas kernels, local(): pl.pallas_call(spread_kernel, in_specs=[VMEM] * 5, out_specs=[VMEM] * 4,...  2.68 us
  transfers between devices with their start and end apart: 21, of which 13 were waited for; matrix products, arithmetic and copies ran while one was open for 2% of the time, Pallas kernels for 12%

profile of v5, /device:TPU:1, one launch (start us, length us, event | category | flops | bytes accessed | tf_op | source)
XLA Modules:
  0.0 110.7 jit_solution(7703682763139710060)
XLA Ops:
  0.7 0.9 fusion.2
  1.6 1.0 fusion
  2.7 0.1 broadcast_select_fusion.1
  2.7 6.1 %collective-permute-start.1 = (bf16[64,1920]{1,0:T(8,128)(2,1)S(1)}, bf16[64,1920]{1,0:T(8,128)(2,1)S(1)}, u32[]{:S(2)}, u32[]{:S(2)}) collective-permute-start(bf16[64,1920]{1,0:T(8,128)(2,1)S(1)} %broadcast_select_fusion.1), channel_id=1, source_target_pairs={{0,1},{1,0},{2,3},{3,2},{4,5},{5,4},{6,7},{7,6},{8,33},{9,32},{10,... | collective-permute-start | bytes 737288 | tf_op jit(solution)/shard_map/ppermute | solution.py:41
  8.8 0.1 broadcast_select_fusion
  8.9 1.9 %collective-permute-start = (bf16[64,1920]{1,0:T(8,128)(2,1)S(1)}, bf16[64,1920]{1,0:T(8,128)(2,1)S(1)}, u32[]{:S(2)}, u32[]{:S(2)}) collective-permute-start(bf16[64,1920]{1,0:T(8,128)(2,1)S(1)} %broadcast_select_fusion), channel_id=1, source_target_pairs={{0,0},{1,1},{2,2},{3,3},{4,4},{5,5},{6,6},{7,7},{8,32},{9,33},{10,... | collective-permute-start | bytes 737288 | tf_op jit(solution)/shard_map/ppermute | solution.py:41
  10.8 0.8 copy.11
  11.6 0.8 copy.13.second
  12.5 0.8 copy.14.second_bias
  13.2 0.1 copy.12.first_bias
  13.4 2.7 %spread.1 = (bf16[1024,336]{1,0:T(8,128)(2,1)}, bf16[512,512]{1,0:T(8,128)(2,1)}, f32[512,128]{1,0:T(8,128)}, bf16[512,576]{1,0:T(8,128)(2,1)S(1)}) custom-call(bf16[40,128]{1,0:T(8,128)(2,1)S(1)} %copy-done, f32[128,1]{1,0:T(8,128)S(1)} %copy.12.first_bias, bf16[128,64]{1,0:T(8,128)(2,1)S(1)} %copy.13.second, f32[64,1]{1,0:T(8,128)S(1)} %copy.14.second_bias, ...), custom_call_target="tpu_custom_call" | custom-call | flops 400000000 | bytes 6000000 | tf_op jit(solution)/shard_map/spread/pallas_call | solution.py:347
  16.0 0.4 collective-permute-done
  16.4 0.1 maximum_select_fusion.refs_0_
  16.5 6.7 %collective-permute-start.4 = (bf16[128,1920]{1,0:T(8,128)(2,1)S(1)}, bf16[128,1920]{1,0:T(8,128)(2,1)S(1)}, u32[]{:S(2)}, u32[]{:S(2)}) collective-permute-start(bf16[128,1920]{1,0:T(8,128)(2,1)S(1)} %maximum_select_fusion.refs_0_), channel_id=1, source_target_pairs={{0,64},{1,65},{2,66},{3,67},{4,68},{5,69},{6,70},{7,71},{8,72},{9,... | collective-permute-start | bytes 1474568 | tf_op jit(solution)/shard_map/ppermute | solution.py:41
  23.2 1.3 %collective-permute-start.3 = (bf16[128,1280]{1,0:T(8,128)(2,1)S(1)}, bf16[128,1280]{1,0:T(8,128)(2,1)S(1)}, u32[]{:S(2)}, u32[]{:S(2)}) collective-permute-start(bf16[128,1280]{1,0:T(8,128)(2,1)S(1)} %slice.39.refs_4_), channel_id=1, source_target_pairs={{0,2},{1,3},{2,4},{3,5},{4,6},{5,7},{6,0},{7,1},{8,10},{9,11},{10,... | collective-permute-start | bytes 983048 | tf_op jit(solution)/shard_map/ppermute | solution.py:41
  24.5 1.5 %collective-permute-start.2 = (bf16[128,1280]{1,0:T(8,128)(2,1)S(1)}, bf16[128,1280]{1,0:T(8,128)(2,1)S(1)}, u32[]{:S(2)}, u32[]{:S(2)}) collective-permute-start(bf16[128,1280]{1,0:T(8,128)(2,1)S(1)} %slice.39.refs_4_), channel_id=1, source_target_pairs={{0,6},{1,7},{2,0},{3,1},{4,2},{5,3},{6,4},{7,5},{8,14},{9,15},{10,... | collective-permute-start | bytes 983048 | tf_op jit(solution)/shard_map/ppermute | solution.py:41
  26.0 0.1 pad_add_fusion.where
  26.1 5.7 %relative.1 = bf16[64,64,512]{2,1,0:T(8,128)(2,1)} custom-call(s32[4]{0:T(128)S(1)} %pad_add_fusion.where, s32[4]{0:T(128)S(1)} %copy-done.1, bf16[512,576]{1,0:T(8,128)(2,1)S(1)} %get-tuple-element.48.table), custom_call_target="tpu_custom_call" | custom-call | flops 2400000000 | bytes 6000000 | tf_op jit(solution)/shard_map/relative/pallas_call | solution.py:393
  31.8 1.0 collective-permute-done.3.refs_5_
  32.8 0.3 collective-permute-done.2.refs_6_
  33.1 0.5 collective-permute-start.6
  33.7 2.7 %collective-permute-start.8 = (bf16[64,1280]{1,0:T(8,128)(2,1)S(1)}, bf16[64,1280]{1,0:T(8,128)(2,1)S(1)}, u32[]{:S(2)}, u32[]{:S(2)}) collective-permute-start(bf16[64,1280]{1,0:T(8,128)(2,1)S(1)} %slice.41), channel_id=1, source_target_pairs={{0,6},{1,7},{2,0},{3,1},{4,2},{5,3},{6,4},{7,5},{8,14},{9,15},{10,... | collective-permute-start | bytes 491528 | tf_op jit(solution)/shard_map/ppermute | solution.py:41
  36.4 3.6 %near.1 = (f32[16,512]{1,0:T(8,128)S(1)}, f32[16,384]{1,0:T(8,128)S(1)}, bf16[5,512,384]{2,1,0:T(8,128)(2,1)S(1)}, bf16[5,512,384]{2,1,0:T(8,128)(2,1)S(1)}, bf1...) custom-call(bf16[128,1920]{1,0:T(8,128)(2,1)S(1)} %maximum_select_fusion.refs_0_, ...), custom_call_target="tpu_custom_call" | custom-call | flops 800000000 | bytes 12000000 | tf_op jit(solution)/shard_map/near/pallas_call | solution.py:423
  40.0 3.1 %collective-permute-done.7.refs_4_ = bf16[64,1280]{1,0:T(8,128)(2,1)S(1)} collective-permute-done((bf16[64,1280]{1,0:T(8,128)(2,1)S(1)}, bf16[64,1280]{1,0:T(8,128)(2,1)S(1)}, u32[]{:S(2)}, u32[]{:S(2)}) %collective-permute-start.7) | collective-permute-done | bytes 163872 | tf_op jit(solution)/shard_map/ppermute | solution.py:41
  43.1 2.2 %far.1 = (f32[16,512]{1,0:T(8,128)S(1)}, f32[8,512]{1,0:T(8,128)S(1)}, f32[16,512]{1,0:T(8,128)S(1)}, bf16[5,512,128]{2,1,0:T(8,128)(2,1)S(1)}, bf16[5,512,128]{...) custom-call(s32[4]{0:T(128)S(1)} %pad_add_fusion.where, bf16[128,1920]{1,0:T(8,128)(2,1)S(1)} %maximum_select_fusion.refs_0_, ...), custom_call_target="tpu_custom_call" | custom-call | flops 300000000 | bytes 5000000 | tf_op jit(solution)/shard_map/far/pallas_call | solution.py:441
  45.3 2.5 %collective-permute-start.11 = (f32[16,512]{1,0:T(8,128)S(1)}, f32[16,512]{1,0:T(8,128)S(1)}, u32[]{:S(2)}, u32[]{:S(2)}) collective-permute-start(f32[16,512]{1,0:T(8,128)S(1)} %get-tuple-element.61.refs_0_), channel_id=1, source_target_pairs={{0,96},{1,97},{2,98},{3,99},{4,100},{5,101},{6,102},{7,103},{8,104... | collective-permute-start | bytes 98312 | tf_op jit(solution)/shard_map/ppermute | solution.py:41
  47.8 0.5 collective-permute-start.9
  48.3 0.6 collective-permute-start.13
  48.9 0.6 collective-permute-done.11.refs_3_
  49.5 0.3 collective-permute-start.12
  49.8 1.2 %collective-permute-done.10.refs_2_ = f32[16,512]{1,0:T(8,128)S(1)} collective-permute-done((f32[16,512]{1,0:T(8,128)S(1)}, f32[16,512]{1,0:T(8,128)S(1)}, u32[]{:S(2)}, u32[]{:S(2)}) %collective-permute-start.10) | collective-permute-done | bytes 32800 | tf_op jit(solution)/shard_map/ppermute | solution.py:41
  50.9 0.1 collective-permute-done.14.refs_7_.refs_3_
  51.0 1.5 %collective-permute-done.13.refs_6_.refs_2_ = f32[16,512]{1,0:T(8,128)S(1)} collective-permute-done((f32[16,512]{1,0:T(8,128)S(1)}, f32[16,512]{1,0:T(8,128)S(1)}, u32[]{:S(2)}, u32[]{:S(2)}) %collective-permute-start.13) | collective-permute-done | bytes 32800 | tf_op jit(solution)/shard_map/ppermute | solution.py:41
  52.6 1.1 %collective-permute-done.12.refs_5_.refs_1_ = f32[16,512]{1,0:T(8,128)S(1)} collective-permute-done((f32[16,512]{1,0:T(8,128)S(1)}, f32[16,512]{1,0:T(8,128)S(1)}, u32[]{:S(2)}, u32[]{:S(2)}) %collective-permute-start.12) | collective-permute-done | bytes 32800 | tf_op jit(solution)/shard_map/ppermute | solution.py:41
  53.7 3.0 %symmetric.1 = bf16[8,5,64,512]{3,2,1,0:T(8,128)(2,1)} custom-call(s32[4]{0:T(128)S(1)} %pad_add_fusion.where, f32[16,512]{1,0:T(8,128)S(1)} %get-tuple-element.61.refs_0_, f32[16,512]{1,0:T(8,128)S(1)} %collective-permute-done.9.refs_1_, f32[16,512]{1,0:T(8,128)S(1)} %collective-permute-done.10.refs_2_, f32[16,512]{1,0:T(8,128)S(1)} %collective-permute-done.11.refs_3_, ...), custom_call_target="tpu_custom_call" | custom-call | flops 10000000 | bytes 9000000 | tf_op jit(solution)/shard_map/symmetric/pallas_call | solution.py:455
  56.7 4.3 %all-to-all-start = ((bf16[8,5,64,512]{3,2,1,0:T(8,128)(2,1)}), bf16[8,5,64,512]{3,2,1,0:T(8,128)(2,1)S(1)}, u32[]{:S(2)}, u32[]{:S(2)}) async-start(bf16[8,5,64,512]{3,2,1,0:T(8,128)(2,1)} %symmetric.1), calls=%async_computation | async-start | bytes 5242880 | tf_op jit(solution)/shard_map/all_to_all | solution.py:478
  61.0 0.6 collective-permute-start.16
  61.6 1.3 %collective-permute-start.15 = (bf16[640,128]{1,0:T(8,128)(2,1)S(1)}, bf16[640,128]{1,0:T(8,128)(2,1)S(1)}, u32[]{:S(2)}, u32[]{:S(2)}) collective-permute-start(bf16[640,128]{1,0:T(8,128)(2,1)S(1)} %get-tuple-element.75), channel_id=1, source_target_pairs={{0,2},{1,3},{2,4},{3,5},{4,6},{5,7},{6,0},{7,1},{8,10},{9,11},{10,... | collective-permute-start | bytes 491528 | tf_op jit(solution)/shard_map/ppermute | solution.py:41
  62.9 1.4 %collective-permute-start.17 = (bf16[640,128]{1,0:T(8,128)(2,1)S(1)}, bf16[640,128]{1,0:T(8,128)(2,1)S(1)}, u32[]{:S(2)}, u32[]{:S(2)}) collective-permute-start(bf16[640,128]{1,0:T(8,128)(2,1)S(1)} %get-tuple-element.77), channel_id=1, source_target_pairs={{0,6},{1,7},{2,0},{3,1},{4,2},{5,3},{6,4},{7,5},{8,14},{9,15},{10,... | collective-permute-start | bytes 491528 | tf_op jit(solution)/shard_map/ppermute | solution.py:41
  64.3 2.5 %collective-permute-done.16.refs_6_ = bf16[640,128]{1,0:T(8,128)(2,1)S(1)} collective-permute-done((bf16[640,128]{1,0:T(8,128)(2,1)S(1)}, bf16[640,128]{1,0:T(8,128)(2,1)S(1)}, u32[]{:S(2)}, u32[]{:S(2)}) %collective-permute-start.16) | collective-permute-done | bytes 163872 | tf_op jit(solution)/shard_map/ppermute | solution.py:41
  66.8 4.3 %collective-permute-done.15.refs_5_ = bf16[640,128]{1,0:T(8,128)(2,1)S(1)} collective-permute-done((bf16[640,128]{1,0:T(8,128)(2,1)S(1)}, bf16[640,128]{1,0:T(8,128)(2,1)S(1)}, u32[]{:S(2)}, u32[]{:S(2)}) %collective-permute-start.15) | collective-permute-done | bytes 163872 | tf_op jit(solution)/shard_map/ppermute | solution.py:41
  71.1 0.8 context.1
  71.9 4.8 %collective-permute-start.18 = (bf16[64,640]{1,0:T(8,128)(2,1)S(1)}, bf16[64,640]{1,0:T(8,128)(2,1)S(1)}, u32[]{:S(2)}, u32[]{:S(2)}) collective-permute-start(bf16[64,640]{1,0:T(8,128)(2,1)S(1)} %get-tuple-element.78), channel_id=1, source_target_pairs={{0,0},{1,1},{2,2},{3,3},{4,4},{5,5},{6,6},{7,7},{8,32},{9,33},{10,... | collective-permute-start | bytes 245768 | tf_op jit(solution)/shard_map/ppermute | solution.py:41
  76.7 2.5 %collective-permute-start.19 = (bf16[64,640]{1,0:T(8,128)(2,1)S(1)}, bf16[64,640]{1,0:T(8,128)(2,1)S(1)}, u32[]{:S(2)}, u32[]{:S(2)}) collective-permute-start(bf16[64,640]{1,0:T(8,128)(2,1)S(1)} %get-tuple-element.79), channel_id=1, source_target_pairs={{0,1},{1,0},{2,3},{3,2},{4,5},{5,4},{6,7},{7,6},{8,33},{9,32},{10,... | collective-permute-start | bytes 245768 | tf_op jit(solution)/shard_map/ppermute | solution.py:41
  79.2 18.0 %collective-permute-done.18.same = bf16[64,640]{1,0:T(8,128)(2,1)S(1)} collective-permute-done((bf16[64,640]{1,0:T(8,128)(2,1)S(1)}, bf16[64,640]{1,0:T(8,128)(2,1)S(1)}, u32[]{:S(2)}, u32[]{:S(2)}) %collective-permute-start.18) | collective-permute-done | bytes 81952 | tf_op jit(solution)/shard_map/ppermute | solution.py:41
  97.2 2.1 %collective-permute-done.19.other = bf16[64,640]{1,0:T(8,128)(2,1)S(1)} collective-permute-done((bf16[64,640]{1,0:T(8,128)(2,1)S(1)}, bf16[64,640]{1,0:T(8,128)(2,1)S(1)}, u32[]{:S(2)}, u32[]{:S(2)}) %collective-permute-start.19) | collective-permute-done | bytes 81952 | tf_op jit(solution)/shard_map/ppermute | solution.py:41
  99.4 0.6 copy-done.4
  100.0 10.8 %pair.1 = (bf16[64,64,512]{2,1,0:T(8,128)(2,1)}, bf16[64,1280]{1,0:T(8,128)(2,1)}) custom-call(s32[4]{0:T(128)S(1)} %pad_add_fusion.where, bf16[40,64,512]{2,1,0:T(8,128)(2,1)S(1)} %bitcast.7, bf16[1024,336]{1,0:T(8,128)(2,1)} %get-tuple-element.70.first, bf16[512,512]{1,0:T(8,128)(2,1)} %get-tuple-element.71.second, ...), custom_call_target="tpu_custom_call" | custom-call | flops 5000000000 | bytes 14000000 | tf_op jit(solution)/shard_map/pair/pallas_call | solution.py:495
  (25 shorter events, 0.2 us)
Async XLA Ops:
  0.6 12.6 %copy-start.2 = (f32[128]{0:T(128)S(1)}, f32[128]{0:T(128)}, u32[]{:S(2)}) copy-start(f32[128]{0:T(128)} %param.13) | copy-start | bytes 1540
  0.6 12.7 %copy-start = (bf16[40,128]{1,0:T(8,128)(2,1)S(1)}, bf16[40,128]{1,0:T(8,128)(2,1)}, u32[]{:S(2)}) copy-start(bf16[40,128]{1,0:T(8,128)(2,1)} %first.1) | copy-start | bytes 30724
  1.6 24.4 %copy-start.1 = (s32[4]{0:T(128)S(1)}, s32[4]{0:T(128)}, u32[]{:S(2)}) copy-start(s32[4]{0:T(128)} %lengths.1) | copy-start | bytes 52
  2.7 13.3 %collective-permute-start.1 = (bf16[64,1920]{1,0:T(8,128)(2,1)S(1)}, bf16[64,1920]{1,0:T(8,128)(2,1)S(1)}, u32[]{:S(2)}, u32[]{:S(2)}) collective-permute-start(bf16[64,1920]{1,0:T(8,128)(2,1)S(1)} %broadcast_select_fusion.1), channel_id=1, source_target_pairs={{0,1},{1,0},{2,3},{3,2},{4,5},{5,4},{6,7},{7,6},{8,33},{9,32},{10,... | collective-permute-start | bytes 737288 | tf_op jit(solution)/shard_map/ppermute | solution.py:41
  8.9 7.5 %collective-permute-start = (bf16[64,1920]{1,0:T(8,128)(2,1)S(1)}, bf16[64,1920]{1,0:T(8,128)(2,1)S(1)}, u32[]{:S(2)}, u32[]{:S(2)}) collective-permute-start(bf16[64,1920]{1,0:T(8,128)(2,1)S(1)} %broadcast_select_fusion), channel_id=1, source_target_pairs={{0,0},{1,1},{2,2},{3,3},{4,4},{5,5},{6,6},{7,7},{8,32},{9,33},{10,... | collective-permute-start | bytes 737288 | tf_op jit(solution)/shard_map/ppermute | solution.py:41
  16.5 16.6 %collective-permute-start.4 = (bf16[128,1920]{1,0:T(8,128)(2,1)S(1)}, bf16[128,1920]{1,0:T(8,128)(2,1)S(1)}, u32[]{:S(2)}, u32[]{:S(2)}) collective-permute-start(bf16[128,1920]{1,0:T(8,128)(2,1)S(1)} %maximum_select_fusion.refs_0_), channel_id=1, source_target_pairs={{0,64},{1,65},{2,66},{3,67},{4,68},{5,69},{6,70},{7,71},{8,72},{9,... | collective-permute-start | bytes 1474568 | tf_op jit(solution)/shard_map/ppermute | solution.py:41
  23.2 9.6 %collective-permute-start.3 = (bf16[128,1280]{1,0:T(8,128)(2,1)S(1)}, bf16[128,1280]{1,0:T(8,128)(2,1)S(1)}, u32[]{:S(2)}, u32[]{:S(2)}) collective-permute-start(bf16[128,1280]{1,0:T(8,128)(2,1)S(1)} %slice.39.refs_4_), channel_id=1, source_target_pairs={{0,2},{1,3},{2,4},{3,5},{4,6},{5,7},{6,0},{7,1},{8,10},{9,11},{10,... | collective-permute-start | bytes 983048 | tf_op jit(solution)/shard_map/ppermute | solution.py:41
  24.5 8.6 %collective-permute-start.2 = (bf16[128,1280]{1,0:T(8,128)(2,1)S(1)}, bf16[128,1280]{1,0:T(8,128)(2,1)S(1)}, u32[]{:S(2)}, u32[]{:S(2)}) collective-permute-start(bf16[128,1280]{1,0:T(8,128)(2,1)S(1)} %slice.39.refs_4_), channel_id=1, source_target_pairs={{0,6},{1,7},{2,0},{3,1},{4,2},{5,3},{6,4},{7,5},{8,14},{9,15},{10,... | collective-permute-start | bytes 983048 | tf_op jit(solution)/shard_map/ppermute | solution.py:41
  33.1 3.3 %collective-permute-start.5 = (bf16[128,1920]{1,0:T(8,128)(2,1)S(1)}, bf16[128,1920]{1,0:T(8,128)(2,1)S(1)}, u32[]{:S(2)}, u32[]{:S(2)}) collective-permute-start(bf16[128,1920]{1,0:T(8,128)(2,1)S(1)} %maximum_select_fusion.refs_0_), channel_id=1, source_target_pairs={{0,32},{1,33},{2,34},{3,35},{4,36},{5,37},{6,38},{7,39},{8,40},{9,... | collective-permute-start | bytes 1474568 | tf_op jit(solution)/shard_map/ppermute | solution.py:41
  33.1 3.3 %collective-permute-start.6 = (bf16[128,1920]{1,0:T(8,128)(2,1)S(1)}, bf16[128,1920]{1,0:T(8,128)(2,1)S(1)}, u32[]{:S(2)}, u32[]{:S(2)}) collective-permute-start(bf16[128,1920]{1,0:T(8,128)(2,1)S(1)} %collective-permute-done.4.refs_2_), channel_id=1, source_target_pairs={{0,32},{1,33},{2,34},{3,35},{4,36},{5,37},{6,38},{7,39},{8,40},{9,... | collective-permute-start | bytes 1474568 | tf_op jit(solution)/shard_map/ppermute | solution.py:41
  33.7 6.4 %collective-permute-start.8 = (bf16[64,1280]{1,0:T(8,128)(2,1)S(1)}, bf16[64,1280]{1,0:T(8,128)(2,1)S(1)}, u32[]{:S(2)}, u32[]{:S(2)}) collective-permute-start(bf16[64,1280]{1,0:T(8,128)(2,1)S(1)} %slice.41), channel_id=1, source_target_pairs={{0,6},{1,7},{2,0},{3,1},{4,2},{5,3},{6,4},{7,5},{8,14},{9,15},{10,... | collective-permute-start | bytes 491528 | tf_op jit(solution)/shard_map/ppermute | solution.py:41
  36.4 6.7 %collective-permute-start.7 = (bf16[64,1280]{1,0:T(8,128)(2,1)S(1)}, bf16[64,1280]{1,0:T(8,128)(2,1)S(1)}, u32[]{:S(2)}, u32[]{:S(2)}) collective-permute-start(bf16[64,1280]{1,0:T(8,128)(2,1)S(1)} %slice.40), channel_id=1, source_target_pairs={{0,2},{1,3},{2,4},{3,5},{4,6},{5,7},{6,0},{7,1},{8,10},{9,11},{10,... | collective-permute-start | bytes 491528 | tf_op jit(solution)/shard_map/ppermute | solution.py:41
  45.3 4.2 %collective-permute-start.11 = (f32[16,512]{1,0:T(8,128)S(1)}, f32[16,512]{1,0:T(8,128)S(1)}, u32[]{:S(2)}, u32[]{:S(2)}) collective-permute-start(f32[16,512]{1,0:T(8,128)S(1)} %get-tuple-element.61.refs_0_), channel_id=1, source_target_pairs={{0,96},{1,97},{2,98},{3,99},{4,100},{5,101},{6,102},{7,103},{8,104... | collective-permute-start | bytes 98312 | tf_op jit(solution)/shard_map/ppermute | solution.py:41
  47.8 3.1 %collective-permute-start.10 = (f32[16,512]{1,0:T(8,128)S(1)}, f32[16,512]{1,0:T(8,128)S(1)}, u32[]{:S(2)}, u32[]{:S(2)}) collective-permute-start(f32[16,512]{1,0:T(8,128)S(1)} %get-tuple-element.61.refs_0_), channel_id=1, source_target_pairs={{0,64},{1,65},{2,66},{3,67},{4,68},{5,69},{6,70},{7,71},{8,72},{9,... | collective-permute-start | bytes 98312 | tf_op jit(solution)/shard_map/ppermute | solution.py:41
  47.8 3.1 %collective-permute-start.9 = (f32[16,512]{1,0:T(8,128)S(1)}, f32[16,512]{1,0:T(8,128)S(1)}, u32[]{:S(2)}, u32[]{:S(2)}) collective-permute-start(f32[16,512]{1,0:T(8,128)S(1)} %get-tuple-element.61.refs_0_), channel_id=1, source_target_pairs={{0,32},{1,33},{2,34},{3,35},{4,36},{5,37},{6,38},{7,39},{8,40},{9,... | collective-permute-start | bytes 98312 | tf_op jit(solution)/shard_map/ppermute | solution.py:41
  48.3 2.8 %collective-permute-start.14 = (f32[16,512]{1,0:T(8,128)S(1)}, f32[16,512]{1,0:T(8,128)S(1)}, u32[]{:S(2)}, u32[]{:S(2)}) collective-permute-start(f32[16,512]{1,0:T(8,128)S(1)} %get-tuple-element.62.refs_4_.refs_0_), channel_id=1, source_target_pairs={{0,6},{1,7},{2,0},{3,1},{4,2},{5,3},{6,4},{7,5},{8,14},{9,15},{10,... | collective-permute-start | bytes 98312 | tf_op jit(solution)/shard_map/ppermute | solution.py:41
  48.3 4.3 %collective-permute-start.13 = (f32[16,512]{1,0:T(8,128)S(1)}, f32[16,512]{1,0:T(8,128)S(1)}, u32[]{:S(2)}, u32[]{:S(2)}) collective-permute-start(f32[16,512]{1,0:T(8,128)S(1)} %get-tuple-element.62.refs_4_.refs_0_), channel_id=1, source_target_pairs={{0,4},{1,5},{2,6},{3,7},{4,0},{5,1},{6,2},{7,3},{8,12},{9,13},{10,... | collective-permute-start | bytes 98312 | tf_op jit(solution)/shard_map/ppermute | solution.py:41
  49.5 4.2 %collective-permute-start.12 = (f32[16,512]{1,0:T(8,128)S(1)}, f32[16,512]{1,0:T(8,128)S(1)}, u32[]{:S(2)}, u32[]{:S(2)}) collective-permute-start(f32[16,512]{1,0:T(8,128)S(1)} %get-tuple-element.62.refs_4_.refs_0_), channel_id=1, source_target_pairs={{0,2},{1,3},{2,4},{3,5},{4,6},{5,7},{6,0},{7,1},{8,10},{9,11},{10,... | collective-permute-start | bytes 98312 | tf_op jit(solution)/shard_map/ppermute | solution.py:41
  56.7 42.6 %all-to-all-start = ((bf16[8,5,64,512]{3,2,1,0:T(8,128)(2,1)}), bf16[8,5,64,512]{3,2,1,0:T(8,128)(2,1)S(1)}, u32[]{:S(2)}, u32[]{:S(2)}) async-start(bf16[8,5,64,512]{3,2,1,0:T(8,128)(2,1)} %symmetric.1), calls=%async_computation | async-start | bytes 5242880 | tf_op jit(solution)/shard_map/all_to_all | solution.py:478
  61.0 5.8 %collective-permute-start.16 = (bf16[640,128]{1,0:T(8,128)(2,1)S(1)}, bf16[640,128]{1,0:T(8,128)(2,1)S(1)}, u32[]{:S(2)}, u32[]{:S(2)}) collective-permute-start(bf16[640,128]{1,0:T(8,128)(2,1)S(1)} %get-tuple-element.76), channel_id=1, source_target_pairs={{0,4},{1,5},{2,6},{3,7},{4,0},{5,1},{6,2},{7,3},{8,12},{9,13},{10,... | collective-permute-start | bytes 491528 | tf_op jit(solution)/shard_map/ppermute | solution.py:41
  61.6 9.5 %collective-permute-start.15 = (bf16[640,128]{1,0:T(8,128)(2,1)S(1)}, bf16[640,128]{1,0:T(8,128)(2,1)S(1)}, u32[]{:S(2)}, u32[]{:S(2)}) collective-permute-start(bf16[640,128]{1,0:T(8,128)(2,1)S(1)} %get-tuple-element.75), channel_id=1, source_target_pairs={{0,2},{1,3},{2,4},{3,5},{4,6},{5,7},{6,0},{7,1},{8,10},{9,11},{10,... | collective-permute-start | bytes 491528 | tf_op jit(solution)/shard_map/ppermute | solution.py:41
  62.9 8.2 %collective-permute-start.17 = (bf16[640,128]{1,0:T(8,128)(2,1)S(1)}, bf16[640,128]{1,0:T(8,128)(2,1)S(1)}, u32[]{:S(2)}, u32[]{:S(2)}) collective-permute-start(bf16[640,128]{1,0:T(8,128)(2,1)S(1)} %get-tuple-element.77), channel_id=1, source_target_pairs={{0,6},{1,7},{2,0},{3,1},{4,2},{5,3},{6,4},{7,5},{8,14},{9,15},{10,... | collective-permute-start | bytes 491528 | tf_op jit(solution)/shard_map/ppermute | solution.py:41
  71.9 25.3 %collective-permute-start.18 = (bf16[64,640]{1,0:T(8,128)(2,1)S(1)}, bf16[64,640]{1,0:T(8,128)(2,1)S(1)}, u32[]{:S(2)}, u32[]{:S(2)}) collective-permute-start(bf16[64,640]{1,0:T(8,128)(2,1)S(1)} %get-tuple-element.78), channel_id=1, source_target_pairs={{0,0},{1,1},{2,2},{3,3},{4,4},{5,5},{6,6},{7,7},{8,32},{9,33},{10,... | collective-permute-start | bytes 245768 | tf_op jit(solution)/shard_map/ppermute | solution.py:41
  76.7 22.6 %collective-permute-start.19 = (bf16[64,640]{1,0:T(8,128)(2,1)S(1)}, bf16[64,640]{1,0:T(8,128)(2,1)S(1)}, u32[]{:S(2)}, u32[]{:S(2)}) collective-permute-start(bf16[64,640]{1,0:T(8,128)(2,1)S(1)} %get-tuple-element.79), channel_id=1, source_target_pairs={{0,1},{1,0},{2,3},{3,2},{4,5},{5,4},{6,7},{7,6},{8,33},{9,32},{10,... | collective-permute-start | bytes 245768 | tf_op jit(solution)/shard_map/ppermute | solution.py:41
  97.2 2.1 %copy-start.3 = (bf16[64,640]{1,0:T(8,128)(2,1)}, bf16[64,640]{1,0:T(8,128)(2,1)S(1)}, u32[]{:S(2)}) copy-start(bf16[64,640]{1,0:T(8,128)(2,1)S(1)} %collective-permute-done.18.same) | copy-start | bytes 245764
  99.3 0.6 copy-start.4

commit v6 on v5

--- a/solution.py
+++ b/solution.py
@@ -49,10 +49,6 @@
     return over_columns_of([value] * 4)
 
 
-def over_rows(value):
-    return [send(value, lambda y, x, z, c, d=d: (y, x, z, c ^ d)) for d in (1, 2, 3)]
-
-
 def nt(a, b):
     return lax.dot_general(a, b, (((1,), (1,)), ((), ())), preferred_element_type=jnp.float32)
 
@@ -83,7 +79,7 @@
     return pl.ds(pl.multiple_of(lax.bitwise_xor(c, d) * BLOCK, BLOCK), BLOCK)
 
 
-def columns_of(rows, columns, by_column, lifted_out, partials):
+def columns_of(rows, columns, by_column, lifted_out):
     by_column[...] = jnp.zeros_like(by_column)
     for h in range(GROUP):
         scores = nt(head(rows, 1, h), head(columns, 0, h)) * SCALE
@@ -91,30 +87,21 @@
         lifted = jnp.exp2(scores - top)
         by_column[h : h + 1, :] = top
         by_column[8 + h : 9 + h, :] = jnp.sum(lifted, axis=0, keepdims=True)
-        lifted = lifted.astype(jnp.bfloat16)
-        lifted_out[h] = lifted
-        part = lax.dot_general(
-            head(rows, 2, h),
-            lifted,
-            (((0,), (0,)), ((), ())),
-            preferred_element_type=jnp.float32,
-        ).astype(jnp.bfloat16)
-        for i, out in enumerate(partials):
-            out[h * HEAD_DIM : (h + 1) * HEAD_DIM, :] = part[:, i * BLOCK : (i + 1) * BLOCK]
+        lifted_out[h] = lifted.astype(jnp.bfloat16)
 
 
 def near_kernel(*refs):
     rows, columns = refs[0:4], refs[4:7]
-    by_row, by_column, row_lifted, column_lifted = refs[7:11]
-    columns_of(rows, columns, by_column, column_lifted, refs[11:14])
+    by_row, by_column, row_lifted, column_lifted = refs[7:]
+    columns_of(rows, columns, by_column, column_lifted)
     by_row[...] = rows_of(rows, columns, row_lifted)
 
 
 def far_kernel(where, *refs):
     rows, columns, near_by_row, near_by_column = refs[0:4], refs[4:6], refs[6], refs[7]
-    by_row, top, by_column, row_lifted, column_lifted, partial, own = refs[8:]
+    by_row, top, by_column, row_lifted, column_lifted, own = refs[8:]
     x, c = where[1], where[3]
-    columns_of(rows, columns, own, column_lifted, [partial])
+    columns_of(rows, columns, own, column_lifted)
     for i, d in enumerate(NEAR):
         by_column[:, place(x, d)] = near_by_column[:, i * BLOCK : (i + 1) * BLOCK]
     by_column[:, place(x, FAR)] = own[...]
@@ -130,19 +117,36 @@
         by_row[8:16, row_place(c, d)] = total[:, d * BLOCK : (d + 1) * BLOCK]
 
 
+def partial_kernel(*refs):
+    values, lifted, outs = refs[0:4], refs[4:6], refs[6:10]
+    for h in range(GROUP):
+        at = slice(h * HEAD_DIM, (h + 1) * HEAD_DIM)
+        own = head(values, 2, h)
+        for half, held in zip(lifted, (outs[:3], outs[3:])):
+            part = lax.dot_general(
+                own, half[h], (((0,), (0,)), ((), ())), preferred_element_type=jnp.float32
+            ).astype(jnp.bfloat16)
+            for i, out in enumerate(held):
+                out[at, :] = part[:, i * BLOCK : (i + 1) * BLOCK]
+
+
 def merged(refs):
     top = functools.reduce(jnp.maximum, [ref[0:8, :] for ref in refs])
     return top, sum(ref[8:16, :] * jnp.exp2(ref[0:8, :] - top) for ref in refs)
 
 
+def merge_kernel(one, other, both):
+    both[0:8, :], both[8:16, :] = merged([one, other])
+
+
 def turned(value):
     return jnp.transpose(jnp.concatenate([value] * 16, axis=0))
 
 
 def symmetric_kernel(where, *refs):
-    row_stats, column_stats = refs[0:4], refs[4:8]
-    row_tops, row_lifted, column_lifted = refs[8:10], refs[10:12], refs[12:14]
-    out, totals, held, sems = refs[14:]
+    row_stats, column_stats = refs[0:2], refs[2:6]
+    row_tops, row_lifted, column_lifted = refs[6:8], refs[8:10], refs[10:12]
+    out, totals, held, sems = refs[12:]
     x, z, c = (where[i] for i in range(1, 4))
     totals[0:8, :], totals[8:16, :] = merged(row_stats)
     top, total = (
@@ -281,7 +285,8 @@
         context[:, pl.ds(pl.multiple_of(z * WIDE, WIDE), WIDE)] = same[...]
         context[:, pl.ds(pl.multiple_of((1 - z) * WIDE, WIDE), WIDE)] = other[...]
 
-    loaded = tiles[...].astype(jnp.float32)
+    start = pl.multiple_of(pl.program_id(0) * ROWS, ROWS)
+    loaded = tiles[:, pl.ds(start, ROWS), :].astype(jnp.float32)
     outs, hid = second.shape[0] // 8, first.shape[0] // 8
     upper = lax.broadcasted_iota(jnp.int32, (outs // 2, 8, TILE), 1) < 4
     ones = jnp.ones((ONES, TILE), jnp.bfloat16)
@@ -417,28 +422,24 @@
         shape((16, TILE), jnp.float32),
         shape((16, near), jnp.float32),
         *[shape((GROUP, TILE, near))] * 2,
-        *[shape((WIDE, BLOCK))] * 3,
     ]
-    near_by_row, near_by_column, *near_lifted, own_partial, right_partial, left_partial = (
-        pl.pallas_call(
-            near_kernel,
-            in_specs=[VMEM] * 7,
-            out_specs=[VMEM] * len(near_outs),
-            out_shape=near_outs,
-            compiler_params=params(16),
-            cost_estimate=cost(8e8, 12e6, 2e6),
-            name="near",
-        )(*row_blocks, *column_blocks[:3])
-    )
+    near_by_row, near_by_column, *near_lifted = pl.pallas_call(
+        near_kernel,
+        in_specs=[VMEM] * 7,
+        out_specs=[VMEM] * len(near_outs),
+        out_shape=near_outs,
+        compiler_params=params(16),
+        cost_estimate=cost(6e8, 11e6, 2e6),
+        name="near",
+    )(*row_blocks, *column_blocks[:3])
     near_by_row, *column_blocks[3:] = lax.optimization_barrier((near_by_row, *column_blocks[3:]))
     far_outs = [
         shape((16, TILE), jnp.float32),
         shape((8, TILE), jnp.float32),
         shape((16, TILE), jnp.float32),
         *[shape((GROUP, TILE, BLOCK))] * 2,
-        shape((WIDE, BLOCK)),
     ]
-    by_row, far_top, by_column, *far_lifted, far_partial = pl.pallas_call(
+    by_row, far_top, by_column, *far_lifted = pl.pallas_call(
         far_kernel,
         in_specs=[SMEM] + [VMEM] * 8,
         out_specs=[VMEM] * len(far_outs),
@@ -448,13 +449,33 @@
         cost_estimate=cost(3e8, 5e6, 7e5),
         name="far",
     )(where, *row_blocks, *column_blocks[3:], near_by_row, near_by_column)
+    own_partial, right_partial, left_partial, far_partial = pl.pallas_call(
+        partial_kernel,
+        in_specs=[VMEM] * 6,
+        out_specs=[VMEM] * 4,
+        out_shape=[shape((WIDE, BLOCK))] * 4,
+        compiler_params=params(12),
+        cost_estimate=cost(3.4e8, 4e6),
+        name="partials",
+    )(*row_blocks, near_lifted[1], far_lifted[1])
     partials = [own_partial, left_partial, far_partial, right_partial]
-    row_stats = [by_row] + over_rows(by_row)
+    beside_by_row = send(by_row, lambda y, x, z, c: (y, x, z, c ^ 1))
+    both_by_row = pl.pallas_call(
+        merge_kernel,
+        in_specs=[VMEM] * 2,
+        out_specs=VMEM,
+        out_shape=shape((16, TILE), jnp.float32),
+        compiler_params=params(2),
+        cost_estimate=cost(0, 1e5),
+        name="merge",
+    )(by_row, beside_by_row)
+    row_stats = [both_by_row, send(both_by_row, lambda y, x, z, c: (y, x, z, c ^ 2))]
     column_stats = [by_column] + over_columns(by_column)
 
+    where, *partials = lax.optimization_barrier((where, *partials))
     tiles = pl.pallas_call(
         symmetric_kernel,
-        in_specs=[SMEM] + [VMEM] * 14,
+        in_specs=[SMEM] + [VMEM] * 12,
         out_specs=HBM,
         out_shape=shape((8, GROUP, HALF, TILE)),
         scratch_shapes=[
@@ -497,7 +518,7 @@
         grid=(HALF // ROWS,),
         in_specs=[
             SMEM,
-            pl.BlockSpec((8 * GROUP, ROWS, TILE), lambda i: (0, i, 0)),
+            VMEM,
             pl.BlockSpec((hid * 8, 8 * GROUP * 8 + ONES), lambda i: (0, 0)),
             pl.BlockSpec((outs * 8, hid * 4), lambda i: (0, 0)),
             pl.BlockSpec((outs * 8, 128), lambda i: (0, 0)),

time: 111 us -> 110 us (level)
  waiting for transfers between devices: 36.3 us -> 32.6 us
  starting transfers between devices: 39.5 us -> 43 us
    ppermute x20 -> x19, waiting for transfers between devices: 36.3 us -> 32.6 us  [send(): return lax.ppermute(value, AXES, moves(to))]
    ppermute x20 -> x19, starting transfers between devices: 35.2 us -> 38.3 us  [send(): return lax.ppermute(value, AXES, moves(to))]
    pallas_call x2 -> x4, Pallas kernels: 13.8 us -> 14.3 us  [the longest x1 10.6 us: local(): pl.pallas_call(pair_kernel, grid=(HALF // ROWS,), in_specs=[SMEM, VMEM, p...]
  transfers between devices with their start and end apart: 21 -> 20, of which waited for: 13 -> 12; matrix products, arithmetic and copies ran while one was open for 2% -> 2% of each run, Pallas kernels for 12% -> 11%
where the time goes in v6:
time: 110 us
  starting transfers between devices  43 us (39%)
  waiting for transfers between devices  32.6 us (30%)
  Pallas kernels  27.9 us (25%)
  local copies, waits for them, and re-layouts  5.21 us (5%)
    ppermute x19, starting transfers between devices, send(): return lax.ppermute(value, AXES, moves(to))  38.3 us
    ppermute x19, waiting for transfers between devices, send(): return lax.ppermute(value, AXES, moves(to))  32.6 us
    pallas_call x1, Pallas kernels, local(): pl.pallas_call(pair_kernel, grid=(HALF // ROWS,), in_specs=[SMEM, VMEM, p...  10.6 us
    pallas_call x1, Pallas kernels, local(): pl.pallas_call(relative_kernel, grid=(HALF // ROWS,), in_specs=[SMEM, SME...  5.74 us
    all_to_all x1, starting transfers between devices, local(): lax.all_to_all(tiles, 'band', split_axis=0, concat_axis=0, axis_index_gro...  4.73 us
    pallas_call x1, Pallas kernels, local(): pl.pallas_call(symmetric_kernel, in_specs=[SMEM] + [VMEM] * 12, out_specs...  3 us
    pallas_call x1, Pallas kernels, local(): pl.pallas_call(spread_kernel, in_specs=[VMEM] * 5, out_specs=[VMEM] * 4,...  2.68 us
    pallas_call x1, Pallas kernels, local(): pl.pallas_call(near_kernel, in_specs=[VMEM] * 7, out_specs=[VMEM] * len(n...  2.5 us
  transfers between devices with their start and end apart: 20, of which 12 were waited for; matrix products, arithmetic and copies ran while one was open for 2% of the time, Pallas kernels for 11%

profile of v6, /device:TPU:1, one launch (start us, length us, event | category | flops | bytes accessed | tf_op | source)
XLA Modules:
  0.0 109.8 jit_solution(5550856531056120804)
XLA Ops:
  0.7 0.9 fusion.2
  1.6 1.0 fusion
  2.7 0.1 broadcast_select_fusion.1
  2.7 6.1 %collective-permute-start.1 = (bf16[64,1920]{1,0:T(8,128)(2,1)S(1)}, bf16[64,1920]{1,0:T(8,128)(2,1)S(1)}, u32[]{:S(2)}, u32[]{:S(2)}) collective-permute-start(bf16[64,1920]{1,0:T(8,128)(2,1)S(1)} %broadcast_select_fusion.1), channel_id=1, source_target_pairs={{0,1},{1,0},{2,3},{3,2},{4,5},{5,4},{6,7},{7,6},{8,33},{9,32},{10,... | collective-permute-start | bytes 737288 | tf_op jit(solution)/shard_map/ppermute | solution.py:41
  8.8 0.1 broadcast_select_fusion
  8.9 1.9 %collective-permute-start = (bf16[64,1920]{1,0:T(8,128)(2,1)S(1)}, bf16[64,1920]{1,0:T(8,128)(2,1)S(1)}, u32[]{:S(2)}, u32[]{:S(2)}) collective-permute-start(bf16[64,1920]{1,0:T(8,128)(2,1)S(1)} %broadcast_select_fusion), channel_id=1, source_target_pairs={{0,0},{1,1},{2,2},{3,3},{4,4},{5,5},{6,6},{7,7},{8,32},{9,33},{10,... | collective-permute-start | bytes 737288 | tf_op jit(solution)/shard_map/ppermute | solution.py:41
  10.8 0.8 copy.11
  11.6 0.8 copy.13.second
  12.5 0.8 copy.14.second_bias
  13.2 0.1 copy.12.first_bias
  13.4 2.7 %spread.1 = (bf16[1024,336]{1,0:T(8,128)(2,1)}, bf16[512,512]{1,0:T(8,128)(2,1)}, f32[512,128]{1,0:T(8,128)}, bf16[512,576]{1,0:T(8,128)(2,1)S(1)}) custom-call(bf16[40,128]{1,0:T(8,128)(2,1)S(1)} %copy-done, f32[128,1]{1,0:T(8,128)S(1)} %copy.12.first_bias, bf16[128,64]{1,0:T(8,128)(2,1)S(1)} %copy.13.second, f32[64,1]{1,0:T(8,128)S(1)} %copy.14.second_bias, ...), custom_call_target="tpu_custom_call" | custom-call | flops 400000000 | bytes 6000000 | tf_op jit(solution)/shard_map/spread/pallas_call | solution.py:352
  16.0 0.4 collective-permute-done
  16.4 0.1 maximum_select_fusion.refs_0_
  16.5 6.7 %collective-permute-start.4 = (bf16[128,1920]{1,0:T(8,128)(2,1)S(1)}, bf16[128,1920]{1,0:T(8,128)(2,1)S(1)}, u32[]{:S(2)}, u32[]{:S(2)}) collective-permute-start(bf16[128,1920]{1,0:T(8,128)(2,1)S(1)} %maximum_select_fusion.refs_0_), channel_id=1, source_target_pairs={{0,64},{1,65},{2,66},{3,67},{4,68},{5,69},{6,70},{7,71},{8,72},{9,... | collective-permute-start | bytes 1474568 | tf_op jit(solution)/shard_map/ppermute | solution.py:41
  23.2 1.3 %collective-permute-start.3 = (bf16[128,1280]{1,0:T(8,128)(2,1)S(1)}, bf16[128,1280]{1,0:T(8,128)(2,1)S(1)}, u32[]{:S(2)}, u32[]{:S(2)}) collective-permute-start(bf16[128,1280]{1,0:T(8,128)(2,1)S(1)} %slice.39.refs_4_), channel_id=1, source_target_pairs={{0,2},{1,3},{2,4},{3,5},{4,6},{5,7},{6,0},{7,1},{8,10},{9,11},{10,... | collective-permute-start | bytes 983048 | tf_op jit(solution)/shard_map/ppermute | solution.py:41
  24.5 1.5 %collective-permute-start.2 = (bf16[128,1280]{1,0:T(8,128)(2,1)S(1)}, bf16[128,1280]{1,0:T(8,128)(2,1)S(1)}, u32[]{:S(2)}, u32[]{:S(2)}) collective-permute-start(bf16[128,1280]{1,0:T(8,128)(2,1)S(1)} %slice.39.refs_4_), channel_id=1, source_target_pairs={{0,6},{1,7},{2,0},{3,1},{4,2},{5,3},{6,4},{7,5},{8,14},{9,15},{10,... | collective-permute-start | bytes 983048 | tf_op jit(solution)/shard_map/ppermute | solution.py:41
  26.0 0.1 pad_add_fusion.where
  26.1 5.7 %relative.1 = bf16[64,64,512]{2,1,0:T(8,128)(2,1)} custom-call(s32[4]{0:T(128)S(1)} %pad_add_fusion.where, s32[4]{0:T(128)S(1)} %copy-done.1, bf16[512,576]{1,0:T(8,128)(2,1)S(1)} %get-tuple-element.53.table), custom_call_target="tpu_custom_call" | custom-call | flops 2400000000 | bytes 6000000 | tf_op jit(solution)/shard_map/relative/pallas_call | solution.py:398
  31.8 1.0 collective-permute-done.3.refs_5_
  32.8 0.3 collective-permute-done.2.refs_6_
  33.1 0.5 collective-permute-start.6
  33.7 2.7 %collective-permute-start.8 = (bf16[64,1280]{1,0:T(8,128)(2,1)S(1)}, bf16[64,1280]{1,0:T(8,128)(2,1)S(1)}, u32[]{:S(2)}, u32[]{:S(2)}) collective-permute-start(bf16[64,1280]{1,0:T(8,128)(2,1)S(1)} %slice.41), channel_id=1, source_target_pairs={{0,6},{1,7},{2,0},{3,1},{4,2},{5,3},{6,4},{7,5},{8,14},{9,15},{10,... | collective-permute-start | bytes 491528 | tf_op jit(solution)/shard_map/ppermute | solution.py:41
  36.4 2.5 %near.1 = (f32[16,512]{1,0:T(8,128)S(1)}, f32[16,384]{1,0:T(8,128)S(1)}, bf16[5,512,384]{2,1,0:T(8,128)(2,1)S(1)}, bf16[5,512,384]{2,1,0:T(8,128)(2,1)S(1)}) custom-call(bf16[128,1920]{1,0:T(8,128)(2,1)S(1)} %maximum_select_fusion.refs_0_, bf16[128,1920]{1,0:T(8,128)(2,1)S(1)} %collective-permute-done.5.refs_1_, ...), custom_call_target="tpu_custom_call" | custom-call | flops 600000000 | bytes 11000000 | tf_op jit(solution)/shard_map/near/pallas_call | solution.py:426
  38.9 1.1 %collective-permute-done.8.refs_5_ = bf16[64,1280]{1,0:T(8,128)(2,1)S(1)} collective-permute-done((bf16[64,1280]{1,0:T(8,128)(2,1)S(1)}, bf16[64,1280]{1,0:T(8,128)(2,1)S(1)}, u32[]{:S(2)}, u32[]{:S(2)}) %collective-permute-start.8) | collective-permute-done | bytes 163872 | tf_op jit(solution)/shard_map/ppermute | solution.py:41
  40.0 3.1 %collective-permute-done.7.refs_4_ = bf16[64,1280]{1,0:T(8,128)(2,1)S(1)} collective-permute-done((bf16[64,1280]{1,0:T(8,128)(2,1)S(1)}, bf16[64,1280]{1,0:T(8,128)(2,1)S(1)}, u32[]{:S(2)}, u32[]{:S(2)}) %collective-permute-start.7) | collective-permute-done | bytes 163872 | tf_op jit(solution)/shard_map/ppermute | solution.py:41
  43.1 1.9 %far.1 = (f32[16,512]{1,0:T(8,128)S(1)}, f32[8,512]{1,0:T(8,128)S(1)}, f32[16,512]{1,0:T(8,128)S(1)}, bf16[5,512,128]{2,1,0:T(8,128)(2,1)S(1)}, bf16[5,512,128]{2,1,0:T(8,128)(2,1)S(1)}) custom-call(s32[4]{0:T(128)S(1)} %pad_add_fusion.where, bf16[128,1920]{1,0:T(8,128)(2,1)S(1)} %maximum_select_fusion.refs_0_, ...), custom_call_target="tpu_custom_call" | custom-call | flops 300000000 | bytes 5000000 | tf_op jit(solution)/shard_map/far/pallas_call | solution.py:442
  45.0 1.2 %collective-permute-start.9 = (f32[16,512]{1,0:T(8,128)S(1)}, f32[16,512]{1,0:T(8,128)S(1)}, u32[]{:S(2)}, u32[]{:S(2)}) collective-permute-start(f32[16,512]{1,0:T(8,128)S(1)} %get-tuple-element.73.one), channel_id=1, source_target_pairs={{0,32},{1,33},{2,34},{3,35},{4,36},{5,37},{6,38},{7,39},{8,40},{9,... | collective-permute-start | bytes 98312 | tf_op jit(solution)/shard_map/ppermute | solution.py:41
  46.2 0.6 collective-permute-start.12
  46.8 0.9 collective-permute-start.11
  47.7 1.7 %collective-permute-start.10 = (f32[16,512]{1,0:T(8,128)S(1)}, f32[16,512]{1,0:T(8,128)S(1)}, u32[]{:S(2)}, u32[]{:S(2)}) collective-permute-start(f32[16,512]{1,0:T(8,128)S(1)} %merge.1.refs_0_), channel_id=1, source_target_pairs={{0,64},{1,65},{2,66},{3,67},{4,68},{5,69},{6,70},{7,71},{8,72},{9,... | collective-permute-start | bytes 98312 | tf_op jit(solution)/shard_map/ppermute | solution.py:41
  49.4 0.7 partials.1
  50.1 0.4 collective-permute-done.12.refs_4_.refs_2_
  50.5 1.2 %collective-permute-done.11.refs_3_.refs_1_ = f32[16,512]{1,0:T(8,128)S(1)} collective-permute-done((f32[16,512]{1,0:T(8,128)S(1)}, f32[16,512]{1,0:T(8,128)S(1)}, u32[]{:S(2)}, u32[]{:S(2)}) %collective-permute-start.11) | collective-permute-done | bytes 32800 | tf_op jit(solution)/shard_map/ppermute | solution.py:41
  51.7 3.0 %symmetric.1 = bf16[8,5,64,512]{3,2,1,0:T(8,128)(2,1)} custom-call(s32[4]{0:T(128)S(1)} %pad_add_fusion.where, f32[16,512]{1,0:T(8,128)S(1)} %merge.1.refs_0_, f32[16,512]{1,0:T(8,128)S(1)} %collective-permute-done.10.refs_1_, f32[16,512]{1,0:T(8,128)S(1)} %get-tuple-element.74.refs_2_.refs_0_, f32[16,512]{1,0:T(8,128)S(1)} %collective-permute-done.11.refs_3_.refs_1_, ...), custom_call_target="tpu_custom_call" | custom-call | flops 10000000 | bytes 9000000 | tf_op jit(solution)/shard_map/symmetric/pallas_call | solution.py:476
  54.7 4.7 %all-to-all-start = ((bf16[8,5,64,512]{3,2,1,0:T(8,128)(2,1)}), bf16[8,5,64,512]{3,2,1,0:T(8,128)(2,1)S(1)}, u32[]{:S(2)}, u32[]{:S(2)}) async-start(bf16[8,5,64,512]{3,2,1,0:T(8,128)(2,1)} %symmetric.1), calls=%async_computation | async-start | bytes 5242880 | tf_op jit(solution)/shard_map/all_to_all | solution.py:499
  59.4 0.3 collective-permute-start.14
  59.7 2.4 %collective-permute-start.15 = (bf16[640,128]{1,0:T(8,128)(2,1)S(1)}, bf16[640,128]{1,0:T(8,128)(2,1)S(1)}, u32[]{:S(2)}, u32[]{:S(2)}) collective-permute-start(bf16[640,128]{1,0:T(8,128)(2,1)S(1)} %get-tuple-element.86), channel_id=1, source_target_pairs={{0,4},{1,5},{2,6},{3,7},{4,0},{5,1},{6,2},{7,3},{8,12},{9,13},{10,... | collective-permute-start | bytes 491528 | tf_op jit(solution)/shard_map/ppermute | solution.py:41
  62.1 2.0 %collective-permute-start.16 = (bf16[640,128]{1,0:T(8,128)(2,1)S(1)}, bf16[640,128]{1,0:T(8,128)(2,1)S(1)}, u32[]{:S(2)}, u32[]{:S(2)}) collective-permute-start(bf16[640,128]{1,0:T(8,128)(2,1)S(1)} %get-tuple-element.87), channel_id=1, source_target_pairs={{0,6},{1,7},{2,0},{3,1},{4,2},{5,3},{6,4},{7,5},{8,14},{9,15},{10,... | collective-permute-start | bytes 491528 | tf_op jit(solution)/shard_map/ppermute | solution.py:41
  64.1 0.7 collective-permute-done.14.refs_5_
  64.8 2.9 %collective-permute-done.15.refs_6_ = bf16[640,128]{1,0:T(8,128)(2,1)S(1)} collective-permute-done((bf16[640,128]{1,0:T(8,128)(2,1)S(1)}, bf16[640,128]{1,0:T(8,128)(2,1)S(1)}, u32[]{:S(2)}, u32[]{:S(2)}) %collective-permute-start.15) | collective-permute-done | bytes 163872 | tf_op jit(solution)/shard_map/ppermute | solution.py:41
  67.7 0.9 collective-permute-done.16.refs_7_
  68.6 0.8 context.1
  69.4 6.0 %collective-permute-start.17 = (bf16[64,640]{1,0:T(8,128)(2,1)S(1)}, bf16[64,640]{1,0:T(8,128)(2,1)S(1)}, u32[]{:S(2)}, u32[]{:S(2)}) collective-permute-start(bf16[64,640]{1,0:T(8,128)(2,1)S(1)} %get-tuple-element.88), channel_id=1, source_target_pairs={{0,0},{1,1},{2,2},{3,3},{4,4},{5,5},{6,6},{7,7},{8,32},{9,33},{10,... | collective-permute-start | bytes 245768 | tf_op jit(solution)/shard_map/ppermute | solution.py:41
  75.4 2.5 %collective-permute-start.18 = (bf16[64,640]{1,0:T(8,128)(2,1)S(1)}, bf16[64,640]{1,0:T(8,128)(2,1)S(1)}, u32[]{:S(2)}, u32[]{:S(2)}) collective-permute-start(bf16[64,640]{1,0:T(8,128)(2,1)S(1)} %get-tuple-element.89), channel_id=1, source_target_pairs={{0,1},{1,0},{2,3},{3,2},{4,5},{5,4},{6,7},{7,6},{8,33},{9,32},{10,... | collective-permute-start | bytes 245768 | tf_op jit(solution)/shard_map/ppermute | solution.py:41
  77.9 18.1 %collective-permute-done.17.same = bf16[64,640]{1,0:T(8,128)(2,1)S(1)} collective-permute-done((bf16[64,640]{1,0:T(8,128)(2,1)S(1)}, bf16[64,640]{1,0:T(8,128)(2,1)S(1)}, u32[]{:S(2)}, u32[]{:S(2)}) %collective-permute-start.17) | collective-permute-done | bytes 81952 | tf_op jit(solution)/shard_map/ppermute | solution.py:41
  96.0 2.6 %collective-permute-done.18.other = bf16[64,640]{1,0:T(8,128)(2,1)S(1)} collective-permute-done((bf16[64,640]{1,0:T(8,128)(2,1)S(1)}, bf16[64,640]{1,0:T(8,128)(2,1)S(1)}, u32[]{:S(2)}, u32[]{:S(2)}) %collective-permute-start.18) | collective-permute-done | bytes 81952 | tf_op jit(solution)/shard_map/ppermute | solution.py:41
  98.6 0.6 copy-done.4
  99.2 10.6 %pair.1 = (bf16[64,64,512]{2,1,0:T(8,128)(2,1)}, bf16[64,1280]{1,0:T(8,128)(2,1)}) custom-call(s32[4]{0:T(128)S(1)} %pad_add_fusion.where, bf16[40,64,512]{2,1,0:T(8,128)(2,1)S(1)} %bitcast.7, bf16[1024,336]{1,0:T(8,128)(2,1)} %get-tuple-element.80.first, bf16[512,512]{1,0:T(8,128)(2,1)} %get-tuple-element.81.second, ...), custom_call_target="tpu_custom_call" | custom-call | flops 5000000000 | bytes 14000000 | tf_op jit(solution)/shard_map/pair/pallas_call | solution.py:516
  (25 shorter events, 0.1 us)
Async XLA Ops:
  0.6 12.6 %copy-start.2 = (f32[128]{0:T(128)S(1)}, f32[128]{0:T(128)}, u32[]{:S(2)}) copy-start(f32[128]{0:T(128)} %param.13) | copy-start | bytes 1540
  0.6 12.7 %copy-start = (bf16[40,128]{1,0:T(8,128)(2,1)S(1)}, bf16[40,128]{1,0:T(8,128)(2,1)}, u32[]{:S(2)}) copy-start(bf16[40,128]{1,0:T(8,128)(2,1)} %first.1) | copy-start | bytes 30724
  1.6 24.4 %copy-start.1 = (s32[4]{0:T(128)S(1)}, s32[4]{0:T(128)}, u32[]{:S(2)}) copy-start(s32[4]{0:T(128)} %lengths.1) | copy-start | bytes 52
  2.7 13.3 %collective-permute-start.1 = (bf16[64,1920]{1,0:T(8,128)(2,1)S(1)}, bf16[64,1920]{1,0:T(8,128)(2,1)S(1)}, u32[]{:S(2)}, u32[]{:S(2)}) collective-permute-start(bf16[64,1920]{1,0:T(8,128)(2,1)S(1)} %broadcast_select_fusion.1), channel_id=1, source_target_pairs={{0,1},{1,0},{2,3},{3,2},{4,5},{5,4},{6,7},{7,6},{8,33},{9,32},{10,... | collective-permute-start | bytes 737288 | tf_op jit(solution)/shard_map/ppermute | solution.py:41
  8.9 7.5 %collective-permute-start = (bf16[64,1920]{1,0:T(8,128)(2,1)S(1)}, bf16[64,1920]{1,0:T(8,128)(2,1)S(1)}, u32[]{:S(2)}, u32[]{:S(2)}) collective-permute-start(bf16[64,1920]{1,0:T(8,128)(2,1)S(1)} %broadcast_select_fusion), channel_id=1, source_target_pairs={{0,0},{1,1},{2,2},{3,3},{4,4},{5,5},{6,6},{7,7},{8,32},{9,33},{10,... | collective-permute-start | bytes 737288 | tf_op jit(solution)/shard_map/ppermute | solution.py:41
  16.5 16.6 %collective-permute-start.4 = (bf16[128,1920]{1,0:T(8,128)(2,1)S(1)}, bf16[128,1920]{1,0:T(8,128)(2,1)S(1)}, u32[]{:S(2)}, u32[]{:S(2)}) collective-permute-start(bf16[128,1920]{1,0:T(8,128)(2,1)S(1)} %maximum_select_fusion.refs_0_), channel_id=1, source_target_pairs={{0,64},{1,65},{2,66},{3,67},{4,68},{5,69},{6,70},{7,71},{8,72},{9,... | collective-permute-start | bytes 1474568 | tf_op jit(solution)/shard_map/ppermute | solution.py:41
  23.2 9.6 %collective-permute-start.3 = (bf16[128,1280]{1,0:T(8,128)(2,1)S(1)}, bf16[128,1280]{1,0:T(8,128)(2,1)S(1)}, u32[]{:S(2)}, u32[]{:S(2)}) collective-permute-start(bf16[128,1280]{1,0:T(8,128)(2,1)S(1)} %slice.39.refs_4_), channel_id=1, source_target_pairs={{0,2},{1,3},{2,4},{3,5},{4,6},{5,7},{6,0},{7,1},{8,10},{9,11},{10,... | collective-permute-start | bytes 983048 | tf_op jit(solution)/shard_map/ppermute | solution.py:41
  24.5 8.6 %collective-permute-start.2 = (bf16[128,1280]{1,0:T(8,128)(2,1)S(1)}, bf16[128,1280]{1,0:T(8,128)(2,1)S(1)}, u32[]{:S(2)}, u32[]{:S(2)}) collective-permute-start(bf16[128,1280]{1,0:T(8,128)(2,1)S(1)} %slice.39.refs_4_), channel_id=1, source_target_pairs={{0,6},{1,7},{2,0},{3,1},{4,2},{5,3},{6,4},{7,5},{8,14},{9,15},{10,... | collective-permute-start | bytes 983048 | tf_op jit(solution)/shard_map/ppermute | solution.py:41
  33.1 3.3 %collective-permute-start.5 = (bf16[128,1920]{1,0:T(8,128)(2,1)S(1)}, bf16[128,1920]{1,0:T(8,128)(2,1)S(1)}, u32[]{:S(2)}, u32[]{:S(2)}) collective-permute-start(bf16[128,1920]{1,0:T(8,128)(2,1)S(1)} %maximum_select_fusion.refs_0_), channel_id=1, source_target_pairs={{0,32},{1,33},{2,34},{3,35},{4,36},{5,37},{6,38},{7,39},{8,40},{9,... | collective-permute-start | bytes 1474568 | tf_op jit(solution)/shard_map/ppermute | solution.py:41
  33.1 3.3 %collective-permute-start.6 = (bf16[128,1920]{1,0:T(8,128)(2,1)S(1)}, bf16[128,1920]{1,0:T(8,128)(2,1)S(1)}, u32[]{:S(2)}, u32[]{:S(2)}) collective-permute-start(bf16[128,1920]{1,0:T(8,128)(2,1)S(1)} %collective-permute-done.4.refs_2_), channel_id=1, source_target_pairs={{0,32},{1,33},{2,34},{3,35},{4,36},{5,37},{6,38},{7,39},{8,40},{9,... | collective-permute-start | bytes 1474568 | tf_op jit(solution)/shard_map/ppermute | solution.py:41
  33.7 6.4 %collective-permute-start.8 = (bf16[64,1280]{1,0:T(8,128)(2,1)S(1)}, bf16[64,1280]{1,0:T(8,128)(2,1)S(1)}, u32[]{:S(2)}, u32[]{:S(2)}) collective-permute-start(bf16[64,1280]{1,0:T(8,128)(2,1)S(1)} %slice.41), channel_id=1, source_target_pairs={{0,6},{1,7},{2,0},{3,1},{4,2},{5,3},{6,4},{7,5},{8,14},{9,15},{10,... | collective-permute-start | bytes 491528 | tf_op jit(solution)/shard_map/ppermute | solution.py:41
  36.4 6.7 %collective-permute-start.7 = (bf16[64,1280]{1,0:T(8,128)(2,1)S(1)}, bf16[64,1280]{1,0:T(8,128)(2,1)S(1)}, u32[]{:S(2)}, u32[]{:S(2)}) collective-permute-start(bf16[64,1280]{1,0:T(8,128)(2,1)S(1)} %slice.40), channel_id=1, source_target_pairs={{0,2},{1,3},{2,4},{3,5},{4,6},{5,7},{6,0},{7,1},{8,10},{9,11},{10,... | collective-permute-start | bytes 491528 | tf_op jit(solution)/shard_map/ppermute | solution.py:41
  45.0 2.7 %collective-permute-start.9 = (f32[16,512]{1,0:T(8,128)S(1)}, f32[16,512]{1,0:T(8,128)S(1)}, u32[]{:S(2)}, u32[]{:S(2)}) collective-permute-start(f32[16,512]{1,0:T(8,128)S(1)} %get-tuple-element.73.one), channel_id=1, source_target_pairs={{0,32},{1,33},{2,34},{3,35},{4,36},{5,37},{6,38},{7,39},{8,40},{9,... | collective-permute-start | bytes 98312 | tf_op jit(solution)/shard_map/ppermute | solution.py:41
  46.2 3.9 %collective-permute-start.13 = (f32[16,512]{1,0:T(8,128)S(1)}, f32[16,512]{1,0:T(8,128)S(1)}, u32[]{:S(2)}, u32[]{:S(2)}) collective-permute-start(f32[16,512]{1,0:T(8,128)S(1)} %get-tuple-element.74.refs_2_.refs_0_), channel_id=1, source_target_pairs={{0,6},{1,7},{2,0},{3,1},{4,2},{5,3},{6,4},{7,5},{8,14},{9,15},{10,... | collective-permute-start | bytes 98312 | tf_op jit(solution)/shard_map/ppermute | solution.py:41
  46.2 4.3 %collective-permute-start.12 = (f32[16,512]{1,0:T(8,128)S(1)}, f32[16,512]{1,0:T(8,128)S(1)}, u32[]{:S(2)}, u32[]{:S(2)}) collective-permute-start(f32[16,512]{1,0:T(8,128)S(1)} %get-tuple-element.74.refs_2_.refs_0_), channel_id=1, source_target_pairs={{0,4},{1,5},{2,6},{3,7},{4,0},{5,1},{6,2},{7,3},{8,12},{9,13},{10,... | collective-permute-start | bytes 98312 | tf_op jit(solution)/shard_map/ppermute | solution.py:41
  46.8 4.9 %collective-permute-start.11 = (f32[16,512]{1,0:T(8,128)S(1)}, f32[16,512]{1,0:T(8,128)S(1)}, u32[]{:S(2)}, u32[]{:S(2)}) collective-permute-start(f32[16,512]{1,0:T(8,128)S(1)} %get-tuple-element.74.refs_2_.refs_0_), channel_id=1, source_target_pairs={{0,2},{1,3},{2,4},{3,5},{4,6},{5,7},{6,0},{7,1},{8,10},{9,11},{10,... | collective-permute-start | bytes 98312 | tf_op jit(solution)/shard_map/ppermute | solution.py:41
  47.7 3.9 %collective-permute-start.10 = (f32[16,512]{1,0:T(8,128)S(1)}, f32[16,512]{1,0:T(8,128)S(1)}, u32[]{:S(2)}, u32[]{:S(2)}) collective-permute-start(f32[16,512]{1,0:T(8,128)S(1)} %merge.1.refs_0_), channel_id=1, source_target_pairs={{0,64},{1,65},{2,66},{3,67},{4,68},{5,69},{6,70},{7,71},{8,72},{9,... | collective-permute-start | bytes 98312 | tf_op jit(solution)/shard_map/ppermute | solution.py:41
  54.7 43.9 %all-to-all-start = ((bf16[8,5,64,512]{3,2,1,0:T(8,128)(2,1)}), bf16[8,5,64,512]{3,2,1,0:T(8,128)(2,1)S(1)}, u32[]{:S(2)}, u32[]{:S(2)}) async-start(bf16[8,5,64,512]{3,2,1,0:T(8,128)(2,1)} %symmetric.1), calls=%async_computation | async-start | bytes 5242880 | tf_op jit(solution)/shard_map/all_to_all | solution.py:499
  59.4 5.4 %collective-permute-start.14 = (bf16[640,128]{1,0:T(8,128)(2,1)S(1)}, bf16[640,128]{1,0:T(8,128)(2,1)S(1)}, u32[]{:S(2)}, u32[]{:S(2)}) collective-permute-start(bf16[640,128]{1,0:T(8,128)(2,1)S(1)} %get-tuple-element.85), channel_id=1, source_target_pairs={{0,2},{1,3},{2,4},{3,5},{4,6},{5,7},{6,0},{7,1},{8,10},{9,11},{10,... | collective-permute-start | bytes 491528 | tf_op jit(solution)/shard_map/ppermute | solution.py:41
  59.7 8.0 %collective-permute-start.15 = (bf16[640,128]{1,0:T(8,128)(2,1)S(1)}, bf16[640,128]{1,0:T(8,128)(2,1)S(1)}, u32[]{:S(2)}, u32[]{:S(2)}) collective-permute-start(bf16[640,128]{1,0:T(8,128)(2,1)S(1)} %get-tuple-element.86), channel_id=1, source_target_pairs={{0,4},{1,5},{2,6},{3,7},{4,0},{5,1},{6,2},{7,3},{8,12},{9,13},{10,... | collective-permute-start | bytes 491528 | tf_op jit(solution)/shard_map/ppermute | solution.py:41
  62.1 6.5 %collective-permute-start.16 = (bf16[640,128]{1,0:T(8,128)(2,1)S(1)}, bf16[640,128]{1,0:T(8,128)(2,1)S(1)}, u32[]{:S(2)}, u32[]{:S(2)}) collective-permute-start(bf16[640,128]{1,0:T(8,128)(2,1)S(1)} %get-tuple-element.87), channel_id=1, source_target_pairs={{0,6},{1,7},{2,0},{3,1},{4,2},{5,3},{6,4},{7,5},{8,14},{9,15},{10,... | collective-permute-start | bytes 491528 | tf_op jit(solution)/shard_map/ppermute | solution.py:41
  69.4 26.6 %collective-permute-start.17 = (bf16[64,640]{1,0:T(8,128)(2,1)S(1)}, bf16[64,640]{1,0:T(8,128)(2,1)S(1)}, u32[]{:S(2)}, u32[]{:S(2)}) collective-permute-start(bf16[64,640]{1,0:T(8,128)(2,1)S(1)} %get-tuple-element.88), channel_id=1, source_target_pairs={{0,0},{1,1},{2,2},{3,3},{4,4},{5,5},{6,6},{7,7},{8,32},{9,33},{10,... | collective-permute-start | bytes 245768 | tf_op jit(solution)/shard_map/ppermute | solution.py:41
  75.4 23.2 %collective-permute-start.18 = (bf16[64,640]{1,0:T(8,128)(2,1)S(1)}, bf16[64,640]{1,0:T(8,128)(2,1)S(1)}, u32[]{:S(2)}, u32[]{:S(2)}) collective-permute-start(bf16[64,640]{1,0:T(8,128)(2,1)S(1)} %get-tuple-element.89), channel_id=1, source_target_pairs={{0,1},{1,0},{2,3},{3,2},{4,5},{5,4},{6,7},{7,6},{8,33},{9,32},{10,... | collective-permute-start | bytes 245768 | tf_op jit(solution)/shard_map/ppermute | solution.py:41
  96.0 2.6 %copy-start.3 = (bf16[64,640]{1,0:T(8,128)(2,1)}, bf16[64,640]{1,0:T(8,128)(2,1)S(1)}, u32[]{:S(2)}) copy-start(bf16[64,640]{1,0:T(8,128)(2,1)S(1)} %collective-permute-done.17.same) | copy-start | bytes 245764
  98.6 0.6 copy-start.4

commit v7 on v6

--- a/solution.py
+++ b/solution.py
@@ -277,14 +277,7 @@
     out[...] = jnp.concatenate(halves, axis=1).astype(jnp.bfloat16)
 
 
-def pair_kernel(where, tiles, first, second, second_bias, relative, same, other, out, context):
-    z = where[2]
-
-    @pl.when(pl.program_id(0) == 0)
-    def _():
-        context[:, pl.ds(pl.multiple_of(z * WIDE, WIDE), WIDE)] = same[...]
-        context[:, pl.ds(pl.multiple_of((1 - z) * WIDE, WIDE), WIDE)] = other[...]
-
+def pair_kernel(tiles, first, second, second_bias, relative, out):
     start = pl.multiple_of(pl.program_id(0) * ROWS, ROWS)
     loaded = tiles[:, pl.ds(start, ROWS), :].astype(jnp.float32)
     outs, hid = second.shape[0] // 8, first.shape[0] // 8
@@ -513,31 +506,27 @@
     same = send(same, lambda y, x, z, c: (c, x, z, y))
     other = send(other, lambda y, x, z, c: (c, x, 1 - z, y))
 
-    pair, context = pl.pallas_call(
+    pair = pl.pallas_call(
         pair_kernel,
         grid=(HALF // ROWS,),
         in_specs=[
-            SMEM,
             VMEM,
             pl.BlockSpec((hid * 8, 8 * GROUP * 8 + ONES), lambda i: (0, 0)),
             pl.BlockSpec((outs * 8, hid * 4), lambda i: (0, 0)),
             pl.BlockSpec((outs * 8, 128), lambda i: (0, 0)),
             pl.BlockSpec((outs, ROWS, TILE), lambda i: (0, i, 0)),
-            pl.BlockSpec((HALF, WIDE), lambda i: (0, 0)),
-            pl.BlockSpec((HALF, WIDE), lambda i: (0, 0)),
         ],
-        out_specs=[
-            pl.BlockSpec((outs, ROWS, TILE), lambda i: (0, i, 0)),
-            pl.BlockSpec((HALF, 2 * WIDE), lambda i: (0, 0)),
-        ],
-        out_shape=[shape((outs, HALF, TILE)), shape((HALF, 2 * WIDE))],
+        out_specs=pl.BlockSpec((outs, ROWS, TILE), lambda i: (0, i, 0)),
+        out_shape=shape((outs, HALF, TILE)),
         compiler_params=params(14),
         cost_estimate=cost(5e9, 14e6),
         name="pair",
-    )(
-        where,
-        received,
-        *(in_hbm(a) for a in (first, second, second_bias, relative, same, other)),
+    )(received, *(in_hbm(a) for a in (first, second, second_bias, relative)))
+    same, other, pair = lax.optimization_barrier((same, other, pair))
+    context = jnp.where(
+        z == 0,
+        jnp.concatenate([same, other], axis=1),
+        jnp.concatenate([other, same], axis=1),
     )
     return (context, pair)
 

time: 110 us -> 109 us (level)
  waiting for transfers between devices: 32.6 us -> 30.7 us
    ppermute x19, waiting for transfers between devices: 32.6 us -> 11.9 us  [send(): return lax.ppermute(value, AXES, moves(to))]
    all_to_all x1, waiting for transfers between devices: 0.01 us -> 18.8 us  [local(): lax.all_to_all(tiles, 'band', split_axis=0, concat_axis=0, axis_index_gro...]
    unnamed x12 -> x8, local copies, waits for them, and re-layouts: 2.3 us -> 1.67 us
  transfers between devices with their start and end apart: 20 -> 20, of which waited for: 12 -> 11; matrix products, arithmetic and copies ran while one was open for 2% -> 3% of each run, Pallas kernels for 11% -> 21%
where the time goes in v7:
time: 109 us; the launch traced here: 108 us
  starting transfers between devices  43 us (39%)
  waiting for transfers between devices  30.7 us (28%)
  Pallas kernels  27.7 us (25%)
  local copies, waits for them, and re-layouts  4.57 us (4%)
    ppermute x19, starting transfers between devices, send(): return lax.ppermute(value, AXES, moves(to))  38.3 us
    all_to_all x1, waiting for transfers between devices, local(): lax.all_to_all(tiles, 'band', split_axis=0, concat_axis=0, axis_index_gro...  18.8 us
    ppermute x19, waiting for transfers between devices, send(): return lax.ppermute(value, AXES, moves(to))  11.9 us
    pallas_call x1, Pallas kernels, local(): pl.pallas_call(pair_kernel, grid=(HALF // ROWS,), in_specs=[VMEM, pl.Bloc...  10.4 us
    pallas_call x1, Pallas kernels, local(): pl.pallas_call(relative_kernel, grid=(HALF // ROWS,), in_specs=[SMEM, SME...  5.66 us
    all_to_all x1, starting transfers between devices, local(): lax.all_to_all(tiles, 'band', split_axis=0, concat_axis=0, axis_index_gro...  4.73 us
    pallas_call x1, Pallas kernels, local(): pl.pallas_call(symmetric_kernel, in_specs=[SMEM] + [VMEM] * 12, out_specs...  3 us
    pallas_call x1, Pallas kernels, local(): pl.pallas_call(spread_kernel, in_specs=[VMEM] * 5, out_specs=[VMEM] * 4,...  2.7 us
  transfers between devices with their start and end apart: 20, of which 11 were waited for; matrix products, arithmetic and copies ran while one was open for 3% of the time, Pallas kernels for 21%

profile of v7, /device:TPU:1, one launch (start us, length us, event | category | flops | bytes accessed | tf_op | source)
XLA Modules:
  0.0 107.8 jit_solution(11690705565234584152)
XLA Ops:
  0.7 0.9 fusion.2
  1.6 1.0 fusion
  2.7 0.1 broadcast_select_fusion.1
  2.7 6.1 %collective-permute-start.1 = (bf16[64,1920]{1,0:T(8,128)(2,1)S(1)}, bf16[64,1920]{1,0:T(8,128)(2,1)S(1)}, u32[]{:S(2)}, u32[]{:S(2)}) collective-permute-start(bf16[64,1920]{1,0:T(8,128)(2,1)S(1)} %broadcast_select_fusion.1), channel_id=1, source_target_pairs={{0,1},{1,0},{2,3},{3,2},{4,5},{5,4},{6,7},{7,6},{8,33},{9,32},{10,... | collective-permute-start | bytes 737288 | tf_op jit(solution)/shard_map/ppermute | solution.py:41
  8.8 0.1 broadcast_select_fusion
  8.9 1.9 %collective-permute-start = (bf16[64,1920]{1,0:T(8,128)(2,1)S(1)}, bf16[64,1920]{1,0:T(8,128)(2,1)S(1)}, u32[]{:S(2)}, u32[]{:S(2)}) collective-permute-start(bf16[64,1920]{1,0:T(8,128)(2,1)S(1)} %broadcast_select_fusion), channel_id=1, source_target_pairs={{0,0},{1,1},{2,2},{3,3},{4,4},{5,5},{6,6},{7,7},{8,32},{9,33},{10,... | collective-permute-start | bytes 737288 | tf_op jit(solution)/shard_map/ppermute | solution.py:41
  10.8 0.8 copy.11
  11.6 0.8 copy.13.second
  12.5 0.8 copy.14.second_bias
  13.2 0.1 copy.12.first_bias
  13.4 2.7 %spread.1 = (bf16[1024,336]{1,0:T(8,128)(2,1)}, bf16[512,512]{1,0:T(8,128)(2,1)}, f32[512,128]{1,0:T(8,128)}, bf16[512,576]{1,0:T(8,128)(2,1)S(1)}) custom-call(bf16[40,128]{1,0:T(8,128)(2,1)S(1)} %copy-done, f32[128,1]{1,0:T(8,128)S(1)} %copy.12.first_bias, bf16[128,64]{1,0:T(8,128)(2,1)S(1)} %copy.13.second, f32[64,1]{1,0:T(8,128)S(1)} %copy.14.second_bias, ...), custom_call_target="tpu_custom_call" | custom-call | flops 400000000 | bytes 6000000 | tf_op jit(solution)/shard_map/spread/pallas_call | solution.py:345
  16.1 0.3 collective-permute-done
  16.4 0.1 maximum_select_fusion.refs_0_
  16.5 6.7 %collective-permute-start.4 = (bf16[128,1920]{1,0:T(8,128)(2,1)S(1)}, bf16[128,1920]{1,0:T(8,128)(2,1)S(1)}, u32[]{:S(2)}, u32[]{:S(2)}) collective-permute-start(bf16[128,1920]{1,0:T(8,128)(2,1)S(1)} %maximum_select_fusion.refs_0_), channel_id=1, source_target_pairs={{0,64},{1,65},{2,66},{3,67},{4,68},{5,69},{6,70},{7,71},{8,72},{9,... | collective-permute-start | bytes 1474568 | tf_op jit(solution)/shard_map/ppermute | solution.py:41
  23.2 1.3 %collective-permute-start.3 = (bf16[128,1280]{1,0:T(8,128)(2,1)S(1)}, bf16[128,1280]{1,0:T(8,128)(2,1)S(1)}, u32[]{:S(2)}, u32[]{:S(2)}) collective-permute-start(bf16[128,1280]{1,0:T(8,128)(2,1)S(1)} %slice.39.refs_4_), channel_id=1, source_target_pairs={{0,2},{1,3},{2,4},{3,5},{4,6},{5,7},{6,0},{7,1},{8,10},{9,11},{10,... | collective-permute-start | bytes 983048 | tf_op jit(solution)/shard_map/ppermute | solution.py:41
  24.5 1.5 %collective-permute-start.2 = (bf16[128,1280]{1,0:T(8,128)(2,1)S(1)}, bf16[128,1280]{1,0:T(8,128)(2,1)S(1)}, u32[]{:S(2)}, u32[]{:S(2)}) collective-permute-start(bf16[128,1280]{1,0:T(8,128)(2,1)S(1)} %slice.39.refs_4_), channel_id=1, source_target_pairs={{0,6},{1,7},{2,0},{3,1},{4,2},{5,3},{6,4},{7,5},{8,14},{9,15},{10,... | collective-permute-start | bytes 983048 | tf_op jit(solution)/shard_map/ppermute | solution.py:41
  26.0 0.1 pad_add_fusion.where
  26.1 5.7 %relative.1 = bf16[64,64,512]{2,1,0:T(8,128)(2,1)} custom-call(s32[4]{0:T(128)S(1)} %pad_add_fusion.where, s32[4]{0:T(128)S(1)} %copy-done.1, bf16[512,576]{1,0:T(8,128)(2,1)S(1)} %get-tuple-element.54.table), custom_call_target="tpu_custom_call" | custom-call | flops 2400000000 | bytes 6000000 | tf_op jit(solution)/shard_map/relative/pallas_call | solution.py:391
  31.7 1.1 %collective-permute-done.3.refs_5_ = bf16[128,1280]{1,0:T(8,128)(2,1)S(1)} collective-permute-done((bf16[128,1280]{1,0:T(8,128)(2,1)S(1)}, bf16[128,1280]{1,0:T(8,128)(2,1)S(1)}, u32[]{:S(2)}, u32[]{:S(2)}) %collective-permute-start.3) | collective-permute-done | bytes 327712 | tf_op jit(solution)/shard_map/ppermute | solution.py:41
  32.8 0.3 collective-permute-done.2.refs_6_
  33.1 0.5 collective-permute-start.6
  33.7 2.7 %collective-permute-start.8 = (bf16[64,1280]{1,0:T(8,128)(2,1)S(1)}, bf16[64,1280]{1,0:T(8,128)(2,1)S(1)}, u32[]{:S(2)}, u32[]{:S(2)}) collective-permute-start(bf16[64,1280]{1,0:T(8,128)(2,1)S(1)} %slice.41), channel_id=1, source_target_pairs={{0,6},{1,7},{2,0},{3,1},{4,2},{5,3},{6,4},{7,5},{8,14},{9,15},{10,... | collective-permute-start | bytes 491528 | tf_op jit(solution)/shard_map/ppermute | solution.py:41
  36.4 2.5 %near.1 = (f32[16,512]{1,0:T(8,128)S(1)}, f32[16,384]{1,0:T(8,128)S(1)}, bf16[5,512,384]{2,1,0:T(8,128)(2,1)S(1)}, bf16[5,512,384]{2,1,0:T(8,128)(2,1)S(1)}) custom-call(bf16[128,1920]{1,0:T(8,128)(2,1)S(1)} %maximum_select_fusion.refs_0_, bf16[128,1920]{1,0:T(8,128)(2,1)S(1)} %collective-permute-done.5.refs_1_, ...), custom_call_target="tpu_custom_call" | custom-call | flops 600000000 | bytes 11000000 | tf_op jit(solution)/shard_map/near/pallas_call | solution.py:419
  38.9 1.1 %collective-permute-done.8.refs_5_ = bf16[64,1280]{1,0:T(8,128)(2,1)S(1)} collective-permute-done((bf16[64,1280]{1,0:T(8,128)(2,1)S(1)}, bf16[64,1280]{1,0:T(8,128)(2,1)S(1)}, u32[]{:S(2)}, u32[]{:S(2)}) %collective-permute-start.8) | collective-permute-done | bytes 163872 | tf_op jit(solution)/shard_map/ppermute | solution.py:41
  40.0 3.1 %collective-permute-done.7.refs_4_ = bf16[64,1280]{1,0:T(8,128)(2,1)S(1)} collective-permute-done((bf16[64,1280]{1,0:T(8,128)(2,1)S(1)}, bf16[64,1280]{1,0:T(8,128)(2,1)S(1)}, u32[]{:S(2)}, u32[]{:S(2)}) %collective-permute-start.7) | collective-permute-done | bytes 163872 | tf_op jit(solution)/shard_map/ppermute | solution.py:41
  43.1 1.9 %far.1 = (f32[16,512]{1,0:T(8,128)S(1)}, f32[8,512]{1,0:T(8,128)S(1)}, f32[16,512]{1,0:T(8,128)S(1)}, bf16[5,512,128]{2,1,0:T(8,128)(2,1)S(1)}, bf16[5,512,128]{2,1,0:T(8,128)(2,1)S(1)}) custom-call(s32[4]{0:T(128)S(1)} %pad_add_fusion.where, bf16[128,1920]{1,0:T(8,128)(2,1)S(1)} %maximum_select_fusion.refs_0_, ...), custom_call_target="tpu_custom_call" | custom-call | flops 300000000 | bytes 5000000 | tf_op jit(solution)/shard_map/far/pallas_call | solution.py:435
  45.0 1.2 %collective-permute-start.9 = (f32[16,512]{1,0:T(8,128)S(1)}, f32[16,512]{1,0:T(8,128)S(1)}, u32[]{:S(2)}, u32[]{:S(2)}) collective-permute-start(f32[16,512]{1,0:T(8,128)S(1)} %get-tuple-element.74.one), channel_id=1, source_target_pairs={{0,32},{1,33},{2,34},{3,35},{4,36},{5,37},{6,38},{7,39},{8,40},{9,... | collective-permute-start | bytes 98312 | tf_op jit(solution)/shard_map/ppermute | solution.py:41
  46.2 0.0 collective-permute-start.13
  46.2 0.6 collective-permute-start.12
  46.8 0.9 collective-permute-start.11
  47.7 1.7 %collective-permute-start.10 = (f32[16,512]{1,0:T(8,128)S(1)}, f32[16,512]{1,0:T(8,128)S(1)}, u32[]{:S(2)}, u32[]{:S(2)}) collective-permute-start(f32[16,512]{1,0:T(8,128)S(1)} %merge.1.refs_0_), channel_id=1, source_target_pairs={{0,64},{1,65},{2,66},{3,67},{4,68},{5,69},{6,70},{7,71},{8,72},{9,... | collective-permute-start | bytes 98312 | tf_op jit(solution)/shard_map/ppermute | solution.py:41
  49.4 0.7 partials.1
  50.1 0.4 collective-permute-done.12.refs_4_.refs_2_
  50.5 1.2 %collective-permute-done.11.refs_3_.refs_1_ = f32[16,512]{1,0:T(8,128)S(1)} collective-permute-done((f32[16,512]{1,0:T(8,128)S(1)}, f32[16,512]{1,0:T(8,128)S(1)}, u32[]{:S(2)}, u32[]{:S(2)}) %collective-permute-start.11) | collective-permute-done | bytes 32800 | tf_op jit(solution)/shard_map/ppermute | solution.py:41
  51.7 3.0 %symmetric.1 = bf16[8,5,64,512]{3,2,1,0:T(8,128)(2,1)} custom-call(s32[4]{0:T(128)S(1)} %pad_add_fusion.where, f32[16,512]{1,0:T(8,128)S(1)} %merge.1.refs_0_, f32[16,512]{1,0:T(8,128)S(1)} %collective-permute-done.10.refs_1_, f32[16,512]{1,0:T(8,128)S(1)} %get-tuple-element.75.refs_2_.refs_0_, f32[16,512]{1,0:T(8,128)S(1)} %collective-permute-done.11.refs_3_.refs_1_, ...), custom_call_target="tpu_custom_call" | custom-call | flops 10000000 | bytes 9000000 | tf_op jit(solution)/shard_map/symmetric/pallas_call | solution.py:469
  54.7 4.7 %all-to-all-start = ((bf16[8,5,64,512]{3,2,1,0:T(8,128)(2,1)}), bf16[8,5,64,512]{3,2,1,0:T(8,128)(2,1)S(1)}, u32[]{:S(2)}, u32[]{:S(2)}) async-start(bf16[8,5,64,512]{3,2,1,0:T(8,128)(2,1)} %symmetric.1), calls=%async_computation | async-start | bytes 5242880 | tf_op jit(solution)/shard_map/all_to_all | solution.py:492
  59.4 0.3 collective-permute-start.14
  59.7 2.4 %collective-permute-start.15 = (bf16[640,128]{1,0:T(8,128)(2,1)S(1)}, bf16[640,128]{1,0:T(8,128)(2,1)S(1)}, u32[]{:S(2)}, u32[]{:S(2)}) collective-permute-start(bf16[640,128]{1,0:T(8,128)(2,1)S(1)} %get-tuple-element.82), channel_id=1, source_target_pairs={{0,4},{1,5},{2,6},{3,7},{4,0},{5,1},{6,2},{7,3},{8,12},{9,13},{10,... | collective-permute-start | bytes 491528 | tf_op jit(solution)/shard_map/ppermute | solution.py:41
  62.1 2.0 %collective-permute-start.16 = (bf16[640,128]{1,0:T(8,128)(2,1)S(1)}, bf16[640,128]{1,0:T(8,128)(2,1)S(1)}, u32[]{:S(2)}, u32[]{:S(2)}) collective-permute-start(bf16[640,128]{1,0:T(8,128)(2,1)S(1)} %get-tuple-element.83), channel_id=1, source_target_pairs={{0,6},{1,7},{2,0},{3,1},{4,2},{5,3},{6,4},{7,5},{8,14},{9,15},{10,... | collective-permute-start | bytes 491528 | tf_op jit(solution)/shard_map/ppermute | solution.py:41
  64.1 0.7 collective-permute-done.14.refs_5_
  64.8 2.9 %collective-permute-done.15.refs_6_ = bf16[640,128]{1,0:T(8,128)(2,1)S(1)} collective-permute-done((bf16[640,128]{1,0:T(8,128)(2,1)S(1)}, bf16[640,128]{1,0:T(8,128)(2,1)S(1)}, u32[]{:S(2)}, u32[]{:S(2)}) %collective-permute-start.15) | collective-permute-done | bytes 163872 | tf_op jit(solution)/shard_map/ppermute | solution.py:41
  67.7 0.9 collective-permute-done.16.refs_7_
  68.6 0.8 context.1
  69.4 6.0 %collective-permute-start.17 = (bf16[64,640]{1,0:T(8,128)(2,1)S(1)}, bf16[64,640]{1,0:T(8,128)(2,1)S(1)}, u32[]{:S(2)}, u32[]{:S(2)}) collective-permute-start(bf16[64,640]{1,0:T(8,128)(2,1)S(1)} %get-tuple-element.84), channel_id=1, source_target_pairs={{0,0},{1,1},{2,2},{3,3},{4,4},{5,5},{6,6},{7,7},{8,32},{9,33},{10,... | collective-permute-start | bytes 245768 | tf_op jit(solution)/shard_map/ppermute | solution.py:41
  75.4 2.5 %collective-permute-start.18 = (bf16[64,640]{1,0:T(8,128)(2,1)S(1)}, bf16[64,640]{1,0:T(8,128)(2,1)S(1)}, u32[]{:S(2)}, u32[]{:S(2)}) collective-permute-start(bf16[64,640]{1,0:T(8,128)(2,1)S(1)} %get-tuple-element.85), channel_id=1, source_target_pairs={{0,1},{1,0},{2,3},{3,2},{4,5},{5,4},{6,7},{7,6},{8,33},{9,32},{10,... | collective-permute-start | bytes 245768 | tf_op jit(solution)/shard_map/ppermute | solution.py:41
  77.9 18.8 %all-to-all-done = bf16[8,5,64,512]{3,2,1,0:T(8,128)(2,1)S(1)} async-done(((bf16[8,5,64,512]{3,2,1,0:T(8,128)(2,1)}), bf16[8,5,64,512]{3,2,1,0:T(8,128)(2,1)S(1)}, u32[]{:S(2)}, u32[]{:S(2)}) %all-to-all-start) | async-done | bytes 2621472 | tf_op jit(solution)/shard_map/all_to_all | solution.py:492
  96.7 10.4 %pair.1 = bf16[64,64,512]{2,1,0:T(8,128)(2,1)} custom-call(bf16[40,64,512]{2,1,0:T(8,128)(2,1)S(1)} %bitcast.7, bf16[1024,336]{1,0:T(8,128)(2,1)} %get-tuple-element.87.first, bf16[512,512]{1,0:T(8,128)(2,1)} %get-tuple-element.88.second, f32[512,128]{1,0:T(8,128)} %get-tuple-element.89.second_bias, bf16[64,64,512]{2,1,0:T(8,128)(2,1)} %relative.1), custom_call_target="tpu_custom_call" | custom-call | flops 5000000000 | bytes 14000000 | tf_op jit(solution)/shard_map/pair/pallas_call | solution.py:509
  107.1 0.7 maximum_select_fusion.1
  (22 shorter events, 0.1 us)
Async XLA Ops:
  0.6 12.6 %copy-start.2 = (f32[128]{0:T(128)S(1)}, f32[128]{0:T(128)}, u32[]{:S(2)}) copy-start(f32[128]{0:T(128)} %param.13) | copy-start | bytes 1540
  0.6 12.7 %copy-start = (bf16[40,128]{1,0:T(8,128)(2,1)S(1)}, bf16[40,128]{1,0:T(8,128)(2,1)}, u32[]{:S(2)}) copy-start(bf16[40,128]{1,0:T(8,128)(2,1)} %first.1) | copy-start | bytes 30724
  1.6 24.4 %copy-start.1 = (s32[4]{0:T(128)S(1)}, s32[4]{0:T(128)}, u32[]{:S(2)}) copy-start(s32[4]{0:T(128)} %lengths.1) | copy-start | bytes 52
  2.7 13.3 %collective-permute-start.1 = (bf16[64,1920]{1,0:T(8,128)(2,1)S(1)}, bf16[64,1920]{1,0:T(8,128)(2,1)S(1)}, u32[]{:S(2)}, u32[]{:S(2)}) collective-permute-start(bf16[64,1920]{1,0:T(8,128)(2,1)S(1)} %broadcast_select_fusion.1), channel_id=1, source_target_pairs={{0,1},{1,0},{2,3},{3,2},{4,5},{5,4},{6,7},{7,6},{8,33},{9,32},{10,... | collective-permute-start | bytes 737288 | tf_op jit(solution)/shard_map/ppermute | solution.py:41
  8.9 7.5 %collective-permute-start = (bf16[64,1920]{1,0:T(8,128)(2,1)S(1)}, bf16[64,1920]{1,0:T(8,128)(2,1)S(1)}, u32[]{:S(2)}, u32[]{:S(2)}) collective-permute-start(bf16[64,1920]{1,0:T(8,128)(2,1)S(1)} %broadcast_select_fusion), channel_id=1, source_target_pairs={{0,0},{1,1},{2,2},{3,3},{4,4},{5,5},{6,6},{7,7},{8,32},{9,33},{10,... | collective-permute-start | bytes 737288 | tf_op jit(solution)/shard_map/ppermute | solution.py:41
  16.5 16.6 %collective-permute-start.4 = (bf16[128,1920]{1,0:T(8,128)(2,1)S(1)}, bf16[128,1920]{1,0:T(8,128)(2,1)S(1)}, u32[]{:S(2)}, u32[]{:S(2)}) collective-permute-start(bf16[128,1920]{1,0:T(8,128)(2,1)S(1)} %maximum_select_fusion.refs_0_), channel_id=1, source_target_pairs={{0,64},{1,65},{2,66},{3,67},{4,68},{5,69},{6,70},{7,71},{8,72},{9,... | collective-permute-start | bytes 1474568 | tf_op jit(solution)/shard_map/ppermute | solution.py:41
  23.2 9.6 %collective-permute-start.3 = (bf16[128,1280]{1,0:T(8,128)(2,1)S(1)}, bf16[128,1280]{1,0:T(8,128)(2,1)S(1)}, u32[]{:S(2)}, u32[]{:S(2)}) collective-permute-start(bf16[128,1280]{1,0:T(8,128)(2,1)S(1)} %slice.39.refs_4_), channel_id=1, source_target_pairs={{0,2},{1,3},{2,4},{3,5},{4,6},{5,7},{6,0},{7,1},{8,10},{9,11},{10,... | collective-permute-start | bytes 983048 | tf_op jit(solution)/shard_map/ppermute | solution.py:41
  24.5 8.6 %collective-permute-start.2 = (bf16[128,1280]{1,0:T(8,128)(2,1)S(1)}, bf16[128,1280]{1,0:T(8,128)(2,1)S(1)}, u32[]{:S(2)}, u32[]{:S(2)}) collective-permute-start(bf16[128,1280]{1,0:T(8,128)(2,1)S(1)} %slice.39.refs_4_), channel_id=1, source_target_pairs={{0,6},{1,7},{2,0},{3,1},{4,2},{5,3},{6,4},{7,5},{8,14},{9,15},{10,... | collective-permute-start | bytes 983048 | tf_op jit(solution)/shard_map/ppermute | solution.py:41
  33.1 3.3 %collective-permute-start.5 = (bf16[128,1920]{1,0:T(8,128)(2,1)S(1)}, bf16[128,1920]{1,0:T(8,128)(2,1)S(1)}, u32[]{:S(2)}, u32[]{:S(2)}) collective-permute-start(bf16[128,1920]{1,0:T(8,128)(2,1)S(1)} %maximum_select_fusion.refs_0_), channel_id=1, source_target_pairs={{0,32},{1,33},{2,34},{3,35},{4,36},{5,37},{6,38},{7,39},{8,40},{9,... | collective-permute-start | bytes 1474568 | tf_op jit(solution)/shard_map/ppermute | solution.py:41
  33.1 3.3 %collective-permute-start.6 = (bf16[128,1920]{1,0:T(8,128)(2,1)S(1)}, bf16[128,1920]{1,0:T(8,128)(2,1)S(1)}, u32[]{:S(2)}, u32[]{:S(2)}) collective-permute-start(bf16[128,1920]{1,0:T(8,128)(2,1)S(1)} %collective-permute-done.4.refs_2_), channel_id=1, source_target_pairs={{0,32},{1,33},{2,34},{3,35},{4,36},{5,37},{6,38},{7,39},{8,40},{9,... | collective-permute-start | bytes 1474568 | tf_op jit(solution)/shard_map/ppermute | solution.py:41
  33.7 6.4 %collective-permute-start.8 = (bf16[64,1280]{1,0:T(8,128)(2,1)S(1)}, bf16[64,1280]{1,0:T(8,128)(2,1)S(1)}, u32[]{:S(2)}, u32[]{:S(2)}) collective-permute-start(bf16[64,1280]{1,0:T(8,128)(2,1)S(1)} %slice.41), channel_id=1, source_target_pairs={{0,6},{1,7},{2,0},{3,1},{4,2},{5,3},{6,4},{7,5},{8,14},{9,15},{10,... | collective-permute-start | bytes 491528 | tf_op jit(solution)/shard_map/ppermute | solution.py:41
  36.4 6.7 %collective-permute-start.7 = (bf16[64,1280]{1,0:T(8,128)(2,1)S(1)}, bf16[64,1280]{1,0:T(8,128)(2,1)S(1)}, u32[]{:S(2)}, u32[]{:S(2)}) collective-permute-start(bf16[64,1280]{1,0:T(8,128)(2,1)S(1)} %slice.40), channel_id=1, source_target_pairs={{0,2},{1,3},{2,4},{3,5},{4,6},{5,7},{6,0},{7,1},{8,10},{9,11},{10,... | collective-permute-start | bytes 491528 | tf_op jit(solution)/shard_map/ppermute | solution.py:41
  45.0 2.7 %collective-permute-start.9 = (f32[16,512]{1,0:T(8,128)S(1)}, f32[16,512]{1,0:T(8,128)S(1)}, u32[]{:S(2)}, u32[]{:S(2)}) collective-permute-start(f32[16,512]{1,0:T(8,128)S(1)} %get-tuple-element.74.one), channel_id=1, source_target_pairs={{0,32},{1,33},{2,34},{3,35},{4,36},{5,37},{6,38},{7,39},{8,40},{9,... | collective-permute-start | bytes 98312 | tf_op jit(solution)/shard_map/ppermute | solution.py:41
  46.2 3.9 %collective-permute-start.13 = (f32[16,512]{1,0:T(8,128)S(1)}, f32[16,512]{1,0:T(8,128)S(1)}, u32[]{:S(2)}, u32[]{:S(2)}) collective-permute-start(f32[16,512]{1,0:T(8,128)S(1)} %get-tuple-element.75.refs_2_.refs_0_), channel_id=1, source_target_pairs={{0,6},{1,7},{2,0},{3,1},{4,2},{5,3},{6,4},{7,5},{8,14},{9,15},{10,... | collective-permute-start | bytes 98312 | tf_op jit(solution)/shard_map/ppermute | solution.py:41
  46.2 4.3 %collective-permute-start.12 = (f32[16,512]{1,0:T(8,128)S(1)}, f32[16,512]{1,0:T(8,128)S(1)}, u32[]{:S(2)}, u32[]{:S(2)}) collective-permute-start(f32[16,512]{1,0:T(8,128)S(1)} %get-tuple-element.75.refs_2_.refs_0_), channel_id=1, source_target_pairs={{0,4},{1,5},{2,6},{3,7},{4,0},{5,1},{6,2},{7,3},{8,12},{9,13},{10,... | collective-permute-start | bytes 98312 | tf_op jit(solution)/shard_map/ppermute | solution.py:41
  46.8 4.9 %collective-permute-start.11 = (f32[16,512]{1,0:T(8,128)S(1)}, f32[16,512]{1,0:T(8,128)S(1)}, u32[]{:S(2)}, u32[]{:S(2)}) collective-permute-start(f32[16,512]{1,0:T(8,128)S(1)} %get-tuple-element.75.refs_2_.refs_0_), channel_id=1, source_target_pairs={{0,2},{1,3},{2,4},{3,5},{4,6},{5,7},{6,0},{7,1},{8,10},{9,11},{10,... | collective-permute-start | bytes 98312 | tf_op jit(solution)/shard_map/ppermute | solution.py:41
  47.7 3.9 %collective-permute-start.10 = (f32[16,512]{1,0:T(8,128)S(1)}, f32[16,512]{1,0:T(8,128)S(1)}, u32[]{:S(2)}, u32[]{:S(2)}) collective-permute-start(f32[16,512]{1,0:T(8,128)S(1)} %merge.1.refs_0_), channel_id=1, source_target_pairs={{0,64},{1,65},{2,66},{3,67},{4,68},{5,69},{6,70},{7,71},{8,72},{9,... | collective-permute-start | bytes 98312 | tf_op jit(solution)/shard_map/ppermute | solution.py:41
  54.7 42.0 %all-to-all-start = ((bf16[8,5,64,512]{3,2,1,0:T(8,128)(2,1)}), bf16[8,5,64,512]{3,2,1,0:T(8,128)(2,1)S(1)}, u32[]{:S(2)}, u32[]{:S(2)}) async-start(bf16[8,5,64,512]{3,2,1,0:T(8,128)(2,1)} %symmetric.1), calls=%async_computation | async-start | bytes 5242880 | tf_op jit(solution)/shard_map/all_to_all | solution.py:492
  59.4 5.4 %collective-permute-start.14 = (bf16[640,128]{1,0:T(8,128)(2,1)S(1)}, bf16[640,128]{1,0:T(8,128)(2,1)S(1)}, u32[]{:S(2)}, u32[]{:S(2)}) collective-permute-start(bf16[640,128]{1,0:T(8,128)(2,1)S(1)} %get-tuple-element.81), channel_id=1, source_target_pairs={{0,2},{1,3},{2,4},{3,5},{4,6},{5,7},{6,0},{7,1},{8,10},{9,11},{10,... | collective-permute-start | bytes 491528 | tf_op jit(solution)/shard_map/ppermute | solution.py:41
  59.7 8.0 %collective-permute-start.15 = (bf16[640,128]{1,0:T(8,128)(2,1)S(1)}, bf16[640,128]{1,0:T(8,128)(2,1)S(1)}, u32[]{:S(2)}, u32[]{:S(2)}) collective-permute-start(bf16[640,128]{1,0:T(8,128)(2,1)S(1)} %get-tuple-element.82), channel_id=1, source_target_pairs={{0,4},{1,5},{2,6},{3,7},{4,0},{5,1},{6,2},{7,3},{8,12},{9,13},{10,... | collective-permute-start | bytes 491528 | tf_op jit(solution)/shard_map/ppermute | solution.py:41
  62.1 6.5 %collective-permute-start.16 = (bf16[640,128]{1,0:T(8,128)(2,1)S(1)}, bf16[640,128]{1,0:T(8,128)(2,1)S(1)}, u32[]{:S(2)}, u32[]{:S(2)}) collective-permute-start(bf16[640,128]{1,0:T(8,128)(2,1)S(1)} %get-tuple-element.83), channel_id=1, source_target_pairs={{0,6},{1,7},{2,0},{3,1},{4,2},{5,3},{6,4},{7,5},{8,14},{9,15},{10,... | collective-permute-start | bytes 491528 | tf_op jit(solution)/shard_map/ppermute | solution.py:41
  69.4 37.7 %collective-permute-start.17 = (bf16[64,640]{1,0:T(8,128)(2,1)S(1)}, bf16[64,640]{1,0:T(8,128)(2,1)S(1)}, u32[]{:S(2)}, u32[]{:S(2)}) collective-permute-start(bf16[64,640]{1,0:T(8,128)(2,1)S(1)} %get-tuple-element.84), channel_id=1, source_target_pairs={{0,0},{1,1},{2,2},{3,3},{4,4},{5,5},{6,6},{7,7},{8,32},{9,33},{10,... | collective-permute-start | bytes 245768 | tf_op jit(solution)/shard_map/ppermute | solution.py:41
  75.4 31.7 %collective-permute-start.18 = (bf16[64,640]{1,0:T(8,128)(2,1)S(1)}, bf16[64,640]{1,0:T(8,128)(2,1)S(1)}, u32[]{:S(2)}, u32[]{:S(2)}) collective-permute-start(bf16[64,640]{1,0:T(8,128)(2,1)S(1)} %get-tuple-element.85), channel_id=1, source_target_pairs={{0,1},{1,0},{2,3},{3,2},{4,5},{5,4},{6,7},{7,6},{8,33},{9,32},{10,... | collective-permute-start | bytes 245768 | tf_op jit(solution)/shard_map/ppermute | solution.py:41

commit v8 on v7

--- a/solution.py
+++ b/solution.py
@@ -140,7 +140,7 @@
 
 
 def turned(value):
-    return jnp.transpose(jnp.concatenate([value] * 16, axis=0))
+    return jnp.transpose(jnp.concatenate([value] * 8, axis=0))
 
 
 def symmetric_kernel(where, *refs):
@@ -153,7 +153,10 @@
         jnp.concatenate([totals[at : at + 8, row_place(c, d)] for d in range(4)], axis=1)
         for at in (0, 8)
     )
-    by_row = [turned(jnp.exp2(ref[0:8, :] - top) * (1024.0 / total)) for ref in row_tops]
+    gain = 1024.0 / total
+    by_row = turned(
+        jnp.concatenate([jnp.exp2(ref[0:8, :] - top) * gain for ref in row_tops], axis=0)
+    )
     top, total = merged(column_stats)
     totals[0:8, :] = jnp.exp2(column_stats[0][0:8, :] - top) * (1024.0 / total)
     places = [place(x, d) for d in (*NEAR, FAR)]
@@ -168,7 +171,7 @@
                 columns = slice(block * BLOCK, (block + 1) * BLOCK)
                 held[p, h, :, at] = (
                     row_lifted[part][h, here, columns].astype(jnp.float32)
-                    * by_row[part][here, h : h + 1]
+                    * by_row[here, part * 8 + h : part * 8 + h + 1]
                     + column_lifted[part][h, here, columns].astype(jnp.float32)
                     * gains[i][h : h + 1, :]
                 ).astype(jnp.bfloat16)

time: 109 us -> 109 us (level)
  no operation moved by 1% of the time
where the time goes in v8:
time: 109 us; the launch traced here: 108 us
  starting transfers between devices  43 us (39%)
  waiting for transfers between devices  30.7 us (28%)
  Pallas kernels  27.6 us (25%)
  local copies, waits for them, and re-layouts  4.57 us (4%)
    ppermute x19, starting transfers between devices, send(): return lax.ppermute(value, AXES, moves(to))  38.3 us
    all_to_all x1, waiting for transfers between devices, local(): lax.all_to_all(tiles, 'band', split_axis=0, concat_axis=0, axis_index_gro...  18.8 us
    ppermute x19, waiting for transfers between devices, send(): return lax.ppermute(value, AXES, moves(to))  11.9 us
    pallas_call x1, Pallas kernels, local(): pl.pallas_call(pair_kernel, grid=(HALF // ROWS,), in_specs=[VMEM, pl.Bloc...  10.4 us
    pallas_call x1, Pallas kernels, local(): pl.pallas_call(relative_kernel, grid=(HALF // ROWS,), in_specs=[SMEM, SME...  5.66 us
    all_to_all x1, starting transfers between devices, local(): lax.all_to_all(tiles, 'band', split_axis=0, concat_axis=0, axis_index_gro...  4.73 us
    pallas_call x1, Pallas kernels, local(): pl.pallas_call(symmetric_kernel, in_specs=[SMEM] + [VMEM] * 12, out_specs...  2.9 us
    pallas_call x1, Pallas kernels, local(): pl.pallas_call(spread_kernel, in_specs=[VMEM] * 5, out_specs=[VMEM] * 4,...  2.7 us
  transfers between devices with their start and end apart: 20, of which 11 were waited for; matrix products, arithmetic and copies ran while one was open for 3% of the time, Pallas kernels for 21%

profile of v8, /device:TPU:1, one launch (start us, length us, event | category | flops | bytes accessed | tf_op | source)
XLA Modules:
  0.0 107.7 jit_solution(5773741366115553244)
XLA Ops:
  0.7 0.9 fusion.2
  1.6 1.0 fusion
  2.7 0.1 broadcast_select_fusion.1
  2.7 6.1 %collective-permute-start.1 = (bf16[64,1920]{1,0:T(8,128)(2,1)S(1)}, bf16[64,1920]{1,0:T(8,128)(2,1)S(1)}, u32[]{:S(2)}, u32[]{:S(2)}) collective-permute-start(bf16[64,1920]{1,0:T(8,128)(2,1)S(1)} %broadcast_select_fusion.1), channel_id=1, source_target_pairs={{0,1},{1,0},{2,3},{3,2},{4,5},{5,4},{6,7},{7,6},{8,33},{9,32},{10,... | collective-permute-start | bytes 737288 | tf_op jit(solution)/shard_map/ppermute | solution.py:41
  8.8 0.1 broadcast_select_fusion
  8.9 1.9 %collective-permute-start = (bf16[64,1920]{1,0:T(8,128)(2,1)S(1)}, bf16[64,1920]{1,0:T(8,128)(2,1)S(1)}, u32[]{:S(2)}, u32[]{:S(2)}) collective-permute-start(bf16[64,1920]{1,0:T(8,128)(2,1)S(1)} %broadcast_select_fusion), channel_id=1, source_target_pairs={{0,0},{1,1},{2,2},{3,3},{4,4},{5,5},{6,6},{7,7},{8,32},{9,33},{10,... | collective-permute-start | bytes 737288 | tf_op jit(solution)/shard_map/ppermute | solution.py:41
  10.8 0.8 copy.11
  11.6 0.8 copy.13.second
  12.5 0.8 copy.14.second_bias
  13.2 0.1 copy.12.first_bias
  13.4 2.7 %spread.1 = (bf16[1024,336]{1,0:T(8,128)(2,1)}, bf16[512,512]{1,0:T(8,128)(2,1)}, f32[512,128]{1,0:T(8,128)}, bf16[512,576]{1,0:T(8,128)(2,1)S(1)}) custom-call(bf16[40,128]{1,0:T(8,128)(2,1)S(1)} %copy-done, f32[128,1]{1,0:T(8,128)S(1)} %copy.12.first_bias, bf16[128,64]{1,0:T(8,128)(2,1)S(1)} %copy.13.second, f32[64,1]{1,0:T(8,128)S(1)} %copy.14.second_bias, ...), custom_call_target="tpu_custom_call" | custom-call | flops 400000000 | bytes 6000000 | tf_op jit(solution)/shard_map/spread/pallas_call | solution.py:348
  16.1 0.3 collective-permute-done
  16.4 0.1 maximum_select_fusion.refs_0_
  16.5 6.7 %collective-permute-start.4 = (bf16[128,1920]{1,0:T(8,128)(2,1)S(1)}, bf16[128,1920]{1,0:T(8,128)(2,1)S(1)}, u32[]{:S(2)}, u32[]{:S(2)}) collective-permute-start(bf16[128,1920]{1,0:T(8,128)(2,1)S(1)} %maximum_select_fusion.refs_0_), channel_id=1, source_target_pairs={{0,64},{1,65},{2,66},{3,67},{4,68},{5,69},{6,70},{7,71},{8,72},{9,... | collective-permute-start | bytes 1474568 | tf_op jit(solution)/shard_map/ppermute | solution.py:41
  23.2 1.3 %collective-permute-start.3 = (bf16[128,1280]{1,0:T(8,128)(2,1)S(1)}, bf16[128,1280]{1,0:T(8,128)(2,1)S(1)}, u32[]{:S(2)}, u32[]{:S(2)}) collective-permute-start(bf16[128,1280]{1,0:T(8,128)(2,1)S(1)} %slice.39.refs_4_), channel_id=1, source_target_pairs={{0,2},{1,3},{2,4},{3,5},{4,6},{5,7},{6,0},{7,1},{8,10},{9,11},{10,... | collective-permute-start | bytes 983048 | tf_op jit(solution)/shard_map/ppermute | solution.py:41
  24.5 1.5 %collective-permute-start.2 = (bf16[128,1280]{1,0:T(8,128)(2,1)S(1)}, bf16[128,1280]{1,0:T(8,128)(2,1)S(1)}, u32[]{:S(2)}, u32[]{:S(2)}) collective-permute-start(bf16[128,1280]{1,0:T(8,128)(2,1)S(1)} %slice.39.refs_4_), channel_id=1, source_target_pairs={{0,6},{1,7},{2,0},{3,1},{4,2},{5,3},{6,4},{7,5},{8,14},{9,15},{10,... | collective-permute-start | bytes 983048 | tf_op jit(solution)/shard_map/ppermute | solution.py:41
  26.0 0.1 pad_add_fusion.where
  26.1 5.7 %relative.1 = bf16[64,64,512]{2,1,0:T(8,128)(2,1)} custom-call(s32[4]{0:T(128)S(1)} %pad_add_fusion.where, s32[4]{0:T(128)S(1)} %copy-done.1, bf16[512,576]{1,0:T(8,128)(2,1)S(1)} %get-tuple-element.54.table), custom_call_target="tpu_custom_call" | custom-call | flops 2400000000 | bytes 6000000 | tf_op jit(solution)/shard_map/relative/pallas_call | solution.py:394
  31.7 1.1 %collective-permute-done.3.refs_5_ = bf16[128,1280]{1,0:T(8,128)(2,1)S(1)} collective-permute-done((bf16[128,1280]{1,0:T(8,128)(2,1)S(1)}, bf16[128,1280]{1,0:T(8,128)(2,1)S(1)}, u32[]{:S(2)}, u32[]{:S(2)}) %collective-permute-start.3) | collective-permute-done | bytes 327712 | tf_op jit(solution)/shard_map/ppermute | solution.py:41
  32.8 0.3 collective-permute-done.2.refs_6_
  33.1 0.5 collective-permute-start.6
  33.7 2.7 %collective-permute-start.8 = (bf16[64,1280]{1,0:T(8,128)(2,1)S(1)}, bf16[64,1280]{1,0:T(8,128)(2,1)S(1)}, u32[]{:S(2)}, u32[]{:S(2)}) collective-permute-start(bf16[64,1280]{1,0:T(8,128)(2,1)S(1)} %slice.41), channel_id=1, source_target_pairs={{0,6},{1,7},{2,0},{3,1},{4,2},{5,3},{6,4},{7,5},{8,14},{9,15},{10,... | collective-permute-start | bytes 491528 | tf_op jit(solution)/shard_map/ppermute | solution.py:41
  36.4 2.5 %near.1 = (f32[16,512]{1,0:T(8,128)S(1)}, f32[16,384]{1,0:T(8,128)S(1)}, bf16[5,512,384]{2,1,0:T(8,128)(2,1)S(1)}, bf16[5,512,384]{2,1,0:T(8,128)(2,1)S(1)}) custom-call(bf16[128,1920]{1,0:T(8,128)(2,1)S(1)} %maximum_select_fusion.refs_0_, bf16[128,1920]{1,0:T(8,128)(2,1)S(1)} %collective-permute-done.5.refs_1_, ...), custom_call_target="tpu_custom_call" | custom-call | flops 600000000 | bytes 11000000 | tf_op jit(solution)/shard_map/near/pallas_call | solution.py:422
  38.9 1.1 %collective-permute-done.8.refs_5_ = bf16[64,1280]{1,0:T(8,128)(2,1)S(1)} collective-permute-done((bf16[64,1280]{1,0:T(8,128)(2,1)S(1)}, bf16[64,1280]{1,0:T(8,128)(2,1)S(1)}, u32[]{:S(2)}, u32[]{:S(2)}) %collective-permute-start.8) | collective-permute-done | bytes 163872 | tf_op jit(solution)/shard_map/ppermute | solution.py:41
  40.0 3.1 %collective-permute-done.7.refs_4_ = bf16[64,1280]{1,0:T(8,128)(2,1)S(1)} collective-permute-done((bf16[64,1280]{1,0:T(8,128)(2,1)S(1)}, bf16[64,1280]{1,0:T(8,128)(2,1)S(1)}, u32[]{:S(2)}, u32[]{:S(2)}) %collective-permute-start.7) | collective-permute-done | bytes 163872 | tf_op jit(solution)/shard_map/ppermute | solution.py:41
  43.1 1.9 %far.1 = (f32[16,512]{1,0:T(8,128)S(1)}, f32[8,512]{1,0:T(8,128)S(1)}, f32[16,512]{1,0:T(8,128)S(1)}, bf16[5,512,128]{2,1,0:T(8,128)(2,1)S(1)}, bf16[5,512,128]{2,1,0:T(8,128)(2,1)S(1)}) custom-call(s32[4]{0:T(128)S(1)} %pad_add_fusion.where, bf16[128,1920]{1,0:T(8,128)(2,1)S(1)} %maximum_select_fusion.refs_0_, ...), custom_call_target="tpu_custom_call" | custom-call | flops 300000000 | bytes 5000000 | tf_op jit(solution)/shard_map/far/pallas_call | solution.py:438
  45.0 1.2 %collective-permute-start.9 = (f32[16,512]{1,0:T(8,128)S(1)}, f32[16,512]{1,0:T(8,128)S(1)}, u32[]{:S(2)}, u32[]{:S(2)}) collective-permute-start(f32[16,512]{1,0:T(8,128)S(1)} %get-tuple-element.74.one), channel_id=1, source_target_pairs={{0,32},{1,33},{2,34},{3,35},{4,36},{5,37},{6,38},{7,39},{8,40},{9,... | collective-permute-start | bytes 98312 | tf_op jit(solution)/shard_map/ppermute | solution.py:41
  46.2 0.0 collective-permute-start.13
  46.2 0.6 collective-permute-start.12
  46.8 0.9 collective-permute-start.11
  47.7 1.7 %collective-permute-start.10 = (f32[16,512]{1,0:T(8,128)S(1)}, f32[16,512]{1,0:T(8,128)S(1)}, u32[]{:S(2)}, u32[]{:S(2)}) collective-permute-start(f32[16,512]{1,0:T(8,128)S(1)} %merge.1.refs_0_), channel_id=1, source_target_pairs={{0,64},{1,65},{2,66},{3,67},{4,68},{5,69},{6,70},{7,71},{8,72},{9,... | collective-permute-start | bytes 98312 | tf_op jit(solution)/shard_map/ppermute | solution.py:41
  49.4 0.7 partials.1
  50.1 0.4 collective-permute-done.12.refs_4_.refs_2_
  50.5 1.2 %collective-permute-done.11.refs_3_.refs_1_ = f32[16,512]{1,0:T(8,128)S(1)} collective-permute-done((f32[16,512]{1,0:T(8,128)S(1)}, f32[16,512]{1,0:T(8,128)S(1)}, u32[]{:S(2)}, u32[]{:S(2)}) %collective-permute-start.11) | collective-permute-done | bytes 32800 | tf_op jit(solution)/shard_map/ppermute | solution.py:41
  51.7 2.9 %symmetric.1 = bf16[8,5,64,512]{3,2,1,0:T(8,128)(2,1)} custom-call(s32[4]{0:T(128)S(1)} %pad_add_fusion.where, f32[16,512]{1,0:T(8,128)S(1)} %merge.1.refs_0_, f32[16,512]{1,0:T(8,128)S(1)} %collective-permute-done.10.refs_1_, f32[16,512]{1,0:T(8,128)S(1)} %get-tuple-element.75.refs_2_.refs_0_, f32[16,512]{1,0:T(8,128)S(1)} %collective-permute-done.11.refs_3_.refs_1_, ...), custom_call_target="tpu_custom_call" | custom-call | flops 10000000 | bytes 9000000 | tf_op jit(solution)/shard_map/symmetric/pallas_call | solution.py:472
  54.6 4.7 %all-to-all-start = ((bf16[8,5,64,512]{3,2,1,0:T(8,128)(2,1)}), bf16[8,5,64,512]{3,2,1,0:T(8,128)(2,1)S(1)}, u32[]{:S(2)}, u32[]{:S(2)}) async-start(bf16[8,5,64,512]{3,2,1,0:T(8,128)(2,1)} %symmetric.1), calls=%async_computation | async-start | bytes 5242880 | tf_op jit(solution)/shard_map/all_to_all | solution.py:495
  59.3 0.3 collective-permute-start.14
  59.6 2.4 %collective-permute-start.15 = (bf16[640,128]{1,0:T(8,128)(2,1)S(1)}, bf16[640,128]{1,0:T(8,128)(2,1)S(1)}, u32[]{:S(2)}, u32[]{:S(2)}) collective-permute-start(bf16[640,128]{1,0:T(8,128)(2,1)S(1)} %get-tuple-element.82), channel_id=1, source_target_pairs={{0,4},{1,5},{2,6},{3,7},{4,0},{5,1},{6,2},{7,3},{8,12},{9,13},{10,... | collective-permute-start | bytes 491528 | tf_op jit(solution)/shard_map/ppermute | solution.py:41
  62.0 2.0 %collective-permute-start.16 = (bf16[640,128]{1,0:T(8,128)(2,1)S(1)}, bf16[640,128]{1,0:T(8,128)(2,1)S(1)}, u32[]{:S(2)}, u32[]{:S(2)}) collective-permute-start(bf16[640,128]{1,0:T(8,128)(2,1)S(1)} %get-tuple-element.83), channel_id=1, source_target_pairs={{0,6},{1,7},{2,0},{3,1},{4,2},{5,3},{6,4},{7,5},{8,14},{9,15},{10,... | collective-permute-start | bytes 491528 | tf_op jit(solution)/shard_map/ppermute | solution.py:41
  64.0 0.7 collective-permute-done.14.refs_5_
  64.7 2.9 %collective-permute-done.15.refs_6_ = bf16[640,128]{1,0:T(8,128)(2,1)S(1)} collective-permute-done((bf16[640,128]{1,0:T(8,128)(2,1)S(1)}, bf16[640,128]{1,0:T(8,128)(2,1)S(1)}, u32[]{:S(2)}, u32[]{:S(2)}) %collective-permute-start.15) | collective-permute-done | bytes 163872 | tf_op jit(solution)/shard_map/ppermute | solution.py:41
  67.6 0.9 collective-permute-done.16.refs_7_
  68.5 0.8 context.1
  69.3 6.0 %collective-permute-start.17 = (bf16[64,640]{1,0:T(8,128)(2,1)S(1)}, bf16[64,640]{1,0:T(8,128)(2,1)S(1)}, u32[]{:S(2)}, u32[]{:S(2)}) collective-permute-start(bf16[64,640]{1,0:T(8,128)(2,1)S(1)} %get-tuple-element.84), channel_id=1, source_target_pairs={{0,0},{1,1},{2,2},{3,3},{4,4},{5,5},{6,6},{7,7},{8,32},{9,33},{10,... | collective-permute-start | bytes 245768 | tf_op jit(solution)/shard_map/ppermute | solution.py:41
  75.3 2.5 %collective-permute-start.18 = (bf16[64,640]{1,0:T(8,128)(2,1)S(1)}, bf16[64,640]{1,0:T(8,128)(2,1)S(1)}, u32[]{:S(2)}, u32[]{:S(2)}) collective-permute-start(bf16[64,640]{1,0:T(8,128)(2,1)S(1)} %get-tuple-element.85), channel_id=1, source_target_pairs={{0,1},{1,0},{2,3},{3,2},{4,5},{5,4},{6,7},{7,6},{8,33},{9,32},{10,... | collective-permute-start | bytes 245768 | tf_op jit(solution)/shard_map/ppermute | solution.py:41
  77.8 18.8 %all-to-all-done = bf16[8,5,64,512]{3,2,1,0:T(8,128)(2,1)S(1)} async-done(((bf16[8,5,64,512]{3,2,1,0:T(8,128)(2,1)}), bf16[8,5,64,512]{3,2,1,0:T(8,128)(2,1)S(1)}, u32[]{:S(2)}, u32[]{:S(2)}) %all-to-all-start) | async-done | bytes 2621472 | tf_op jit(solution)/shard_map/all_to_all | solution.py:495
  96.6 10.4 %pair.1 = bf16[64,64,512]{2,1,0:T(8,128)(2,1)} custom-call(bf16[40,64,512]{2,1,0:T(8,128)(2,1)S(1)} %bitcast.7, bf16[1024,336]{1,0:T(8,128)(2,1)} %get-tuple-element.87.first, bf16[512,512]{1,0:T(8,128)(2,1)} %get-tuple-element.88.second, f32[512,128]{1,0:T(8,128)} %get-tuple-element.89.second_bias, bf16[64,64,512]{2,1,0:T(8,128)(2,1)} %relative.1), custom_call_target="tpu_custom_call" | custom-call | flops 5000000000 | bytes 14000000 | tf_op jit(solution)/shard_map/pair/pallas_call | solution.py:512
  107.0 0.7 maximum_select_fusion.1
  (22 shorter events, 0.1 us)
Async XLA Ops:
  0.6 12.6 %copy-start.2 = (f32[128]{0:T(128)S(1)}, f32[128]{0:T(128)}, u32[]{:S(2)}) copy-start(f32[128]{0:T(128)} %param.13) | copy-start | bytes 1540
  0.6 12.7 %copy-start = (bf16[40,128]{1,0:T(8,128)(2,1)S(1)}, bf16[40,128]{1,0:T(8,128)(2,1)}, u32[]{:S(2)}) copy-start(bf16[40,128]{1,0:T(8,128)(2,1)} %first.1) | copy-start | bytes 30724
  1.6 24.4 %copy-start.1 = (s32[4]{0:T(128)S(1)}, s32[4]{0:T(128)}, u32[]{:S(2)}) copy-start(s32[4]{0:T(128)} %lengths.1) | copy-start | bytes 52
  2.7 13.3 %collective-permute-start.1 = (bf16[64,1920]{1,0:T(8,128)(2,1)S(1)}, bf16[64,1920]{1,0:T(8,128)(2,1)S(1)}, u32[]{:S(2)}, u32[]{:S(2)}) collective-permute-start(bf16[64,1920]{1,0:T(8,128)(2,1)S(1)} %broadcast_select_fusion.1), channel_id=1, source_target_pairs={{0,1},{1,0},{2,3},{3,2},{4,5},{5,4},{6,7},{7,6},{8,33},{9,32},{10,... | collective-permute-start | bytes 737288 | tf_op jit(solution)/shard_map/ppermute | solution.py:41
  8.9 7.5 %collective-permute-start = (bf16[64,1920]{1,0:T(8,128)(2,1)S(1)}, bf16[64,1920]{1,0:T(8,128)(2,1)S(1)}, u32[]{:S(2)}, u32[]{:S(2)}) collective-permute-start(bf16[64,1920]{1,0:T(8,128)(2,1)S(1)} %broadcast_select_fusion), channel_id=1, source_target_pairs={{0,0},{1,1},{2,2},{3,3},{4,4},{5,5},{6,6},{7,7},{8,32},{9,33},{10,... | collective-permute-start | bytes 737288 | tf_op jit(solution)/shard_map/ppermute | solution.py:41
  16.5 16.6 %collective-permute-start.4 = (bf16[128,1920]{1,0:T(8,128)(2,1)S(1)}, bf16[128,1920]{1,0:T(8,128)(2,1)S(1)}, u32[]{:S(2)}, u32[]{:S(2)}) collective-permute-start(bf16[128,1920]{1,0:T(8,128)(2,1)S(1)} %maximum_select_fusion.refs_0_), channel_id=1, source_target_pairs={{0,64},{1,65},{2,66},{3,67},{4,68},{5,69},{6,70},{7,71},{8,72},{9,... | collective-permute-start | bytes 1474568 | tf_op jit(solution)/shard_map/ppermute | solution.py:41
  23.2 9.6 %collective-permute-start.3 = (bf16[128,1280]{1,0:T(8,128)(2,1)S(1)}, bf16[128,1280]{1,0:T(8,128)(2,1)S(1)}, u32[]{:S(2)}, u32[]{:S(2)}) collective-permute-start(bf16[128,1280]{1,0:T(8,128)(2,1)S(1)} %slice.39.refs_4_), channel_id=1, source_target_pairs={{0,2},{1,3},{2,4},{3,5},{4,6},{5,7},{6,0},{7,1},{8,10},{9,11},{10,... | collective-permute-start | bytes 983048 | tf_op jit(solution)/shard_map/ppermute | solution.py:41
  24.5 8.6 %collective-permute-start.2 = (bf16[128,1280]{1,0:T(8,128)(2,1)S(1)}, bf16[128,1280]{1,0:T(8,128)(2,1)S(1)}, u32[]{:S(2)}, u32[]{:S(2)}) collective-permute-start(bf16[128,1280]{1,0:T(8,128)(2,1)S(1)} %slice.39.refs_4_), channel_id=1, source_target_pairs={{0,6},{1,7},{2,0},{3,1},{4,2},{5,3},{6,4},{7,5},{8,14},{9,15},{10,... | collective-permute-start | bytes 983048 | tf_op jit(solution)/shard_map/ppermute | solution.py:41
  33.1 3.3 %collective-permute-start.5 = (bf16[128,1920]{1,0:T(8,128)(2,1)S(1)}, bf16[128,1920]{1,0:T(8,128)(2,1)S(1)}, u32[]{:S(2)}, u32[]{:S(2)}) collective-permute-start(bf16[128,1920]{1,0:T(8,128)(2,1)S(1)} %maximum_select_fusion.refs_0_), channel_id=1, source_target_pairs={{0,32},{1,33},{2,34},{3,35},{4,36},{5,37},{6,38},{7,39},{8,40},{9,... | collective-permute-start | bytes 1474568 | tf_op jit(solution)/shard_map/ppermute | solution.py:41
  33.1 3.3 %collective-permute-start.6 = (bf16[128,1920]{1,0:T(8,128)(2,1)S(1)}, bf16[128,1920]{1,0:T(8,128)(2,1)S(1)}, u32[]{:S(2)}, u32[]{:S(2)}) collective-permute-start(bf16[128,1920]{1,0:T(8,128)(2,1)S(1)} %collective-permute-done.4.refs_2_), channel_id=1, source_target_pairs={{0,32},{1,33},{2,34},{3,35},{4,36},{5,37},{6,38},{7,39},{8,40},{9,... | collective-permute-start | bytes 1474568 | tf_op jit(solution)/shard_map/ppermute | solution.py:41
  33.7 6.4 %collective-permute-start.8 = (bf16[64,1280]{1,0:T(8,128)(2,1)S(1)}, bf16[64,1280]{1,0:T(8,128)(2,1)S(1)}, u32[]{:S(2)}, u32[]{:S(2)}) collective-permute-start(bf16[64,1280]{1,0:T(8,128)(2,1)S(1)} %slice.41), channel_id=1, source_target_pairs={{0,6},{1,7},{2,0},{3,1},{4,2},{5,3},{6,4},{7,5},{8,14},{9,15},{10,... | collective-permute-start | bytes 491528 | tf_op jit(solution)/shard_map/ppermute | solution.py:41
  36.4 6.7 %collective-permute-start.7 = (bf16[64,1280]{1,0:T(8,128)(2,1)S(1)}, bf16[64,1280]{1,0:T(8,128)(2,1)S(1)}, u32[]{:S(2)}, u32[]{:S(2)}) collective-permute-start(bf16[64,1280]{1,0:T(8,128)(2,1)S(1)} %slice.40), channel_id=1, source_target_pairs={{0,2},{1,3},{2,4},{3,5},{4,6},{5,7},{6,0},{7,1},{8,10},{9,11},{10,... | collective-permute-start | bytes 491528 | tf_op jit(solution)/shard_map/ppermute | solution.py:41
  45.0 2.7 %collective-permute-start.9 = (f32[16,512]{1,0:T(8,128)S(1)}, f32[16,512]{1,0:T(8,128)S(1)}, u32[]{:S(2)}, u32[]{:S(2)}) collective-permute-start(f32[16,512]{1,0:T(8,128)S(1)} %get-tuple-element.74.one), channel_id=1, source_target_pairs={{0,32},{1,33},{2,34},{3,35},{4,36},{5,37},{6,38},{7,39},{8,40},{9,... | collective-permute-start | bytes 98312 | tf_op jit(solution)/shard_map/ppermute | solution.py:41
  46.2 3.9 %collective-permute-start.13 = (f32[16,512]{1,0:T(8,128)S(1)}, f32[16,512]{1,0:T(8,128)S(1)}, u32[]{:S(2)}, u32[]{:S(2)}) collective-permute-start(f32[16,512]{1,0:T(8,128)S(1)} %get-tuple-element.75.refs_2_.refs_0_), channel_id=1, source_target_pairs={{0,6},{1,7},{2,0},{3,1},{4,2},{5,3},{6,4},{7,5},{8,14},{9,15},{10,... | collective-permute-start | bytes 98312 | tf_op jit(solution)/shard_map/ppermute | solution.py:41
  46.2 4.3 %collective-permute-start.12 = (f32[16,512]{1,0:T(8,128)S(1)}, f32[16,512]{1,0:T(8,128)S(1)}, u32[]{:S(2)}, u32[]{:S(2)}) collective-permute-start(f32[16,512]{1,0:T(8,128)S(1)} %get-tuple-element.75.refs_2_.refs_0_), channel_id=1, source_target_pairs={{0,4},{1,5},{2,6},{3,7},{4,0},{5,1},{6,2},{7,3},{8,12},{9,13},{10,... | collective-permute-start | bytes 98312 | tf_op jit(solution)/shard_map/ppermute | solution.py:41
  46.8 4.9 %collective-permute-start.11 = (f32[16,512]{1,0:T(8,128)S(1)}, f32[16,512]{1,0:T(8,128)S(1)}, u32[]{:S(2)}, u32[]{:S(2)}) collective-permute-start(f32[16,512]{1,0:T(8,128)S(1)} %get-tuple-element.75.refs_2_.refs_0_), channel_id=1, source_target_pairs={{0,2},{1,3},{2,4},{3,5},{4,6},{5,7},{6,0},{7,1},{8,10},{9,11},{10,... | collective-permute-start | bytes 98312 | tf_op jit(solution)/shard_map/ppermute | solution.py:41
  47.7 3.9 %collective-permute-start.10 = (f32[16,512]{1,0:T(8,128)S(1)}, f32[16,512]{1,0:T(8,128)S(1)}, u32[]{:S(2)}, u32[]{:S(2)}) collective-permute-start(f32[16,512]{1,0:T(8,128)S(1)} %merge.1.refs_0_), channel_id=1, source_target_pairs={{0,64},{1,65},{2,66},{3,67},{4,68},{5,69},{6,70},{7,71},{8,72},{9,... | collective-permute-start | bytes 98312 | tf_op jit(solution)/shard_map/ppermute | solution.py:41
  54.6 42.0 %all-to-all-start = ((bf16[8,5,64,512]{3,2,1,0:T(8,128)(2,1)}), bf16[8,5,64,512]{3,2,1,0:T(8,128)(2,1)S(1)}, u32[]{:S(2)}, u32[]{:S(2)}) async-start(bf16[8,5,64,512]{3,2,1,0:T(8,128)(2,1)} %symmetric.1), calls=%async_computation | async-start | bytes 5242880 | tf_op jit(solution)/shard_map/all_to_all | solution.py:495
  59.3 5.4 %collective-permute-start.14 = (bf16[640,128]{1,0:T(8,128)(2,1)S(1)}, bf16[640,128]{1,0:T(8,128)(2,1)S(1)}, u32[]{:S(2)}, u32[]{:S(2)}) collective-permute-start(bf16[640,128]{1,0:T(8,128)(2,1)S(1)} %get-tuple-element.81), channel_id=1, source_target_pairs={{0,2},{1,3},{2,4},{3,5},{4,6},{5,7},{6,0},{7,1},{8,10},{9,11},{10,... | collective-permute-start | bytes 491528 | tf_op jit(solution)/shard_map/ppermute | solution.py:41
  59.6 8.0 %collective-permute-start.15 = (bf16[640,128]{1,0:T(8,128)(2,1)S(1)}, bf16[640,128]{1,0:T(8,128)(2,1)S(1)}, u32[]{:S(2)}, u32[]{:S(2)}) collective-permute-start(bf16[640,128]{1,0:T(8,128)(2,1)S(1)} %get-tuple-element.82), channel_id=1, source_target_pairs={{0,4},{1,5},{2,6},{3,7},{4,0},{5,1},{6,2},{7,3},{8,12},{9,13},{10,... | collective-permute-start | bytes 491528 | tf_op jit(solution)/shard_map/ppermute | solution.py:41
  62.0 6.5 %collective-permute-start.16 = (bf16[640,128]{1,0:T(8,128)(2,1)S(1)}, bf16[640,128]{1,0:T(8,128)(2,1)S(1)}, u32[]{:S(2)}, u32[]{:S(2)}) collective-permute-start(bf16[640,128]{1,0:T(8,128)(2,1)S(1)} %get-tuple-element.83), channel_id=1, source_target_pairs={{0,6},{1,7},{2,0},{3,1},{4,2},{5,3},{6,4},{7,5},{8,14},{9,15},{10,... | collective-permute-start | bytes 491528 | tf_op jit(solution)/shard_map/ppermute | solution.py:41
  69.3 37.7 %collective-permute-start.17 = (bf16[64,640]{1,0:T(8,128)(2,1)S(1)}, bf16[64,640]{1,0:T(8,128)(2,1)S(1)}, u32[]{:S(2)}, u32[]{:S(2)}) collective-permute-start(bf16[64,640]{1,0:T(8,128)(2,1)S(1)} %get-tuple-element.84), channel_id=1, source_target_pairs={{0,0},{1,1},{2,2},{3,3},{4,4},{5,5},{6,6},{7,7},{8,32},{9,33},{10,... | collective-permute-start | bytes 245768 | tf_op jit(solution)/shard_map/ppermute | solution.py:41
  75.3 31.7 %collective-permute-start.18 = (bf16[64,640]{1,0:T(8,128)(2,1)S(1)}, bf16[64,640]{1,0:T(8,128)(2,1)S(1)}, u32[]{:S(2)}, u32[]{:S(2)}) collective-permute-start(bf16[64,640]{1,0:T(8,128)(2,1)S(1)} %get-tuple-element.85), channel_id=1, source_target_pairs={{0,1},{1,0},{2,3},{3,2},{4,5},{5,4},{6,7},{7,6},{8,33},{9,32},{10,... | collective-permute-start | bytes 245768 | tf_op jit(solution)/shard_map/ppermute | solution.py:41

commit v9 on v7

--- a/solution.py
+++ b/solution.py
@@ -166,12 +166,14 @@
             for i, at in enumerate(places):
                 part, block = divmod(i, len(NEAR))
                 columns = slice(block * BLOCK, (block + 1) * BLOCK)
+                row_gain, column_gain = (
+                    jnp.broadcast_to(gain, (HALF, BLOCK)).astype(jnp.bfloat16)
+                    for gain in (by_row[part][here, h : h + 1], gains[i][h : h + 1, :])
+                )
                 held[p, h, :, at] = (
-                    row_lifted[part][h, here, columns].astype(jnp.float32)
-                    * by_row[part][here, h : h + 1]
-                    + column_lifted[part][h, here, columns].astype(jnp.float32)
-                    * gains[i][h : h + 1, :]
-                ).astype(jnp.bfloat16)
+                    row_lifted[part][h, here, columns] * row_gain
+                    + column_lifted[part][h, here, columns] * column_gain
+                )
         copies.append(pltpu.make_async_copy(held.at[p], out.at[owner], sems.at[p]))
         copies[p].start()
     for copy in copies:

time: 109 us -> 109 us (level)
  no operation moved by 1% of the time
where the time goes in v9:
time: 109 us; the launch traced here: 107 us
  starting transfers between devices  43 us (39%)
  waiting for transfers between devices  30.7 us (28%)
  Pallas kernels  27.3 us (25%)
  local copies, waits for them, and re-layouts  4.57 us (4%)
    ppermute x19, starting transfers between devices, send(): return lax.ppermute(value, AXES, moves(to))  38.3 us
    all_to_all x1, waiting for transfers between devices, local(): lax.all_to_all(tiles, 'band', split_axis=0, concat_axis=0, axis_index_gro...  18.8 us
    ppermute x19, waiting for transfers between devices, send(): return lax.ppermute(value, AXES, moves(to))  11.9 us
    pallas_call x1, Pallas kernels, local(): pl.pallas_call(pair_kernel, grid=(HALF // ROWS,), in_specs=[VMEM, pl.Bloc...  10.4 us
    pallas_call x1, Pallas kernels, local(): pl.pallas_call(relative_kernel, grid=(HALF // ROWS,), in_specs=[SMEM, SME...  5.66 us
    all_to_all x1, starting transfers between devices, local(): lax.all_to_all(tiles, 'band', split_axis=0, concat_axis=0, axis_index_gro...  4.73 us
    pallas_call x1, Pallas kernels, local(): pl.pallas_call(spread_kernel, in_specs=[VMEM] * 5, out_specs=[VMEM] * 4,...  2.7 us
    pallas_call x1, Pallas kernels, local(): pl.pallas_call(symmetric_kernel, in_specs=[SMEM] + [VMEM] * 12, out_specs...  2.61 us
  transfers between devices with their start and end apart: 20, of which 11 were waited for; matrix products, arithmetic and copies ran while one was open for 3% of the time, Pallas kernels for 21%

profile of v9, /device:TPU:1, one launch (start us, length us, event | category | flops | bytes accessed | tf_op | source)
XLA Modules:
  0.0 107.4 jit_solution(8897910054213998364)
XLA Ops:
  0.7 0.9 fusion.2
  1.6 1.0 fusion
  2.7 0.1 broadcast_select_fusion.1
  2.7 6.1 %collective-permute-start.1 = (bf16[64,1920]{1,0:T(8,128)(2,1)S(1)}, bf16[64,1920]{1,0:T(8,128)(2,1)S(1)}, u32[]{:S(2)}, u32[]{:S(2)}) collective-permute-start(bf16[64,1920]{1,0:T(8,128)(2,1)S(1)} %broadcast_select_fusion.1), channel_id=1, source_target_pairs={{0,1},{1,0},{2,3},{3,2},{4,5},{5,4},{6,7},{7,6},{8,33},{9,32},{10,... | collective-permute-start | bytes 737288 | tf_op jit(solution)/shard_map/ppermute | solution.py:41
  8.8 0.1 broadcast_select_fusion
  8.9 1.9 %collective-permute-start = (bf16[64,1920]{1,0:T(8,128)(2,1)S(1)}, bf16[64,1920]{1,0:T(8,128)(2,1)S(1)}, u32[]{:S(2)}, u32[]{:S(2)}) collective-permute-start(bf16[64,1920]{1,0:T(8,128)(2,1)S(1)} %broadcast_select_fusion), channel_id=1, source_target_pairs={{0,0},{1,1},{2,2},{3,3},{4,4},{5,5},{6,6},{7,7},{8,32},{9,33},{10,... | collective-permute-start | bytes 737288 | tf_op jit(solution)/shard_map/ppermute | solution.py:41
  10.8 0.8 copy.11
  11.6 0.8 copy.13.second
  12.5 0.8 copy.14.second_bias
  13.2 0.1 copy.12.first_bias
  13.4 2.7 %spread.1 = (bf16[1024,336]{1,0:T(8,128)(2,1)}, bf16[512,512]{1,0:T(8,128)(2,1)}, f32[512,128]{1,0:T(8,128)}, bf16[512,576]{1,0:T(8,128)(2,1)S(1)}) custom-call(bf16[40,128]{1,0:T(8,128)(2,1)S(1)} %copy-done, f32[128,1]{1,0:T(8,128)S(1)} %copy.12.first_bias, bf16[128,64]{1,0:T(8,128)(2,1)S(1)} %copy.13.second, f32[64,1]{1,0:T(8,128)S(1)} %copy.14.second_bias, ...), custom_call_target="tpu_custom_call" | custom-call | flops 400000000 | bytes 6000000 | tf_op jit(solution)/shard_map/spread/pallas_call | solution.py:347
  16.1 0.3 collective-permute-done
  16.4 0.1 maximum_select_fusion.refs_0_
  16.5 6.7 %collective-permute-start.4 = (bf16[128,1920]{1,0:T(8,128)(2,1)S(1)}, bf16[128,1920]{1,0:T(8,128)(2,1)S(1)}, u32[]{:S(2)}, u32[]{:S(2)}) collective-permute-start(bf16[128,1920]{1,0:T(8,128)(2,1)S(1)} %maximum_select_fusion.refs_0_), channel_id=1, source_target_pairs={{0,64},{1,65},{2,66},{3,67},{4,68},{5,69},{6,70},{7,71},{8,72},{9,... | collective-permute-start | bytes 1474568 | tf_op jit(solution)/shard_map/ppermute | solution.py:41
  23.2 1.3 %collective-permute-start.3 = (bf16[128,1280]{1,0:T(8,128)(2,1)S(1)}, bf16[128,1280]{1,0:T(8,128)(2,1)S(1)}, u32[]{:S(2)}, u32[]{:S(2)}) collective-permute-start(bf16[128,1280]{1,0:T(8,128)(2,1)S(1)} %slice.39.refs_4_), channel_id=1, source_target_pairs={{0,2},{1,3},{2,4},{3,5},{4,6},{5,7},{6,0},{7,1},{8,10},{9,11},{10,... | collective-permute-start | bytes 983048 | tf_op jit(solution)/shard_map/ppermute | solution.py:41
  24.5 1.5 %collective-permute-start.2 = (bf16[128,1280]{1,0:T(8,128)(2,1)S(1)}, bf16[128,1280]{1,0:T(8,128)(2,1)S(1)}, u32[]{:S(2)}, u32[]{:S(2)}) collective-permute-start(bf16[128,1280]{1,0:T(8,128)(2,1)S(1)} %slice.39.refs_4_), channel_id=1, source_target_pairs={{0,6},{1,7},{2,0},{3,1},{4,2},{5,3},{6,4},{7,5},{8,14},{9,15},{10,... | collective-permute-start | bytes 983048 | tf_op jit(solution)/shard_map/ppermute | solution.py:41
  26.0 0.1 pad_add_fusion.where
  26.1 5.7 %relative.1 = bf16[64,64,512]{2,1,0:T(8,128)(2,1)} custom-call(s32[4]{0:T(128)S(1)} %pad_add_fusion.where, s32[4]{0:T(128)S(1)} %copy-done.1, bf16[512,576]{1,0:T(8,128)(2,1)S(1)} %get-tuple-element.54.table), custom_call_target="tpu_custom_call" | custom-call | flops 2400000000 | bytes 6000000 | tf_op jit(solution)/shard_map/relative/pallas_call | solution.py:393
  31.7 1.1 %collective-permute-done.3.refs_5_ = bf16[128,1280]{1,0:T(8,128)(2,1)S(1)} collective-permute-done((bf16[128,1280]{1,0:T(8,128)(2,1)S(1)}, bf16[128,1280]{1,0:T(8,128)(2,1)S(1)}, u32[]{:S(2)}, u32[]{:S(2)}) %collective-permute-start.3) | collective-permute-done | bytes 327712 | tf_op jit(solution)/shard_map/ppermute | solution.py:41
  32.8 0.3 collective-permute-done.2.refs_6_
  33.1 0.5 collective-permute-start.6
  33.7 2.7 %collective-permute-start.8 = (bf16[64,1280]{1,0:T(8,128)(2,1)S(1)}, bf16[64,1280]{1,0:T(8,128)(2,1)S(1)}, u32[]{:S(2)}, u32[]{:S(2)}) collective-permute-start(bf16[64,1280]{1,0:T(8,128)(2,1)S(1)} %slice.41), channel_id=1, source_target_pairs={{0,6},{1,7},{2,0},{3,1},{4,2},{5,3},{6,4},{7,5},{8,14},{9,15},{10,... | collective-permute-start | bytes 491528 | tf_op jit(solution)/shard_map/ppermute | solution.py:41
  36.4 2.5 %near.1 = (f32[16,512]{1,0:T(8,128)S(1)}, f32[16,384]{1,0:T(8,128)S(1)}, bf16[5,512,384]{2,1,0:T(8,128)(2,1)S(1)}, bf16[5,512,384]{2,1,0:T(8,128)(2,1)S(1)}) custom-call(bf16[128,1920]{1,0:T(8,128)(2,1)S(1)} %maximum_select_fusion.refs_0_, bf16[128,1920]{1,0:T(8,128)(2,1)S(1)} %collective-permute-done.5.refs_1_, ...), custom_call_target="tpu_custom_call" | custom-call | flops 600000000 | bytes 11000000 | tf_op jit(solution)/shard_map/near/pallas_call | solution.py:421
  38.9 1.1 %collective-permute-done.8.refs_5_ = bf16[64,1280]{1,0:T(8,128)(2,1)S(1)} collective-permute-done((bf16[64,1280]{1,0:T(8,128)(2,1)S(1)}, bf16[64,1280]{1,0:T(8,128)(2,1)S(1)}, u32[]{:S(2)}, u32[]{:S(2)}) %collective-permute-start.8) | collective-permute-done | bytes 163872 | tf_op jit(solution)/shard_map/ppermute | solution.py:41
  40.0 3.1 %collective-permute-done.7.refs_4_ = bf16[64,1280]{1,0:T(8,128)(2,1)S(1)} collective-permute-done((bf16[64,1280]{1,0:T(8,128)(2,1)S(1)}, bf16[64,1280]{1,0:T(8,128)(2,1)S(1)}, u32[]{:S(2)}, u32[]{:S(2)}) %collective-permute-start.7) | collective-permute-done | bytes 163872 | tf_op jit(solution)/shard_map/ppermute | solution.py:41
  43.1 1.9 %far.1 = (f32[16,512]{1,0:T(8,128)S(1)}, f32[8,512]{1,0:T(8,128)S(1)}, f32[16,512]{1,0:T(8,128)S(1)}, bf16[5,512,128]{2,1,0:T(8,128)(2,1)S(1)}, bf16[5,512,128]{2,1,0:T(8,128)(2,1)S(1)}) custom-call(s32[4]{0:T(128)S(1)} %pad_add_fusion.where, bf16[128,1920]{1,0:T(8,128)(2,1)S(1)} %maximum_select_fusion.refs_0_, ...), custom_call_target="tpu_custom_call" | custom-call | flops 300000000 | bytes 5000000 | tf_op jit(solution)/shard_map/far/pallas_call | solution.py:437
  45.0 1.2 %collective-permute-start.9 = (f32[16,512]{1,0:T(8,128)S(1)}, f32[16,512]{1,0:T(8,128)S(1)}, u32[]{:S(2)}, u32[]{:S(2)}) collective-permute-start(f32[16,512]{1,0:T(8,128)S(1)} %get-tuple-element.74.one), channel_id=1, source_target_pairs={{0,32},{1,33},{2,34},{3,35},{4,36},{5,37},{6,38},{7,39},{8,40},{9,... | collective-permute-start | bytes 98312 | tf_op jit(solution)/shard_map/ppermute | solution.py:41
  46.2 0.0 collective-permute-start.13
  46.2 0.6 collective-permute-start.12
  46.8 0.9 collective-permute-start.11
  47.7 1.7 %collective-permute-start.10 = (f32[16,512]{1,0:T(8,128)S(1)}, f32[16,512]{1,0:T(8,128)S(1)}, u32[]{:S(2)}, u32[]{:S(2)}) collective-permute-start(f32[16,512]{1,0:T(8,128)S(1)} %merge.1.refs_0_), channel_id=1, source_target_pairs={{0,64},{1,65},{2,66},{3,67},{4,68},{5,69},{6,70},{7,71},{8,72},{9,... | collective-permute-start | bytes 98312 | tf_op jit(solution)/shard_map/ppermute | solution.py:41
  49.4 0.7 partials.1
  50.1 0.4 collective-permute-done.12.refs_4_.refs_2_
  50.5 1.2 %collective-permute-done.11.refs_3_.refs_1_ = f32[16,512]{1,0:T(8,128)S(1)} collective-permute-done((f32[16,512]{1,0:T(8,128)S(1)}, f32[16,512]{1,0:T(8,128)S(1)}, u32[]{:S(2)}, u32[]{:S(2)}) %collective-permute-start.11) | collective-permute-done | bytes 32800 | tf_op jit(solution)/shard_map/ppermute | solution.py:41
  51.7 2.6 %symmetric.1 = bf16[8,5,64,512]{3,2,1,0:T(8,128)(2,1)} custom-call(s32[4]{0:T(128)S(1)} %pad_add_fusion.where, f32[16,512]{1,0:T(8,128)S(1)} %merge.1.refs_0_, f32[16,512]{1,0:T(8,128)S(1)} %collective-permute-done.10.refs_1_, f32[16,512]{1,0:T(8,128)S(1)} %get-tuple-element.75.refs_2_.refs_0_, f32[16,512]{1,0:T(8,128)S(1)} %collective-permute-done.11.refs_3_.refs_1_, ...), custom_call_target="tpu_custom_call" | custom-call | flops 10000000 | bytes 9000000 | tf_op jit(solution)/shard_map/symmetric/pallas_call | solution.py:471
  54.3 4.7 %all-to-all-start = ((bf16[8,5,64,512]{3,2,1,0:T(8,128)(2,1)}), bf16[8,5,64,512]{3,2,1,0:T(8,128)(2,1)S(1)}, u32[]{:S(2)}, u32[]{:S(2)}) async-start(bf16[8,5,64,512]{3,2,1,0:T(8,128)(2,1)} %symmetric.1), calls=%async_computation | async-start | bytes 5242880 | tf_op jit(solution)/shard_map/all_to_all | solution.py:494
  59.0 0.3 collective-permute-start.14
  59.3 2.4 %collective-permute-start.15 = (bf16[640,128]{1,0:T(8,128)(2,1)S(1)}, bf16[640,128]{1,0:T(8,128)(2,1)S(1)}, u32[]{:S(2)}, u32[]{:S(2)}) collective-permute-start(bf16[640,128]{1,0:T(8,128)(2,1)S(1)} %get-tuple-element.82), channel_id=1, source_target_pairs={{0,4},{1,5},{2,6},{3,7},{4,0},{5,1},{6,2},{7,3},{8,12},{9,13},{10,... | collective-permute-start | bytes 491528 | tf_op jit(solution)/shard_map/ppermute | solution.py:41
  61.7 2.0 %collective-permute-start.16 = (bf16[640,128]{1,0:T(8,128)(2,1)S(1)}, bf16[640,128]{1,0:T(8,128)(2,1)S(1)}, u32[]{:S(2)}, u32[]{:S(2)}) collective-permute-start(bf16[640,128]{1,0:T(8,128)(2,1)S(1)} %get-tuple-element.83), channel_id=1, source_target_pairs={{0,6},{1,7},{2,0},{3,1},{4,2},{5,3},{6,4},{7,5},{8,14},{9,15},{10,... | collective-permute-start | bytes 491528 | tf_op jit(solution)/shard_map/ppermute | solution.py:41
  63.7 0.7 collective-permute-done.14.refs_5_
  64.4 2.9 %collective-permute-done.15.refs_6_ = bf16[640,128]{1,0:T(8,128)(2,1)S(1)} collective-permute-done((bf16[640,128]{1,0:T(8,128)(2,1)S(1)}, bf16[640,128]{1,0:T(8,128)(2,1)S(1)}, u32[]{:S(2)}, u32[]{:S(2)}) %collective-permute-start.15) | collective-permute-done | bytes 163872 | tf_op jit(solution)/shard_map/ppermute | solution.py:41
  67.3 0.9 collective-permute-done.16.refs_7_
  68.2 0.8 context.1
  69.0 6.0 %collective-permute-start.17 = (bf16[64,640]{1,0:T(8,128)(2,1)S(1)}, bf16[64,640]{1,0:T(8,128)(2,1)S(1)}, u32[]{:S(2)}, u32[]{:S(2)}) collective-permute-start(bf16[64,640]{1,0:T(8,128)(2,1)S(1)} %get-tuple-element.84), channel_id=1, source_target_pairs={{0,0},{1,1},{2,2},{3,3},{4,4},{5,5},{6,6},{7,7},{8,32},{9,33},{10,... | collective-permute-start | bytes 245768 | tf_op jit(solution)/shard_map/ppermute | solution.py:41
  75.0 2.5 %collective-permute-start.18 = (bf16[64,640]{1,0:T(8,128)(2,1)S(1)}, bf16[64,640]{1,0:T(8,128)(2,1)S(1)}, u32[]{:S(2)}, u32[]{:S(2)}) collective-permute-start(bf16[64,640]{1,0:T(8,128)(2,1)S(1)} %get-tuple-element.85), channel_id=1, source_target_pairs={{0,1},{1,0},{2,3},{3,2},{4,5},{5,4},{6,7},{7,6},{8,33},{9,32},{10,... | collective-permute-start | bytes 245768 | tf_op jit(solution)/shard_map/ppermute | solution.py:41
  77.5 18.8 %all-to-all-done = bf16[8,5,64,512]{3,2,1,0:T(8,128)(2,1)S(1)} async-done(((bf16[8,5,64,512]{3,2,1,0:T(8,128)(2,1)}), bf16[8,5,64,512]{3,2,1,0:T(8,128)(2,1)S(1)}, u32[]{:S(2)}, u32[]{:S(2)}) %all-to-all-start) | async-done | bytes 2621472 | tf_op jit(solution)/shard_map/all_to_all | solution.py:494
  96.3 10.4 %pair.1 = bf16[64,64,512]{2,1,0:T(8,128)(2,1)} custom-call(bf16[40,64,512]{2,1,0:T(8,128)(2,1)S(1)} %bitcast.7, bf16[1024,336]{1,0:T(8,128)(2,1)} %get-tuple-element.87.first, bf16[512,512]{1,0:T(8,128)(2,1)} %get-tuple-element.88.second, f32[512,128]{1,0:T(8,128)} %get-tuple-element.89.second_bias, bf16[64,64,512]{2,1,0:T(8,128)(2,1)} %relative.1), custom_call_target="tpu_custom_call" | custom-call | flops 5000000000 | bytes 14000000 | tf_op jit(solution)/shard_map/pair/pallas_call | solution.py:511
  106.7 0.7 maximum_select_fusion.1
  (22 shorter events, 0.1 us)
Async XLA Ops:
  0.6 12.6 %copy-start.2 = (f32[128]{0:T(128)S(1)}, f32[128]{0:T(128)}, u32[]{:S(2)}) copy-start(f32[128]{0:T(128)} %param.13) | copy-start | bytes 1540
  0.6 12.7 %copy-start = (bf16[40,128]{1,0:T(8,128)(2,1)S(1)}, bf16[40,128]{1,0:T(8,128)(2,1)}, u32[]{:S(2)}) copy-start(bf16[40,128]{1,0:T(8,128)(2,1)} %first.1) | copy-start | bytes 30724
  1.6 24.4 %copy-start.1 = (s32[4]{0:T(128)S(1)}, s32[4]{0:T(128)}, u32[]{:S(2)}) copy-start(s32[4]{0:T(128)} %lengths.1) | copy-start | bytes 52
  2.7 13.3 %collective-permute-start.1 = (bf16[64,1920]{1,0:T(8,128)(2,1)S(1)}, bf16[64,1920]{1,0:T(8,128)(2,1)S(1)}, u32[]{:S(2)}, u32[]{:S(2)}) collective-permute-start(bf16[64,1920]{1,0:T(8,128)(2,1)S(1)} %broadcast_select_fusion.1), channel_id=1, source_target_pairs={{0,1},{1,0},{2,3},{3,2},{4,5},{5,4},{6,7},{7,6},{8,33},{9,32},{10,... | collective-permute-start | bytes 737288 | tf_op jit(solution)/shard_map/ppermute | solution.py:41
  8.9 7.5 %collective-permute-start = (bf16[64,1920]{1,0:T(8,128)(2,1)S(1)}, bf16[64,1920]{1,0:T(8,128)(2,1)S(1)}, u32[]{:S(2)}, u32[]{:S(2)}) collective-permute-start(bf16[64,1920]{1,0:T(8,128)(2,1)S(1)} %broadcast_select_fusion), channel_id=1, source_target_pairs={{0,0},{1,1},{2,2},{3,3},{4,4},{5,5},{6,6},{7,7},{8,32},{9,33},{10,... | collective-permute-start | bytes 737288 | tf_op jit(solution)/shard_map/ppermute | solution.py:41
  16.5 16.6 %collective-permute-start.4 = (bf16[128,1920]{1,0:T(8,128)(2,1)S(1)}, bf16[128,1920]{1,0:T(8,128)(2,1)S(1)}, u32[]{:S(2)}, u32[]{:S(2)}) collective-permute-start(bf16[128,1920]{1,0:T(8,128)(2,1)S(1)} %maximum_select_fusion.refs_0_), channel_id=1, source_target_pairs={{0,64},{1,65},{2,66},{3,67},{4,68},{5,69},{6,70},{7,71},{8,72},{9,... | collective-permute-start | bytes 1474568 | tf_op jit(solution)/shard_map/ppermute | solution.py:41
  23.2 9.6 %collective-permute-start.3 = (bf16[128,1280]{1,0:T(8,128)(2,1)S(1)}, bf16[128,1280]{1,0:T(8,128)(2,1)S(1)}, u32[]{:S(2)}, u32[]{:S(2)}) collective-permute-start(bf16[128,1280]{1,0:T(8,128)(2,1)S(1)} %slice.39.refs_4_), channel_id=1, source_target_pairs={{0,2},{1,3},{2,4},{3,5},{4,6},{5,7},{6,0},{7,1},{8,10},{9,11},{10,... | collective-permute-start | bytes 983048 | tf_op jit(solution)/shard_map/ppermute | solution.py:41
  24.5 8.6 %collective-permute-start.2 = (bf16[128,1280]{1,0:T(8,128)(2,1)S(1)}, bf16[128,1280]{1,0:T(8,128)(2,1)S(1)}, u32[]{:S(2)}, u32[]{:S(2)}) collective-permute-start(bf16[128,1280]{1,0:T(8,128)(2,1)S(1)} %slice.39.refs_4_), channel_id=1, source_target_pairs={{0,6},{1,7},{2,0},{3,1},{4,2},{5,3},{6,4},{7,5},{8,14},{9,15},{10,... | collective-permute-start | bytes 983048 | tf_op jit(solution)/shard_map/ppermute | solution.py:41
  33.1 3.3 %collective-permute-start.5 = (bf16[128,1920]{1,0:T(8,128)(2,1)S(1)}, bf16[128,1920]{1,0:T(8,128)(2,1)S(1)}, u32[]{:S(2)}, u32[]{:S(2)}) collective-permute-start(bf16[128,1920]{1,0:T(8,128)(2,1)S(1)} %maximum_select_fusion.refs_0_), channel_id=1, source_target_pairs={{0,32},{1,33},{2,34},{3,35},{4,36},{5,37},{6,38},{7,39},{8,40},{9,... | collective-permute-start | bytes 1474568 | tf_op jit(solution)/shard_map/ppermute | solution.py:41
  33.1 3.3 %collective-permute-start.6 = (bf16[128,1920]{1,0:T(8,128)(2,1)S(1)}, bf16[128,1920]{1,0:T(8,128)(2,1)S(1)}, u32[]{:S(2)}, u32[]{:S(2)}) collective-permute-start(bf16[128,1920]{1,0:T(8,128)(2,1)S(1)} %collective-permute-done.4.refs_2_), channel_id=1, source_target_pairs={{0,32},{1,33},{2,34},{3,35},{4,36},{5,37},{6,38},{7,39},{8,40},{9,... | collective-permute-start | bytes 1474568 | tf_op jit(solution)/shard_map/ppermute | solution.py:41
  33.7 6.4 %collective-permute-start.8 = (bf16[64,1280]{1,0:T(8,128)(2,1)S(1)}, bf16[64,1280]{1,0:T(8,128)(2,1)S(1)}, u32[]{:S(2)}, u32[]{:S(2)}) collective-permute-start(bf16[64,1280]{1,0:T(8,128)(2,1)S(1)} %slice.41), channel_id=1, source_target_pairs={{0,6},{1,7},{2,0},{3,1},{4,2},{5,3},{6,4},{7,5},{8,14},{9,15},{10,... | collective-permute-start | bytes 491528 | tf_op jit(solution)/shard_map/ppermute | solution.py:41
  36.4 6.7 %collective-permute-start.7 = (bf16[64,1280]{1,0:T(8,128)(2,1)S(1)}, bf16[64,1280]{1,0:T(8,128)(2,1)S(1)}, u32[]{:S(2)}, u32[]{:S(2)}) collective-permute-start(bf16[64,1280]{1,0:T(8,128)(2,1)S(1)} %slice.40), channel_id=1, source_target_pairs={{0,2},{1,3},{2,4},{3,5},{4,6},{5,7},{6,0},{7,1},{8,10},{9,11},{10,... | collective-permute-start | bytes 491528 | tf_op jit(solution)/shard_map/ppermute | solution.py:41
  45.0 2.7 %collective-permute-start.9 = (f32[16,512]{1,0:T(8,128)S(1)}, f32[16,512]{1,0:T(8,128)S(1)}, u32[]{:S(2)}, u32[]{:S(2)}) collective-permute-start(f32[16,512]{1,0:T(8,128)S(1)} %get-tuple-element.74.one), channel_id=1, source_target_pairs={{0,32},{1,33},{2,34},{3,35},{4,36},{5,37},{6,38},{7,39},{8,40},{9,... | collective-permute-start | bytes 98312 | tf_op jit(solution)/shard_map/ppermute | solution.py:41
  46.2 3.9 %collective-permute-start.13 = (f32[16,512]{1,0:T(8,128)S(1)}, f32[16,512]{1,0:T(8,128)S(1)}, u32[]{:S(2)}, u32[]{:S(2)}) collective-permute-start(f32[16,512]{1,0:T(8,128)S(1)} %get-tuple-element.75.refs_2_.refs_0_), channel_id=1, source_target_pairs={{0,6},{1,7},{2,0},{3,1},{4,2},{5,3},{6,4},{7,5},{8,14},{9,15},{10,... | collective-permute-start | bytes 98312 | tf_op jit(solution)/shard_map/ppermute | solution.py:41
  46.2 4.3 %collective-permute-start.12 = (f32[16,512]{1,0:T(8,128)S(1)}, f32[16,512]{1,0:T(8,128)S(1)}, u32[]{:S(2)}, u32[]{:S(2)}) collective-permute-start(f32[16,512]{1,0:T(8,128)S(1)} %get-tuple-element.75.refs_2_.refs_0_), channel_id=1, source_target_pairs={{0,4},{1,5},{2,6},{3,7},{4,0},{5,1},{6,2},{7,3},{8,12},{9,13},{10,... | collective-permute-start | bytes 98312 | tf_op jit(solution)/shard_map/ppermute | solution.py:41
  46.8 4.9 %collective-permute-start.11 = (f32[16,512]{1,0:T(8,128)S(1)}, f32[16,512]{1,0:T(8,128)S(1)}, u32[]{:S(2)}, u32[]{:S(2)}) collective-permute-start(f32[16,512]{1,0:T(8,128)S(1)} %get-tuple-element.75.refs_2_.refs_0_), channel_id=1, source_target_pairs={{0,2},{1,3},{2,4},{3,5},{4,6},{5,7},{6,0},{7,1},{8,10},{9,11},{10,... | collective-permute-start | bytes 98312 | tf_op jit(solution)/shard_map/ppermute | solution.py:41
  47.7 3.9 %collective-permute-start.10 = (f32[16,512]{1,0:T(8,128)S(1)}, f32[16,512]{1,0:T(8,128)S(1)}, u32[]{:S(2)}, u32[]{:S(2)}) collective-permute-start(f32[16,512]{1,0:T(8,128)S(1)} %merge.1.refs_0_), channel_id=1, source_target_pairs={{0,64},{1,65},{2,66},{3,67},{4,68},{5,69},{6,70},{7,71},{8,72},{9,... | collective-permute-start | bytes 98312 | tf_op jit(solution)/shard_map/ppermute | solution.py:41
  54.3 42.0 %all-to-all-start = ((bf16[8,5,64,512]{3,2,1,0:T(8,128)(2,1)}), bf16[8,5,64,512]{3,2,1,0:T(8,128)(2,1)S(1)}, u32[]{:S(2)}, u32[]{:S(2)}) async-start(bf16[8,5,64,512]{3,2,1,0:T(8,128)(2,1)} %symmetric.1), calls=%async_computation | async-start | bytes 5242880 | tf_op jit(solution)/shard_map/all_to_all | solution.py:494
  59.0 5.4 %collective-permute-start.14 = (bf16[640,128]{1,0:T(8,128)(2,1)S(1)}, bf16[640,128]{1,0:T(8,128)(2,1)S(1)}, u32[]{:S(2)}, u32[]{:S(2)}) collective-permute-start(bf16[640,128]{1,0:T(8,128)(2,1)S(1)} %get-tuple-element.81), channel_id=1, source_target_pairs={{0,2},{1,3},{2,4},{3,5},{4,6},{5,7},{6,0},{7,1},{8,10},{9,11},{10,... | collective-permute-start | bytes 491528 | tf_op jit(solution)/shard_map/ppermute | solution.py:41
  59.3 8.0 %collective-permute-start.15 = (bf16[640,128]{1,0:T(8,128)(2,1)S(1)}, bf16[640,128]{1,0:T(8,128)(2,1)S(1)}, u32[]{:S(2)}, u32[]{:S(2)}) collective-permute-start(bf16[640,128]{1,0:T(8,128)(2,1)S(1)} %get-tuple-element.82), channel_id=1, source_target_pairs={{0,4},{1,5},{2,6},{3,7},{4,0},{5,1},{6,2},{7,3},{8,12},{9,13},{10,... | collective-permute-start | bytes 491528 | tf_op jit(solution)/shard_map/ppermute | solution.py:41
  61.7 6.5 %collective-permute-start.16 = (bf16[640,128]{1,0:T(8,128)(2,1)S(1)}, bf16[640,128]{1,0:T(8,128)(2,1)S(1)}, u32[]{:S(2)}, u32[]{:S(2)}) collective-permute-start(bf16[640,128]{1,0:T(8,128)(2,1)S(1)} %get-tuple-element.83), channel_id=1, source_target_pairs={{0,6},{1,7},{2,0},{3,1},{4,2},{5,3},{6,4},{7,5},{8,14},{9,15},{10,... | collective-permute-start | bytes 491528 | tf_op jit(solution)/shard_map/ppermute | solution.py:41
  69.0 37.7 %collective-permute-start.17 = (bf16[64,640]{1,0:T(8,128)(2,1)S(1)}, bf16[64,640]{1,0:T(8,128)(2,1)S(1)}, u32[]{:S(2)}, u32[]{:S(2)}) collective-permute-start(bf16[64,640]{1,0:T(8,128)(2,1)S(1)} %get-tuple-element.84), channel_id=1, source_target_pairs={{0,0},{1,1},{2,2},{3,3},{4,4},{5,5},{6,6},{7,7},{8,32},{9,33},{10,... | collective-permute-start | bytes 245768 | tf_op jit(solution)/shard_map/ppermute | solution.py:41
  75.0 31.7 %collective-permute-start.18 = (bf16[64,640]{1,0:T(8,128)(2,1)S(1)}, bf16[64,640]{1,0:T(8,128)(2,1)S(1)}, u32[]{:S(2)}, u32[]{:S(2)}) collective-permute-start(bf16[64,640]{1,0:T(8,128)(2,1)S(1)} %get-tuple-element.85), channel_id=1, source_target_pairs={{0,1},{1,0},{2,3},{3,2},{4,5},{5,4},{6,7},{7,6},{8,33},{9,32},{10,... | collective-permute-start | bytes 245768 | tf_op jit(solution)/shard_map/ppermute | solution.py:41
